TPU v7x, 512 devices: a whole 4x8x8 slice. The times are simulated.
512 devices in a mesh: dp: 2 (over z_hi), context: 32 (over x, z_lo, core), tensor: 8 (over y).
Axes of the slice: x: 4, y: 8, z: 8 (z_hi: 2, z_lo: 4; z = z_hi * 4 + z_lo), core: 2. Of those that a mesh axis runs over, the one named last changes fastest.
Arguments:
- query_branch: bfloat16 [2, 4096, 4096], P('dp', 'context', 'tensor'), may hold values from -6 to 6
- key_branch: bfloat16 [2, 4096, 4096], P('dp', 'context', 'tensor'), may hold values from -6 to 6
- value_branch: bfloat16 [2, 4096, 4096], P('dp', 'context', 'tensor'), may hold values from -6 to 6
- cotangent: bfloat16 [2, 4096, 8192], P('dp', ('context', 'tensor')), may hold values from -6 to 6
- out_weight: bfloat16 [8192, 4096], P(('dp', 'context'), 'tensor'), may hold values from -0.0625 to 0.0625
- filters: bfloat16 [256, 128], P('tensor'), may hold values from -0.5 to 0.5
Outputs:
- query_grad: bfloat16 [2, 4096, 4096], P('dp', 'context', 'tensor')
- key_grad: bfloat16 [2, 4096, 4096], P('dp', 'context', 'tensor')
- value_grad: bfloat16 [2, 4096, 4096], P('dp', 'context', 'tensor')
- filter_grad: float32 [256, 128], P('tensor')
All inputs are finite; a program needn't handle non-finite values.
Results may differ from a plain program's by a relative error of at most 0.0051.
Values may be sent and summed in bfloat16 or wider, within the bound.
No kernel may reach another device: no remote copies, remote signals or barrier semaphores. Data moves between devices by JAX's collectives and lax.ppermute only.
A program may use at most 64 MiB of HBM per device.

v0:
```python
import math

import jax
import jax.numpy as jnp
from jax import lax
from jax.sharding import PartitionSpec as P

GROUP = 16
TAPS = 128


def from_behind(block, axis, distance):
    devices = range(lax.axis_size(axis))
    route = [(i - distance, i) for i in devices if i - distance in devices]
    return lax.ppermute(block, axis, route)


def toeplitz_table(filters):
    groups = filters.shape[0]
    taps = filters.shape[1]
    reversed_taps = filters[:, ::-1]
    period = jnp.concatenate([reversed_taps, jnp.zeros((groups, taps + 1), filters.dtype)], 1)
    tiled = jnp.tile(period, (1, taps))
    flat = jnp.concatenate([jnp.zeros((groups, 1), filters.dtype), tiled], 1)[:, : 2 * taps * taps]
    return flat.reshape(groups, taps, 2 * taps)


def lag_totals(outer):
    groups = outer.shape[0]
    taps = outer.shape[1]
    flat = outer.reshape(groups, taps * 2 * taps)
    flat = jnp.concatenate([flat, jnp.zeros((groups, taps), jnp.float32)], 1)
    skewed = flat.reshape(groups, taps, 2 * taps + 1)
    column_sums = jnp.sum(skewed, axis=1)
    return column_sums[:, taps:0:-1]


def windows_of(rows, blocks, taps, groups, group):
    first = rows[: blocks * taps].reshape(blocks, taps, groups, group)
    second = rows[taps:].reshape(blocks, taps, groups, group)
    return jnp.concatenate([first, second], 1)


def local(query_branch, key_branch, value_branch, cotangent, out_weight, filters):
    tokens = query_branch.shape[1]
    width = query_branch.shape[2]
    groups = filters.shape[0]
    blocks = tokens // TAPS
    keys = key_branch[0].astype(jnp.float32)
    values = value_branch[0].astype(jnp.float32)
    mixed = (keys * values).astype(jnp.bfloat16)
    before = from_behind(mixed[tokens - (TAPS - 1) :], "context", 1)
    rows = jnp.concatenate([jnp.zeros((1, width), jnp.bfloat16), before, mixed], 0)
    windows = windows_of(rows, blocks, TAPS, groups, GROUP)
    table = toeplitz_table(filters)
    conv = jnp.einsum("gim,bmgs->bigs", table, windows, preferred_element_type=jnp.float32).reshape(
        tokens, width
    )
    weights = lax.all_gather(out_weight, ("dp", "context"), axis=0, tiled=True)
    branch_grad = jnp.dot(
        lax.all_gather(cotangent, "tensor", axis=1, tiled=True)[0],
        weights,
        preferred_element_type=jnp.float32,
    )[None][0]
    query_grad = (branch_grad * conv).astype(jnp.bfloat16)
    conv_grad = (branch_grad * query_branch[0].astype(jnp.float32)).astype(jnp.bfloat16)
    after = from_behind(conv_grad[: TAPS - 1], "context", -1)
    grad_rows = jnp.concatenate([conv_grad, after, jnp.zeros((1, width), jnp.bfloat16)], 0)
    grad_windows = windows_of(grad_rows, blocks, TAPS, groups, GROUP)
    upper = jnp.concatenate([table[:, :, TAPS:], table[:, :, :TAPS]], 1)
    mixed_grad = jnp.einsum(
        "gim,bigs->bmgs", upper, grad_windows, preferred_element_type=jnp.float32
    ).reshape(tokens, width)
    key_grad = (mixed_grad * values).astype(jnp.bfloat16)
    value_grad = (mixed_grad * keys).astype(jnp.bfloat16)
    outer = jnp.einsum(
        "bigs,bmgs->gim",
        conv_grad.reshape(blocks, TAPS, groups, GROUP),
        windows,
        preferred_element_type=jnp.float32,
    )
    local_lags = lag_totals(outer)
    lag_sum = lax.psum(local_lags, ("dp", "context"))
    scale = 1.0 / math.sqrt(lax.axis_size("dp") * lax.axis_size("context") * tokens * GROUP)
    filter_grad = lag_sum * scale
    return (query_grad[None], key_grad[None], value_grad[None], filter_grad)


def solution(mesh):
    placed = (
        P("dp", "context", "tensor"),
        P("dp", "context", "tensor"),
        P("dp", "context", "tensor"),
        P("dp", ("context", "tensor"), None),
        P(("dp", "context"), "tensor"),
        P("tensor", None),
    )
    return jax.shard_map(
        local,
        mesh=mesh,
        in_specs=placed,
        out_specs=(
            P("dp", "context", "tensor"),
            P("dp", "context", "tensor"),
            P("dp", "context", "tensor"),
            P("tensor", None),
        ),
        check_vma=False,
    )
```

profile of v0, /device:TPU:1, one launch (start us, length us, event | category | flops | bytes accessed | tf_op | source)
XLA Modules:
  0.0 470.8 jit_solution(5258206049970730859)
XLA Ops:
  7.2 0.7 all-gather.3.cloned.1.call-update
  7.9 0.7 all-gather.5.cloned.1.call-update
  8.6 0.8 rev.6
  9.7 4.4 tile.10
  14.2 2.2 pad_slice_fusion
  16.9 38.6 %all-gather.3.cloned.1.call-done = bf16[1,128,8192]{2,1,0:T(8,128)(2,1)} async-done(((bf16[1,16,8192]{2,1,0:T(8,128)(2,1)}), bf16[1,128,8192]{2,1,0:T(8,128)(2,1)}) %all-gather.3.cloned.1.call-update) | async-done | bytes 2097168 | tf_op jit(solution)/shard_map/all_gather | solution.py:61
  55.5 128.9 %all-gather.5.cloned.1.call-done = bf16[8192,512]{1,0:T(8,128)(2,1)} async-done(((bf16[128,512]{1,0:T(8,128)(2,1)}), bf16[8192,512]{1,0:T(8,128)(2,1)}) %all-gather.5.cloned.1.call-update) | async-done | bytes 8388624 | tf_op jit(solution)/shard_map/all_gather | solution.py:59
  184.4 5.3 %fusion.11 = (bf16[128,512]{1,0:T(8,128)(2,1)S(1)}, f32[128,512]{1,0:T(8,128)S(1)}) fusion(bf16[1,128,512]{2,1,0:T(8,128)(2,1)S(1)} %copy-done, bf16[8192,512]{1,0:T(8,128)(2,1)} %all-gather.5.cloned.1.call-done, bf16[1,128,8192]{2,1,0:T(8,128)(2,1)} %all-gather.3.cloned.1.call-done), kind=kOutput, calls=%fused_computation.18 | convolution fusion | flops 1073938432 | bytes 11010048 | tf_op jit(solution)/shard_map/dot_general | solution.py:60
  189.7 2.2 collective-permute-start.1
  191.9 1.9 fusion.18
  194.0 2.1 collective-permute-done.1
  196.3 2.0 fusion
  198.4 0.8 fusion.6
  199.2 1.9 collective-permute-start
  201.3 1.8 collective-permute-done
  203.3 0.6 fusion.13
  204.1 0.7 fusion.12
  204.9 2.4 copy.29
  207.3 2.3 concatenate.31
  209.6 8.0 %reshape.100 = f32[32,128,257]{2,1,0:T(8,128)} reshape(f32[32,32896]{1,0:T(8,128)} %concatenate.31) | data formatting | bytes 8421376 | tf_op jit(solution)/shard_map/reshape | solution.py:33
  217.6 3.3 reduce_sum.9
  221.0 241.6 %psum.7 = f32[32,128]{1,0:T(8,128)S(1)} all-reduce(f32[32,128]{1,0:T(8,128)S(1)} %rev.7), channel_id=1, replica_groups=mesh['dp'=2,'context'=32,'tensor'=8] {'dp','context'}, use_global_device_ids=true, to_apply=%region_1.0 | all-reduce | flops 4096 | bytes 32768 | tf_op jit(solution)/shard_map/psum | solution.py:83
  462.7 0.6 broadcast_multiply_fusion
  463.3 0.7 fusion.14
  (22 shorter events, 2.0 us)
Async XLA Ops:
  7.2 48.3 %all-gather.3.cloned.1.call-start = ((), (), s32[]{:S(2)}) async-start(), calls=%async_computation | async-start | bytes 2359296 | tf_op jit(solution)/shard_map/all_gather | solution.py:61
  7.9 176.5 %all-gather.5.cloned.1.call-start = ((), (), s32[]{:S(2)}) async-start(), calls=%async_computation.1 | async-start | bytes 8519680 | tf_op jit(solution)/shard_map/all_gather | solution.py:59
  16.4 168.1 %copy-start = (bf16[1,128,512]{2,1,0:T(8,128)(2,1)S(1)}, bf16[1,128,512]{2,1,0:T(8,128)(2,1)}, u32[]{:S(2)}) copy-start(bf16[1,128,512]{2,1,0:T(8,128)(2,1)} %param.6) | copy-start | bytes 393220
  189.7 6.4 %collective-permute-start.1 = (bf16[127,512]{1,0:T(8,128)(2,1)S(1)}, bf16[127,512]{1,0:T(8,128)(2,1)S(1)}, u32[]{:S(2)}, u32[]{:S(2)}) collective-permute-start(bf16[127,512]{1,0:T(8,128)(2,1)S(1)} %bitcast.52), channel_id=1, source_target_pairs={{8,0},{16,8},{24,16},{32,24},{40,32},{48,40},{56,48},{64,56},{72,6... | collective-permute-start | bytes 390152 | tf_op jit(solution)/shard_map/ppermute | solution.py:15
  196.3 2.1 copy-start.1
  196.3 2.1 copy-start.2
  199.2 3.9 collective-permute-start
Sparse Core Ops, SparseCore 0:
  10.1 45.3 all-gather.2
  57.7 126.7 all-gather.4
where the time goes:
time: 475 us; the launch traced here: 471 us
  blocking collectives  242 us (51%)
  waiting for transfers between devices  173 us (36%)
  local copies, waits for them, and re-layouts  24 us (5%)
  between operations  14.2 us (3%)
  matrix products  8.63 us (2%)
  other arithmetic  5.37 us (1%)
    psum x1, blocking collectives, local(): lag_sum = lax.psum(local_lags, ('dp', 'context'))  242 us
    all_gather x1, waiting for transfers between devices, local(): weights = lax.all_gather(out_weight, ('dp', 'context'), axis=0, tiled=True)  129 us
    all_gather x1, waiting for transfers between devices, local(): lax.all_gather(cotangent, 'tensor', axis=1, tiled=True)[0]  38.6 us
  transfers between devices with their start and end apart: 4, of which 4 were waited for; matrix products, arithmetic and copies ran while one was open for 2% of the time, Pallas kernels for 0%

commit v1 on v0

v1 whole, which is shorter than its diff:
```python
import math

import jax
import jax.numpy as jnp
from jax import lax
from jax.sharding import Mesh, PartitionSpec as P

GROUP = 16
TAPS = 128
F32 = jnp.float32
BF16 = jnp.bfloat16

X = ("xh", "xp")
Z = ("zh", "zl")
CONTEXT = ("xh", "xp", "zl", "co")


def swap(block, axis):
    return lax.ppermute(block, axis, [(0, 1), (1, 0)])


def from_behind(block, distance):
    n = lax.axis_size(CONTEXT)
    route = [(i - distance, i) for i in range(n) if 0 <= i - distance < n]
    return lax.ppermute(block, CONTEXT, route)


def exchange_copies(block, axes):
    n = lax.axis_size(axes)
    copies = jnp.broadcast_to(block[None], (n,) + block.shape)
    return lax.all_to_all(copies, axes, split_axis=0, concat_axis=0)


def toeplitz_table(filters):
    groups = filters.shape[0]
    taps = filters.shape[1]
    reversed_taps = filters[:, ::-1]
    period = jnp.concatenate([reversed_taps, jnp.zeros((groups, taps + 1), filters.dtype)], 1)
    tiled = jnp.tile(period, (1, taps))
    flat = jnp.concatenate([jnp.zeros((groups, 1), filters.dtype), tiled], 1)[:, : 2 * taps * taps]
    return flat.reshape(groups, taps, 2 * taps)


def lag_totals(outer):
    groups = outer.shape[0]
    taps = outer.shape[1]
    flat = outer.reshape(groups, taps * 2 * taps)
    flat = jnp.concatenate([flat, jnp.zeros((groups, taps), F32)], 1)
    skewed = flat.reshape(groups, taps, 2 * taps + 1)
    column_sums = jnp.sum(skewed, axis=1)
    return column_sums[:, taps:0:-1]


def windows_of(rows, blocks, taps, groups, group):
    first = rows[: blocks * taps].reshape(blocks, taps, groups, group)
    second = rows[taps:].reshape(blocks, taps, groups, group)
    return jnp.concatenate([first, second], 1)


def branch_gradient(cotangent, out_weight):
    rows = cotangent.shape[0]
    width = out_weight.shape[1]
    depth = out_weight.shape[0]
    parts = cotangent.reshape(rows, 2, 4, 4, 2, depth).transpose(2, 4, 0, 1, 3, 5)
    parts = parts.reshape(8, rows, 8 * depth)
    parts = lax.all_to_all(parts, X + ("co",), split_axis=0, concat_axis=0)
    gathered = lax.all_gather(parts, "y", axis=0)
    weights = exchange_copies(out_weight, Z).reshape(8 * depth, width)
    partial = jnp.einsum("ybrk,kn->byrn", gathered, weights, preferred_element_type=F32)
    partial = partial.reshape(4, 2, 8 * rows, width)
    co = lax.axis_index("co")
    mine = lax.dynamic_index_in_dim(partial, co, 1, keepdims=False)
    other = lax.dynamic_index_in_dim(partial, 1 - co, 1, keepdims=False)
    summed = (mine + swap(other, "co")).astype(BF16)
    terms = lax.all_to_all(summed, X, split_axis=0, concat_axis=0)
    return jnp.sum(terms.astype(F32), axis=0)


def local(query_branch, key_branch, value_branch, cotangent, out_weight, filters):
    tokens = query_branch.shape[1]
    width = query_branch.shape[2]
    groups = filters.shape[0]
    blocks = tokens // TAPS
    keys = key_branch[0].astype(F32)
    values = value_branch[0].astype(F32)
    mixed = (keys * values).astype(BF16)
    before = from_behind(mixed[tokens - (TAPS - 1) :], 1)
    rows = jnp.concatenate([jnp.zeros((1, width), BF16), before, mixed], 0)
    windows = windows_of(rows, blocks, TAPS, groups, GROUP)
    table = toeplitz_table(filters)
    conv = jnp.einsum("gim,bmgs->bigs", table, windows, preferred_element_type=F32).reshape(tokens, width)
    branch_grad = branch_gradient(cotangent[0], out_weight)
    query_grad = (branch_grad * conv).astype(BF16)
    conv_grad = (branch_grad * query_branch[0].astype(F32)).astype(BF16)
    after = from_behind(conv_grad[: TAPS - 1], -1)
    outer = jnp.einsum(
        "bigs,bmgs->gim",
        conv_grad.reshape(blocks, TAPS, groups, GROUP),
        windows,
        preferred_element_type=F32,
    )
    lags = lag_totals(outer)
    lags = lags + swap(lags, "co")
    lag_sum = jnp.sum(exchange_copies(lags, ("zh", "xh", "xp", "zl")), axis=0)
    grad_rows = jnp.concatenate([conv_grad, after, jnp.zeros((1, width), BF16)], 0)
    grad_windows = windows_of(grad_rows, blocks, TAPS, groups, GROUP)
    upper = jnp.concatenate([table[:, :, TAPS:], table[:, :, :TAPS]], 1)
    mixed_grad = jnp.einsum("gim,bigs->bmgs", upper, grad_windows, preferred_element_type=F32).reshape(tokens, width)
    key_grad = (mixed_grad * values).astype(BF16)
    value_grad = (mixed_grad * keys).astype(BF16)
    scale = 1.0 / math.sqrt(2 * lax.axis_size(CONTEXT) * tokens * GROUP)
    filter_grad = lag_sum * scale
    return (query_grad[None], key_grad[None], value_grad[None], filter_grad)


def solution(mesh):
    fine = Mesh(mesh.devices.reshape(2, 2, 2, 4, 2, 8), ("zh", "xh", "xp", "zl", "co", "y"))
    branch = P("zh", CONTEXT, "y")
    return jax.shard_map(
        local,
        mesh=fine,
        in_specs=(
            branch,
            branch,
            branch,
            P("zh", CONTEXT + ("y",), None),
            P(("zh",) + CONTEXT, "y"),
            P("y", None),
        ),
        out_specs=(branch, branch, branch, P("y", None)),
        check_vma=False,
    )
```

time: 475 us -> 166 us (0.35)
  blocking collectives: 242 us -> 16.4 us
  waiting for transfers between devices: 173 us -> 55.2 us
  starting transfers between devices: 4.17 us -> 35.8 us
    psum x1 -> x0, blocking collectives: 242 us -> none  [local(): lag_sum = lax.psum(local_lags, ('dp', 'context'))]
    all_gather x2 -> x1, waiting for transfers between devices: 168 us -> 2.82 us  [branch_gradient(): gathered = lax.all_gather(parts, 'y', axis=0)]
    all_to_all x0 -> x3, waiting for transfers between devices: none -> 45.3 us  [the longest x2 40.6 us: exchange_copies(): return lax.all_to_all(copies, axes, split_axis=0, concat_axis=0)]
    all_to_all x0 -> x3, starting transfers between devices: none -> 22.3 us  [the longest x2 18 us: exchange_copies(): return lax.all_to_all(copies, axes, split_axis=0, concat_axis=0)]
    all_to_all x0 -> x1, blocking collectives: none -> 16.4 us  [branch_gradient(): parts = lax.all_to_all(parts, X + ('co',), split_axis=0, concat_axis=0)]
    ppermute x2 -> x4, starting transfers between devices: 4.09 us -> 13.5 us  [the longest x2 8.15 us: swap(): return lax.ppermute(block, axis, [(0, 1), (1, 0)])]
  transfers between devices with their start and end apart: 4 -> 8, of which waited for: 4 -> 8; matrix products, arithmetic and copies ran while one was open for 2% -> 8% of each run, Pallas kernels for 0% -> 0%
where the time goes in v1:
time: 166 us; the launch traced here: 165 us
  waiting for transfers between devices  55.2 us (33%)
  starting transfers between devices  35.8 us (22%)
  local copies, waits for them, and re-layouts  28.4 us (17%)
  blocking collectives  16.4 us (10%)
  between operations  14.3 us (9%)
  other arithmetic  8.68 us (5%)
  matrix products  6.52 us (4%)
    all_to_all x2, waiting for transfers between devices, exchange_copies(): return lax.all_to_all(copies, axes, split_axis=0, concat_axis=0)  40.6 us
    all_to_all x2, starting transfers between devices, exchange_copies(): return lax.all_to_all(copies, axes, split_axis=0, concat_axis=0)  18 us
    all_to_all x1, blocking collectives, branch_gradient(): parts = lax.all_to_all(parts, X + ('co',), split_axis=0, concat_axis=0)  16.4 us
    ppermute x2, starting transfers between devices, swap(): return lax.ppermute(block, axis, [(0, 1), (1, 0)])  8.15 us
    reshape x1, local copies, waits for them, and re-layouts, lag_totals(): skewed = flat.reshape(groups, taps, 2 * taps + 1)  7.97 us
    ppermute x2, waiting for transfers between devices, from_behind(): return lax.ppermute(block, CONTEXT, route)  5.38 us
    ppermute x2, starting transfers between devices, from_behind(): return lax.ppermute(block, CONTEXT, route)  5.35 us
    unnamed x14, local copies, waits for them, and re-layouts  4.8 us
  transfers between devices with their start and end apart: 8, of which 8 were waited for; matrix products, arithmetic and copies ran while one was open for 8% of the time, Pallas kernels for 0%

profile of v1, /device:TPU:1, one launch (start us, length us, event | category | flops | bytes accessed | tf_op | source)
XLA Modules:
  0.0 165.3 jit_solution(18295240029669968077)
XLA Ops:
  8.6 16.4 %all_to_all.20 = bf16[8,16,1024]{2,1,0:T(8,128)(2,1)} all-to-all(bf16[8,16,1024]{2,1,0:T(8,128)(2,1)S(1)} %reshape.143), channel_id=1, replica_groups=mesh['zh'=2,'xh'=2,'xp'=2,'zl'=4,'co'=2,'y'=8] {'xh','xp','co'}, dimensions={0} | all-to-all | bytes 524288 | tf_op jit(solution)/shard_map/all_to_all | solution.py:66
  26.2 5.8 %all-to-all-start = ((bf16[8,128,512]{2,1,0:T(8,128)(2,1)}), bf16[8,128,512]{2,1,0:T(8,128)(2,1)}, u32[]{:S(2)}, u32[]{:S(2)}) async-start(bf16[8,128,512]{2,1,0:T(8,128)(2,1)} %broadcast_in_dim.4), calls=%async_computation | async-start | bytes 2097152 | tf_op jit(solution)/shard_map/all_to_all | solution.py:31
  32.4 4.4 %tile.10 = bf16[32,32896]{1,0:T(8,128)(2,1)} reshape(bf16[32,128,257]{2,1,0:T(8,128)(2,1)S(1)} %tile.4) | data formatting | bytes 4210688 | tf_op jit(solution)/shard_map/tile | solution.py:39
  36.8 24.5 %all-to-all-done = bf16[8,128,512]{2,1,0:T(8,128)(2,1)} async-done(((bf16[8,128,512]{2,1,0:T(8,128)(2,1)}), bf16[8,128,512]{2,1,0:T(8,128)(2,1)}, u32[]{:S(2)}, u32[]{:S(2)}) %all-to-all-start) | async-done | bytes 1048608 | tf_op jit(solution)/shard_map/all_to_all | solution.py:31
  61.3 2.8 %all-gather.3.cloned.1.call-done = bf16[64,16,1024]{2,1,0:T(8,128)(2,1)} async-done(((bf16[8,16,1024]{2,1,0:T(8,128)(2,1)}), bf16[64,16,1024]{2,1,0:T(8,128)(2,1)}) %all-gather.3.cloned.1.call-update) | async-done | bytes 2097168 | tf_op jit(solution)/shard_map/all_gather | solution.py:67
  64.1 3.2 %convolution_bitcast_fusion = f32[8,8,16,512]{3,2,0,1:T(8,128)S(1)} fusion(bf16[1024,512,1,1]{1,0,3,2:T(8,128)(2,1)} %bitcast.2, bf16[8,8,16,1024]{3,2,1,0:T(8,128)(2,1)} %bitcast.76), kind=kOutput, calls=%fused_computation.5 | convolution fusion | flops 1073741824 | bytes 5242880 | tf_op jit(solution)/shard_map/ybrk,kn->byrn/dot_general | solution.py:69
  67.7 6.2 %collective-permute-start = (f32[4,128,512]{2,1,0:T(8,128)S(1)}, f32[4,128,512]{2,1,0:T(8,128)}, u32[]{:S(2)}, u32[]{:S(2)}) collective-permute-start(f32[4,128,512]{2,1,0:T(8,128)S(1)} %dynamic-slice_bitcast_fusion), channel_id=1, source_target_pairs={{0,8},{8,0},{1,9},{9,1},{2,10},{10,2},{3,11},{11,3},{4,12},{12,4},... | collective-permute-start | bytes 3145736 | tf_op jit(solution)/shard_map/ppermute | solution.py:19
  73.9 1.9 %pad_slice_fusion = bf16[32,32768]{1,0:T(8,128)(2,1)} fusion(bf16[32,32896]{1,0:T(8,128)(2,1)S(1)} %copy-done), kind=kLoop, calls=%fused_computation | loop fusion | bytes 4202496 | tf_op jit(solution)/shard_map/slice | solution.py:40
  76.3 2.2 %fusion.4 = bf16[4,128,512]{2,1,0:T(8,128)(2,1)} fusion(f32[4,128,512]{2,1,0:T(8,128)} %collective-permute-done, f32[4,2,128,512]{3,2,1,0:T(8,128)S(1)} %bitcast.63, s32[]{:T(128)S(6)} %select_n.7), kind=kLoop, calls=%fused_computation.7 | loop fusion | flops 524288 | bytes 2621444 | tf_op jit(solution)/shard_map/convert_element_type | solution.py:74
  78.5 4.2 %all-to-all-start.2 = ((bf16[4,128,512]{2,1,0:T(8,128)(2,1)}), bf16[4,128,512]{2,1,0:T(8,128)(2,1)S(1)}, u32[]{:S(2)}, u32[]{:S(2)}) async-start(bf16[4,128,512]{2,1,0:T(8,128)(2,1)} %fusion.4), calls=%async_computation.2 | async-start | bytes 1048576 | tf_op jit(solution)/shard_map/all_to_all | solution.py:75
  82.9 2.1 %copy.56 = bf16[4,8,128,256]{3,2,1,0:T(8,128)(2,1)S(1)} copy(bf16[4,8,128,256]{3,1,2,0:T(8,128)(2,1)} %bitcast.61) | data formatting | bytes 4194304
  85.0 1.9 %fusion.17 = (bf16[32,128,128]{2,1,0:T(8,128)(2,1)}, bf16[32,128,128]{2,1,0:T(8,128)(2,1)}) fusion(bf16[32,128,256]{2,1,0:T(8,128)(2,1)S(1)} %bitcast.57), kind=kLoop, calls=%fused_computation.35 | loop fusion | bytes 4194304 | tf_op jit(solution)/shard_map/slice | solution.py:107
  86.9 4.7 %all-to-all-done.2 = bf16[4,128,512]{2,1,0:T(8,128)(2,1)S(1)} async-done(((bf16[4,128,512]{2,1,0:T(8,128)(2,1)}), bf16[4,128,512]{2,1,0:T(8,128)(2,1)S(1)}, u32[]{:S(2)}, u32[]{:S(2)}) %all-to-all-start.2) | async-done | bytes 524320 | tf_op jit(solution)/shard_map/all_to_all | solution.py:75
  91.9 3.4 %collective-permute-start.2 = (bf16[127,512]{1,0:T(8,128)(2,1)S(1)}, bf16[127,512]{1,0:T(8,128)(2,1)S(1)}, u32[]{:S(2)}, u32[]{:S(2)}) collective-permute-start(bf16[127,512]{1,0:T(8,128)(2,1)S(1)} %fusion.8), channel_id=1, source_target_pairs={{8,0},{16,8},{24,16},{32,24},{40,32},{48,40},{56,48},{64,56},{72,6... | collective-permute-start | bytes 390152 | tf_op jit(solution)/shard_map/ppermute | solution.py:25
  95.4 3.6 %collective-permute-done.2 = bf16[127,512]{1,0:T(8,128)(2,1)S(1)} collective-permute-done((bf16[127,512]{1,0:T(8,128)(2,1)S(1)}, bf16[127,512]{1,0:T(8,128)(2,1)S(1)}, u32[]{:S(2)}, u32[]{:S(2)}) %collective-permute-start.2) | collective-permute-done | bytes 130080 | tf_op jit(solution)/shard_map/ppermute | solution.py:25
  99.2 2.0 %fusion = f32[32,16,128]{2,1,0:T(8,128)S(1)} fusion(bf16[32,128,128]{2,1,0:T(8,128)(2,1)} %get-tuple-element.9, bf16[32,128,128]{2,1,0:T(8,128)(2,1)} %get-tuple-element.8, bf16[1,128,32,16]{1,3,2,0:T(8,128)(2,1)S(1)} %bitcast.75, bf16[1,128,32,16]{1,3,2,0:T(8,128)(2,1)S(1)} %multiply_convert_fusion.1), kind=kOutput, calls=%fused_computation.1 | convolution fusion | flops 38273024 | bytes 2621440 | tf_op jit(solution)/shard_map/gim,bigs->bmgs/dot_general | solution.py:108
  103.0 1.9 %collective-permute-start.1 = (bf16[127,512]{1,0:T(8,128)(2,1)S(1)}, bf16[127,512]{1,0:T(8,128)(2,1)S(1)}, u32[]{:S(2)}, u32[]{:S(2)}) collective-permute-start(bf16[127,512]{1,0:T(8,128)(2,1)S(1)} %slice_bitcast_fusion), channel_id=1, source_target_pairs={{0,8},{8,16},{16,24},{24,32},{32,40},{40,48},{48,56},{56,64},{64,7... | collective-permute-start | bytes 390152 | tf_op jit(solution)/shard_map/ppermute | solution.py:25
  107.8 2.4 %copy.57 = f32[4,8,128,256]{3,1,2,0:T(8,128)S(1)} copy(f32[4,8,128,256]{3,2,1,0:T(8,128)S(1)} %bitcast.59) | data formatting | bytes 8388608
  110.3 2.3 %concatenate.31 = f32[32,32896]{1,0:T(8,128)} pad(f32[32,32768]{1,0:T(8,128)S(1)} %bitcast.60, f32[]{:T(128)} %constant.24.clone.1), padding=0_0x0_128 | pad | bytes 8404996 | tf_op jit(solution)/shard_map/concatenate | solution.py:48
  112.6 8.0 %reshape.153 = f32[32,128,257]{2,1,0:T(8,128)} reshape(f32[32,32896]{1,0:T(8,128)} %concatenate.31) | data formatting | bytes 8421376 | tf_op jit(solution)/shard_map/reshape | solution.py:49
  120.6 3.3 %reduce_sum.37 = f32[32,257]{1,0:T(8,128)S(1)} reduce(f32[32,128,257]{2,1,0:T(8,128)} %reshape.153, f32[]{:T(128)} %constant.24.clone.1), dimensions={1}, to_apply=%region_1.2 | reduce | flops 1044448 | bytes 4243588 | tf_op jit(solution)/shard_map/reduce_sum | solution.py:50
  124.0 1.9 %collective-permute-start.3 = (f32[32,128]{1,0:T(8,128)S(1)}, f32[32,128]{1,0:T(8,128)S(1)}, u32[]{:S(2)}, u32[]{:S(2)}) collective-permute-start(f32[32,128]{1,0:T(8,128)S(1)} %rev.7), channel_id=1, source_target_pairs={{0,8},{8,0},{1,9},{9,1},{2,10},{10,2},{3,11},{11,3},{4,12},{12,4},... | collective-permute-start | bytes 49160 | tf_op jit(solution)/shard_map/ppermute | solution.py:19
  127.9 12.2 %all-to-all-start.3 = ((f32[32,32,128]{2,1,0:T(8,128)}), f32[32,32,128]{2,1,0:T(8,128)S(1)}, u32[]{:S(2)}, u32[]{:S(2)}) async-start(f32[32,32,128]{2,1,0:T(8,128)} %broadcast_in_dim.5), calls=%async_computation.3 | async-start | bytes 1048576 | tf_op jit(solution)/shard_map/all_to_all | solution.py:31
  141.7 16.1 %all-to-all-done.3 = f32[32,32,128]{2,1,0:T(8,128)S(1)} async-done(((f32[32,32,128]{2,1,0:T(8,128)}), f32[32,32,128]{2,1,0:T(8,128)S(1)}, u32[]{:S(2)}, u32[]{:S(2)}) %all-to-all-start.3) | async-done | bytes 524320 | tf_op jit(solution)/shard_map/all_to_all | solution.py:31
  (48 shorter events, 13.3 us)
Async XLA Ops:
  7.2 17.9 %copy-start.2 = (bf16[128,512]{1,0:T(8,128)(2,1)S(1)}, bf16[128,512]{1,0:T(8,128)(2,1)}, u32[]{:S(2)}) copy-start(bf16[128,512]{1,0:T(8,128)(2,1)} %param.10) | copy-start | bytes 393220
  7.2 56.9 %all-gather.3.cloned.1.call-start = ((), (), s32[]{:S(2)}) async-start(), calls=%async_computation.4 | async-start | bytes 2359296 | tf_op jit(solution)/shard_map/all_gather | solution.py:67
  8.6 23.4 %copy-start.4 = (bf16[32,128]{1,0:T(8,128)(2,1)S(1)}, bf16[32,128]{1,0:T(8,128)(2,1)}, u32[]{:S(2)}) copy-start(bf16[32,128]{1,0:T(8,128)(2,1)} %param.11) | copy-start | bytes 24580
  26.2 35.1 %all-to-all-start = ((bf16[8,128,512]{2,1,0:T(8,128)(2,1)}), bf16[8,128,512]{2,1,0:T(8,128)(2,1)}, u32[]{:S(2)}, u32[]{:S(2)}) async-start(bf16[8,128,512]{2,1,0:T(8,128)(2,1)} %broadcast_in_dim.4), calls=%async_computation | async-start | bytes 2097152 | tf_op jit(solution)/shard_map/all_to_all | solution.py:31
  67.3 6.7 %copy-start = (bf16[32,32896]{1,0:T(8,128)(2,1)S(1)}, bf16[32,32896]{1,0:T(8,128)(2,1)}, u32[]{:S(2)}) copy-start(bf16[32,32896]{1,0:T(8,128)(2,1)} %tile.10) | copy-start | bytes 6316036
  67.7 8.6 %collective-permute-start = (f32[4,128,512]{2,1,0:T(8,128)S(1)}, f32[4,128,512]{2,1,0:T(8,128)}, u32[]{:S(2)}, u32[]{:S(2)}) collective-permute-start(f32[4,128,512]{2,1,0:T(8,128)S(1)} %dynamic-slice_bitcast_fusion), channel_id=1, source_target_pairs={{0,8},{8,0},{1,9},{9,1},{2,10},{10,2},{3,11},{11,3},{4,12},{12,4},... | collective-permute-start | bytes 3145736 | tf_op jit(solution)/shard_map/ppermute | solution.py:19
  75.9 6.9 %copy-start.1 = (bf16[1,128,512]{2,1,0:T(8,128)(2,1)S(1)}, bf16[1,128,512]{2,1,0:T(8,128)(2,1)}, u32[]{:S(2)}) copy-start(bf16[1,128,512]{2,1,0:T(8,128)(2,1)} %param.6) | copy-start | bytes 393220
  78.5 13.1 %all-to-all-start.2 = ((bf16[4,128,512]{2,1,0:T(8,128)(2,1)}), bf16[4,128,512]{2,1,0:T(8,128)(2,1)S(1)}, u32[]{:S(2)}, u32[]{:S(2)}) async-start(bf16[4,128,512]{2,1,0:T(8,128)(2,1)} %fusion.4), calls=%async_computation.2 | async-start | bytes 1048576 | tf_op jit(solution)/shard_map/all_to_all | solution.py:75
  91.9 7.1 %collective-permute-start.2 = (bf16[127,512]{1,0:T(8,128)(2,1)S(1)}, bf16[127,512]{1,0:T(8,128)(2,1)S(1)}, u32[]{:S(2)}, u32[]{:S(2)}) collective-permute-start(bf16[127,512]{1,0:T(8,128)(2,1)S(1)} %fusion.8), channel_id=1, source_target_pairs={{8,0},{16,8},{24,16},{32,24},{40,32},{48,40},{56,48},{64,56},{72,6... | collective-permute-start | bytes 390152 | tf_op jit(solution)/shard_map/ppermute | solution.py:25
  99.1 2.1 %copy-start.3 = (bf16[1,128,512]{2,1,0:T(8,128)(2,1)S(1)}, bf16[1,128,512]{2,1,0:T(8,128)(2,1)}, u32[]{:S(2)}) copy-start(bf16[1,128,512]{2,1,0:T(8,128)(2,1)} %param.7) | copy-start | bytes 393220
  103.0 3.9 %collective-permute-start.1 = (bf16[127,512]{1,0:T(8,128)(2,1)S(1)}, bf16[127,512]{1,0:T(8,128)(2,1)S(1)}, u32[]{:S(2)}, u32[]{:S(2)}) collective-permute-start(bf16[127,512]{1,0:T(8,128)(2,1)S(1)} %slice_bitcast_fusion), channel_id=1, source_target_pairs={{0,8},{8,16},{16,24},{24,32},{32,40},{40,48},{48,56},{56,64},{64,7... | collective-permute-start | bytes 390152 | tf_op jit(solution)/shard_map/ppermute | solution.py:25
  124.0 3.1 %collective-permute-start.3 = (f32[32,128]{1,0:T(8,128)S(1)}, f32[32,128]{1,0:T(8,128)S(1)}, u32[]{:S(2)}, u32[]{:S(2)}) collective-permute-start(f32[32,128]{1,0:T(8,128)S(1)} %rev.7), channel_id=1, source_target_pairs={{0,8},{8,0},{1,9},{9,1},{2,10},{10,2},{3,11},{11,3},{4,12},{12,4},... | collective-permute-start | bytes 49160 | tf_op jit(solution)/shard_map/ppermute | solution.py:19
  127.9 29.9 %all-to-all-start.3 = ((f32[32,32,128]{2,1,0:T(8,128)}), f32[32,32,128]{2,1,0:T(8,128)S(1)}, u32[]{:S(2)}, u32[]{:S(2)}) async-start(f32[32,32,128]{2,1,0:T(8,128)} %broadcast_in_dim.5), calls=%async_computation.3 | async-start | bytes 1048576 | tf_op jit(solution)/shard_map/all_to_all | solution.py:31
Sparse Core Ops, SparseCore 0:
  25.2 38.8 all-gather.2

commit v2 on v1

v2 whole, which is shorter than its diff:
```python
import math

import jax
import jax.numpy as jnp
from jax import lax
from jax.experimental import pallas as pl
from jax.experimental.pallas import tpu as pltpu
from jax.sharding import Mesh, PartitionSpec as P

GROUP = 16
TAPS = 128
LANES = 128
PER = LANES // GROUP
F32 = jnp.float32
BF16 = jnp.bfloat16

X = ("xh", "xp")
Z = ("zh", "zl")
CONTEXT = ("xh", "xp", "zl", "co")
VMEM = pltpu.CompilerParams(vmem_limit_bytes=32 * 1024 * 1024)


def swap(block, axis):
    return lax.ppermute(block, axis, [(0, 1), (1, 0)])


def in_order(mine, theirs, axis):
    first = lax.axis_index(axis) == 0
    return jnp.stack([jnp.where(first, mine, theirs), jnp.where(first, theirs, mine)])


def from_behind(block, distance):
    n = lax.axis_size(CONTEXT)
    route = [(i - distance, i) for i in range(n) if 0 <= i - distance < n]
    return lax.ppermute(block, CONTEXT, route)


def sum_over(block, axes):
    n = lax.axis_size(axes)
    copies = jnp.broadcast_to(block[None], (n,) + block.shape)
    return jnp.sum(lax.all_to_all(copies, axes, split_axis=0, concat_axis=0), axis=0)


def shifted_rows(row):
    return pltpu.roll(jnp.broadcast_to(row, (TAPS, 2 * TAPS)), 0, 1, stride=1, stride_axis=0)


def lane_group(shape):
    return lax.broadcasted_iota(jnp.int32, shape, 1) >> 4


def filtered(rows_ref, window):
    owner = lane_group((TAPS, LANES))
    total = jnp.zeros((TAPS, LANES), F32)
    for g in range(PER):
        table = shifted_rows(rows_ref[g : g + 1, :]).astype(BF16)
        term = jnp.dot(table, window, preferred_element_type=F32)
        total = jnp.where(owner == g, term, total)
    return total


def conv_kernel(rows_ref, window_ref, conv_ref):
    conv_ref[...] = filtered(rows_ref, window_ref[...])


def mixed_grad_kernel(rows_ref, grad_ref, after_ref, key_ref, value_ref, key_grad_ref, value_grad_ref):
    window = jnp.concatenate([grad_ref[...], after_ref[...]], 0)
    mixed_grad = filtered(rows_ref, window)
    key_grad_ref[...] = (mixed_grad * value_ref[...].astype(F32)).astype(BF16)
    value_grad_ref[...] = (mixed_grad * key_ref[...].astype(F32)).astype(BF16)


def regroup(blocks):
    rows = blocks[0].shape[0]
    group = lane_group((rows, LANES))
    for bit in (1, 2):
        low = (group & bit) == 0
        out = list(blocks)
        for b in range(4):
            if b & bit:
                continue
            x0, x1 = blocks[b], blocks[b | bit]
            out[b] = jnp.where(low, x0, pltpu.roll(x1, GROUP * bit, 1))
            out[b | bit] = jnp.where(low, pltpu.roll(x0, LANES - GROUP * bit, 1), x1)
        blocks = out
    return blocks


def window_kernel(window_ref, out_ref):
    n = 2 * TAPS
    across = lax.broadcasted_iota(jnp.int32, (n, n), 0) + lax.broadcasted_iota(jnp.int32, (n, n), 1)
    turn = (across == n - 1).astype(F32).astype(BF16)
    turned = [jnp.dot(turn, window_ref[b], preferred_element_type=F32) for b in range(4)]
    for a, block in enumerate(regroup(turned)):
        out_ref[a] = block.astype(BF16)


def lag_kernel(mine_ref, other_ref, query_ref, window_ref, lag_ref):
    grads = [mine_ref[0], mine_ref[1], other_ref[0], other_ref[1]]
    grads = [g * query_ref[b].astype(F32) for b, g in enumerate(grads)]
    half = lax.broadcasted_iota(jnp.int32, (TAPS, LANES), 1) >> 6
    for a, block in enumerate(regroup(grads)):
        for h in range(2):
            part = jnp.where(half == h, block, 0.0).astype(BF16)
            outer = lax.dot_general(part, window_ref[a], (((1,), (1,)), ((), ())), preferred_element_type=F32)
            skewed = pltpu.roll(outer, 1, 1, stride=1, stride_axis=0)
            sums = jnp.sum(skewed, axis=0, keepdims=True)
            lag_ref[4 * h + a : 4 * h + a + 1, :] = sums[:, TAPS:]


def product_kernel(place_ref, cot_ref, *refs):
    weights, (mine_ref, other_ref) = refs[:-2], refs[-2:]
    start = place_ref[0]
    core = place_ref[1]
    depth = weights[0].shape[0]
    pieces = []
    for weight_ref, step, part in zip(weights, (0, 1, 7, 2, 6, 3, 5, 4, 4), (None,) * 7 + (0, 1)):
        column = lax.rem(start + step, 8) * depth
        size = depth
        if part is not None:
            size = depth // 2
            column = column + part * size
        pieces.append((pl.multiple_of(column, LANES), size, weight_ref))
    for out_ref, c in ((other_ref, 1 - core), (mine_ref, core)):
        for p in range(2):
            rows = pl.ds(pl.multiple_of((2 * p + c) * TAPS, TAPS), TAPS)
            total = jnp.zeros(out_ref.shape[1:], F32)
            for column, size, weight_ref in pieces:
                total += jnp.dot(cot_ref[rows, pl.ds(column, size)], weight_ref[...], preferred_element_type=F32)
            out_ref[p] = total


def lane_blocks(*lead):
    return pl.BlockSpec(lead + (LANES,), lambda l: (0,) * len(lead) + (l,))


def convolve(rows, window):
    width = window.shape[1]
    return pl.pallas_call(
        conv_kernel,
        grid=(width // LANES,),
        in_specs=[pl.BlockSpec((PER, 2 * TAPS), lambda l: (l, 0)), lane_blocks(2 * TAPS)],
        out_specs=lane_blocks(TAPS),
        out_shape=jax.ShapeDtypeStruct((TAPS, width), F32),
        compiler_params=VMEM,
        name="conv",
    )(rows, window)


def mixed_gradient(rows, grad, after, keys, values):
    width = grad.shape[1]
    tile = lane_blocks(TAPS)
    return pl.pallas_call(
        mixed_grad_kernel,
        grid=(width // LANES,),
        in_specs=[pl.BlockSpec((PER, 2 * TAPS), lambda l: (l, 0)), tile, tile, tile, tile],
        out_specs=[tile, tile],
        out_shape=[jax.ShapeDtypeStruct((TAPS, width), BF16)] * 2,
        compiler_params=VMEM,
        name="mixed_grad",
    )(rows, grad, after, keys, values)


def turned_windows(windows):
    width = windows.shape[2]
    return pl.pallas_call(
        window_kernel,
        grid=(width // LANES,),
        in_specs=[lane_blocks(4, 2 * TAPS)],
        out_specs=lane_blocks(4, 2 * TAPS),
        out_shape=jax.ShapeDtypeStruct(windows.shape, BF16),
        compiler_params=VMEM,
        name="windows",
    )(windows)


def lag_totals(mine, other, queries, windows):
    width = mine.shape[2]
    return pl.pallas_call(
        lag_kernel,
        grid=(width // LANES,),
        in_specs=[lane_blocks(2, TAPS), lane_blocks(2, TAPS), lane_blocks(4, TAPS), lane_blocks(4, 2 * TAPS)],
        out_specs=pl.BlockSpec((PER, TAPS), lambda l: (l, 0)),
        out_shape=jax.ShapeDtypeStruct((width // GROUP, TAPS), F32),
        compiler_params=VMEM,
        name="lags",
    )(mine, other, queries, windows)


def partial_products(cotangent, weights):
    width = weights[0].shape[1]
    place = jnp.stack([lax.axis_index(Z), lax.axis_index("co")]).astype(jnp.int32)
    whole = pl.BlockSpec(memory_space=pltpu.VMEM)
    out = jax.ShapeDtypeStruct((2, TAPS, width), F32)
    return pl.pallas_call(
        product_kernel,
        in_specs=[pl.BlockSpec(memory_space=pltpu.SMEM)] + [whole] * (1 + len(weights)),
        out_specs=[whole, whole],
        out_shape=[out, out],
        compiler_params=VMEM,
        name="product",
    )(place, cotangent, *weights)


def cotangent_columns(cotangent):
    rows, width = cotangent.shape
    depth = width // 64
    parts = cotangent.reshape(rows, 2, 2, 2, 4, 2, depth).transpose(3, 5, 0, 1, 4, 2, 6)
    parts = parts.reshape(4, 1, rows, 16 * depth)
    copies = jnp.broadcast_to(parts, (4, 8, rows, 16 * depth)).reshape(32, rows, 16 * depth)
    return lax.all_to_all(copies, ("xp", "co", "y"), split_axis=0, concat_axis=0).reshape(32 * rows, 16 * depth)


def weight_blocks(out_weight):
    depth, width = out_weight.shape
    own = in_order(out_weight, swap(out_weight, "xh"), "xh").reshape(2 * depth, width)
    n = 8
    up = [(i, (i + 1) % n) for i in range(n)]
    down = [(i, (i - 1) % n) for i in range(n)]
    blocks = [own]
    ahead = behind = own
    for _ in range(3):
        ahead = lax.ppermute(ahead, Z, down)
        behind = lax.ppermute(behind, Z, up)
        blocks += [ahead, behind]
    blocks.append(lax.ppermute(ahead[:depth], Z, down))
    blocks.append(lax.ppermute(behind[depth:], Z, up))
    return blocks


def local(query_branch, key_branch, value_branch, cotangent, out_weight, filters):
    query, keys, values = query_branch[0], key_branch[0], value_branch[0]
    tokens, width = query.shape
    groups = filters.shape[0]
    gathered = cotangent_columns(cotangent[0])
    weights = weight_blocks(out_weight)

    mixed = (keys.astype(F32) * values.astype(F32)).astype(BF16)
    before = from_behind(mixed, 1)
    window = jnp.concatenate([before, mixed], 0)
    taps = filters.astype(F32)
    zero = jnp.zeros((groups, TAPS), F32)
    rows = jnp.concatenate([taps, zero], 1)
    turned_rows = jnp.concatenate([zero[:, :1], taps[:, ::-1], zero[:, 1:]], 1)
    conv = convolve(turned_rows, window)

    saved = jnp.concatenate([query, window], 0)
    saved = in_order(saved, swap(saved, "xp"), "xp")
    saved = jnp.concatenate([saved, swap(saved, "co")], 0)
    queries = saved[:, :tokens]
    windows = turned_windows(saved[:, tokens:])

    mine, other = partial_products(gathered, weights)
    lags = lag_totals(mine, other, queries, windows)
    lag_sum = sum_over(sum_over(lags, X + ("co",)), Z)
    filter_grad = lag_sum * (1.0 / math.sqrt(2 * lax.axis_size(CONTEXT) * tokens * GROUP))

    summed = mine + swap(other, "co")
    xp = lax.axis_index("xp")
    keep = lax.dynamic_index_in_dim(summed, xp, 0, keepdims=False)
    give = lax.dynamic_index_in_dim(summed, 1 - xp, 0, keepdims=False)
    branch_grad = keep + swap(give.astype(BF16), "xp").astype(F32)
    query_grad = (branch_grad * conv).astype(BF16)
    conv_grad = (branch_grad * query.astype(F32)).astype(BF16)
    after = from_behind(conv_grad, -1)
    key_grad, value_grad = mixed_gradient(rows, conv_grad, after, keys, values)
    return (query_grad[None], key_grad[None], value_grad[None], filter_grad)


def solution(mesh):
    fine = Mesh(mesh.devices.reshape(2, 2, 2, 4, 2, 8), ("zh", "xh", "xp", "zl", "co", "y"))
    branch = P("zh", CONTEXT, "y")
    return jax.shard_map(
        local,
        mesh=fine,
        in_specs=(
            branch,
            branch,
            branch,
            P("zh", CONTEXT + ("y",), None),
            P(("zh",) + CONTEXT, "y"),
            P("y", None),
        ),
        out_specs=(branch, branch, branch, P("y", None)),
        check_vma=False,
    )
```

time: 166 us -> 135 us (0.81)
  starting transfers between devices: 35.8 us -> 73.8 us
  waiting for transfers between devices: 55.2 us -> 29 us
  local copies, waits for them, and re-layouts: 28.4 us -> 9.85 us
  blocking collectives: 16.4 us -> 0 us
  Pallas kernels: 0 us -> 13.2 us
  between operations: 14.3 us -> 1.15 us
  matrix products: 6.52 us -> 0 us
  other arithmetic: 8.68 us -> 6.84 us
    all_to_all x3, waiting for transfers between devices: 45.3 us -> 8.68 us  [the longest x2 8.67 us: sum_over(): lax.all_to_all(copies, axes, split_axis=0, concat_axis=0)]
    ppermute x0 -> x8, starting transfers between devices: none -> 30.7 us  [the longest x3 17.7 us: weight_blocks(): ahead = lax.ppermute(ahead, Z, down)]
    all_to_all x1 -> x0, blocking collectives: 16.4 us -> none  [branch_gradient(): parts = lax.all_to_all(parts, X + ('co',), split_axis=0, concat_axis=0)]
    pallas_call x0 -> x5, Pallas kernels: none -> 13.2 us  [the longest x1 3.93 us: lag_totals(): pl.pallas_call(lag_kernel, grid=(width // LANES,), in_specs=[lane_blocks(...]
    ppermute x0 -> x8, waiting for transfers between devices: none -> 12.9 us  [the longest x3 7.45 us: weight_blocks(): ahead = lax.ppermute(ahead, Z, down)]
    reshape x4 -> x0, local copies, waits for them, and re-layouts: 8.43 us -> none  [the longest x1 7.97 us: lag_totals(): skewed = flat.reshape(groups, taps, 2 * taps + 1)]
    ppermute x2 -> x5, starting transfers between devices: 8.15 us -> 16 us  [swap(): return lax.ppermute(block, axis, [(0, 1), (1, 0)])]
    dot_general x4 -> x0, matrix products: 6.52 us -> none  [the longest x1 3.16 us: branch_gradient(): jnp.einsum('ybrk,kn->byrn', gathered, weights, preferred_element_type=F32)]
  transfers between devices with their start and end apart: 8 -> 18, of which waited for: 8 -> 8; matrix products, arithmetic and copies ran while one was open for 8% -> 7% of each run, Pallas kernels for 0% -> 8%
where the time goes in v2:
time: 135 us; the launch traced here: 134 us
  starting transfers between devices  73.8 us (55%)
  waiting for transfers between devices  29 us (21%)
  Pallas kernels  13.2 us (10%)
  local copies, waits for them, and re-layouts  9.85 us (7%)
  other arithmetic  6.84 us (5%)
    ppermute x3, starting transfers between devices, weight_blocks(): ahead = lax.ppermute(ahead, Z, down)  17.7 us
    ppermute x5, starting transfers between devices, swap(): return lax.ppermute(block, axis, [(0, 1), (1, 0)])  16 us
    all_to_all x1, starting transfers between devices, cotangent_columns(): lax.all_to_all(copies, ('xp', 'co', 'y'), split_axis=0, concat_axis=0)  10.7 us
    all_to_all x2, starting transfers between devices, sum_over(): lax.all_to_all(copies, axes, split_axis=0, concat_axis=0)  9.04 us
    all_to_all x2, waiting for transfers between devices, sum_over(): lax.all_to_all(copies, axes, split_axis=0, concat_axis=0)  8.67 us
    ppermute x3, waiting for transfers between devices, weight_blocks(): ahead = lax.ppermute(ahead, Z, down)  7.45 us
    ppermute x2, starting transfers between devices, from_behind(): return lax.ppermute(block, CONTEXT, route)  7.39 us
    ppermute x3, starting transfers between devices, weight_blocks(): behind = lax.ppermute(behind, Z, up)  5.75 us
  transfers between devices with their start and end apart: 18, of which 8 were waited for; matrix products, arithmetic and copies ran while one was open for 7% of the time, Pallas kernels for 8%

profile of v2, /device:TPU:1, one launch (start us, length us, event | category | flops | bytes accessed | tf_op | source)
XLA Modules:
  0.0 133.9 jit_solution(14547893498553583676)
XLA Ops:
  3.8 10.7 %all-to-all-start = ((bf16[32,16,2048]{2,1,0:T(8,128)(2,1)}), bf16[32,16,2048]{2,1,0:T(8,128)(2,1)S(1)}, u32[]{:S(2)}, u32[]{:S(2)}) async-start(bf16[32,16,2048]{2,1,0:T(8,128)(2,1)} %bitcast.43), calls=%async_computation | async-start | bytes 4194304 | tf_op jit(solution)/shard_map/all_to_all | solution.py:211
  14.6 3.2 %collective-permute-start.11 = (bf16[128,512]{1,0:T(8,128)(2,1)S(1)}, bf16[128,512]{1,0:T(8,128)(2,1)S(1)}, u32[]{:S(2)}, u32[]{:S(2)}) collective-permute-start(bf16[128,512]{1,0:T(8,128)(2,1)S(1)} %multiply_convert_fusion.2), channel_id=1, source_target_pairs={{0,8},{8,16},{16,24},{24,32},{32,40},{40,48},{48,56},{56,64},{64,7... | collective-permute-start | bytes 393224 | tf_op jit(solution)/shard_map/ppermute | solution.py:35
  17.8 4.4 %collective-permute-start = (bf16[128,512]{1,0:T(8,128)(2,1)S(1)}, bf16[128,512]{1,0:T(8,128)(2,1)S(1)}, u32[]{:S(2)}, u32[]{:S(2)}) collective-permute-start(bf16[128,512]{1,0:T(8,128)(2,1)S(1)} %copy-done.21), channel_id=1, source_target_pairs={{0,128},{128,0},{1,129},{129,1},{2,130},{130,2},{3,131},{131,3},{4... | collective-permute-start | bytes 393224 | tf_op jit(solution)/shard_map/ppermute | solution.py:24
  23.0 2.8 %collective-permute-start.13 = (bf16[384,512]{1,0:T(8,128)(2,1)}, bf16[384,512]{1,0:T(8,128)(2,1)}, u32[]{:S(2)}, u32[]{:S(2)}) collective-permute-start(bf16[384,512]{1,0:T(8,128)(2,1)} %pad_maximum_fusion.4), channel_id=1, source_target_pairs={{0,64},{64,0},{1,65},{65,1},{2,66},{66,2},{3,67},{67,3},{4,68},{68... | collective-permute-start | bytes 1179656 | tf_op jit(solution)/shard_map/ppermute | solution.py:24
  25.9 5.2 %collective-permute-done = bf16[128,512]{1,0:T(8,128)(2,1)S(1)} collective-permute-done((bf16[128,512]{1,0:T(8,128)(2,1)S(1)}, bf16[128,512]{1,0:T(8,128)(2,1)S(1)}, u32[]{:S(2)}, u32[]{:S(2)}) %collective-permute-start) | collective-permute-done | bytes 131104 | tf_op jit(solution)/shard_map/ppermute | solution.py:24
  31.1 7.5 %collective-permute-start.1 = (bf16[256,512]{1,0:T(8,128)(2,1)S(1)}, bf16[256,512]{1,0:T(8,128)(2,1)S(1)}, u32[]{:S(2)}, u32[]{:S(2)}) collective-permute-start(bf16[256,512]{1,0:T(8,128)(2,1)S(1)} %bitcast.38), channel_id=1, source_target_pairs={{0,304},{16,0},{32,16},{48,32},{256,48},{272,256},{288,272},{304,2... | collective-permute-start | bytes 786440 | tf_op jit(solution)/shard_map/ppermute | solution.py:223
  40.6 3.9 %collective-permute-done.1.refs_1_ = bf16[256,512]{1,0:T(8,128)(2,1)S(1)} collective-permute-done((bf16[256,512]{1,0:T(8,128)(2,1)S(1)}, bf16[256,512]{1,0:T(8,128)(2,1)S(1)}, u32[]{:S(2)}, u32[]{:S(2)}) %collective-permute-start.1) | collective-permute-done | bytes 262176 | tf_op jit(solution)/shard_map/ppermute | solution.py:223
  44.5 5.3 %collective-permute-start.3 = (bf16[256,512]{1,0:T(8,128)(2,1)S(1)}, bf16[256,512]{1,0:T(8,128)(2,1)S(1)}, u32[]{:S(2)}, u32[]{:S(2)}) collective-permute-start(bf16[256,512]{1,0:T(8,128)(2,1)S(1)} %collective-permute-done.1.refs_1_), channel_id=1, source_target_pairs={{0,304},{16,0},{32,16},{48,32},{256,48},{272,256},{288,272},{304,2... | collective-permute-start | bytes 786440 | tf_op jit(solution)/shard_map/ppermute | solution.py:223
  54.3 2.3 %collective-permute-start.14 = (bf16[2,384,512]{2,1,0:T(8,128)(2,1)}, bf16[2,384,512]{2,1,0:T(8,128)(2,1)}, u32[]{:S(2)}, u32[]{:S(2)}) collective-permute-start(bf16[2,384,512]{2,1,0:T(8,128)(2,1)} %pad_maximum_fusion.2), channel_id=1, source_target_pairs={{0,8},{8,0},{1,9},{9,1},{2,10},{10,2},{3,11},{11,3},{4,12},{12,4},... | collective-permute-start | bytes 2359304 | tf_op jit(solution)/shard_map/ppermute | solution.py:24
  56.6 4.9 %collective-permute-start.5 = (bf16[256,512]{1,0:T(8,128)(2,1)S(1)}, bf16[256,512]{1,0:T(8,128)(2,1)S(1)}, u32[]{:S(2)}, u32[]{:S(2)}) collective-permute-start(bf16[256,512]{1,0:T(8,128)(2,1)S(1)} %collective-permute-done.3.refs_3_), channel_id=1, source_target_pairs={{0,304},{16,0},{32,16},{48,32},{256,48},{272,256},{288,272},{304,2... | collective-permute-start | bytes 786440 | tf_op jit(solution)/shard_map/ppermute | solution.py:223
  63.4 3.6 %collective-permute-done.5.refs_5_ = bf16[256,512]{1,0:T(8,128)(2,1)S(1)} collective-permute-done((bf16[256,512]{1,0:T(8,128)(2,1)S(1)}, bf16[256,512]{1,0:T(8,128)(2,1)S(1)}, u32[]{:S(2)}, u32[]{:S(2)}) %collective-permute-start.5) | collective-permute-done | bytes 262176 | tf_op jit(solution)/shard_map/ppermute | solution.py:223
  67.6 5.3 %collective-permute-start.7 = (bf16[128,512]{1,0:T(8,128)(2,1)}, bf16[128,512]{1,0:T(8,128)(2,1)}, u32[]{:S(2)}, u32[]{:S(2)}) collective-permute-start(bf16[128,512]{1,0:T(8,128)(2,1)} %slice.24), channel_id=1, source_target_pairs={{0,304},{16,0},{32,16},{48,32},{256,48},{272,256},{288,272},{304,2... | collective-permute-start | bytes 393224 | tf_op jit(solution)/shard_map/ppermute | solution.py:226
  75.6 5.2 %collective-permute-done.8.refs_8_ = bf16[128,512]{1,0:T(8,128)(2,1)} collective-permute-done((bf16[128,512]{1,0:T(8,128)(2,1)}, bf16[128,512]{1,0:T(8,128)(2,1)}, u32[]{:S(2)}, u32[]{:S(2)}) %collective-permute-start.8) | collective-permute-done | bytes 131104 | tf_op jit(solution)/shard_map/ppermute | solution.py:227
  84.7 3.0 %product.1 = (f32[2,128,512]{2,1,0:T(8,128)S(1)}, f32[2,128,512]{2,1,0:T(8,128)}) custom-call(s32[2]{0:T(128)S(1)} %pad_add_fusion.place_ref, bf16[512,2048]{1,0:T(8,128)(2,1)S(1)} %bitcast.37, bf16[256,512]{1,0:T(8,128)(2,1)S(1)} %bitcast.40, bf16[256,512]{1,0:T(8,128)(2,1)S(1)} %copy-done.4, bf16[256,512]{1,0:T(8,128)(2,1)S(1)} %copy-done.6, ...), custom_call_target="tpu_custom_call" | custom-call | tf_op jit(solution)/shard_map/product/pallas_call | solution.py:195
  87.7 4.3 %collective-permute-start.9 = (f32[2,128,512]{2,1,0:T(8,128)}, f32[2,128,512]{2,1,0:T(8,128)S(1)}, u32[]{:S(2)}, u32[]{:S(2)}) collective-permute-start(f32[2,128,512]{2,1,0:T(8,128)} %get-tuple-element.9.other_ref), channel_id=1, source_target_pairs={{0,8},{8,0},{1,9},{9,1},{2,10},{10,2},{3,11},{11,3},{4,12},{12,4},... | collective-permute-start | bytes 1572872 | tf_op jit(solution)/shard_map/ppermute | solution.py:24
  96.3 3.9 %lags.1 = f32[32,128]{1,0:T(8,128)S(1)} custom-call(f32[2,128,512]{2,1,0:T(8,128)S(1)} %get-tuple-element.8.mine_ref, f32[2,128,512]{2,1,0:T(8,128)} %get-tuple-element.9.other_ref, bf16[4,128,512]{2,1,0:T(8,128)(2,1)S(1)} %pad_maximum_fusion.3.query_ref, bf16[4,256,512]{2,1,0:T(8,128)(2,1)S(1)} %windows.1.window_ref), custom_call_target="tpu_custom_call" | custom-call | tf_op jit(solution)/shard_map/lags/pallas_call | solution.py:179
  101.0 5.7 %all-to-all-start.1 = ((f32[8,32,128]{2,1,0:T(8,128)}), f32[8,32,128]{2,1,0:T(8,128)S(1)}, u32[]{:S(2)}, u32[]{:S(2)}) async-start(f32[8,32,128]{2,1,0:T(8,128)} %broadcast_in_dim.34), calls=%async_computation.1 | async-start | bytes 262144 | tf_op jit(solution)/shard_map/all_to_all | solution.py:41
  106.8 5.1 %all-to-all-done.1 = f32[8,32,128]{2,1,0:T(8,128)S(1)} async-done(((f32[8,32,128]{2,1,0:T(8,128)}), f32[8,32,128]{2,1,0:T(8,128)S(1)}, u32[]{:S(2)}, u32[]{:S(2)}) %all-to-all-start.1) | async-done | bytes 131104 | tf_op jit(solution)/shard_map/all_to_all | solution.py:41
  112.6 3.4 %all-to-all-start.2 = ((f32[8,32,128]{2,1,0:T(8,128)}), f32[8,32,128]{2,1,0:T(8,128)S(1)}, u32[]{:S(2)}, u32[]{:S(2)}) async-start(f32[8,32,128]{2,1,0:T(8,128)} %broadcast_in_dim.35), calls=%async_computation.2 | async-start | bytes 262144 | tf_op jit(solution)/shard_map/all_to_all | solution.py:41
  116.1 2.2 %collective-permute-start.10 = (bf16[128,512]{1,0:T(8,128)(2,1)S(1)}, bf16[128,512]{1,0:T(8,128)(2,1)S(1)}, u32[]{:S(2)}, u32[]{:S(2)}) collective-permute-start(bf16[128,512]{1,0:T(8,128)(2,1)S(1)} %fusion), channel_id=1, source_target_pairs={{0,64},{64,0},{1,65},{65,1},{2,66},{66,2},{3,67},{67,3},{4,68},{68... | collective-permute-start | bytes 393224 | tf_op jit(solution)/shard_map/ppermute | solution.py:24
  120.1 3.6 %all-to-all-done.2 = f32[8,32,128]{2,1,0:T(8,128)S(1)} async-done(((f32[8,32,128]{2,1,0:T(8,128)}), f32[8,32,128]{2,1,0:T(8,128)S(1)}, u32[]{:S(2)}, u32[]{:S(2)}) %all-to-all-start.2) | async-done | bytes 131104 | tf_op jit(solution)/shard_map/all_to_all | solution.py:41
  124.4 4.2 %collective-permute-start.12 = (bf16[128,512]{1,0:T(8,128)(2,1)S(1)}, bf16[128,512]{1,0:T(8,128)(2,1)S(1)}, u32[]{:S(2)}, u32[]{:S(2)}) collective-permute-start(bf16[128,512]{1,0:T(8,128)(2,1)S(1)} %get-tuple-element.14.grad_ref), channel_id=1, source_target_pairs={{8,0},{16,8},{24,16},{32,24},{40,32},{48,40},{56,48},{64,56},{72,6... | collective-permute-start | bytes 393224 | tf_op jit(solution)/shard_map/ppermute | solution.py:35
  129.2 2.2 %collective-permute-done.12.after_ref = bf16[128,512]{1,0:T(8,128)(2,1)S(1)} collective-permute-done((bf16[128,512]{1,0:T(8,128)(2,1)S(1)}, bf16[128,512]{1,0:T(8,128)(2,1)S(1)}, u32[]{:S(2)}, u32[]{:S(2)}) %collective-permute-start.12) | collective-permute-done | bytes 131104 | tf_op jit(solution)/shard_map/ppermute | solution.py:35
  131.4 2.5 %mixed_grad.1 = (bf16[128,512]{1,0:T(8,128)(2,1)}, bf16[128,512]{1,0:T(8,128)(2,1)}) custom-call(f32[32,256]{1,0:T(8,128)S(1)} %concatenate.19.rows_ref, bf16[128,512]{1,0:T(8,128)(2,1)S(1)} %get-tuple-element.14.grad_ref, bf16[128,512]{1,0:T(8,128)(2,1)S(1)} %collective-permute-done.12.after_ref, bf16[128,512]{1,0:T(8,128)(2,1)S(1)} %bitcast.42, ...), custom_call_target="tpu_custom_call" | custom-call | tf_op jit(solution)/shard_map/mixed_grad/pallas_call | solution.py:153
  (93 shorter events, 28.4 us)
Async XLA Ops:
  3.8 77.1 %all-to-all-start = ((bf16[32,16,2048]{2,1,0:T(8,128)(2,1)}), bf16[32,16,2048]{2,1,0:T(8,128)(2,1)S(1)}, u32[]{:S(2)}, u32[]{:S(2)}) async-start(bf16[32,16,2048]{2,1,0:T(8,128)(2,1)} %bitcast.43), calls=%async_computation | async-start | bytes 4194304 | tf_op jit(solution)/shard_map/all_to_all | solution.py:211
  14.6 39.7 %copy-start.15 = (bf16[128,512]{1,0:T(8,128)(2,1)}, bf16[128,512]{1,0:T(8,128)(2,1)S(1)}, u32[]{:S(2)}) copy-start(bf16[128,512]{1,0:T(8,128)(2,1)S(1)} %multiply_convert_fusion.2) | copy-start | bytes 393220
  14.6 7.6 %collective-permute-start.11 = (bf16[128,512]{1,0:T(8,128)(2,1)S(1)}, bf16[128,512]{1,0:T(8,128)(2,1)S(1)}, u32[]{:S(2)}, u32[]{:S(2)}) collective-permute-start(bf16[128,512]{1,0:T(8,128)(2,1)S(1)} %multiply_convert_fusion.2), channel_id=1, source_target_pairs={{0,8},{8,16},{16,24},{24,32},{32,40},{40,48},{48,56},{56,64},{64,7... | collective-permute-start | bytes 393224 | tf_op jit(solution)/shard_map/ppermute | solution.py:35
  17.8 13.2 %collective-permute-start = (bf16[128,512]{1,0:T(8,128)(2,1)S(1)}, bf16[128,512]{1,0:T(8,128)(2,1)S(1)}, u32[]{:S(2)}, u32[]{:S(2)}) collective-permute-start(bf16[128,512]{1,0:T(8,128)(2,1)S(1)} %copy-done.21), channel_id=1, source_target_pairs={{0,128},{128,0},{1,129},{129,1},{2,130},{130,2},{3,131},{131,3},{4... | collective-permute-start | bytes 393224 | tf_op jit(solution)/shard_map/ppermute | solution.py:24
  22.2 32.0 %copy-start.17 = (bf16[128,512]{1,0:T(8,128)(2,1)}, bf16[128,512]{1,0:T(8,128)(2,1)S(1)}, u32[]{:S(2)}) copy-start(bf16[128,512]{1,0:T(8,128)(2,1)S(1)} %collective-permute-done.11) | copy-start | bytes 393220
  23.0 29.0 %collective-permute-start.13 = (bf16[384,512]{1,0:T(8,128)(2,1)}, bf16[384,512]{1,0:T(8,128)(2,1)}, u32[]{:S(2)}, u32[]{:S(2)}) collective-permute-start(bf16[384,512]{1,0:T(8,128)(2,1)} %pad_maximum_fusion.4), channel_id=1, source_target_pairs={{0,64},{64,0},{1,65},{65,1},{2,66},{66,2},{3,67},{67,3},{4,68},{68... | collective-permute-start | bytes 1179656 | tf_op jit(solution)/shard_map/ppermute | solution.py:24
  31.1 13.4 %collective-permute-start.1 = (bf16[256,512]{1,0:T(8,128)(2,1)S(1)}, bf16[256,512]{1,0:T(8,128)(2,1)S(1)}, u32[]{:S(2)}, u32[]{:S(2)}) collective-permute-start(bf16[256,512]{1,0:T(8,128)(2,1)S(1)} %bitcast.38), channel_id=1, source_target_pairs={{0,304},{16,0},{32,16},{48,32},{256,48},{272,256},{288,272},{304,2... | collective-permute-start | bytes 786440 | tf_op jit(solution)/shard_map/ppermute | solution.py:223
  38.6 11.4 %collective-permute-start.2 = (bf16[256,512]{1,0:T(8,128)(2,1)S(1)}, bf16[256,512]{1,0:T(8,128)(2,1)S(1)}, u32[]{:S(2)}, u32[]{:S(2)}) collective-permute-start(bf16[256,512]{1,0:T(8,128)(2,1)S(1)} %bitcast.39), channel_id=1, source_target_pairs={{0,16},{16,32},{32,48},{48,256},{256,272},{272,288},{288,304},{304... | collective-permute-start | bytes 786440 | tf_op jit(solution)/shard_map/ppermute | solution.py:224
  44.5 36.4 %copy-start.3 = (bf16[256,512]{1,0:T(8,128)(2,1)}, bf16[256,512]{1,0:T(8,128)(2,1)S(1)}, u32[]{:S(2)}) copy-start(bf16[256,512]{1,0:T(8,128)(2,1)S(1)} %collective-permute-done.1.refs_1_) | copy-start | bytes 786436
  44.5 12.1 %collective-permute-start.3 = (bf16[256,512]{1,0:T(8,128)(2,1)S(1)}, bf16[256,512]{1,0:T(8,128)(2,1)S(1)}, u32[]{:S(2)}, u32[]{:S(2)}) collective-permute-start(bf16[256,512]{1,0:T(8,128)(2,1)S(1)} %collective-permute-done.1.refs_1_), channel_id=1, source_target_pairs={{0,304},{16,0},{32,16},{48,32},{256,48},{272,256},{288,272},{304,2... | collective-permute-start | bytes 786440 | tf_op jit(solution)/shard_map/ppermute | solution.py:223
  50.1 30.8 %copy-start.5 = (bf16[256,512]{1,0:T(8,128)(2,1)}, bf16[256,512]{1,0:T(8,128)(2,1)S(1)}, u32[]{:S(2)}) copy-start(bf16[256,512]{1,0:T(8,128)(2,1)S(1)} %collective-permute-done.2.refs_2_) | copy-start | bytes 786436
  50.1 11.4 %collective-permute-start.4 = (bf16[256,512]{1,0:T(8,128)(2,1)S(1)}, bf16[256,512]{1,0:T(8,128)(2,1)S(1)}, u32[]{:S(2)}, u32[]{:S(2)}) collective-permute-start(bf16[256,512]{1,0:T(8,128)(2,1)S(1)} %collective-permute-done.2.refs_2_), channel_id=1, source_target_pairs={{0,16},{16,32},{32,48},{48,256},{256,272},{272,288},{288,304},{304... | collective-permute-start | bytes 786440 | tf_op jit(solution)/shard_map/ppermute | solution.py:224
  53.1 20.5 %copy-start.11 = (bf16[1,384,512]{2,1,0:T(8,128)(2,1)}, bf16[1,384,512]{2,1,0:T(8,128)(2,1)S(1)}, u32[]{:S(2)}) copy-start(bf16[1,384,512]{2,1,0:T(8,128)(2,1)S(1)} %get-tuple-element.12) | copy-start | bytes 1179652
  54.3 37.8 %collective-permute-start.14 = (bf16[2,384,512]{2,1,0:T(8,128)(2,1)}, bf16[2,384,512]{2,1,0:T(8,128)(2,1)}, u32[]{:S(2)}, u32[]{:S(2)}) collective-permute-start(bf16[2,384,512]{2,1,0:T(8,128)(2,1)} %pad_maximum_fusion.2), channel_id=1, source_target_pairs={{0,8},{8,0},{1,9},{9,1},{2,10},{10,2},{3,11},{11,3},{4,12},{12,4},... | collective-permute-start | bytes 2359304 | tf_op jit(solution)/shard_map/ppermute | solution.py:24
  56.6 10.4 %collective-permute-start.5 = (bf16[256,512]{1,0:T(8,128)(2,1)S(1)}, bf16[256,512]{1,0:T(8,128)(2,1)S(1)}, u32[]{:S(2)}, u32[]{:S(2)}) collective-permute-start(bf16[256,512]{1,0:T(8,128)(2,1)S(1)} %collective-permute-done.3.refs_3_), channel_id=1, source_target_pairs={{0,304},{16,0},{32,16},{48,32},{256,48},{272,256},{288,272},{304,2... | collective-permute-start | bytes 786440 | tf_op jit(solution)/shard_map/ppermute | solution.py:223
  61.5 11.5 %collective-permute-start.6 = (bf16[256,512]{1,0:T(8,128)(2,1)S(1)}, bf16[256,512]{1,0:T(8,128)(2,1)S(1)}, u32[]{:S(2)}, u32[]{:S(2)}) collective-permute-start(bf16[256,512]{1,0:T(8,128)(2,1)S(1)} %collective-permute-done.4.refs_4_), channel_id=1, source_target_pairs={{0,16},{16,32},{32,48},{48,256},{256,272},{272,288},{288,304},{304... | collective-permute-start | bytes 786440 | tf_op jit(solution)/shard_map/ppermute | solution.py:224
  67.6 8.0 %collective-permute-start.7 = (bf16[128,512]{1,0:T(8,128)(2,1)}, bf16[128,512]{1,0:T(8,128)(2,1)}, u32[]{:S(2)}, u32[]{:S(2)}) collective-permute-start(bf16[128,512]{1,0:T(8,128)(2,1)} %slice.24), channel_id=1, source_target_pairs={{0,304},{16,0},{32,16},{48,32},{256,48},{272,256},{288,272},{304,2... | collective-permute-start | bytes 393224 | tf_op jit(solution)/shard_map/ppermute | solution.py:226
  73.6 7.2 %collective-permute-start.8 = (bf16[128,512]{1,0:T(8,128)(2,1)}, bf16[128,512]{1,0:T(8,128)(2,1)}, u32[]{:S(2)}, u32[]{:S(2)}) collective-permute-start(bf16[128,512]{1,0:T(8,128)(2,1)} %slice.25), channel_id=1, source_target_pairs={{0,16},{16,32},{32,48},{48,256},{256,272},{272,288},{288,304},{304... | collective-permute-start | bytes 393224 | tf_op jit(solution)/shard_map/ppermute | solution.py:227
  87.7 28.3 %collective-permute-start.9 = (f32[2,128,512]{2,1,0:T(8,128)}, f32[2,128,512]{2,1,0:T(8,128)S(1)}, u32[]{:S(2)}, u32[]{:S(2)}) collective-permute-start(f32[2,128,512]{2,1,0:T(8,128)} %get-tuple-element.9.other_ref), channel_id=1, source_target_pairs={{0,8},{8,0},{1,9},{9,1},{2,10},{10,2},{3,11},{11,3},{4,12},{12,4},... | collective-permute-start | bytes 1572872 | tf_op jit(solution)/shard_map/ppermute | solution.py:24
  100.3 23.4 %copy-start.20 = (bf16[1,128,512]{2,1,0:T(8,128)(2,1)S(1)}, bf16[1,128,512]{2,1,0:T(8,128)(2,1)}, u32[]{:S(2)}) copy-start(bf16[1,128,512]{2,1,0:T(8,128)(2,1)} %param.6) | copy-start | bytes 393220
  101.0 10.9 %all-to-all-start.1 = ((f32[8,32,128]{2,1,0:T(8,128)}), f32[8,32,128]{2,1,0:T(8,128)S(1)}, u32[]{:S(2)}, u32[]{:S(2)}) async-start(f32[8,32,128]{2,1,0:T(8,128)} %broadcast_in_dim.34), calls=%async_computation.1 | async-start | bytes 262144 | tf_op jit(solution)/shard_map/all_to_all | solution.py:41
  112.6 11.1 %all-to-all-start.2 = ((f32[8,32,128]{2,1,0:T(8,128)}), f32[8,32,128]{2,1,0:T(8,128)S(1)}, u32[]{:S(2)}, u32[]{:S(2)}) async-start(f32[8,32,128]{2,1,0:T(8,128)} %broadcast_in_dim.35), calls=%async_computation.2 | async-start | bytes 262144 | tf_op jit(solution)/shard_map/all_to_all | solution.py:41
  116.1 7.5 %collective-permute-start.10 = (bf16[128,512]{1,0:T(8,128)(2,1)S(1)}, bf16[128,512]{1,0:T(8,128)(2,1)S(1)}, u32[]{:S(2)}, u32[]{:S(2)}) collective-permute-start(bf16[128,512]{1,0:T(8,128)(2,1)S(1)} %fusion), channel_id=1, source_target_pairs={{0,64},{64,0},{1,65},{65,1},{2,66},{66,2},{3,67},{67,3},{4,68},{68... | collective-permute-start | bytes 393224 | tf_op jit(solution)/shard_map/ppermute | solution.py:24
  124.4 7.0 %collective-permute-start.12 = (bf16[128,512]{1,0:T(8,128)(2,1)S(1)}, bf16[128,512]{1,0:T(8,128)(2,1)S(1)}, u32[]{:S(2)}, u32[]{:S(2)}) collective-permute-start(bf16[128,512]{1,0:T(8,128)(2,1)S(1)} %get-tuple-element.14.grad_ref), channel_id=1, source_target_pairs={{8,0},{16,8},{24,16},{32,24},{40,32},{48,40},{56,48},{64,56},{72,6... | collective-permute-start | bytes 393224 | tf_op jit(solution)/shard_map/ppermute | solution.py:35
  (17 other events, 184.6 us)

commit v3 on v2

--- a/solution.py
+++ b/solution.py
@@ -14,9 +14,9 @@
 F32 = jnp.float32
 BF16 = jnp.bfloat16
 
-X = ("xh", "xp")
-Z = ("zh", "zl")
-CONTEXT = ("xh", "xp", "zl", "co")
+Z = ("zh", "zm", "zp")
+PAIRS = ("zh", "zm")
+CONTEXT = ("x", "zm", "zp", "co")
 VMEM = pltpu.CompilerParams(vmem_limit_bytes=32 * 1024 * 1024)
 
 
@@ -108,26 +108,31 @@
             lag_ref[4 * h + a : 4 * h + a + 1, :] = sums[:, TAPS:]
 
 
-def product_kernel(place_ref, cot_ref, *refs):
-    weights, (mine_ref, other_ref) = refs[:-2], refs[-2:]
-    start = place_ref[0]
-    core = place_ref[1]
-    depth = weights[0].shape[0]
-    pieces = []
-    for weight_ref, step, part in zip(weights, (0, 1, 7, 2, 6, 3, 5, 4, 4), (None,) * 7 + (0, 1)):
-        column = lax.rem(start + step, 8) * depth
-        size = depth
-        if part is not None:
-            size = depth // 2
-            column = column + part * size
-        pieces.append((pl.multiple_of(column, LANES), size, weight_ref))
-    for out_ref, c in ((other_ref, 1 - core), (mine_ref, core)):
-        for p in range(2):
-            rows = pl.ds(pl.multiple_of((2 * p + c) * TAPS, TAPS), TAPS)
-            total = jnp.zeros(out_ref.shape[1:], F32)
-            for column, size, weight_ref in pieces:
-                total += jnp.dot(cot_ref[rows, pl.ds(column, size)], weight_ref[...], preferred_element_type=F32)
-            out_ref[p] = total
+PIECES = ((0, (0, 1, 3, 2)), (1, (0, 1, 3, 2)), (3, (0, 1, 3, 2)), (2, (0, 1)), (2, (3, 2)))
+
+
+def product_kernel(place_ref, cot_hbm, *refs):
+    count = len(PIECES)
+    weights_hbm, (mine_ref, other_ref, cot_ref), rest = refs[:count], refs[count : count + 3], refs[count + 3 :]
+    weights, (cot_sem, weight_sems) = rest[:count], rest[count:]
+    copies = [pltpu.make_async_copy(cot_hbm, cot_ref, cot_sem)]
+    for i in range(count):
+        copies.append(pltpu.make_async_copy(weights_hbm[i], weights[i], weight_sems.at[i]))
+    for copy in copies:
+        copy.start()
+    x, pair, core = place_ref[0], place_ref[1], place_ref[2]
+    copies[0].wait()
+    for i, (x_step, z_steps) in enumerate(PIECES):
+        copies[1 + i].wait()
+        weight = weights[i][...]
+        first = lax.rem(x + x_step, 4) * 4
+        columns = [pl.multiple_of((first + lax.rem(pair + z, 4)) * TAPS, TAPS) for z in z_steps]
+        for out_ref, c in ((other_ref, 1 - core), (mine_ref, core)):
+            for p in range(2):
+                rows = pl.ds(pl.multiple_of((2 * p + c) * TAPS, TAPS), TAPS)
+                part = jnp.concatenate([cot_ref[rows, pl.ds(column, TAPS)] for column in columns], 1)
+                term = jnp.dot(part, weight, preferred_element_type=F32)
+                out_ref[p] = term if i == 0 else out_ref[p] + term
 
 
 def lane_blocks(*lead):
@@ -189,14 +194,17 @@
 
 def partial_products(cotangent, weights):
     width = weights[0].shape[1]
-    place = jnp.stack([lax.axis_index(Z), lax.axis_index("co")]).astype(jnp.int32)
+    place = [lax.axis_index("x"), lax.axis_index(PAIRS), lax.axis_index("co")]
+    place = jnp.stack(place).astype(jnp.int32)
     whole = pl.BlockSpec(memory_space=pltpu.VMEM)
     out = jax.ShapeDtypeStruct((2, TAPS, width), F32)
     return pl.pallas_call(
         product_kernel,
-        in_specs=[pl.BlockSpec(memory_space=pltpu.SMEM)] + [whole] * (1 + len(weights)),
+        in_specs=[pl.BlockSpec(memory_space=pltpu.SMEM)] + [pl.BlockSpec(memory_space=pl.ANY)] * (1 + len(weights)),
         out_specs=[whole, whole],
         out_shape=[out, out],
+        scratch_shapes=[pltpu.VMEM(a.shape, a.dtype) for a in (cotangent, *weights)]
+        + [pltpu.SemaphoreType.DMA, pltpu.SemaphoreType.DMA((len(weights),))],
         compiler_params=VMEM,
         name="product",
     )(place, cotangent, *weights)
@@ -205,36 +213,35 @@
 def cotangent_columns(cotangent):
     rows, width = cotangent.shape
     depth = width // 64
-    parts = cotangent.reshape(rows, 2, 2, 2, 4, 2, depth).transpose(3, 5, 0, 1, 4, 2, 6)
+    parts = cotangent.reshape(rows, 2, 4, 2, 2, 2, depth).transpose(4, 5, 0, 2, 1, 3, 6)
     parts = parts.reshape(4, 1, rows, 16 * depth)
     copies = jnp.broadcast_to(parts, (4, 8, rows, 16 * depth)).reshape(32, rows, 16 * depth)
-    return lax.all_to_all(copies, ("xp", "co", "y"), split_axis=0, concat_axis=0).reshape(32 * rows, 16 * depth)
+    gathered = lax.all_to_all(copies, ("zp", "co", "y"), split_axis=0, concat_axis=0)
+    return copies, gathered.reshape(32 * rows, 16 * depth)
+
+
+def turn(block, axes, distance):
+    n = lax.axis_size(axes)
+    return lax.ppermute(block, axes, [((i + distance) % n, i) for i in range(n)])
 
 
 def weight_blocks(out_weight):
-    depth, width = out_weight.shape
-    own = in_order(out_weight, swap(out_weight, "xh"), "xh").reshape(2 * depth, width)
-    n = 8
-    up = [(i, (i + 1) % n) for i in range(n)]
-    down = [(i, (i - 1) % n) for i in range(n)]
-    blocks = [own]
-    ahead = behind = own
-    for _ in range(3):
-        ahead = lax.ppermute(ahead, Z, down)
-        behind = lax.ppermute(behind, Z, up)
-        blocks += [ahead, behind]
-    blocks.append(lax.ppermute(ahead[:depth], Z, down))
-    blocks.append(lax.ppermute(behind[depth:], Z, up))
-    return blocks
+    near = [out_weight, turn(out_weight, PAIRS, 1), turn(out_weight, PAIRS, -1), turn(out_weight, PAIRS, 2)]
+    near = jnp.concatenate(near, 0)
+    half = near.shape[0] // 2
+    ahead, behind = turn(near, "x", 1), turn(near, "x", -1)
+    return near, [near, ahead, behind, turn(ahead[:half], "x", 1), turn(behind[half:], "x", -1)]
 
 
 def local(query_branch, key_branch, value_branch, cotangent, out_weight, filters):
     query, keys, values = query_branch[0], key_branch[0], value_branch[0]
     tokens, width = query.shape
     groups = filters.shape[0]
-    gathered = cotangent_columns(cotangent[0])
-    weights = weight_blocks(out_weight)
-
+    copies, gathered = cotangent_columns(cotangent[0])
+    out_weight, _ = lax.optimization_barrier((out_weight, copies))
+    near, weights = weight_blocks(out_weight)
+
+    keys, near = lax.optimization_barrier((keys, near))
     mixed = (keys.astype(F32) * values.astype(F32)).astype(BF16)
     before = from_behind(mixed, 1)
     window = jnp.concatenate([before, mixed], 0)
@@ -245,21 +252,25 @@
     conv = convolve(turned_rows, window)
 
     saved = jnp.concatenate([query, window], 0)
-    saved = in_order(saved, swap(saved, "xp"), "xp")
+    saved = in_order(saved, swap(saved, "zp"), "zp")
     saved = jnp.concatenate([saved, swap(saved, "co")], 0)
     queries = saved[:, :tokens]
     windows = turned_windows(saved[:, tokens:])
 
+    gathered, conv, windows, queries, rows = lax.optimization_barrier((gathered, conv, windows, queries, rows))
     mine, other = partial_products(gathered, weights)
     lags = lag_totals(mine, other, queries, windows)
-    lag_sum = sum_over(sum_over(lags, X + ("co",)), Z)
+    summed = mine + swap(other, "co")
+    zp = lax.axis_index("zp")
+    keep = lax.dynamic_index_in_dim(summed, zp, 0, keepdims=False)
+    give = lax.dynamic_index_in_dim(summed, 1 - zp, 0, keepdims=False).astype(BF16)
+
+    lag_sum = sum_over(lags, ("x", "co"))
+    lag_sum, give = lax.optimization_barrier((lag_sum, give))
+    lag_sum = sum_over(lag_sum, Z)
     filter_grad = lag_sum * (1.0 / math.sqrt(2 * lax.axis_size(CONTEXT) * tokens * GROUP))
 
-    summed = mine + swap(other, "co")
-    xp = lax.axis_index("xp")
-    keep = lax.dynamic_index_in_dim(summed, xp, 0, keepdims=False)
-    give = lax.dynamic_index_in_dim(summed, 1 - xp, 0, keepdims=False)
-    branch_grad = keep + swap(give.astype(BF16), "xp").astype(F32)
+    branch_grad = keep + swap(give, "zp").astype(F32)
     query_grad = (branch_grad * conv).astype(BF16)
     conv_grad = (branch_grad * query.astype(F32)).astype(BF16)
     after = from_behind(conv_grad, -1)
@@ -268,7 +279,7 @@
 
 
 def solution(mesh):
-    fine = Mesh(mesh.devices.reshape(2, 2, 2, 4, 2, 8), ("zh", "xh", "xp", "zl", "co", "y"))
+    fine = Mesh(mesh.devices.reshape(2, 4, 2, 2, 2, 8), ("zh", "x", "zm", "zp", "co", "y"))
     branch = P("zh", CONTEXT, "y")
     return jax.shard_map(
         local,

time: 135 us -> 156 us (1.16)
  waiting for transfers between devices: 29 us -> 43.1 us
  starting transfers between devices: 73.8 us -> 76.2 us
  local copies, waits for them, and re-layouts: 9.85 us -> 12.2 us
    ppermute x8 -> x7, waiting for transfers between devices: 12.9 us -> 20.4 us  [turn(): lax.ppermute(block, axes, [((i + distance) % n, i) for i in range(n)])]
    ppermute x2, waiting for transfers between devices: 2.2 us -> 5.44 us  [from_behind(): return lax.ppermute(block, CONTEXT, route)]
    ppermute x5 -> x4, waiting for transfers between devices: 5.19 us -> 8.02 us  [swap(): return lax.ppermute(block, axis, [(0, 1), (1, 0)])]
    ppermute x5 -> x4, starting transfers between devices: 16 us -> 18.5 us  [swap(): return lax.ppermute(block, axis, [(0, 1), (1, 0)])]
    ppermute x2, starting transfers between devices: 7.39 us -> 5.29 us  [from_behind(): return lax.ppermute(block, CONTEXT, route)]
    ppermute x8 -> x7, starting transfers between devices: 30.7 us -> 31.7 us  [turn(): lax.ppermute(block, axes, [((i + distance) % n, i) for i in range(n)])]
    unnamed x46 -> x39, local copies, waits for them, and re-layouts: 3.88 us -> 4.12 us
  transfers between devices with their start and end apart: 18 -> 16, of which waited for: 8 -> 9; matrix products, arithmetic and copies ran while one was open for 7% -> 9% of each run, Pallas kernels for 8% -> 5%
where the time goes in v3:
time: 156 us; the launch traced here: 155 us
  starting transfers between devices  76.2 us (49%)
  waiting for transfers between devices  43.1 us (28%)
  Pallas kernels  14.2 us (9%)
  local copies, waits for them, and re-layouts  12.2 us (8%)
  other arithmetic  7.8 us (5%)
    ppermute x7, starting transfers between devices, turn(): lax.ppermute(block, axes, [((i + distance) % n, i) for i in range(n)])  31.7 us
    ppermute x7, waiting for transfers between devices, turn(): lax.ppermute(block, axes, [((i + distance) % n, i) for i in range(n)])  20.4 us
    ppermute x4, starting transfers between devices, swap(): return lax.ppermute(block, axis, [(0, 1), (1, 0)])  18.5 us
    all_to_all x1, starting transfers between devices, cotangent_columns(): lax.all_to_all(copies, ('zp', 'co', 'y'), split_axis=0, concat_axis=0)  10.7 us
    all_to_all x2, starting transfers between devices, sum_over(): lax.all_to_all(copies, axes, split_axis=0, concat_axis=0)  9.93 us
    all_to_all x2, waiting for transfers between devices, sum_over(): lax.all_to_all(copies, axes, split_axis=0, concat_axis=0)  9.21 us
    ppermute x4, waiting for transfers between devices, swap(): return lax.ppermute(block, axis, [(0, 1), (1, 0)])  8.02 us
    ppermute x2, waiting for transfers between devices, from_behind(): return lax.ppermute(block, CONTEXT, route)  5.44 us
  transfers between devices with their start and end apart: 16, of which 9 were waited for; matrix products, arithmetic and copies ran while one was open for 9% of the time, Pallas kernels for 5%

profile of v3, /device:TPU:1, one launch (start us, length us, event | category | flops | bytes accessed | tf_op | source)
XLA Modules:
  0.0 154.6 jit_solution(7116649313126602785)
XLA Ops:
  3.8 10.7 %all-to-all-start = ((bf16[32,16,2048]{2,1,0:T(8,128)(2,1)}), bf16[32,16,2048]{2,1,0:T(8,128)(2,1)S(1)}, u32[]{:S(2)}, u32[]{:S(2)}) async-start(bf16[32,16,2048]{2,1,0:T(8,128)(2,1)} %bitcast.36), calls=%async_computation | async-start | bytes 4194304 | tf_op jit(solution)/shard_map/all_to_all | solution.py:219
  14.5 9.7 %collective-permute-start = (bf16[128,512]{1,0:T(8,128)(2,1)S(1)}, bf16[128,512]{1,0:T(8,128)(2,1)S(1)}, u32[]{:S(2)}, u32[]{:S(2)}) collective-permute-start(bf16[128,512]{1,0:T(8,128)(2,1)S(1)} %copy-done.16), channel_id=1, source_target_pairs={{32,0},{256,32},{288,256},{0,288},{33,1},{257,33},{289,257},{1,289... | collective-permute-start | bytes 393224 | tf_op jit(solution)/shard_map/ppermute | solution.py:225
  24.3 1.9 %collective-permute-start.1 = (bf16[128,512]{1,0:T(8,128)(2,1)S(1)}, bf16[128,512]{1,0:T(8,128)(2,1)S(1)}, u32[]{:S(2)}, u32[]{:S(2)}) collective-permute-start(bf16[128,512]{1,0:T(8,128)(2,1)S(1)} %copy-done.16), channel_id=1, source_target_pairs={{288,0},{0,32},{32,256},{256,288},{289,1},{1,33},{33,257},{257,289... | collective-permute-start | bytes 393224 | tf_op jit(solution)/shard_map/ppermute | solution.py:225
  26.2 4.2 %collective-permute-start.2 = (bf16[128,512]{1,0:T(8,128)(2,1)S(1)}, bf16[128,512]{1,0:T(8,128)(2,1)S(1)}, u32[]{:S(2)}, u32[]{:S(2)}) collective-permute-start(bf16[128,512]{1,0:T(8,128)(2,1)S(1)} %copy-done.16), channel_id=1, source_target_pairs={{256,0},{288,32},{0,256},{32,288},{257,1},{289,33},{1,257},{33,289... | collective-permute-start | bytes 393224 | tf_op jit(solution)/shard_map/ppermute | solution.py:225
  31.7 11.4 %collective-permute-done.1 = bf16[128,512]{1,0:T(8,128)(2,1)S(1)} collective-permute-done((bf16[128,512]{1,0:T(8,128)(2,1)S(1)}, bf16[128,512]{1,0:T(8,128)(2,1)S(1)}, u32[]{:S(2)}, u32[]{:S(2)}) %collective-permute-start.1) | collective-permute-done | bytes 131104 | tf_op jit(solution)/shard_map/ppermute | solution.py:225
  44.9 2.0 %collective-permute-start.3 = (bf16[128,512]{1,0:T(8,128)(2,1)S(1)}, bf16[128,512]{1,0:T(8,128)(2,1)S(1)}, u32[]{:S(2)}, u32[]{:S(2)}) collective-permute-start(bf16[128,512]{1,0:T(8,128)(2,1)S(1)} %multiply_convert_fusion.2), channel_id=1, source_target_pairs={{0,8},{8,16},{16,24},{24,32},{32,40},{40,48},{48,56},{56,64},{64,7... | collective-permute-start | bytes 393224 | tf_op jit(solution)/shard_map/ppermute | solution.py:35
  46.9 5.3 %collective-permute-done.3 = bf16[128,512]{1,0:T(8,128)(2,1)S(1)} collective-permute-done((bf16[128,512]{1,0:T(8,128)(2,1)S(1)}, bf16[128,512]{1,0:T(8,128)(2,1)S(1)}, u32[]{:S(2)}, u32[]{:S(2)}) %collective-permute-start.3) | collective-permute-done | bytes 131104 | tf_op jit(solution)/shard_map/ppermute | solution.py:35
  52.2 9.7 %collective-permute-start.4 = (bf16[384,512]{1,0:T(8,128)(2,1)S(1)}, bf16[384,512]{1,0:T(8,128)(2,1)S(1)}, u32[]{:S(2)}, u32[]{:S(2)}) collective-permute-start(bf16[384,512]{1,0:T(8,128)(2,1)S(1)} %pad_maximum_fusion.3), channel_id=1, source_target_pairs={{0,16},{16,0},{1,17},{17,1},{2,18},{18,2},{3,19},{19,3},{4,20},{20... | collective-permute-start | bytes 1179656 | tf_op jit(solution)/shard_map/ppermute | solution.py:24
  62.0 8.0 %collective-permute-done.4 = bf16[384,512]{1,0:T(8,128)(2,1)S(1)} collective-permute-done((bf16[384,512]{1,0:T(8,128)(2,1)S(1)}, bf16[384,512]{1,0:T(8,128)(2,1)S(1)}, u32[]{:S(2)}, u32[]{:S(2)}) %collective-permute-start.4) | collective-permute-done | bytes 393248 | tf_op jit(solution)/shard_map/ppermute | solution.py:24
  73.1 6.8 %collective-permute-start.6 = (bf16[512,512]{1,0:T(8,128)(2,1)}, bf16[512,512]{1,0:T(8,128)(2,1)S(1)}, u32[]{:S(2)}, u32[]{:S(2)}) collective-permute-start(bf16[512,512]{1,0:T(8,128)(2,1)} %constant_dynamic-update-slice_fusion.refs_0_), channel_id=1, source_target_pairs={{64,0},{128,64},{192,128},{0,192},{65,1},{129,65},{193,129},{1,193... | collective-permute-start | bytes 1572872 | tf_op jit(solution)/shard_map/ppermute | solution.py:225
  85.8 5.7 %collective-permute-done.6.refs_1_ = bf16[512,512]{1,0:T(8,128)(2,1)S(1)} collective-permute-done((bf16[512,512]{1,0:T(8,128)(2,1)}, bf16[512,512]{1,0:T(8,128)(2,1)S(1)}, u32[]{:S(2)}, u32[]{:S(2)}) %collective-permute-start.6) | collective-permute-done | bytes 524320 | tf_op jit(solution)/shard_map/ppermute | solution.py:225
  92.3 5.2 %collective-permute-start.8 = (bf16[256,512]{1,0:T(8,128)(2,1)}, bf16[256,512]{1,0:T(8,128)(2,1)}, u32[]{:S(2)}, u32[]{:S(2)}) collective-permute-start(bf16[256,512]{1,0:T(8,128)(2,1)} %slice.25), channel_id=1, source_target_pairs={{64,0},{128,64},{192,128},{0,192},{65,1},{129,65},{193,129},{1,193... | collective-permute-start | bytes 786440 | tf_op jit(solution)/shard_map/ppermute | solution.py:225
  101.6 2.1 %windows.1.window_ref = bf16[4,256,512]{2,1,0:T(8,128)(2,1)S(1)} custom-call(bf16[4,256,512]{2,1,0:T(8,128)(2,1)S(1)} %slice.24.window_ref), custom_call_target="tpu_custom_call" | custom-call | tf_op jit(solution)/shard_map/windows/pallas_call | solution.py:171
  105.6 2.9 %collective-permute-done.9.refs_4_ = bf16[256,512]{1,0:T(8,128)(2,1)} collective-permute-done((bf16[256,512]{1,0:T(8,128)(2,1)}, bf16[256,512]{1,0:T(8,128)(2,1)}, u32[]{:S(2)}, u32[]{:S(2)}) %collective-permute-start.9) | collective-permute-done | bytes 262176 | tf_op jit(solution)/shard_map/ppermute | solution.py:225
  110.5 4.0 %product.1 = (f32[2,128,512]{2,1,0:T(8,128)S(1)}, f32[2,128,512]{2,1,0:T(8,128)}) custom-call(s32[3]{0:T(128)S(1)} %pad_add_fusion.place_ref, bf16[512,2048]{1,0:T(8,128)(2,1)S(1)} %bitcast.32, bf16[512,512]{1,0:T(8,128)(2,1)} %constant_dynamic-update-slice_fusion.refs_0_, bf16[512,512]{1,0:T(8,128)(2,1)S(1)} %copy-done.3, bf16[512,512]{1,0:T(8,128)(2,1)S(1)} %copy-done.5, ...), custom_call_target="tpu_custom_call" | custom-call | tf_op jit(solution)/shard_map/product/pallas_call | solution.py:201
  114.6 3.9 %collective-permute-start.10 = (f32[2,128,512]{2,1,0:T(8,128)}, f32[2,128,512]{2,1,0:T(8,128)S(1)}, u32[]{:S(2)}, u32[]{:S(2)}) collective-permute-start(f32[2,128,512]{2,1,0:T(8,128)} %get-tuple-element.21.other_ref), channel_id=1, source_target_pairs={{0,8},{8,0},{1,9},{9,1},{2,10},{10,2},{3,11},{11,3},{4,12},{12,4},... | collective-permute-start | bytes 1572872 | tf_op jit(solution)/shard_map/ppermute | solution.py:24
  118.5 3.9 %lags.1 = f32[32,128]{1,0:T(8,128)S(1)} custom-call(f32[2,128,512]{2,1,0:T(8,128)S(1)} %get-tuple-element.20.mine_ref, f32[2,128,512]{2,1,0:T(8,128)} %get-tuple-element.21.other_ref, bf16[4,128,512]{2,1,0:T(8,128)(2,1)S(1)} %copy-done.1, bf16[4,256,512]{2,1,0:T(8,128)(2,1)S(1)} %windows.1.window_ref), custom_call_target="tpu_custom_call" | custom-call | tf_op jit(solution)/shard_map/lags/pallas_call | solution.py:184
  123.1 3.3 %all-to-all-start.1 = ((f32[8,32,128]{2,1,0:T(8,128)}), f32[8,32,128]{2,1,0:T(8,128)S(1)}, u32[]{:S(2)}, u32[]{:S(2)}) async-start(f32[8,32,128]{2,1,0:T(8,128)} %broadcast_in_dim.31), calls=%async_computation.1 | async-start | bytes 262144 | tf_op jit(solution)/shard_map/all_to_all | solution.py:41
  126.4 5.3 %all-to-all-done.1 = f32[8,32,128]{2,1,0:T(8,128)S(1)} async-done(((f32[8,32,128]{2,1,0:T(8,128)}), f32[8,32,128]{2,1,0:T(8,128)S(1)}, u32[]{:S(2)}, u32[]{:S(2)}) %all-to-all-start.1) | async-done | bytes 131104 | tf_op jit(solution)/shard_map/all_to_all | solution.py:41
  132.9 3.0 %collective-permute-start.11 = (bf16[128,512]{1,0:T(8,128)(2,1)S(1)}, bf16[128,512]{1,0:T(8,128)(2,1)S(1)}, u32[]{:S(2)}, u32[]{:S(2)}) collective-permute-start(bf16[128,512]{1,0:T(8,128)(2,1)S(1)} %fusion), channel_id=1, source_target_pairs={{0,16},{16,0},{1,17},{17,1},{2,18},{18,2},{3,19},{19,3},{4,20},{20... | collective-permute-start | bytes 393224 | tf_op jit(solution)/shard_map/ppermute | solution.py:24
  136.6 6.6 %all-to-all-start.2 = ((f32[8,32,128]{2,1,0:T(8,128)}), f32[8,32,128]{2,1,0:T(8,128)S(1)}, u32[]{:S(2)}, u32[]{:S(2)}) async-start(f32[8,32,128]{2,1,0:T(8,128)} %broadcast_in_dim.35), calls=%async_computation.2 | async-start | bytes 262144 | tf_op jit(solution)/shard_map/all_to_all | solution.py:41
  144.0 3.3 %collective-permute-start.12 = (bf16[128,512]{1,0:T(8,128)(2,1)S(1)}, bf16[128,512]{1,0:T(8,128)(2,1)S(1)}, u32[]{:S(2)}, u32[]{:S(2)}) collective-permute-start(bf16[128,512]{1,0:T(8,128)(2,1)S(1)} %get-tuple-element.32.grad_ref), channel_id=1, source_target_pairs={{8,0},{16,8},{24,16},{32,24},{40,32},{48,40},{56,48},{64,56},{72,6... | collective-permute-start | bytes 393224 | tf_op jit(solution)/shard_map/ppermute | solution.py:35
  147.3 4.0 %all-to-all-done.2 = f32[8,32,128]{2,1,0:T(8,128)S(1)} async-done(((f32[8,32,128]{2,1,0:T(8,128)}), f32[8,32,128]{2,1,0:T(8,128)S(1)}, u32[]{:S(2)}, u32[]{:S(2)}) %all-to-all-start.2) | async-done | bytes 131104 | tf_op jit(solution)/shard_map/all_to_all | solution.py:41
  152.0 2.5 %mixed_grad.1 = (bf16[128,512]{1,0:T(8,128)(2,1)}, bf16[128,512]{1,0:T(8,128)(2,1)}) custom-call(f32[32,256]{1,0:T(8,128)S(1)} %copy-done.9, bf16[128,512]{1,0:T(8,128)(2,1)S(1)} %get-tuple-element.32.grad_ref, bf16[128,512]{1,0:T(8,128)(2,1)S(1)} %collective-permute-done.12.after_ref, bf16[128,512]{1,0:T(8,128)(2,1)S(1)} %bitcast.34, ...), custom_call_target="tpu_custom_call" | custom-call | tf_op jit(solution)/shard_map/mixed_grad/pallas_call | solution.py:158
  (82 shorter events, 27.9 us)
Async XLA Ops:
  3.7 41.1 %copy-start.6 = (bf16[1,128,512]{2,1,0:T(8,128)(2,1)S(1)}, bf16[1,128,512]{2,1,0:T(8,128)(2,1)}, u32[]{:S(2)}) copy-start(bf16[1,128,512]{2,1,0:T(8,128)(2,1)} %param.7) | copy-start | bytes 393220
  3.8 41.1 %copy-start.7 = (bf16[1,128,512]{2,1,0:T(8,128)(2,1)S(1)}, bf16[1,128,512]{2,1,0:T(8,128)(2,1)}, u32[]{:S(2)}) copy-start(bf16[1,128,512]{2,1,0:T(8,128)(2,1)} %param.8) | copy-start | bytes 393220
  3.8 48.4 %copy-start.14 = (bf16[1,128,512]{2,1,0:T(8,128)(2,1)S(1)}, bf16[1,128,512]{2,1,0:T(8,128)(2,1)}, u32[]{:S(2)}) copy-start(bf16[1,128,512]{2,1,0:T(8,128)(2,1)} %param.6) | copy-start | bytes 393220
  3.8 101.8 %all-to-all-start = ((bf16[32,16,2048]{2,1,0:T(8,128)(2,1)}), bf16[32,16,2048]{2,1,0:T(8,128)(2,1)S(1)}, u32[]{:S(2)}, u32[]{:S(2)}) async-start(bf16[32,16,2048]{2,1,0:T(8,128)(2,1)} %bitcast.36), calls=%async_computation | async-start | bytes 4194304 | tf_op jit(solution)/shard_map/all_to_all | solution.py:219
  14.5 16.6 %collective-permute-start = (bf16[128,512]{1,0:T(8,128)(2,1)S(1)}, bf16[128,512]{1,0:T(8,128)(2,1)S(1)}, u32[]{:S(2)}, u32[]{:S(2)}) collective-permute-start(bf16[128,512]{1,0:T(8,128)(2,1)S(1)} %copy-done.16), channel_id=1, source_target_pairs={{32,0},{256,32},{288,256},{0,288},{33,1},{257,33},{289,257},{1,289... | collective-permute-start | bytes 393224 | tf_op jit(solution)/shard_map/ppermute | solution.py:225
  24.3 18.9 %collective-permute-start.1 = (bf16[128,512]{1,0:T(8,128)(2,1)S(1)}, bf16[128,512]{1,0:T(8,128)(2,1)S(1)}, u32[]{:S(2)}, u32[]{:S(2)}) collective-permute-start(bf16[128,512]{1,0:T(8,128)(2,1)S(1)} %copy-done.16), channel_id=1, source_target_pairs={{288,0},{0,32},{32,256},{256,288},{289,1},{1,33},{33,257},{257,289... | collective-permute-start | bytes 393224 | tf_op jit(solution)/shard_map/ppermute | solution.py:225
  26.2 18.0 %collective-permute-start.2 = (bf16[128,512]{1,0:T(8,128)(2,1)S(1)}, bf16[128,512]{1,0:T(8,128)(2,1)S(1)}, u32[]{:S(2)}, u32[]{:S(2)}) collective-permute-start(bf16[128,512]{1,0:T(8,128)(2,1)S(1)} %copy-done.16), channel_id=1, source_target_pairs={{256,0},{288,32},{0,256},{32,288},{257,1},{289,33},{1,257},{33,289... | collective-permute-start | bytes 393224 | tf_op jit(solution)/shard_map/ppermute | solution.py:225
  44.9 7.3 %collective-permute-start.3 = (bf16[128,512]{1,0:T(8,128)(2,1)S(1)}, bf16[128,512]{1,0:T(8,128)(2,1)S(1)}, u32[]{:S(2)}, u32[]{:S(2)}) collective-permute-start(bf16[128,512]{1,0:T(8,128)(2,1)S(1)} %multiply_convert_fusion.2), channel_id=1, source_target_pairs={{0,8},{8,16},{16,24},{24,32},{32,40},{40,48},{48,56},{56,64},{64,7... | collective-permute-start | bytes 393224 | tf_op jit(solution)/shard_map/ppermute | solution.py:35
  52.2 17.8 %collective-permute-start.4 = (bf16[384,512]{1,0:T(8,128)(2,1)S(1)}, bf16[384,512]{1,0:T(8,128)(2,1)S(1)}, u32[]{:S(2)}, u32[]{:S(2)}) collective-permute-start(bf16[384,512]{1,0:T(8,128)(2,1)S(1)} %pad_maximum_fusion.3), channel_id=1, source_target_pairs={{0,16},{16,0},{1,17},{17,1},{2,18},{18,2},{3,19},{19,3},{4,20},{20... | collective-permute-start | bytes 1179656 | tf_op jit(solution)/shard_map/ppermute | solution.py:24
  61.9 19.9 %copy-start.17 = (bf16[32,128]{1,0:T(8,128)(2,1)S(1)}, bf16[32,128]{1,0:T(8,128)(2,1)}, u32[]{:S(2)}) copy-start(bf16[32,128]{1,0:T(8,128)(2,1)} %param.11) | copy-start | bytes 24580
  71.2 29.0 %collective-permute-start.5 = (bf16[2,384,512]{2,1,0:T(8,128)(2,1)}, bf16[2,384,512]{2,1,0:T(8,128)(2,1)}, u32[]{:S(2)}, u32[]{:S(2)}) collective-permute-start(bf16[2,384,512]{2,1,0:T(8,128)(2,1)} %pad_maximum_fusion.1), channel_id=1, source_target_pairs={{0,8},{8,0},{1,9},{9,1},{2,10},{10,2},{3,11},{11,3},{4,12},{12,4},... | collective-permute-start | bytes 2359304 | tf_op jit(solution)/shard_map/ppermute | solution.py:24
  73.1 18.4 %collective-permute-start.6 = (bf16[512,512]{1,0:T(8,128)(2,1)}, bf16[512,512]{1,0:T(8,128)(2,1)S(1)}, u32[]{:S(2)}, u32[]{:S(2)}) collective-permute-start(bf16[512,512]{1,0:T(8,128)(2,1)} %constant_dynamic-update-slice_fusion.refs_0_), channel_id=1, source_target_pairs={{64,0},{128,64},{192,128},{0,192},{65,1},{129,65},{193,129},{1,193... | collective-permute-start | bytes 1572872 | tf_op jit(solution)/shard_map/ppermute | solution.py:225
  79.9 17.6 %collective-permute-start.7 = (bf16[512,512]{1,0:T(8,128)(2,1)}, bf16[512,512]{1,0:T(8,128)(2,1)S(1)}, u32[]{:S(2)}, u32[]{:S(2)}) collective-permute-start(bf16[512,512]{1,0:T(8,128)(2,1)} %constant_dynamic-update-slice_fusion.refs_0_), channel_id=1, source_target_pairs={{192,0},{0,64},{64,128},{128,192},{193,1},{1,65},{65,129},{129,193... | collective-permute-start | bytes 1572872 | tf_op jit(solution)/shard_map/ppermute | solution.py:225
  83.2 17.0 %copy-start.13 = (bf16[1,384,512]{2,1,0:T(8,128)(2,1)S(1)}, bf16[1,384,512]{2,1,0:T(8,128)(2,1)}, u32[]{:S(2)}) copy-start(bf16[1,384,512]{2,1,0:T(8,128)(2,1)} %copy-done.12) | copy-start | bytes 1179652
  92.3 13.2 %collective-permute-start.8 = (bf16[256,512]{1,0:T(8,128)(2,1)}, bf16[256,512]{1,0:T(8,128)(2,1)}, u32[]{:S(2)}, u32[]{:S(2)}) collective-permute-start(bf16[256,512]{1,0:T(8,128)(2,1)} %slice.25), channel_id=1, source_target_pairs={{64,0},{128,64},{192,128},{0,192},{65,1},{129,65},{193,129},{1,193... | collective-permute-start | bytes 786440 | tf_op jit(solution)/shard_map/ppermute | solution.py:225
  98.3 10.1 %collective-permute-start.9 = (bf16[256,512]{1,0:T(8,128)(2,1)}, bf16[256,512]{1,0:T(8,128)(2,1)}, u32[]{:S(2)}, u32[]{:S(2)}) collective-permute-start(bf16[256,512]{1,0:T(8,128)(2,1)} %slice.26), channel_id=1, source_target_pairs={{192,0},{0,64},{64,128},{128,192},{193,1},{1,65},{65,129},{129,193... | collective-permute-start | bytes 786440 | tf_op jit(solution)/shard_map/ppermute | solution.py:225
  114.6 17.2 %collective-permute-start.10 = (f32[2,128,512]{2,1,0:T(8,128)}, f32[2,128,512]{2,1,0:T(8,128)S(1)}, u32[]{:S(2)}, u32[]{:S(2)}) collective-permute-start(f32[2,128,512]{2,1,0:T(8,128)} %get-tuple-element.21.other_ref), channel_id=1, source_target_pairs={{0,8},{8,0},{1,9},{9,1},{2,10},{10,2},{3,11},{11,3},{4,12},{12,4},... | collective-permute-start | bytes 1572872 | tf_op jit(solution)/shard_map/ppermute | solution.py:24
  122.4 20.8 %copy-start.15 = (bf16[1,128,512]{2,1,0:T(8,128)(2,1)S(1)}, bf16[1,128,512]{2,1,0:T(8,128)(2,1)}, u32[]{:S(2)}) copy-start(bf16[1,128,512]{2,1,0:T(8,128)(2,1)} %param.6) | copy-start | bytes 393220
  123.1 8.6 %all-to-all-start.1 = ((f32[8,32,128]{2,1,0:T(8,128)}), f32[8,32,128]{2,1,0:T(8,128)S(1)}, u32[]{:S(2)}, u32[]{:S(2)}) async-start(f32[8,32,128]{2,1,0:T(8,128)} %broadcast_in_dim.31), calls=%async_computation.1 | async-start | bytes 262144 | tf_op jit(solution)/shard_map/all_to_all | solution.py:41
  131.7 20.3 %copy-start.8 = (bf16[1,128,512]{2,1,0:T(8,128)(2,1)S(1)}, bf16[1,128,512]{2,1,0:T(8,128)(2,1)}, u32[]{:S(2)}) copy-start(bf16[1,128,512]{2,1,0:T(8,128)(2,1)} %param.8) | copy-start | bytes 393220
  131.7 20.3 %copy-start.9 = (f32[32,256]{1,0:T(8,128)S(1)}, f32[32,256]{1,0:T(8,128)}, u32[]{:S(2)}) copy-start(f32[32,256]{1,0:T(8,128)} %concatenate.25.rows_ref) | copy-start | bytes 98308
  132.9 10.3 %collective-permute-start.11 = (bf16[128,512]{1,0:T(8,128)(2,1)S(1)}, bf16[128,512]{1,0:T(8,128)(2,1)S(1)}, u32[]{:S(2)}, u32[]{:S(2)}) collective-permute-start(bf16[128,512]{1,0:T(8,128)(2,1)S(1)} %fusion), channel_id=1, source_target_pairs={{0,16},{16,0},{1,17},{17,1},{2,18},{18,2},{3,19},{19,3},{4,20},{20... | collective-permute-start | bytes 393224 | tf_op jit(solution)/shard_map/ppermute | solution.py:24
  136.6 14.6 %all-to-all-start.2 = ((f32[8,32,128]{2,1,0:T(8,128)}), f32[8,32,128]{2,1,0:T(8,128)S(1)}, u32[]{:S(2)}, u32[]{:S(2)}) async-start(f32[8,32,128]{2,1,0:T(8,128)} %broadcast_in_dim.35), calls=%async_computation.2 | async-start | bytes 262144 | tf_op jit(solution)/shard_map/all_to_all | solution.py:41
  144.0 8.1 %collective-permute-start.12 = (bf16[128,512]{1,0:T(8,128)(2,1)S(1)}, bf16[128,512]{1,0:T(8,128)(2,1)S(1)}, u32[]{:S(2)}, u32[]{:S(2)}) collective-permute-start(bf16[128,512]{1,0:T(8,128)(2,1)S(1)} %get-tuple-element.32.grad_ref), channel_id=1, source_target_pairs={{8,0},{16,8},{24,16},{32,24},{40,32},{48,40},{56,48},{64,56},{72,6... | collective-permute-start | bytes 393224 | tf_op jit(solution)/shard_map/ppermute | solution.py:35
  (10 other events, 77.4 us)

commit v4 on v2

v4 whole, which is shorter than its diff:
```python
import math

import jax
import jax.numpy as jnp
from jax import lax
from jax.experimental import pallas as pl
from jax.experimental.pallas import tpu as pltpu
from jax.sharding import Mesh, PartitionSpec as P

GROUP = 16
TAPS = 128
LANES = 128
PER = LANES // GROUP
F32 = jnp.float32
BF16 = jnp.bfloat16

Z = ("zh", "zl")
CONTEXT = ("xh", "xp", "zl", "co")
VMEM = pltpu.CompilerParams(vmem_limit_bytes=8 * 1024 * 1024)


def swap(block, axis):
    return lax.ppermute(block, axis, [(0, 1), (1, 0)])


def in_order(mine, theirs, axis):
    first = lax.axis_index(axis) == 0
    return jnp.stack([jnp.where(first, mine, theirs), jnp.where(first, theirs, mine)])


def from_behind(block, distance):
    n = lax.axis_size(CONTEXT)
    route = [(i - distance, i) for i in range(n) if 0 <= i - distance < n]
    return lax.ppermute(block, CONTEXT, route)


def sum_over(block, axes):
    n = lax.axis_size(axes)
    copies = jnp.broadcast_to(block[None], (n,) + block.shape)
    return jnp.sum(lax.all_to_all(copies, axes, split_axis=0, concat_axis=0), axis=0)


def shifted_rows(row):
    return pltpu.roll(jnp.broadcast_to(row, (TAPS, 2 * TAPS)), 0, 1, stride=1, stride_axis=0)


def lane_group(shape):
    return lax.broadcasted_iota(jnp.int32, shape, 1) >> 4


def filtered(rows_ref, window):
    owner = lane_group((TAPS, LANES))
    total = jnp.zeros((TAPS, LANES), F32)
    for g in range(PER):
        table = shifted_rows(rows_ref[g : g + 1, :]).astype(BF16)
        term = jnp.dot(table, window, preferred_element_type=F32)
        total = jnp.where(owner == g, term, total)
    return total


def conv_kernel(rows_ref, window_ref, conv_ref):
    conv_ref[...] = filtered(rows_ref, window_ref[...])


def mixed_grad_kernel(rows_ref, grad_ref, after_ref, key_ref, value_ref, key_grad_ref, value_grad_ref):
    window = jnp.concatenate([grad_ref[...], after_ref[...]], 0)
    mixed_grad = filtered(rows_ref, window)
    key_grad_ref[...] = (mixed_grad * value_ref[...].astype(F32)).astype(BF16)
    value_grad_ref[...] = (mixed_grad * key_ref[...].astype(F32)).astype(BF16)


def regroup(first, second):
    low = (lane_group(first.shape) & 1) == 0
    even = jnp.where(low, first, pltpu.roll(second, GROUP, 1))
    odd = jnp.where(low, pltpu.roll(first, LANES - GROUP, 1), second)
    return even, odd


def window_kernel(window_ref, out_ref):
    n = 2 * TAPS
    across = lax.broadcasted_iota(jnp.int32, (n, n), 0) + lax.broadcasted_iota(jnp.int32, (n, n), 1)
    turn = (across == n - 1).astype(F32).astype(BF16)
    turned = [jnp.dot(turn, window_ref[b], preferred_element_type=F32) for b in range(2)]
    for a, block in enumerate(regroup(*turned)):
        out_ref[a] = block.astype(BF16)


def lag_kernel(keep_ref, give_ref, query_ref, window_ref, lag_ref):
    keep = keep_ref[...] * query_ref[0].astype(F32)
    give = give_ref[...].astype(F32) * query_ref[1].astype(F32)
    quarter = lax.broadcasted_iota(jnp.int32, (TAPS, LANES), 1) >> 5
    for a, block in enumerate(regroup(keep, give)):
        for q in range(4):
            part = jnp.where(quarter == q, block, 0.0).astype(BF16)
            outer = lax.dot_general(part, window_ref[a], (((1,), (1,)), ((), ())), preferred_element_type=F32)
            skewed = pltpu.roll(outer, 1, 1, stride=1, stride_axis=0)
            sums = jnp.sum(skewed, axis=0, keepdims=True)
            lag_ref[2 * q + a : 2 * q + a + 1, :] = sums[:, TAPS:]


def product_kernel(place_ref, cot_ref, *refs):
    weights, (keep_ref, give_ref) = refs[:-2], refs[-2:]
    z, core, xp = place_ref[0], place_ref[1], place_ref[2]
    depth = weights[0].shape[0]
    pieces = [(z, 0)]
    for step in (1, 2, 3):
        below, above = lax.rem(z + 8 - step, 8), lax.rem(z + step, 8)
        pieces += [(jnp.where(core == 0, below, above), 0), (jnp.where(core == 0, above, below), 0)]
    far = lax.rem(z + 4, 8)
    pieces += [(far, jnp.where(core == 0, 0, depth // 2)), (far, jnp.where(core == 0, depth // 2, 0))]
    for out_ref, p in ((give_ref, 1 - xp), (keep_ref, xp)):
        rows = pl.ds(pl.multiple_of(p * TAPS, TAPS), TAPS)
        total = jnp.zeros(out_ref.shape, F32)
        for weight_ref, (place, offset) in zip(weights, pieces):
            columns = pl.ds(pl.multiple_of(place * depth + offset, LANES), weight_ref.shape[0])
            total += jnp.dot(cot_ref[rows, columns], weight_ref[...], preferred_element_type=F32)
        out_ref[...] = total.astype(out_ref.dtype)


def lane_blocks(*lead):
    return pl.BlockSpec(lead + (LANES,), lambda l: (0,) * len(lead) + (l,))


def convolve(rows, window):
    width = window.shape[1]
    return pl.pallas_call(
        conv_kernel,
        grid=(width // LANES,),
        in_specs=[pl.BlockSpec((PER, 2 * TAPS), lambda l: (l, 0)), lane_blocks(2 * TAPS)],
        out_specs=lane_blocks(TAPS),
        out_shape=jax.ShapeDtypeStruct((TAPS, width), F32),
        compiler_params=VMEM,
        name="conv",
    )(rows, window)


def mixed_gradient(rows, grad, after, keys, values):
    width = grad.shape[1]
    tile = lane_blocks(TAPS)
    return pl.pallas_call(
        mixed_grad_kernel,
        grid=(width // LANES,),
        in_specs=[pl.BlockSpec((PER, 2 * TAPS), lambda l: (l, 0)), tile, tile, tile, tile],
        out_specs=[tile, tile],
        out_shape=[jax.ShapeDtypeStruct((TAPS, width), BF16)] * 2,
        compiler_params=VMEM,
        name="mixed_grad",
    )(rows, grad, after, keys, values)


def turned_windows(windows):
    width = windows.shape[2]
    return pl.pallas_call(
        window_kernel,
        grid=(width // LANES,),
        in_specs=[lane_blocks(2, 2 * TAPS)],
        out_specs=lane_blocks(2, 2 * TAPS),
        out_shape=jax.ShapeDtypeStruct(windows.shape, BF16),
        compiler_params=VMEM,
        name="windows",
    )(windows)


def lag_totals(keep, give, queries, windows):
    width = keep.shape[1]
    return pl.pallas_call(
        lag_kernel,
        grid=(width // LANES,),
        in_specs=[lane_blocks(TAPS), lane_blocks(TAPS), lane_blocks(2, TAPS), lane_blocks(2, 2 * TAPS)],
        out_specs=pl.BlockSpec((PER, TAPS), lambda l: (l, 0)),
        out_shape=jax.ShapeDtypeStruct((width // GROUP, TAPS), F32),
        compiler_params=VMEM,
        name="lags",
    )(keep, give, queries, windows)


def partial_products(cotangent, weights):
    width = weights[0].shape[1]
    place = jnp.stack([lax.axis_index(Z), lax.axis_index("co"), lax.axis_index("xp")]).astype(jnp.int32)
    whole = pl.BlockSpec(memory_space=pltpu.VMEM)
    return pl.pallas_call(
        product_kernel,
        in_specs=[pl.BlockSpec(memory_space=pltpu.SMEM)] + [whole] * (1 + len(weights)),
        out_specs=[whole, whole],
        out_shape=[jax.ShapeDtypeStruct((TAPS, width), F32), jax.ShapeDtypeStruct((TAPS, width), BF16)],
        compiler_params=VMEM,
        name="product",
    )(place, cotangent, *weights)


def cotangent_columns(cotangent, after):
    rows, width = cotangent.shape
    depth = width // 64
    parts = cotangent.reshape(rows, 2, 2, 2, 4, 2, depth).transpose(3, 0, 1, 4, 5, 2, 6)
    parts, _ = lax.optimization_barrier((parts.reshape(2, 1, rows, 32 * depth), after))
    copies = jnp.broadcast_to(parts, (2, 8, rows, 32 * depth)).reshape(16, rows, 32 * depth)
    return lax.all_to_all(copies, ("xp", "y"), split_axis=0, concat_axis=0).reshape(16 * rows, 32 * depth)


def chip_weights(both):
    rows, width = both.shape[0] * both.shape[1], both.shape[2]
    both = both.reshape(rows, width)
    return in_order(both, swap(both, "co"), "co").reshape(2 * rows, width)


def weight_blocks(chip):
    n = lax.axis_size(Z)
    route = [(2 * i, 2 * ((i + 1) % n)) for i in range(n)] + [(2 * i + 1, 2 * ((i - 1) % n) + 1) for i in range(n)]
    blocks = [chip]
    got = chip
    for _ in range(3):
        got = lax.ppermute(got, Z + ("co",), route)
        blocks += [got, swap(got, "co")]
    half = got.shape[0] // 2
    got = jnp.where(lax.axis_index("co") == 0, got[:half], got[half:])
    got = lax.ppermute(got, Z + ("co",), route)
    return blocks + [got, swap(got, "co")]


def local(query_branch, key_branch, value_branch, cotangent, out_weight, filters):
    query, keys, values = query_branch[0], key_branch[0], value_branch[0]
    tokens, width = query.shape
    groups = filters.shape[0]
    both = in_order(out_weight, swap(out_weight, "xh"), "xh")
    gathered = cotangent_columns(cotangent[0], both)
    chip = chip_weights(both)
    weights = weight_blocks(chip)

    keys, _ = lax.optimization_barrier((keys, chip))
    mixed = (keys.astype(F32) * values.astype(F32)).astype(BF16)
    before = from_behind(mixed, 1)
    window = jnp.concatenate([before, mixed], 0)
    taps = filters.astype(F32)
    zero = jnp.zeros((groups, TAPS), F32)
    rows = jnp.concatenate([taps, zero], 1)
    turned_rows = jnp.concatenate([zero[:, :1], taps[:, ::-1], zero[:, 1:]], 1)
    conv = convolve(turned_rows, window)

    saved = jnp.concatenate([query, window], 0)
    saved = jnp.stack([saved, swap(saved, "xp")])
    queries = saved[:, :tokens]
    windows = turned_windows(saved[:, tokens:])

    gathered, conv, windows, queries, rows = lax.optimization_barrier((gathered, conv, windows, queries, rows))
    keep, give = partial_products(gathered, weights)
    lags = lag_totals(keep, give, queries, windows)
    lag_sum = sum_over(lags, ("xh", "xp", "co"))
    branch_grad = keep + swap(give, "xp").astype(F32)
    query_grad = (branch_grad * conv).astype(BF16)
    conv_grad = (branch_grad * query.astype(F32)).astype(BF16)
    lag_sum, conv_grad = lax.optimization_barrier((lag_sum, conv_grad))
    lag_sum = sum_over(lag_sum, Z)
    filter_grad = lag_sum * (1.0 / math.sqrt(2 * lax.axis_size(CONTEXT) * tokens * GROUP))
    after = from_behind(conv_grad, -1)
    key_grad, value_grad = mixed_gradient(rows, conv_grad, after, keys, values)
    return (query_grad[None], key_grad[None], value_grad[None], filter_grad)


def solution(mesh):
    fine = Mesh(mesh.devices.reshape(2, 2, 2, 4, 2, 8), ("zh", "xh", "xp", "zl", "co", "y"))
    branch = P("zh", CONTEXT, "y")
    return jax.shard_map(
        local,
        mesh=fine,
        in_specs=(
            branch,
            branch,
            branch,
            P("zh", CONTEXT + ("y",), None),
            P(("zh",) + CONTEXT, "y"),
            P("y", None),
        ),
        out_specs=(branch, branch, branch, P("y", None)),
        check_vma=False,
    )
```

time: 135 us -> 136 us (level)
  blocking collectives: 0 us -> 9.58 us
  waiting for transfers between devices: 29 us -> 22.3 us
  other arithmetic: 6.84 us -> 9.52 us
  starting transfers between devices: 73.8 us -> 71.3 us
    ppermute x5 -> x8, starting transfers between devices: 16 us -> 29.7 us  [swap(): return lax.ppermute(block, axis, [(0, 1), (1, 0)])]
    all_to_all x0 -> x1, blocking collectives: none -> 9.58 us  [sum_over(): lax.all_to_all(copies, axes, split_axis=0, concat_axis=0)]
    all_to_all x2 -> x1, waiting for transfers between devices: 8.67 us -> 0.01 us  [sum_over(): lax.all_to_all(copies, axes, split_axis=0, concat_axis=0)]
    ppermute x8 -> x4, starting transfers between devices: 30.7 us -> 23.5 us  [weight_blocks(): got = lax.ppermute(got, Z + ('co',), route)]
    ppermute x2, waiting for transfers between devices: 2.2 us -> 7.41 us  [from_behind(): return lax.ppermute(block, CONTEXT, route)]
    all_to_all x2 -> x1, starting transfers between devices: 9.04 us -> 4.45 us  [sum_over(): lax.all_to_all(copies, axes, split_axis=0, concat_axis=0)]
    ppermute x5 -> x8, waiting for transfers between devices: 5.19 us -> 2.11 us  [swap(): return lax.ppermute(block, axis, [(0, 1), (1, 0)])]
    another operation x1 -> x3, other arithmetic: 0.08 us -> 2.77 us  [the longest x2 2.69 us: local(): saved = jnp.stack([saved, swap(saved, 'xp')])]
  transfers between devices with their start and end apart: 18 -> 16, of which waited for: 8 -> 7; matrix products, arithmetic and copies ran while one was open for 7% -> 7% of each run, Pallas kernels for 8% -> 7%
where the time goes in v4:
time: 136 us; the launch traced here: 135 us
  starting transfers between devices  71.3 us (52%)
  waiting for transfers between devices  22.3 us (16%)
  Pallas kernels  12.1 us (9%)
  blocking collectives  9.58 us (7%)
  other arithmetic  9.52 us (7%)
  local copies, waits for them, and re-layouts  8.7 us (6%)
    ppermute x8, starting transfers between devices, swap(): return lax.ppermute(block, axis, [(0, 1), (1, 0)])  29.7 us
    ppermute x4, starting transfers between devices, weight_blocks(): got = lax.ppermute(got, Z + ('co',), route)  23.5 us
    ppermute x4, waiting for transfers between devices, weight_blocks(): got = lax.ppermute(got, Z + ('co',), route)  12.8 us
    all_to_all x1, blocking collectives, sum_over(): lax.all_to_all(copies, axes, split_axis=0, concat_axis=0)  9.58 us
    all_to_all x1, starting transfers between devices, cotangent_columns(): lax.all_to_all(copies, ('xp', 'y'), split_axis=0, concat_axis=0)  8.61 us
    ppermute x2, waiting for transfers between devices, from_behind(): return lax.ppermute(block, CONTEXT, route)  7.41 us
    ppermute x2, starting transfers between devices, from_behind(): return lax.ppermute(block, CONTEXT, route)  4.96 us
    all_to_all x1, starting transfers between devices, sum_over(): lax.all_to_all(copies, axes, split_axis=0, concat_axis=0)  4.45 us
  transfers between devices with their start and end apart: 16, of which 7 were waited for; matrix products, arithmetic and copies ran while one was open for 7% of the time, Pallas kernels for 7%

profile of v4, /device:TPU:1, one launch (start us, length us, event | category | flops | bytes accessed | tf_op | source)
XLA Modules:
  0.0 134.6 jit_solution(4670999208398928127)
XLA Ops:
  0.6 5.5 %collective-permute-start = (bf16[128,512]{1,0:T(8,128)(2,1)}, bf16[128,512]{1,0:T(8,128)(2,1)S(1)}, u32[]{:S(2)}, u32[]{:S(2)}) collective-permute-start(bf16[128,512]{1,0:T(8,128)(2,1)} %param.10), channel_id=1, source_target_pairs={{0,128},{128,0},{1,129},{129,1},{2,130},{130,2},{3,131},{131,3},{4... | collective-permute-start | bytes 393224 | tf_op jit(solution)/shard_map/ppermute | solution.py:23
  11.2 8.6 %all-to-all-start = ((bf16[16,16,4096]{2,1,0:T(8,128)(2,1)}), bf16[16,16,4096]{2,1,0:T(8,128)(2,1)S(1)}, u32[]{:S(2)}, u32[]{:S(2)}) async-start(bf16[16,16,4096]{2,1,0:T(8,128)(2,1)} %bitcast.40), calls=%async_computation | async-start | bytes 4194304 | tf_op jit(solution)/shard_map/all_to_all | solution.py:197
  19.9 4.6 %collective-permute-start.1 = (bf16[256,512]{1,0:T(8,128)(2,1)S(1)}, bf16[256,512]{1,0:T(8,128)(2,1)S(1)}, u32[]{:S(2)}, u32[]{:S(2)}) collective-permute-start(bf16[256,512]{1,0:T(8,128)(2,1)S(1)} %bitcast.43), channel_id=1, source_target_pairs={{0,8},{8,0},{1,9},{9,1},{2,10},{10,2},{3,11},{11,3},{4,12},{12,4},... | collective-permute-start | bytes 786440 | tf_op jit(solution)/shard_map/ppermute | solution.py:23
  25.7 10.0 %collective-permute-start.4 = (bf16[512,512]{1,0:T(8,128)(2,1)S(1)}, bf16[512,512]{1,0:T(8,128)(2,1)S(1)}, u32[]{:S(2)}, u32[]{:S(2)}) collective-permute-start(bf16[512,512]{1,0:T(8,128)(2,1)S(1)} %bitcast.35), channel_id=1, source_target_pairs={{0,16},{16,32},{32,48},{48,256},{256,272},{272,288},{288,304},{304... | collective-permute-start | bytes 1572872 | tf_op jit(solution)/shard_map/ppermute | solution.py:212
  35.7 6.1 %collective-permute-done.4.refs_1_ = bf16[512,512]{1,0:T(8,128)(2,1)S(1)} collective-permute-done((bf16[512,512]{1,0:T(8,128)(2,1)S(1)}, bf16[512,512]{1,0:T(8,128)(2,1)S(1)}, u32[]{:S(2)}, u32[]{:S(2)}) %collective-permute-start.4) | collective-permute-done | bytes 524320 | tf_op jit(solution)/shard_map/ppermute | solution.py:212
  41.8 5.3 %collective-permute-start.6 = (bf16[512,512]{1,0:T(8,128)(2,1)S(1)}, bf16[512,512]{1,0:T(8,128)(2,1)}, u32[]{:S(2)}, u32[]{:S(2)}) collective-permute-start(bf16[512,512]{1,0:T(8,128)(2,1)S(1)} %collective-permute-done.4.refs_1_), channel_id=1, source_target_pairs={{0,16},{16,32},{32,48},{48,256},{256,272},{272,288},{288,304},{304... | collective-permute-start | bytes 1572872 | tf_op jit(solution)/shard_map/ppermute | solution.py:212
  47.1 6.1 %collective-permute-done.6.refs_3_ = bf16[512,512]{1,0:T(8,128)(2,1)} collective-permute-done((bf16[512,512]{1,0:T(8,128)(2,1)S(1)}, bf16[512,512]{1,0:T(8,128)(2,1)}, u32[]{:S(2)}, u32[]{:S(2)}) %collective-permute-start.6) | collective-permute-done | bytes 524320 | tf_op jit(solution)/shard_map/ppermute | solution.py:212
  53.2 5.2 %collective-permute-start.8 = (bf16[512,512]{1,0:T(8,128)(2,1)}, bf16[512,512]{1,0:T(8,128)(2,1)S(1)}, u32[]{:S(2)}, u32[]{:S(2)}) collective-permute-start(bf16[512,512]{1,0:T(8,128)(2,1)} %collective-permute-done.6.refs_3_), channel_id=1, source_target_pairs={{0,16},{16,32},{32,48},{48,256},{256,272},{272,288},{288,304},{304... | collective-permute-start | bytes 1572872 | tf_op jit(solution)/shard_map/ppermute | solution.py:212
  58.4 1.9 %collective-permute-start.2 = (bf16[128,512]{1,0:T(8,128)(2,1)S(1)}, bf16[128,512]{1,0:T(8,128)(2,1)S(1)}, u32[]{:S(2)}, u32[]{:S(2)}) collective-permute-start(bf16[128,512]{1,0:T(8,128)(2,1)S(1)} %multiply_convert_fusion.2), channel_id=1, source_target_pairs={{0,8},{8,16},{16,24},{24,32},{32,40},{40,48},{48,56},{56,64},{64,7... | collective-permute-start | bytes 393224 | tf_op jit(solution)/shard_map/ppermute | solution.py:34
  61.2 2.5 %collective-permute-done.2 = bf16[128,512]{1,0:T(8,128)(2,1)S(1)} collective-permute-done((bf16[128,512]{1,0:T(8,128)(2,1)S(1)}, bf16[128,512]{1,0:T(8,128)(2,1)S(1)}, u32[]{:S(2)}, u32[]{:S(2)}) %collective-permute-start.2) | collective-permute-done | bytes 131104 | tf_op jit(solution)/shard_map/ppermute | solution.py:34
  65.6 3.5 %collective-permute-start.3 = (bf16[384,512]{1,0:T(8,128)(2,1)}, bf16[384,512]{1,0:T(8,128)(2,1)}, u32[]{:S(2)}, u32[]{:S(2)}) collective-permute-start(bf16[384,512]{1,0:T(8,128)(2,1)} %get-tuple-element.34), channel_id=1, source_target_pairs={{0,64},{64,0},{1,65},{65,1},{2,66},{66,2},{3,67},{67,3},{4,68},{68... | collective-permute-start | bytes 1179656 | tf_op jit(solution)/shard_map/ppermute | solution.py:23
  69.1 5.8 %collective-permute-start.5 = (bf16[512,512]{1,0:T(8,128)(2,1)}, bf16[512,512]{1,0:T(8,128)(2,1)}, u32[]{:S(2)}, u32[]{:S(2)}) collective-permute-start(bf16[512,512]{1,0:T(8,128)(2,1)} %copy-done.4), channel_id=1, source_target_pairs={{0,8},{8,0},{1,9},{9,1},{2,10},{10,2},{3,11},{11,3},{4,12},{12,4},... | collective-permute-start | bytes 1572872 | tf_op jit(solution)/shard_map/ppermute | solution.py:23
  75.0 1.9 %collective-permute-start.7 = (bf16[512,512]{1,0:T(8,128)(2,1)}, bf16[512,512]{1,0:T(8,128)(2,1)}, u32[]{:S(2)}, u32[]{:S(2)}) collective-permute-start(bf16[512,512]{1,0:T(8,128)(2,1)} %collective-permute-done.6.refs_3_), channel_id=1, source_target_pairs={{0,8},{8,0},{1,9},{9,1},{2,10},{10,2},{3,11},{11,3},{4,12},{12,4},... | collective-permute-start | bytes 1572872 | tf_op jit(solution)/shard_map/ppermute | solution.py:23
  77.6 3.1 %collective-permute-start.10 = (bf16[256,512]{1,0:T(8,128)(2,1)}, bf16[256,512]{1,0:T(8,128)(2,1)}, u32[]{:S(2)}, u32[]{:S(2)}) collective-permute-start(bf16[256,512]{1,0:T(8,128)(2,1)} %slice_select_fusion), channel_id=1, source_target_pairs={{0,16},{16,32},{32,48},{48,256},{256,272},{272,288},{288,304},{304... | collective-permute-start | bytes 786440 | tf_op jit(solution)/shard_map/ppermute | solution.py:216
  80.7 1.9 %collective-permute-start.9 = (bf16[512,512]{1,0:T(8,128)(2,1)S(1)}, bf16[512,512]{1,0:T(8,128)(2,1)}, u32[]{:S(2)}, u32[]{:S(2)}) collective-permute-start(bf16[512,512]{1,0:T(8,128)(2,1)S(1)} %collective-permute-done.8.refs_5_), channel_id=1, source_target_pairs={{0,8},{8,0},{1,9},{9,1},{2,10},{10,2},{3,11},{11,3},{4,12},{12,4},... | collective-permute-start | bytes 1572872 | tf_op jit(solution)/shard_map/ppermute | solution.py:23
  85.3 4.5 %collective-permute-start.11 = (bf16[256,512]{1,0:T(8,128)(2,1)}, bf16[256,512]{1,0:T(8,128)(2,1)}, u32[]{:S(2)}, u32[]{:S(2)}) collective-permute-start(bf16[256,512]{1,0:T(8,128)(2,1)} %collective-permute-done.10.refs_7_), channel_id=1, source_target_pairs={{0,8},{8,0},{1,9},{9,1},{2,10},{10,2},{3,11},{11,3},{4,12},{12,4},... | collective-permute-start | bytes 786440 | tf_op jit(solution)/shard_map/ppermute | solution.py:23
  98.3 3.3 %product.1 = (f32[128,512]{1,0:T(8,128)S(1)}, bf16[128,512]{1,0:T(8,128)(2,1)}) custom-call(s32[3]{0:T(128)S(1)} %pad_add_fusion.place_ref, bf16[256,4096]{1,0:T(8,128)(2,1)S(1)} %bitcast.34, bf16[512,512]{1,0:T(8,128)(2,1)S(1)} %bitcast.36, bf16[512,512]{1,0:T(8,128)(2,1)S(1)} %copy-done.5, bf16[512,512]{1,0:T(8,128)(2,1)} %collective-permute-done.5.refs_2_, ...), custom_call_target="tpu_custom_call" | custom-call | tf_op jit(solution)/shard_map/product/pallas_call | solution.py:181
  101.6 2.1 %collective-permute-start.12 = (bf16[128,512]{1,0:T(8,128)(2,1)}, bf16[128,512]{1,0:T(8,128)(2,1)S(1)}, u32[]{:S(2)}, u32[]{:S(2)}) collective-permute-start(bf16[128,512]{1,0:T(8,128)(2,1)} %get-tuple-element.21.give_ref), channel_id=1, source_target_pairs={{0,64},{64,0},{1,65},{65,1},{2,66},{66,2},{3,67},{67,3},{4,68},{68... | collective-permute-start | bytes 393224 | tf_op jit(solution)/shard_map/ppermute | solution.py:23
  103.7 3.3 %lags.1 = f32[32,128]{1,0:T(8,128)S(1)} custom-call(f32[128,512]{1,0:T(8,128)S(1)} %get-tuple-element.20.keep_ref, bf16[128,512]{1,0:T(8,128)(2,1)} %get-tuple-element.21.give_ref, bf16[2,128,512]{2,1,0:T(8,128)(2,1)S(1)} %copy-done.2, bf16[2,256,512]{2,1,0:T(8,128)(2,1)S(1)} %copy-done.1), custom_call_target="tpu_custom_call" | custom-call | tf_op jit(solution)/shard_map/lags/pallas_call | solution.py:166
  107.0 9.6 %all_to_all.15 = f32[8,32,128]{2,1,0:T(8,128)S(1)} all-to-all(f32[8,32,128]{2,1,0:T(8,128)S(1)} %broadcast_in_dim.32), channel_id=1, replica_groups=mesh['zh'=2,'xh'=2,'xp'=2,'zl'=4,'co'=2,'y'=8] {'xh','xp','co'}, dimensions={0} | all-to-all | bytes 262144 | tf_op jit(solution)/shard_map/all_to_all | solution.py:40
  119.0 4.4 %all-to-all-start.2 = ((f32[8,32,128]{2,1,0:T(8,128)}), f32[8,32,128]{2,1,0:T(8,128)S(1)}, u32[]{:S(2)}, u32[]{:S(2)}) async-start(f32[8,32,128]{2,1,0:T(8,128)} %broadcast_in_dim.35), calls=%async_computation.2 | async-start | bytes 262144 | tf_op jit(solution)/shard_map/all_to_all | solution.py:40
  123.5 3.0 %collective-permute-start.13 = (bf16[128,512]{1,0:T(8,128)(2,1)S(1)}, bf16[128,512]{1,0:T(8,128)(2,1)S(1)}, u32[]{:S(2)}, u32[]{:S(2)}) collective-permute-start(bf16[128,512]{1,0:T(8,128)(2,1)S(1)} %get-tuple-element.26.grad_ref), channel_id=1, source_target_pairs={{8,0},{16,8},{24,16},{32,24},{40,32},{48,40},{56,48},{64,56},{72,6... | collective-permute-start | bytes 393224 | tf_op jit(solution)/shard_map/ppermute | solution.py:34
  126.5 4.9 %collective-permute-done.13.after_ref = bf16[128,512]{1,0:T(8,128)(2,1)S(1)} collective-permute-done((bf16[128,512]{1,0:T(8,128)(2,1)S(1)}, bf16[128,512]{1,0:T(8,128)(2,1)S(1)}, u32[]{:S(2)}, u32[]{:S(2)}) %collective-permute-start.13) | collective-permute-done | bytes 131104 | tf_op jit(solution)/shard_map/ppermute | solution.py:34
  131.4 2.5 %mixed_grad.1 = (bf16[128,512]{1,0:T(8,128)(2,1)}, bf16[128,512]{1,0:T(8,128)(2,1)}) custom-call(f32[32,256]{1,0:T(8,128)S(1)} %copy-done.9, bf16[128,512]{1,0:T(8,128)(2,1)S(1)} %get-tuple-element.26.grad_ref, bf16[128,512]{1,0:T(8,128)(2,1)S(1)} %collective-permute-done.13.after_ref, bf16[128,512]{1,0:T(8,128)(2,1)S(1)} %bitcast.38, ...), custom_call_target="tpu_custom_call" | custom-call | tf_op jit(solution)/shard_map/mixed_grad/pallas_call | solution.py:140
  (65 shorter events, 23.9 us)
Async XLA Ops:
  0.6 8.0 %collective-permute-start = (bf16[128,512]{1,0:T(8,128)(2,1)}, bf16[128,512]{1,0:T(8,128)(2,1)S(1)}, u32[]{:S(2)}, u32[]{:S(2)}) collective-permute-start(bf16[128,512]{1,0:T(8,128)(2,1)} %param.10), channel_id=1, source_target_pairs={{0,128},{128,0},{1,129},{129,1},{2,130},{130,2},{3,131},{131,3},{4... | collective-permute-start | bytes 393224 | tf_op jit(solution)/shard_map/ppermute | solution.py:23
  11.2 85.9 %all-to-all-start = ((bf16[16,16,4096]{2,1,0:T(8,128)(2,1)}), bf16[16,16,4096]{2,1,0:T(8,128)(2,1)S(1)}, u32[]{:S(2)}, u32[]{:S(2)}) async-start(bf16[16,16,4096]{2,1,0:T(8,128)(2,1)} %bitcast.40), calls=%async_computation | async-start | bytes 4194304 | tf_op jit(solution)/shard_map/all_to_all | solution.py:197
  19.9 38.5 %copy-start.6 = (bf16[1,128,512]{2,1,0:T(8,128)(2,1)S(1)}, bf16[1,128,512]{2,1,0:T(8,128)(2,1)}, u32[]{:S(2)}) copy-start(bf16[1,128,512]{2,1,0:T(8,128)(2,1)} %param.7) | copy-start | bytes 393220
  19.9 38.5 %copy-start.7 = (bf16[1,128,512]{2,1,0:T(8,128)(2,1)S(1)}, bf16[1,128,512]{2,1,0:T(8,128)(2,1)}, u32[]{:S(2)}) copy-start(bf16[1,128,512]{2,1,0:T(8,128)(2,1)} %param.8) | copy-start | bytes 393220
  19.9 5.7 %collective-permute-start.1 = (bf16[256,512]{1,0:T(8,128)(2,1)S(1)}, bf16[256,512]{1,0:T(8,128)(2,1)S(1)}, u32[]{:S(2)}, u32[]{:S(2)}) collective-permute-start(bf16[256,512]{1,0:T(8,128)(2,1)S(1)} %bitcast.43), channel_id=1, source_target_pairs={{0,8},{8,0},{1,9},{9,1},{2,10},{10,2},{3,11},{11,3},{4,12},{12,4},... | collective-permute-start | bytes 786440 | tf_op jit(solution)/shard_map/ppermute | solution.py:23
  25.7 16.1 %collective-permute-start.4 = (bf16[512,512]{1,0:T(8,128)(2,1)S(1)}, bf16[512,512]{1,0:T(8,128)(2,1)S(1)}, u32[]{:S(2)}, u32[]{:S(2)}) collective-permute-start(bf16[512,512]{1,0:T(8,128)(2,1)S(1)} %bitcast.35), channel_id=1, source_target_pairs={{0,16},{16,32},{32,48},{48,256},{256,272},{272,288},{288,304},{304... | collective-permute-start | bytes 1572872 | tf_op jit(solution)/shard_map/ppermute | solution.py:212
  41.8 11.4 %collective-permute-start.6 = (bf16[512,512]{1,0:T(8,128)(2,1)S(1)}, bf16[512,512]{1,0:T(8,128)(2,1)}, u32[]{:S(2)}, u32[]{:S(2)}) collective-permute-start(bf16[512,512]{1,0:T(8,128)(2,1)S(1)} %collective-permute-done.4.refs_1_), channel_id=1, source_target_pairs={{0,16},{16,32},{32,48},{48,256},{256,272},{272,288},{288,304},{304... | collective-permute-start | bytes 1572872 | tf_op jit(solution)/shard_map/ppermute | solution.py:212
  53.2 23.7 %collective-permute-start.8 = (bf16[512,512]{1,0:T(8,128)(2,1)}, bf16[512,512]{1,0:T(8,128)(2,1)S(1)}, u32[]{:S(2)}, u32[]{:S(2)}) collective-permute-start(bf16[512,512]{1,0:T(8,128)(2,1)} %collective-permute-done.6.refs_3_), channel_id=1, source_target_pairs={{0,16},{16,32},{32,48},{48,256},{256,272},{272,288},{288,304},{304... | collective-permute-start | bytes 1572872 | tf_op jit(solution)/shard_map/ppermute | solution.py:212
  58.4 5.3 %collective-permute-start.2 = (bf16[128,512]{1,0:T(8,128)(2,1)S(1)}, bf16[128,512]{1,0:T(8,128)(2,1)S(1)}, u32[]{:S(2)}, u32[]{:S(2)}) collective-permute-start(bf16[128,512]{1,0:T(8,128)(2,1)S(1)} %multiply_convert_fusion.2), channel_id=1, source_target_pairs={{0,8},{8,16},{16,24},{24,32},{32,40},{40,48},{48,56},{56,64},{64,7... | collective-permute-start | bytes 393224 | tf_op jit(solution)/shard_map/ppermute | solution.py:34
  65.6 26.6 %collective-permute-start.3 = (bf16[384,512]{1,0:T(8,128)(2,1)}, bf16[384,512]{1,0:T(8,128)(2,1)}, u32[]{:S(2)}, u32[]{:S(2)}) collective-permute-start(bf16[384,512]{1,0:T(8,128)(2,1)} %get-tuple-element.34), channel_id=1, source_target_pairs={{0,64},{64,0},{1,65},{65,1},{2,66},{66,2},{3,67},{67,3},{4,68},{68... | collective-permute-start | bytes 1179656 | tf_op jit(solution)/shard_map/ppermute | solution.py:23
  69.1 28.0 %collective-permute-start.5 = (bf16[512,512]{1,0:T(8,128)(2,1)}, bf16[512,512]{1,0:T(8,128)(2,1)}, u32[]{:S(2)}, u32[]{:S(2)}) collective-permute-start(bf16[512,512]{1,0:T(8,128)(2,1)} %copy-done.4), channel_id=1, source_target_pairs={{0,8},{8,0},{1,9},{9,1},{2,10},{10,2},{3,11},{11,3},{4,12},{12,4},... | collective-permute-start | bytes 1572872 | tf_op jit(solution)/shard_map/ppermute | solution.py:23
  75.0 22.2 %collective-permute-start.7 = (bf16[512,512]{1,0:T(8,128)(2,1)}, bf16[512,512]{1,0:T(8,128)(2,1)}, u32[]{:S(2)}, u32[]{:S(2)}) collective-permute-start(bf16[512,512]{1,0:T(8,128)(2,1)} %collective-permute-done.6.refs_3_), channel_id=1, source_target_pairs={{0,8},{8,0},{1,9},{9,1},{2,10},{10,2},{3,11},{11,3},{4,12},{12,4},... | collective-permute-start | bytes 1572872 | tf_op jit(solution)/shard_map/ppermute | solution.py:23
  77.6 7.7 %collective-permute-start.10 = (bf16[256,512]{1,0:T(8,128)(2,1)}, bf16[256,512]{1,0:T(8,128)(2,1)}, u32[]{:S(2)}, u32[]{:S(2)}) collective-permute-start(bf16[256,512]{1,0:T(8,128)(2,1)} %slice_select_fusion), channel_id=1, source_target_pairs={{0,16},{16,32},{32,48},{48,256},{256,272},{272,288},{288,304},{304... | collective-permute-start | bytes 786440 | tf_op jit(solution)/shard_map/ppermute | solution.py:216
  80.7 16.4 %collective-permute-start.9 = (bf16[512,512]{1,0:T(8,128)(2,1)S(1)}, bf16[512,512]{1,0:T(8,128)(2,1)}, u32[]{:S(2)}, u32[]{:S(2)}) collective-permute-start(bf16[512,512]{1,0:T(8,128)(2,1)S(1)} %collective-permute-done.8.refs_5_), channel_id=1, source_target_pairs={{0,8},{8,0},{1,9},{9,1},{2,10},{10,2},{3,11},{11,3},{4,12},{12,4},... | collective-permute-start | bytes 1572872 | tf_op jit(solution)/shard_map/ppermute | solution.py:23
  84.7 10.8 %copy-start.11 = (bf16[1,384,512]{2,1,0:T(8,128)(2,1)S(1)}, bf16[1,384,512]{2,1,0:T(8,128)(2,1)}, u32[]{:S(2)}) copy-start(bf16[1,384,512]{2,1,0:T(8,128)(2,1)} %get-tuple-element.35) | copy-start | bytes 1179652
  85.3 11.8 %collective-permute-start.11 = (bf16[256,512]{1,0:T(8,128)(2,1)}, bf16[256,512]{1,0:T(8,128)(2,1)}, u32[]{:S(2)}, u32[]{:S(2)}) collective-permute-start(bf16[256,512]{1,0:T(8,128)(2,1)} %collective-permute-done.10.refs_7_), channel_id=1, source_target_pairs={{0,8},{8,0},{1,9},{9,1},{2,10},{10,2},{3,11},{11,3},{4,12},{12,4},... | collective-permute-start | bytes 786440 | tf_op jit(solution)/shard_map/ppermute | solution.py:23
  97.1 6.5 %copy-start.1 = (bf16[2,256,512]{2,1,0:T(8,128)(2,1)S(1)}, bf16[2,256,512]{2,1,0:T(8,128)(2,1)}, u32[]{:S(2)}) copy-start(bf16[2,256,512]{2,1,0:T(8,128)(2,1)} %copy-done) | copy-start | bytes 1572868
  97.1 6.6 %copy-start.2 = (bf16[2,128,512]{2,1,0:T(8,128)(2,1)S(1)}, bf16[2,128,512]{2,1,0:T(8,128)(2,1)}, u32[]{:S(2)}) copy-start(bf16[2,128,512]{2,1,0:T(8,128)(2,1)} %pad_maximum_fusion.2.query_ref) | copy-start | bytes 786436
  101.6 5.4 %copy-start.3 = (f32[128,512]{1,0:T(8,128)}, f32[128,512]{1,0:T(8,128)S(1)}, u32[]{:S(2)}) copy-start(f32[128,512]{1,0:T(8,128)S(1)} %get-tuple-element.20.keep_ref) | copy-start | bytes 786436
  101.6 29.8 %copy-start.8 = (bf16[1,128,512]{2,1,0:T(8,128)(2,1)S(1)}, bf16[1,128,512]{2,1,0:T(8,128)(2,1)}, u32[]{:S(2)}) copy-start(bf16[1,128,512]{2,1,0:T(8,128)(2,1)} %param.8) | copy-start | bytes 393220
  101.6 29.8 %copy-start.9 = (f32[32,256]{1,0:T(8,128)S(1)}, f32[32,256]{1,0:T(8,128)}, u32[]{:S(2)}) copy-start(f32[32,256]{1,0:T(8,128)} %concatenate.16.rows_ref) | copy-start | bytes 98308
  101.6 15.0 %collective-permute-start.12 = (bf16[128,512]{1,0:T(8,128)(2,1)}, bf16[128,512]{1,0:T(8,128)(2,1)S(1)}, u32[]{:S(2)}, u32[]{:S(2)}) collective-permute-start(bf16[128,512]{1,0:T(8,128)(2,1)} %get-tuple-element.21.give_ref), channel_id=1, source_target_pairs={{0,64},{64,0},{1,65},{65,1},{2,66},{66,2},{3,67},{67,3},{4,68},{68... | collective-permute-start | bytes 393224 | tf_op jit(solution)/shard_map/ppermute | solution.py:23
  119.0 14.9 %all-to-all-start.2 = ((f32[8,32,128]{2,1,0:T(8,128)}), f32[8,32,128]{2,1,0:T(8,128)S(1)}, u32[]{:S(2)}, u32[]{:S(2)}) async-start(f32[8,32,128]{2,1,0:T(8,128)} %broadcast_in_dim.35), calls=%async_computation.2 | async-start | bytes 262144 | tf_op jit(solution)/shard_map/all_to_all | solution.py:40
  123.5 8.0 %collective-permute-start.13 = (bf16[128,512]{1,0:T(8,128)(2,1)S(1)}, bf16[128,512]{1,0:T(8,128)(2,1)S(1)}, u32[]{:S(2)}, u32[]{:S(2)}) collective-permute-start(bf16[128,512]{1,0:T(8,128)(2,1)S(1)} %get-tuple-element.26.grad_ref), channel_id=1, source_target_pairs={{8,0},{16,8},{24,16},{32,24},{40,32},{48,40},{56,48},{64,56},{72,6... | collective-permute-start | bytes 393224 | tf_op jit(solution)/shard_map/ppermute | solution.py:34
  (4 other events, 8.0 us)

commit v5 on v4

--- a/solution.py
+++ b/solution.py
@@ -109,11 +109,12 @@
     far = lax.rem(z + 4, 8)
     pieces += [(far, jnp.where(core == 0, 0, depth // 2)), (far, jnp.where(core == 0, depth // 2, 0))]
     for out_ref, p in ((give_ref, 1 - xp), (keep_ref, xp)):
-        rows = pl.ds(pl.multiple_of(p * TAPS, TAPS), TAPS)
         total = jnp.zeros(out_ref.shape, F32)
         for weight_ref, (place, offset) in zip(weights, pieces):
-            columns = pl.ds(pl.multiple_of(place * depth + offset, LANES), weight_ref.shape[0])
-            total += jnp.dot(cot_ref[rows, columns], weight_ref[...], preferred_element_type=F32)
+            size = weight_ref.shape[0]
+            columns = pl.ds(pl.multiple_of(place * depth + offset, LANES), size)
+            part = cot_ref[:, p, :, columns].reshape(TAPS, size)
+            total += jnp.dot(part, weight_ref[...], preferred_element_type=F32)
         out_ref[...] = total.astype(out_ref.dtype)
 
 
@@ -188,13 +189,16 @@
     )(place, cotangent, *weights)
 
 
-def cotangent_columns(cotangent, after):
+def cotangent_columns(cotangent):
     rows, width = cotangent.shape
     depth = width // 64
     parts = cotangent.reshape(rows, 2, 2, 2, 4, 2, depth).transpose(3, 0, 1, 4, 5, 2, 6)
-    parts, _ = lax.optimization_barrier((parts.reshape(2, 1, rows, 32 * depth), after))
-    copies = jnp.broadcast_to(parts, (2, 8, rows, 32 * depth)).reshape(16, rows, 32 * depth)
-    return lax.all_to_all(copies, ("xp", "y"), split_axis=0, concat_axis=0).reshape(16 * rows, 32 * depth)
+    parts = parts.reshape(2, rows, 32 * depth)
+    xp = lax.axis_index("xp")
+    keep = lax.dynamic_index_in_dim(parts, xp, 0, keepdims=False)
+    give = lax.dynamic_index_in_dim(parts, 1 - xp, 0, keepdims=False)
+    ready = in_order(keep, swap(give, "xp"), "xp")
+    return ready, lax.all_gather(ready, "y", axis=0)
 
 
 def chip_weights(both):
@@ -221,8 +225,9 @@
     query, keys, values = query_branch[0], key_branch[0], value_branch[0]
     tokens, width = query.shape
     groups = filters.shape[0]
+    ready, gathered = cotangent_columns(cotangent[0])
     both = in_order(out_weight, swap(out_weight, "xh"), "xh")
-    gathered = cotangent_columns(cotangent[0], both)
+    both, _ = lax.optimization_barrier((both, ready))
     chip = chip_weights(both)
     weights = weight_blocks(chip)
 

time: 136 us -> 144 us (1.059)
  between operations: 1.02 us -> 14.5 us
  waiting for transfers between devices: 22.3 us -> 27.2 us
  starting transfers between devices: 71.3 us -> 67.5 us
  other arithmetic: 9.52 us -> 6.22 us
  local copies, waits for them, and re-layouts: 8.7 us -> 5.65 us
    all_to_all x1 -> x0, starting transfers between devices: 8.61 us -> none  [cotangent_columns(): lax.all_to_all(copies, ('xp', 'y'), split_axis=0, concat_axis=0)]
    ppermute x8 -> x9, starting transfers between devices: 29.7 us -> 37.6 us  [swap(): return lax.ppermute(block, axis, [(0, 1), (1, 0)])]
    ppermute x8 -> x9, waiting for transfers between devices: 2.11 us -> 5.82 us  [swap(): return lax.ppermute(block, axis, [(0, 1), (1, 0)])]
    ppermute x4, starting transfers between devices: 23.5 us -> 20 us  [weight_blocks(): got = lax.ppermute(got, Z + ('co',), route)]
    broadcast_in_dim x1 -> x0, local copies, waits for them, and re-layouts: 1.59 us -> none  [cotangent_columns(): jnp.broadcast_to(parts, (2, 8, rows, 32 * depth))]
  transfers between devices with their start and end apart: 16 -> 17, of which waited for: 7 -> 8; matrix products, arithmetic and copies ran while one was open for 7% -> 3% of each run, Pallas kernels for 7% -> 6%
where the time goes in v5:
time: 144 us; the launch traced here: 143 us
  starting transfers between devices  67.5 us (47%)
  waiting for transfers between devices  27.2 us (19%)
  between operations  14.5 us (10%)
  Pallas kernels  12.1 us (8%)
  blocking collectives  9.91 us (7%)
  other arithmetic  6.22 us (4%)
  local copies, waits for them, and re-layouts  5.65 us (4%)
    ppermute x9, starting transfers between devices, swap(): return lax.ppermute(block, axis, [(0, 1), (1, 0)])  37.6 us
    ppermute x4, starting transfers between devices, weight_blocks(): got = lax.ppermute(got, Z + ('co',), route)  20 us
    ppermute x4, waiting for transfers between devices, weight_blocks(): got = lax.ppermute(got, Z + ('co',), route)  13.3 us
    all_to_all x1, blocking collectives, sum_over(): lax.all_to_all(copies, axes, split_axis=0, concat_axis=0)  9.91 us
    ppermute x2, waiting for transfers between devices, from_behind(): return lax.ppermute(block, CONTEXT, route)  8.09 us
    ppermute x9, waiting for transfers between devices, swap(): return lax.ppermute(block, axis, [(0, 1), (1, 0)])  5.82 us
    ppermute x2, starting transfers between devices, from_behind(): return lax.ppermute(block, CONTEXT, route)  4.96 us
    all_to_all x1, starting transfers between devices, sum_over(): lax.all_to_all(copies, axes, split_axis=0, concat_axis=0)  4.92 us
  transfers between devices with their start and end apart: 17, of which 8 were waited for; matrix products, arithmetic and copies ran while one was open for 3% of the time, Pallas kernels for 6%

profile of v5, /device:TPU:1, one launch (start us, length us, event | category | flops | bytes accessed | tf_op | source)
XLA Modules:
  0.0 143.1 jit_solution(15701818187322410446)
XLA Ops:
  8.9 3.9 %collective-permute-start = (bf16[16,4096]{1,0:T(8,128)(2,1)S(1)}, bf16[16,4096]{1,0:T(8,128)(2,1)S(1)}, u32[]{:S(2)}, u32[]{:S(2)}) collective-permute-start(bf16[16,4096]{1,0:T(8,128)(2,1)S(1)} %dynamic-slice_bitcast_fusion), channel_id=1, source_target_pairs={{0,64},{64,0},{1,65},{65,1},{2,66},{66,2},{3,67},{67,3},{4,68},{68... | collective-permute-start | bytes 393224 | tf_op jit(solution)/shard_map/ppermute | solution.py:23
  12.8 2.3 %collective-permute-done = bf16[16,4096]{1,0:T(8,128)(2,1)S(1)} collective-permute-done((bf16[16,4096]{1,0:T(8,128)(2,1)S(1)}, bf16[16,4096]{1,0:T(8,128)(2,1)S(1)}, u32[]{:S(2)}, u32[]{:S(2)}) %collective-permute-start) | collective-permute-done | bytes 131104 | tf_op jit(solution)/shard_map/ppermute | solution.py:23
  16.0 5.4 %collective-permute-start.1 = (bf16[128,512]{1,0:T(8,128)(2,1)S(1)}, bf16[128,512]{1,0:T(8,128)(2,1)S(1)}, u32[]{:S(2)}, u32[]{:S(2)}) collective-permute-start(bf16[128,512]{1,0:T(8,128)(2,1)S(1)} %copy-done.9), channel_id=1, source_target_pairs={{0,128},{128,0},{1,129},{129,1},{2,130},{130,2},{3,131},{131,3},{4... | collective-permute-start | bytes 393224 | tf_op jit(solution)/shard_map/ppermute | solution.py:23
  21.5 2.3 %collective-permute-done.1 = bf16[128,512]{1,0:T(8,128)(2,1)S(1)} collective-permute-done((bf16[128,512]{1,0:T(8,128)(2,1)S(1)}, bf16[128,512]{1,0:T(8,128)(2,1)S(1)}, u32[]{:S(2)}, u32[]{:S(2)}) %collective-permute-start.1) | collective-permute-done | bytes 131104 | tf_op jit(solution)/shard_map/ppermute | solution.py:23
  23.9 9.9 %collective-permute-start.2 = (bf16[256,512]{1,0:T(8,128)(2,1)S(1)}, bf16[256,512]{1,0:T(8,128)(2,1)S(1)}, u32[]{:S(2)}, u32[]{:S(2)}) collective-permute-start(bf16[256,512]{1,0:T(8,128)(2,1)S(1)} %bitcast.52), channel_id=1, source_target_pairs={{0,8},{8,0},{1,9},{9,1},{2,10},{10,2},{3,11},{11,3},{4,12},{12,4},... | collective-permute-start | bytes 786440 | tf_op jit(solution)/shard_map/ppermute | solution.py:23
  35.1 5.6 %collective-permute-start.5 = (bf16[512,512]{1,0:T(8,128)(2,1)S(1)}, bf16[512,512]{1,0:T(8,128)(2,1)S(1)}, u32[]{:S(2)}, u32[]{:S(2)}) collective-permute-start(bf16[512,512]{1,0:T(8,128)(2,1)S(1)} %bitcast.46), channel_id=1, source_target_pairs={{0,16},{16,32},{32,48},{48,256},{256,272},{272,288},{288,304},{304... | collective-permute-start | bytes 1572872 | tf_op jit(solution)/shard_map/ppermute | solution.py:216
  40.6 6.1 %collective-permute-done.5.refs_1_ = bf16[512,512]{1,0:T(8,128)(2,1)S(1)} collective-permute-done((bf16[512,512]{1,0:T(8,128)(2,1)S(1)}, bf16[512,512]{1,0:T(8,128)(2,1)S(1)}, u32[]{:S(2)}, u32[]{:S(2)}) %collective-permute-start.5) | collective-permute-done | bytes 524320 | tf_op jit(solution)/shard_map/ppermute | solution.py:216
  46.7 5.4 %collective-permute-start.7 = (bf16[512,512]{1,0:T(8,128)(2,1)S(1)}, bf16[512,512]{1,0:T(8,128)(2,1)S(1)}, u32[]{:S(2)}, u32[]{:S(2)}) collective-permute-start(bf16[512,512]{1,0:T(8,128)(2,1)S(1)} %collective-permute-done.5.refs_1_), channel_id=1, source_target_pairs={{0,16},{16,32},{32,48},{48,256},{256,272},{272,288},{288,304},{304... | collective-permute-start | bytes 1572872 | tf_op jit(solution)/shard_map/ppermute | solution.py:216
  52.2 6.1 %collective-permute-done.7.refs_3_ = bf16[512,512]{1,0:T(8,128)(2,1)S(1)} collective-permute-done((bf16[512,512]{1,0:T(8,128)(2,1)S(1)}, bf16[512,512]{1,0:T(8,128)(2,1)S(1)}, u32[]{:S(2)}, u32[]{:S(2)}) %collective-permute-start.7) | collective-permute-done | bytes 524320 | tf_op jit(solution)/shard_map/ppermute | solution.py:216
  58.3 5.4 %collective-permute-start.9 = (bf16[512,512]{1,0:T(8,128)(2,1)S(1)}, bf16[512,512]{1,0:T(8,128)(2,1)S(1)}, u32[]{:S(2)}, u32[]{:S(2)}) collective-permute-start(bf16[512,512]{1,0:T(8,128)(2,1)S(1)} %collective-permute-done.7.refs_3_), channel_id=1, source_target_pairs={{0,16},{16,32},{32,48},{48,256},{256,272},{272,288},{288,304},{304... | collective-permute-start | bytes 1572872 | tf_op jit(solution)/shard_map/ppermute | solution.py:216
  65.9 3.2 %collective-permute-done.3 = bf16[128,512]{1,0:T(8,128)(2,1)S(1)} collective-permute-done((bf16[128,512]{1,0:T(8,128)(2,1)S(1)}, bf16[128,512]{1,0:T(8,128)(2,1)S(1)}, u32[]{:S(2)}, u32[]{:S(2)}) %collective-permute-start.3) | collective-permute-done | bytes 131104 | tf_op jit(solution)/shard_map/ppermute | solution.py:34
  69.8 3.1 %collective-permute-start.4 = (bf16[384,512]{1,0:T(8,128)(2,1)}, bf16[384,512]{1,0:T(8,128)(2,1)}, u32[]{:S(2)}, u32[]{:S(2)}) collective-permute-start(bf16[384,512]{1,0:T(8,128)(2,1)} %get-tuple-element.34), channel_id=1, source_target_pairs={{0,64},{64,0},{1,65},{65,1},{2,66},{66,2},{3,67},{67,3},{4,68},{68... | collective-permute-start | bytes 1179656 | tf_op jit(solution)/shard_map/ppermute | solution.py:23
  73.0 4.8 %collective-permute-start.6 = (bf16[512,512]{1,0:T(8,128)(2,1)S(1)}, bf16[512,512]{1,0:T(8,128)(2,1)}, u32[]{:S(2)}, u32[]{:S(2)}) collective-permute-start(bf16[512,512]{1,0:T(8,128)(2,1)S(1)} %collective-permute-done.5.refs_1_), channel_id=1, source_target_pairs={{0,8},{8,0},{1,9},{9,1},{2,10},{10,2},{3,11},{11,3},{4,12},{12,4},... | collective-permute-start | bytes 1572872 | tf_op jit(solution)/shard_map/ppermute | solution.py:23
  77.8 1.9 %collective-permute-start.8 = (bf16[512,512]{1,0:T(8,128)(2,1)S(1)}, bf16[512,512]{1,0:T(8,128)(2,1)}, u32[]{:S(2)}, u32[]{:S(2)}) collective-permute-start(bf16[512,512]{1,0:T(8,128)(2,1)S(1)} %collective-permute-done.7.refs_3_), channel_id=1, source_target_pairs={{0,8},{8,0},{1,9},{9,1},{2,10},{10,2},{3,11},{11,3},{4,12},{12,4},... | collective-permute-start | bytes 1572872 | tf_op jit(solution)/shard_map/ppermute | solution.py:23
  79.8 3.6 %collective-permute-start.11 = (bf16[256,512]{1,0:T(8,128)(2,1)S(1)}, bf16[256,512]{1,0:T(8,128)(2,1)S(1)}, u32[]{:S(2)}, u32[]{:S(2)}) collective-permute-start(bf16[256,512]{1,0:T(8,128)(2,1)S(1)} %slice_select_fusion), channel_id=1, source_target_pairs={{0,16},{16,32},{32,48},{48,256},{256,272},{272,288},{288,304},{304... | collective-permute-start | bytes 786440 | tf_op jit(solution)/shard_map/ppermute | solution.py:220
  87.2 4.5 %collective-permute-start.12 = (bf16[256,512]{1,0:T(8,128)(2,1)S(1)}, bf16[256,512]{1,0:T(8,128)(2,1)}, u32[]{:S(2)}, u32[]{:S(2)}) collective-permute-start(bf16[256,512]{1,0:T(8,128)(2,1)S(1)} %collective-permute-done.11.refs_7_), channel_id=1, source_target_pairs={{0,8},{8,0},{1,9},{9,1},{2,10},{10,2},{3,11},{11,3},{4,12},{12,4},... | collective-permute-start | bytes 786440 | tf_op jit(solution)/shard_map/ppermute | solution.py:23
  99.3 3.3 %product.1 = (f32[128,512]{1,0:T(8,128)S(1)}, bf16[128,512]{1,0:T(8,128)(2,1)}) custom-call(s32[3]{0:T(128)S(1)} %pad_add_fusion.place_ref, bf16[8,2,16,4096]{3,2,1,0:T(8,128)(2,1)S(1)} %bitcast.45, bf16[512,512]{1,0:T(8,128)(2,1)S(1)} %bitcast.47, bf16[512,512]{1,0:T(8,128)(2,1)S(1)} %collective-permute-done.5.refs_1_, ...), custom_call_target="tpu_custom_call" | custom-call | tf_op jit(solution)/shard_map/product/pallas_call | solution.py:182
  102.6 2.0 %collective-permute-start.13 = (bf16[128,512]{1,0:T(8,128)(2,1)}, bf16[128,512]{1,0:T(8,128)(2,1)S(1)}, u32[]{:S(2)}, u32[]{:S(2)}) collective-permute-start(bf16[128,512]{1,0:T(8,128)(2,1)} %get-tuple-element.21.give_ref), channel_id=1, source_target_pairs={{0,64},{64,0},{1,65},{65,1},{2,66},{66,2},{3,67},{67,3},{4,68},{68... | collective-permute-start | bytes 393224 | tf_op jit(solution)/shard_map/ppermute | solution.py:23
  104.6 3.3 %lags.1 = f32[32,128]{1,0:T(8,128)S(1)} custom-call(f32[128,512]{1,0:T(8,128)S(1)} %get-tuple-element.20.keep_ref, bf16[128,512]{1,0:T(8,128)(2,1)} %get-tuple-element.21.give_ref, bf16[2,128,512]{2,1,0:T(8,128)(2,1)S(1)} %pad_maximum_fusion.2.query_ref, bf16[2,256,512]{2,1,0:T(8,128)(2,1)S(1)} %windows.1.window_ref), custom_call_target="tpu_custom_call" | custom-call | tf_op jit(solution)/shard_map/lags/pallas_call | solution.py:167
  108.0 9.9 %all_to_all.10 = f32[8,32,128]{2,1,0:T(8,128)S(1)} all-to-all(f32[8,32,128]{2,1,0:T(8,128)S(1)} %broadcast_in_dim.11), channel_id=1, replica_groups=mesh['zh'=2,'xh'=2,'xp'=2,'zl'=4,'co'=2,'y'=8] {'xh','xp','co'}, dimensions={0} | all-to-all | bytes 262144 | tf_op jit(solution)/shard_map/all_to_all | solution.py:40
  120.2 4.9 %all-to-all-start.1 = ((f32[8,32,128]{2,1,0:T(8,128)}), f32[8,32,128]{2,1,0:T(8,128)S(1)}, u32[]{:S(2)}, u32[]{:S(2)}) async-start(f32[8,32,128]{2,1,0:T(8,128)} %broadcast_in_dim.26), calls=%async_computation.1 | async-start | bytes 262144 | tf_op jit(solution)/shard_map/all_to_all | solution.py:40
  125.1 3.0 %collective-permute-start.14 = (bf16[128,512]{1,0:T(8,128)(2,1)S(1)}, bf16[128,512]{1,0:T(8,128)(2,1)S(1)}, u32[]{:S(2)}, u32[]{:S(2)}) collective-permute-start(bf16[128,512]{1,0:T(8,128)(2,1)S(1)} %get-tuple-element.26.grad_ref), channel_id=1, source_target_pairs={{8,0},{16,8},{24,16},{32,24},{40,32},{48,40},{56,48},{64,56},{72,6... | collective-permute-start | bytes 393224 | tf_op jit(solution)/shard_map/ppermute | solution.py:34
  128.2 4.9 %collective-permute-done.14.after_ref = bf16[128,512]{1,0:T(8,128)(2,1)S(1)} collective-permute-done((bf16[128,512]{1,0:T(8,128)(2,1)S(1)}, bf16[128,512]{1,0:T(8,128)(2,1)S(1)}, u32[]{:S(2)}, u32[]{:S(2)}) %collective-permute-start.14) | collective-permute-done | bytes 131104 | tf_op jit(solution)/shard_map/ppermute | solution.py:34
  133.1 2.5 %mixed_grad.1 = (bf16[128,512]{1,0:T(8,128)(2,1)}, bf16[128,512]{1,0:T(8,128)(2,1)}) custom-call(f32[32,256]{1,0:T(8,128)S(1)} %copy-done.6, bf16[128,512]{1,0:T(8,128)(2,1)S(1)} %get-tuple-element.26.grad_ref, bf16[128,512]{1,0:T(8,128)(2,1)S(1)} %collective-permute-done.14.after_ref, bf16[128,512]{1,0:T(8,128)(2,1)S(1)} %bitcast.49, ...), custom_call_target="tpu_custom_call" | custom-call | tf_op jit(solution)/shard_map/mixed_grad/pallas_call | solution.py:141
  (68 shorter events, 21.0 us)
Async XLA Ops:
  7.2 89.6 %all-gather.3.cloned.1.call-start = ((), (), s32[]{:S(2)}) async-start(), calls=%async_computation.2 | async-start | bytes 2359296 | tf_op jit(solution)/shard_map/all_gather | solution.py:201
  8.9 6.3 %collective-permute-start = (bf16[16,4096]{1,0:T(8,128)(2,1)S(1)}, bf16[16,4096]{1,0:T(8,128)(2,1)S(1)}, u32[]{:S(2)}, u32[]{:S(2)}) collective-permute-start(bf16[16,4096]{1,0:T(8,128)(2,1)S(1)} %dynamic-slice_bitcast_fusion), channel_id=1, source_target_pairs={{0,64},{64,0},{1,65},{65,1},{2,66},{66,2},{3,67},{67,3},{4,68},{68... | collective-permute-start | bytes 393224 | tf_op jit(solution)/shard_map/ppermute | solution.py:23
  15.2 48.5 %copy-start.1 = (bf16[1,128,512]{2,1,0:T(8,128)(2,1)S(1)}, bf16[1,128,512]{2,1,0:T(8,128)(2,1)}, u32[]{:S(2)}) copy-start(bf16[1,128,512]{2,1,0:T(8,128)(2,1)} %param.7) | copy-start | bytes 393220
  15.2 48.5 %copy-start.2 = (bf16[1,128,512]{2,1,0:T(8,128)(2,1)S(1)}, bf16[1,128,512]{2,1,0:T(8,128)(2,1)}, u32[]{:S(2)}) copy-start(bf16[1,128,512]{2,1,0:T(8,128)(2,1)} %param.8) | copy-start | bytes 393220
  15.2 50.6 %copy-start.10 = (bf16[32,128]{1,0:T(8,128)(2,1)S(1)}, bf16[32,128]{1,0:T(8,128)(2,1)}, u32[]{:S(2)}) copy-start(bf16[32,128]{1,0:T(8,128)(2,1)} %param.11) | copy-start | bytes 24580
  15.2 53.8 %copy-start.8 = (bf16[1,128,512]{2,1,0:T(8,128)(2,1)S(1)}, bf16[1,128,512]{2,1,0:T(8,128)(2,1)}, u32[]{:S(2)}) copy-start(bf16[1,128,512]{2,1,0:T(8,128)(2,1)} %param.6) | copy-start | bytes 393220
  16.0 7.8 %collective-permute-start.1 = (bf16[128,512]{1,0:T(8,128)(2,1)S(1)}, bf16[128,512]{1,0:T(8,128)(2,1)S(1)}, u32[]{:S(2)}, u32[]{:S(2)}) collective-permute-start(bf16[128,512]{1,0:T(8,128)(2,1)S(1)} %copy-done.9), channel_id=1, source_target_pairs={{0,128},{128,0},{1,129},{129,1},{2,130},{130,2},{3,131},{131,3},{4... | collective-permute-start | bytes 393224 | tf_op jit(solution)/shard_map/ppermute | solution.py:23
  23.9 11.1 %collective-permute-start.2 = (bf16[256,512]{1,0:T(8,128)(2,1)S(1)}, bf16[256,512]{1,0:T(8,128)(2,1)S(1)}, u32[]{:S(2)}, u32[]{:S(2)}) collective-permute-start(bf16[256,512]{1,0:T(8,128)(2,1)S(1)} %bitcast.52), channel_id=1, source_target_pairs={{0,8},{8,0},{1,9},{9,1},{2,10},{10,2},{3,11},{11,3},{4,12},{12,4},... | collective-permute-start | bytes 786440 | tf_op jit(solution)/shard_map/ppermute | solution.py:23
  35.1 11.7 %collective-permute-start.5 = (bf16[512,512]{1,0:T(8,128)(2,1)S(1)}, bf16[512,512]{1,0:T(8,128)(2,1)S(1)}, u32[]{:S(2)}, u32[]{:S(2)}) collective-permute-start(bf16[512,512]{1,0:T(8,128)(2,1)S(1)} %bitcast.46), channel_id=1, source_target_pairs={{0,16},{16,32},{32,48},{48,256},{256,272},{272,288},{288,304},{304... | collective-permute-start | bytes 1572872 | tf_op jit(solution)/shard_map/ppermute | solution.py:216
  46.7 11.5 %collective-permute-start.7 = (bf16[512,512]{1,0:T(8,128)(2,1)S(1)}, bf16[512,512]{1,0:T(8,128)(2,1)S(1)}, u32[]{:S(2)}, u32[]{:S(2)}) collective-permute-start(bf16[512,512]{1,0:T(8,128)(2,1)S(1)} %collective-permute-done.5.refs_1_), channel_id=1, source_target_pairs={{0,16},{16,32},{32,48},{48,256},{256,272},{272,288},{288,304},{304... | collective-permute-start | bytes 1572872 | tf_op jit(solution)/shard_map/ppermute | solution.py:216
  58.3 21.5 %collective-permute-start.9 = (bf16[512,512]{1,0:T(8,128)(2,1)S(1)}, bf16[512,512]{1,0:T(8,128)(2,1)S(1)}, u32[]{:S(2)}, u32[]{:S(2)}) collective-permute-start(bf16[512,512]{1,0:T(8,128)(2,1)S(1)} %collective-permute-done.7.refs_3_), channel_id=1, source_target_pairs={{0,16},{16,32},{32,48},{48,256},{256,272},{272,288},{288,304},{304... | collective-permute-start | bytes 1572872 | tf_op jit(solution)/shard_map/ppermute | solution.py:216
  63.7 5.3 %collective-permute-start.3 = (bf16[128,512]{1,0:T(8,128)(2,1)S(1)}, bf16[128,512]{1,0:T(8,128)(2,1)S(1)}, u32[]{:S(2)}, u32[]{:S(2)}) collective-permute-start(bf16[128,512]{1,0:T(8,128)(2,1)S(1)} %multiply_convert_fusion.2), channel_id=1, source_target_pairs={{0,8},{8,16},{16,24},{24,32},{32,40},{40,48},{48,56},{56,64},{64,7... | collective-permute-start | bytes 393224 | tf_op jit(solution)/shard_map/ppermute | solution.py:34
  69.8 23.5 %copy-start.7 = (bf16[1,384,512]{2,1,0:T(8,128)(2,1)}, bf16[1,384,512]{2,1,0:T(8,128)(2,1)S(1)}, u32[]{:S(2)}) copy-start(bf16[1,384,512]{2,1,0:T(8,128)(2,1)S(1)} %get-tuple-element.35) | copy-start | bytes 1179652
  69.8 23.5 %collective-permute-start.4 = (bf16[384,512]{1,0:T(8,128)(2,1)}, bf16[384,512]{1,0:T(8,128)(2,1)}, u32[]{:S(2)}, u32[]{:S(2)}) collective-permute-start(bf16[384,512]{1,0:T(8,128)(2,1)} %get-tuple-element.34), channel_id=1, source_target_pairs={{0,64},{64,0},{1,65},{65,1},{2,66},{66,2},{3,67},{67,3},{4,68},{68... | collective-permute-start | bytes 1179656 | tf_op jit(solution)/shard_map/ppermute | solution.py:23
  73.0 23.8 %collective-permute-start.6 = (bf16[512,512]{1,0:T(8,128)(2,1)S(1)}, bf16[512,512]{1,0:T(8,128)(2,1)}, u32[]{:S(2)}, u32[]{:S(2)}) collective-permute-start(bf16[512,512]{1,0:T(8,128)(2,1)S(1)} %collective-permute-done.5.refs_1_), channel_id=1, source_target_pairs={{0,8},{8,0},{1,9},{9,1},{2,10},{10,2},{3,11},{11,3},{4,12},{12,4},... | collective-permute-start | bytes 1572872 | tf_op jit(solution)/shard_map/ppermute | solution.py:23
  77.8 19.0 %collective-permute-start.8 = (bf16[512,512]{1,0:T(8,128)(2,1)S(1)}, bf16[512,512]{1,0:T(8,128)(2,1)}, u32[]{:S(2)}, u32[]{:S(2)}) collective-permute-start(bf16[512,512]{1,0:T(8,128)(2,1)S(1)} %collective-permute-done.7.refs_3_), channel_id=1, source_target_pairs={{0,8},{8,0},{1,9},{9,1},{2,10},{10,2},{3,11},{11,3},{4,12},{12,4},... | collective-permute-start | bytes 1572872 | tf_op jit(solution)/shard_map/ppermute | solution.py:23
  79.8 7.4 %collective-permute-start.11 = (bf16[256,512]{1,0:T(8,128)(2,1)S(1)}, bf16[256,512]{1,0:T(8,128)(2,1)S(1)}, u32[]{:S(2)}, u32[]{:S(2)}) collective-permute-start(bf16[256,512]{1,0:T(8,128)(2,1)S(1)} %slice_select_fusion), channel_id=1, source_target_pairs={{0,16},{16,32},{32,48},{48,256},{256,272},{272,288},{288,304},{304... | collective-permute-start | bytes 786440 | tf_op jit(solution)/shard_map/ppermute | solution.py:220
  83.4 13.4 %collective-permute-start.10 = (bf16[512,512]{1,0:T(8,128)(2,1)S(1)}, bf16[512,512]{1,0:T(8,128)(2,1)}, u32[]{:S(2)}, u32[]{:S(2)}) collective-permute-start(bf16[512,512]{1,0:T(8,128)(2,1)S(1)} %collective-permute-done.9.refs_5_), channel_id=1, source_target_pairs={{0,8},{8,0},{1,9},{9,1},{2,10},{10,2},{3,11},{11,3},{4,12},{12,4},... | collective-permute-start | bytes 1572872 | tf_op jit(solution)/shard_map/ppermute | solution.py:23
  87.2 9.6 %collective-permute-start.12 = (bf16[256,512]{1,0:T(8,128)(2,1)S(1)}, bf16[256,512]{1,0:T(8,128)(2,1)}, u32[]{:S(2)}, u32[]{:S(2)}) collective-permute-start(bf16[256,512]{1,0:T(8,128)(2,1)S(1)} %collective-permute-done.11.refs_7_), channel_id=1, source_target_pairs={{0,8},{8,0},{1,9},{9,1},{2,10},{10,2},{3,11},{11,3},{4,12},{12,4},... | collective-permute-start | bytes 786440 | tf_op jit(solution)/shard_map/ppermute | solution.py:23
  102.6 30.5 %copy-start.3 = (bf16[1,128,512]{2,1,0:T(8,128)(2,1)S(1)}, bf16[1,128,512]{2,1,0:T(8,128)(2,1)}, u32[]{:S(2)}) copy-start(bf16[1,128,512]{2,1,0:T(8,128)(2,1)} %param.8) | copy-start | bytes 393220
  102.6 30.5 %copy-start.6 = (f32[32,256]{1,0:T(8,128)S(1)}, f32[32,256]{1,0:T(8,128)}, u32[]{:S(2)}) copy-start(f32[32,256]{1,0:T(8,128)} %concatenate.16.rows_ref) | copy-start | bytes 98308
  102.6 15.3 %collective-permute-start.13 = (bf16[128,512]{1,0:T(8,128)(2,1)}, bf16[128,512]{1,0:T(8,128)(2,1)S(1)}, u32[]{:S(2)}, u32[]{:S(2)}) collective-permute-start(bf16[128,512]{1,0:T(8,128)(2,1)} %get-tuple-element.21.give_ref), channel_id=1, source_target_pairs={{0,64},{64,0},{1,65},{65,1},{2,66},{66,2},{3,67},{67,3},{4,68},{68... | collective-permute-start | bytes 393224 | tf_op jit(solution)/shard_map/ppermute | solution.py:23
  120.2 15.4 %all-to-all-start.1 = ((f32[8,32,128]{2,1,0:T(8,128)}), f32[8,32,128]{2,1,0:T(8,128)S(1)}, u32[]{:S(2)}, u32[]{:S(2)}) async-start(f32[8,32,128]{2,1,0:T(8,128)} %broadcast_in_dim.26), calls=%async_computation.1 | async-start | bytes 262144 | tf_op jit(solution)/shard_map/all_to_all | solution.py:40
  125.1 8.0 %collective-permute-start.14 = (bf16[128,512]{1,0:T(8,128)(2,1)S(1)}, bf16[128,512]{1,0:T(8,128)(2,1)S(1)}, u32[]{:S(2)}, u32[]{:S(2)}) collective-permute-start(bf16[128,512]{1,0:T(8,128)(2,1)S(1)} %get-tuple-element.26.grad_ref), channel_id=1, source_target_pairs={{8,0},{16,8},{24,16},{32,24},{40,32},{48,40},{56,48},{64,56},{72,6... | collective-permute-start | bytes 393224 | tf_op jit(solution)/shard_map/ppermute | solution.py:34
  (4 other events, 20.9 us)
Sparse Core Ops, SparseCore 0:
  16.1 46.2 all-gather.2

commit v6 on v4

--- a/solution.py
+++ b/solution.py
@@ -15,7 +15,8 @@
 BF16 = jnp.bfloat16
 
 Z = ("zh", "zl")
-CONTEXT = ("xh", "xp", "zl", "co")
+CONTEXT = ("x", "zl", "co")
+TURNS = (0, 1, 2, 3)
 VMEM = pltpu.CompilerParams(vmem_limit_bytes=8 * 1024 * 1024)
 
 
@@ -69,38 +70,47 @@
     value_grad_ref[...] = (mixed_grad * key_ref[...].astype(F32)).astype(BF16)
 
 
-def regroup(first, second):
-    low = (lane_group(first.shape) & 1) == 0
-    even = jnp.where(low, first, pltpu.roll(second, GROUP, 1))
-    odd = jnp.where(low, pltpu.roll(first, LANES - GROUP, 1), second)
-    return even, odd
+def regroup(blocks):
+    rows = blocks[0].shape[0]
+    group = lane_group((rows, LANES))
+    for bit in (1, 2):
+        low = (group & bit) == 0
+        out = list(blocks)
+        for b in range(4):
+            if b & bit:
+                continue
+            x0, x1 = blocks[b], blocks[b | bit]
+            out[b] = jnp.where(low, x0, pltpu.roll(x1, GROUP * bit, 1))
+            out[b | bit] = jnp.where(low, pltpu.roll(x0, LANES - GROUP * bit, 1), x1)
+        blocks = out
+    return blocks
 
 
 def window_kernel(window_ref, out_ref):
     n = 2 * TAPS
     across = lax.broadcasted_iota(jnp.int32, (n, n), 0) + lax.broadcasted_iota(jnp.int32, (n, n), 1)
     turn = (across == n - 1).astype(F32).astype(BF16)
-    turned = [jnp.dot(turn, window_ref[b], preferred_element_type=F32) for b in range(2)]
-    for a, block in enumerate(regroup(*turned)):
+    turned = [jnp.dot(turn, window_ref[b], preferred_element_type=F32) for b in range(4)]
+    for a, block in enumerate(regroup(turned)):
         out_ref[a] = block.astype(BF16)
 
 
 def lag_kernel(keep_ref, give_ref, query_ref, window_ref, lag_ref):
-    keep = keep_ref[...] * query_ref[0].astype(F32)
-    give = give_ref[...].astype(F32) * query_ref[1].astype(F32)
-    quarter = lax.broadcasted_iota(jnp.int32, (TAPS, LANES), 1) >> 5
-    for a, block in enumerate(regroup(keep, give)):
-        for q in range(4):
-            part = jnp.where(quarter == q, block, 0.0).astype(BF16)
+    grads = [keep_ref[...]] + [give_ref[b].astype(F32) for b in range(3)]
+    grads = [g * query_ref[b].astype(F32) for b, g in enumerate(grads)]
+    half = lax.broadcasted_iota(jnp.int32, (TAPS, LANES), 1) >> 6
+    for a, block in enumerate(regroup(grads)):
+        for h in range(2):
+            part = jnp.where(half == h, block, 0.0).astype(BF16)
             outer = lax.dot_general(part, window_ref[a], (((1,), (1,)), ((), ())), preferred_element_type=F32)
             skewed = pltpu.roll(outer, 1, 1, stride=1, stride_axis=0)
             sums = jnp.sum(skewed, axis=0, keepdims=True)
-            lag_ref[2 * q + a : 2 * q + a + 1, :] = sums[:, TAPS:]
+            lag_ref[4 * h + a : 4 * h + a + 1, :] = sums[:, TAPS:]
 
 
 def product_kernel(place_ref, cot_ref, *refs):
     weights, (keep_ref, give_ref) = refs[:-2], refs[-2:]
-    z, core, xp = place_ref[0], place_ref[1], place_ref[2]
+    z, core, x = place_ref[0], place_ref[1], place_ref[2]
     depth = weights[0].shape[0]
     pieces = [(z, 0)]
     for step in (1, 2, 3):
@@ -108,13 +118,16 @@
         pieces += [(jnp.where(core == 0, below, above), 0), (jnp.where(core == 0, above, below), 0)]
     far = lax.rem(z + 4, 8)
     pieces += [(far, jnp.where(core == 0, 0, depth // 2)), (far, jnp.where(core == 0, depth // 2, 0))]
-    for out_ref, p in ((give_ref, 1 - xp), (keep_ref, xp)):
-        rows = pl.ds(pl.multiple_of(p * TAPS, TAPS), TAPS)
-        total = jnp.zeros(out_ref.shape, F32)
+    for turned in (1, 2, 3, 0):
+        rows = pl.ds(pl.multiple_of(lax.rem(x + turned, 4) * TAPS, TAPS), TAPS)
+        total = jnp.zeros(keep_ref.shape, F32)
         for weight_ref, (place, offset) in zip(weights, pieces):
             columns = pl.ds(pl.multiple_of(place * depth + offset, LANES), weight_ref.shape[0])
             total += jnp.dot(cot_ref[rows, columns], weight_ref[...], preferred_element_type=F32)
-        out_ref[...] = total.astype(out_ref.dtype)
+        if turned:
+            give_ref[turned - 1] = total.astype(BF16)
+        else:
+            keep_ref[...] = total
 
 
 def lane_blocks(*lead):
@@ -153,8 +166,8 @@
     return pl.pallas_call(
         window_kernel,
         grid=(width // LANES,),
-        in_specs=[lane_blocks(2, 2 * TAPS)],
-        out_specs=lane_blocks(2, 2 * TAPS),
+        in_specs=[lane_blocks(4, 2 * TAPS)],
+        out_specs=lane_blocks(4, 2 * TAPS),
         out_shape=jax.ShapeDtypeStruct(windows.shape, BF16),
         compiler_params=VMEM,
         name="windows",
@@ -166,7 +179,7 @@
     return pl.pallas_call(
         lag_kernel,
         grid=(width // LANES,),
-        in_specs=[lane_blocks(TAPS), lane_blocks(TAPS), lane_blocks(2, TAPS), lane_blocks(2, 2 * TAPS)],
+        in_specs=[lane_blocks(TAPS), lane_blocks(3, TAPS), lane_blocks(4, TAPS), lane_blocks(4, 2 * TAPS)],
         out_specs=pl.BlockSpec((PER, TAPS), lambda l: (l, 0)),
         out_shape=jax.ShapeDtypeStruct((width // GROUP, TAPS), F32),
         compiler_params=VMEM,
@@ -176,31 +189,30 @@
 
 def partial_products(cotangent, weights):
     width = weights[0].shape[1]
-    place = jnp.stack([lax.axis_index(Z), lax.axis_index("co"), lax.axis_index("xp")]).astype(jnp.int32)
+    place = jnp.stack([lax.axis_index(Z), lax.axis_index("co"), lax.axis_index("x")]).astype(jnp.int32)
     whole = pl.BlockSpec(memory_space=pltpu.VMEM)
     return pl.pallas_call(
         product_kernel,
         in_specs=[pl.BlockSpec(memory_space=pltpu.SMEM)] + [whole] * (1 + len(weights)),
         out_specs=[whole, whole],
-        out_shape=[jax.ShapeDtypeStruct((TAPS, width), F32), jax.ShapeDtypeStruct((TAPS, width), BF16)],
+        out_shape=[jax.ShapeDtypeStruct((TAPS, width), F32), jax.ShapeDtypeStruct((3, TAPS, width), BF16)],
         compiler_params=VMEM,
         name="product",
     )(place, cotangent, *weights)
+
+
+def turn(block, axes, distance):
+    n = lax.axis_size(axes)
+    return lax.ppermute(block, axes, [((i + distance) % n, i) for i in range(n)])
 
 
 def cotangent_columns(cotangent, after):
     rows, width = cotangent.shape
     depth = width // 64
-    parts = cotangent.reshape(rows, 2, 2, 2, 4, 2, depth).transpose(3, 0, 1, 4, 5, 2, 6)
-    parts, _ = lax.optimization_barrier((parts.reshape(2, 1, rows, 32 * depth), after))
-    copies = jnp.broadcast_to(parts, (2, 8, rows, 32 * depth)).reshape(16, rows, 32 * depth)
-    return lax.all_to_all(copies, ("xp", "y"), split_axis=0, concat_axis=0).reshape(16 * rows, 32 * depth)
-
-
-def chip_weights(both):
-    rows, width = both.shape[0] * both.shape[1], both.shape[2]
-    both = both.reshape(rows, width)
-    return in_order(both, swap(both, "co"), "co").reshape(2 * rows, width)
+    parts = cotangent.reshape(rows, 2, 4, 4, 2, depth).transpose(2, 0, 1, 3, 4, 5)
+    parts, _ = lax.optimization_barrier((parts.reshape(4, 1, rows, 16 * depth), after))
+    copies = jnp.broadcast_to(parts, (4, 8, rows, 16 * depth)).reshape(32, rows, 16 * depth)
+    return lax.all_to_all(copies, ("x", "y"), split_axis=0, concat_axis=0).reshape(32 * rows, 16 * depth)
 
 
 def weight_blocks(chip):
@@ -221,12 +233,11 @@
     query, keys, values = query_branch[0], key_branch[0], value_branch[0]
     tokens, width = query.shape
     groups = filters.shape[0]
-    both = in_order(out_weight, swap(out_weight, "xh"), "xh")
-    gathered = cotangent_columns(cotangent[0], both)
-    chip = chip_weights(both)
+    chip = in_order(out_weight, swap(out_weight, "co"), "co").reshape(2 * out_weight.shape[0], width)
+    gathered = cotangent_columns(cotangent[0], chip)
     weights = weight_blocks(chip)
 
-    keys, _ = lax.optimization_barrier((keys, chip))
+    keys, _ = lax.optimization_barrier((keys, weights[1]))
     mixed = (keys.astype(F32) * values.astype(F32)).astype(BF16)
     before = from_behind(mixed, 1)
     window = jnp.concatenate([before, mixed], 0)
@@ -237,15 +248,17 @@
     conv = convolve(turned_rows, window)
 
     saved = jnp.concatenate([query, window], 0)
-    saved = jnp.stack([saved, swap(saved, "xp")])
+    saved = jnp.stack([saved if t == 0 else turn(saved, "x", t) for t in TURNS])
     queries = saved[:, :tokens]
     windows = turned_windows(saved[:, tokens:])
 
     gathered, conv, windows, queries, rows = lax.optimization_barrier((gathered, conv, windows, queries, rows))
     keep, give = partial_products(gathered, weights)
     lags = lag_totals(keep, give, queries, windows)
-    lag_sum = sum_over(lags, ("xh", "xp", "co"))
-    branch_grad = keep + swap(give, "xp").astype(F32)
+    lag_sum = sum_over(lags, ("x", "co"))
+    branch_grad = keep
+    for t in TURNS[1:]:
+        branch_grad = branch_grad + turn(give[t - 1], "x", -t).astype(F32)
     query_grad = (branch_grad * conv).astype(BF16)
     conv_grad = (branch_grad * query.astype(F32)).astype(BF16)
     lag_sum, conv_grad = lax.optimization_barrier((lag_sum, conv_grad))
@@ -257,7 +270,7 @@
 
 
 def solution(mesh):
-    fine = Mesh(mesh.devices.reshape(2, 2, 2, 4, 2, 8), ("zh", "xh", "xp", "zl", "co", "y"))
+    fine = Mesh(mesh.devices.reshape(2, 4, 4, 2, 8), ("zh", "x", "zl", "co", "y"))
     branch = P("zh", CONTEXT, "y")
     return jax.shard_map(
         local,

time: 136 us -> 131 us (0.963)
  starting transfers between devices: 71.3 us -> 79.3 us
  other arithmetic: 9.52 us -> 2.76 us
  waiting for transfers between devices: 22.3 us -> 18.2 us
  local copies, waits for them, and re-layouts: 8.7 us -> 7.32 us
    ppermute x0 -> x6, starting transfers between devices: none -> 20.6 us  [turn(): lax.ppermute(block, axes, [((i + distance) % n, i) for i in range(n)])]
    ppermute x8 -> x5, starting transfers between devices: 29.7 us -> 18.1 us  [swap(): return lax.ppermute(block, axis, [(0, 1), (1, 0)])]
    ppermute x0 -> x6, waiting for transfers between devices: none -> 8.54 us  [turn(): lax.ppermute(block, axes, [((i + distance) % n, i) for i in range(n)])]
    ppermute x4, waiting for transfers between devices: 12.8 us -> 4.75 us  [weight_blocks(): got = lax.ppermute(got, Z + ('co',), route)]
    all_to_all x1, starting transfers between devices: 8.61 us -> 4.44 us  [cotangent_columns(): lax.all_to_all(copies, ('x', 'y'), split_axis=0, concat_axis=0)]
    all_to_all x1, starting transfers between devices: 4.45 us -> 8.34 us  [sum_over(): lax.all_to_all(copies, axes, split_axis=0, concat_axis=0)]
    ppermute x2, waiting for transfers between devices: 7.41 us -> 4.91 us  [from_behind(): return lax.ppermute(block, CONTEXT, route)]
    another operation x3, other arithmetic: 2.77 us -> 0.33 us  [the longest x2 0.25 us: local(): saved = jnp.stack([saved if t == 0 else turn(saved, 'x', t) for t in TURNS])]
  transfers between devices with their start and end apart: 16 -> 19, of which waited for: 7 -> 6; matrix products, arithmetic and copies ran while one was open for 7% -> 3% of each run, Pallas kernels for 7% -> 7%
where the time goes in v6:
time: 131 us; the launch traced here: 130 us
  starting transfers between devices  79.3 us (61%)
  waiting for transfers between devices  18.2 us (14%)
  Pallas kernels  12.1 us (9%)
  blocking collectives  8.97 us (7%)
  local copies, waits for them, and re-layouts  7.32 us (6%)
  other arithmetic  2.76 us (2%)
    ppermute x4, starting transfers between devices, weight_blocks(): got = lax.ppermute(got, Z + ('co',), route)  22.9 us
    ppermute x6, starting transfers between devices, turn(): lax.ppermute(block, axes, [((i + distance) % n, i) for i in range(n)])  20.6 us
    ppermute x5, starting transfers between devices, swap(): return lax.ppermute(block, axis, [(0, 1), (1, 0)])  18.1 us
    all_to_all x1, blocking collectives, sum_over(): lax.all_to_all(copies, axes, split_axis=0, concat_axis=0)  8.97 us
    ppermute x6, waiting for transfers between devices, turn(): lax.ppermute(block, axes, [((i + distance) % n, i) for i in range(n)])  8.54 us
    all_to_all x1, starting transfers between devices, sum_over(): lax.all_to_all(copies, axes, split_axis=0, concat_axis=0)  8.34 us
    ppermute x2, starting transfers between devices, from_behind(): return lax.ppermute(block, CONTEXT, route)  4.96 us
    ppermute x2, waiting for transfers between devices, from_behind(): return lax.ppermute(block, CONTEXT, route)  4.91 us
  transfers between devices with their start and end apart: 19, of which 6 were waited for; matrix products, arithmetic and copies ran while one was open for 3% of the time, Pallas kernels for 7%

profile of v6, /device:TPU:1, one launch (start us, length us, event | category | flops | bytes accessed | tf_op | source)
XLA Modules:
  0.0 129.8 jit_solution(17004147335682539802)
XLA Ops:
  0.6 8.9 %collective-permute-start = (bf16[128,512]{1,0:T(8,128)(2,1)}, bf16[128,512]{1,0:T(8,128)(2,1)S(1)}, u32[]{:S(2)}, u32[]{:S(2)}) collective-permute-start(bf16[128,512]{1,0:T(8,128)(2,1)} %param.10), channel_id=1, source_target_pairs={{0,8},{8,0},{1,9},{9,1},{2,10},{10,2},{3,11},{11,3},{4,12},{12,4},... | collective-permute-start | bytes 393224 | tf_op jit(solution)/shard_map/ppermute | solution.py:24
  12.8 4.4 %all-to-all-start = ((bf16[32,16,2048]{2,1,0:T(8,128)(2,1)}), bf16[32,16,2048]{2,1,0:T(8,128)(2,1)S(1)}, u32[]{:S(2)}, u32[]{:S(2)}) async-start(bf16[32,16,2048]{2,1,0:T(8,128)(2,1)} %bitcast.41), calls=%async_computation | async-start | bytes 4194304 | tf_op jit(solution)/shard_map/all_to_all | solution.py:215
  17.2 10.7 %collective-permute-start.1 = (bf16[256,512]{1,0:T(8,128)(2,1)S(1)}, bf16[256,512]{1,0:T(8,128)(2,1)}, u32[]{:S(2)}, u32[]{:S(2)}) collective-permute-start(bf16[256,512]{1,0:T(8,128)(2,1)S(1)} %bitcast.36), channel_id=1, source_target_pairs={{0,16},{16,32},{32,48},{48,256},{256,272},{272,288},{288,304},{304... | collective-permute-start | bytes 786440 | tf_op jit(solution)/shard_map/ppermute | solution.py:224
  27.9 3.3 %collective-permute-done.1.refs_1_ = bf16[256,512]{1,0:T(8,128)(2,1)} collective-permute-done((bf16[256,512]{1,0:T(8,128)(2,1)S(1)}, bf16[256,512]{1,0:T(8,128)(2,1)}, u32[]{:S(2)}, u32[]{:S(2)}) %collective-permute-start.1) | collective-permute-done | bytes 262176 | tf_op jit(solution)/shard_map/ppermute | solution.py:224
  31.2 5.1 %collective-permute-start.7 = (bf16[256,512]{1,0:T(8,128)(2,1)}, bf16[256,512]{1,0:T(8,128)(2,1)}, u32[]{:S(2)}, u32[]{:S(2)}) collective-permute-start(bf16[256,512]{1,0:T(8,128)(2,1)} %collective-permute-done.1.refs_1_), channel_id=1, source_target_pairs={{0,16},{16,32},{32,48},{48,256},{256,272},{272,288},{288,304},{304... | collective-permute-start | bytes 786440 | tf_op jit(solution)/shard_map/ppermute | solution.py:224
  39.9 5.2 %collective-permute-start.9 = (bf16[256,512]{1,0:T(8,128)(2,1)}, bf16[256,512]{1,0:T(8,128)(2,1)S(1)}, u32[]{:S(2)}, u32[]{:S(2)}) collective-permute-start(bf16[256,512]{1,0:T(8,128)(2,1)} %collective-permute-done.7.refs_3_), channel_id=1, source_target_pairs={{0,16},{16,32},{32,48},{48,256},{256,272},{272,288},{288,304},{304... | collective-permute-start | bytes 786440 | tf_op jit(solution)/shard_map/ppermute | solution.py:224
  45.3 4.6 %collective-permute-start.3 = (bf16[384,512]{1,0:T(8,128)(2,1)S(1)}, bf16[384,512]{1,0:T(8,128)(2,1)S(1)}, u32[]{:S(2)}, u32[]{:S(2)}) collective-permute-start(bf16[384,512]{1,0:T(8,128)(2,1)S(1)} %get-tuple-element.36), channel_id=1, source_target_pairs={{64,0},{128,64},{192,128},{0,192},{65,1},{129,65},{193,129},{1,193... | collective-permute-start | bytes 1179656 | tf_op jit(solution)/shard_map/ppermute | solution.py:206
  49.9 2.4 %collective-permute-start.4 = (bf16[384,512]{1,0:T(8,128)(2,1)S(1)}, bf16[384,512]{1,0:T(8,128)(2,1)S(1)}, u32[]{:S(2)}, u32[]{:S(2)}) collective-permute-start(bf16[384,512]{1,0:T(8,128)(2,1)S(1)} %get-tuple-element.36), channel_id=1, source_target_pairs={{128,0},{192,64},{0,128},{64,192},{129,1},{193,65},{1,129},{65,193... | collective-permute-start | bytes 1179656 | tf_op jit(solution)/shard_map/ppermute | solution.py:206
  52.4 2.5 %collective-permute-start.5 = (bf16[384,512]{1,0:T(8,128)(2,1)S(1)}, bf16[384,512]{1,0:T(8,128)(2,1)S(1)}, u32[]{:S(2)}, u32[]{:S(2)}) collective-permute-start(bf16[384,512]{1,0:T(8,128)(2,1)S(1)} %get-tuple-element.36), channel_id=1, source_target_pairs={{192,0},{0,64},{64,128},{128,192},{193,1},{1,65},{65,129},{129,193... | collective-permute-start | bytes 1179656 | tf_op jit(solution)/shard_map/ppermute | solution.py:206
  57.5 2.3 %collective-permute-start.6 = (bf16[256,512]{1,0:T(8,128)(2,1)}, bf16[256,512]{1,0:T(8,128)(2,1)}, u32[]{:S(2)}, u32[]{:S(2)}) collective-permute-start(bf16[256,512]{1,0:T(8,128)(2,1)} %collective-permute-done.1.refs_1_), channel_id=1, source_target_pairs={{0,8},{8,0},{1,9},{9,1},{2,10},{10,2},{3,11},{11,3},{4,12},{12,4},... | collective-permute-start | bytes 786440 | tf_op jit(solution)/shard_map/ppermute | solution.py:24
  62.2 2.9 %collective-permute-done.3 = bf16[384,512]{1,0:T(8,128)(2,1)S(1)} collective-permute-done((bf16[384,512]{1,0:T(8,128)(2,1)S(1)}, bf16[384,512]{1,0:T(8,128)(2,1)S(1)}, u32[]{:S(2)}, u32[]{:S(2)}) %collective-permute-start.3) | collective-permute-done | bytes 393248 | tf_op jit(solution)/shard_map/ppermute | solution.py:206
  65.1 2.4 %collective-permute-start.8 = (bf16[256,512]{1,0:T(8,128)(2,1)}, bf16[256,512]{1,0:T(8,128)(2,1)}, u32[]{:S(2)}, u32[]{:S(2)}) collective-permute-start(bf16[256,512]{1,0:T(8,128)(2,1)} %collective-permute-done.7.refs_3_), channel_id=1, source_target_pairs={{0,8},{8,0},{1,9},{9,1},{2,10},{10,2},{3,11},{11,3},{4,12},{12,4},... | collective-permute-start | bytes 786440 | tf_op jit(solution)/shard_map/ppermute | solution.py:24
  69.3 2.5 %collective-permute-start.10 = (bf16[256,512]{1,0:T(8,128)(2,1)S(1)}, bf16[256,512]{1,0:T(8,128)(2,1)}, u32[]{:S(2)}, u32[]{:S(2)}) collective-permute-start(bf16[256,512]{1,0:T(8,128)(2,1)S(1)} %collective-permute-done.9.refs_5_), channel_id=1, source_target_pairs={{0,8},{8,0},{1,9},{9,1},{2,10},{10,2},{3,11},{11,3},{4,12},{12,4},... | collective-permute-start | bytes 786440 | tf_op jit(solution)/shard_map/ppermute | solution.py:24
  73.7 3.9 %collective-permute-done.5 = bf16[384,512]{1,0:T(8,128)(2,1)S(1)} collective-permute-done((bf16[384,512]{1,0:T(8,128)(2,1)S(1)}, bf16[384,512]{1,0:T(8,128)(2,1)S(1)}, u32[]{:S(2)}, u32[]{:S(2)}) %collective-permute-start.5) | collective-permute-done | bytes 393248 | tf_op jit(solution)/shard_map/ppermute | solution.py:206
  82.9 2.8 %product.1 = (f32[128,512]{1,0:T(8,128)S(1)}, bf16[3,128,512]{2,1,0:T(8,128)(2,1)S(1)}) custom-call(s32[3]{0:T(128)S(1)} %pad_add_fusion.place_ref, bf16[512,2048]{1,0:T(8,128)(2,1)S(1)} %bitcast.35, bf16[256,512]{1,0:T(8,128)(2,1)S(1)} %bitcast.37, bf16[256,512]{1,0:T(8,128)(2,1)} %collective-permute-done.1.refs_1_, ...), custom_call_target="tpu_custom_call" | custom-call | tf_op jit(solution)/shard_map/product/pallas_call | solution.py:194
  85.7 4.8 %collective-permute-start.13 = (bf16[128,512]{1,0:T(8,128)(2,1)S(1)}, bf16[128,512]{1,0:T(8,128)(2,1)S(1)}, u32[]{:S(2)}, u32[]{:S(2)}) collective-permute-start(bf16[128,512]{1,0:T(8,128)(2,1)S(1)} %get-tuple-element.32), channel_id=1, source_target_pairs={{192,0},{0,64},{64,128},{128,192},{193,1},{1,65},{65,129},{129,193... | collective-permute-start | bytes 393224 | tf_op jit(solution)/shard_map/ppermute | solution.py:206
  90.6 3.7 %collective-permute-start.14 = (bf16[128,512]{1,0:T(8,128)(2,1)S(1)}, bf16[128,512]{1,0:T(8,128)(2,1)S(1)}, u32[]{:S(2)}, u32[]{:S(2)}) collective-permute-start(bf16[128,512]{1,0:T(8,128)(2,1)S(1)} %get-tuple-element.34), channel_id=1, source_target_pairs={{128,0},{192,64},{0,128},{64,192},{129,1},{193,65},{1,129},{65,193... | collective-permute-start | bytes 393224 | tf_op jit(solution)/shard_map/ppermute | solution.py:206
  94.3 2.5 %collective-permute-start.15 = (bf16[128,512]{1,0:T(8,128)(2,1)S(1)}, bf16[128,512]{1,0:T(8,128)(2,1)S(1)}, u32[]{:S(2)}, u32[]{:S(2)}) collective-permute-start(bf16[128,512]{1,0:T(8,128)(2,1)S(1)} %get-tuple-element.33), channel_id=1, source_target_pairs={{64,0},{128,64},{192,128},{0,192},{65,1},{129,65},{193,129},{1,193... | collective-permute-start | bytes 393224 | tf_op jit(solution)/shard_map/ppermute | solution.py:206
  96.8 3.0 %lags.1 = f32[32,128]{1,0:T(8,128)S(1)} custom-call(f32[128,512]{1,0:T(8,128)S(1)} %get-tuple-element.20.keep_ref, bf16[3,128,512]{2,1,0:T(8,128)(2,1)S(1)} %get-tuple-element.21.give_ref, bf16[4,128,512]{2,1,0:T(8,128)(2,1)S(1)} %copy-done, bf16[4,256,512]{2,1,0:T(8,128)(2,1)S(1)} %windows.1.window_ref), custom_call_target="tpu_custom_call" | custom-call | tf_op jit(solution)/shard_map/lags/pallas_call | solution.py:179
  99.9 9.0 %all_to_all.15 = f32[8,32,128]{2,1,0:T(8,128)S(1)} all-to-all(f32[8,32,128]{2,1,0:T(8,128)S(1)} %broadcast_in_dim.32), channel_id=1, replica_groups=mesh['zh'=2,'x'=4,'zl'=4,'co'=2,'y'=8] {'x','co'}, dimensions={0} | all-to-all | bytes 262144 | tf_op jit(solution)/shard_map/all_to_all | solution.py:41
  110.3 8.3 %all-to-all-start.2 = ((f32[8,32,128]{2,1,0:T(8,128)}), f32[8,32,128]{2,1,0:T(8,128)S(1)}, u32[]{:S(2)}, u32[]{:S(2)}) async-start(f32[8,32,128]{2,1,0:T(8,128)} %broadcast_in_dim.35), calls=%async_computation.2 | async-start | bytes 262144 | tf_op jit(solution)/shard_map/all_to_all | solution.py:41
  118.7 3.0 %collective-permute-start.16 = (bf16[128,512]{1,0:T(8,128)(2,1)S(1)}, bf16[128,512]{1,0:T(8,128)(2,1)S(1)}, u32[]{:S(2)}, u32[]{:S(2)}) collective-permute-start(bf16[128,512]{1,0:T(8,128)(2,1)S(1)} %get-tuple-element.26.grad_ref), channel_id=1, source_target_pairs={{8,0},{16,8},{24,16},{32,24},{40,32},{48,40},{56,48},{64,56},{72,6... | collective-permute-start | bytes 393224 | tf_op jit(solution)/shard_map/ppermute | solution.py:35
  121.7 4.9 %collective-permute-done.16.after_ref = bf16[128,512]{1,0:T(8,128)(2,1)S(1)} collective-permute-done((bf16[128,512]{1,0:T(8,128)(2,1)S(1)}, bf16[128,512]{1,0:T(8,128)(2,1)S(1)}, u32[]{:S(2)}, u32[]{:S(2)}) %collective-permute-start.16) | collective-permute-done | bytes 131104 | tf_op jit(solution)/shard_map/ppermute | solution.py:35
  126.6 2.5 %mixed_grad.1 = (bf16[128,512]{1,0:T(8,128)(2,1)}, bf16[128,512]{1,0:T(8,128)(2,1)}) custom-call(f32[32,256]{1,0:T(8,128)S(1)} %copy-done.10, bf16[128,512]{1,0:T(8,128)(2,1)S(1)} %get-tuple-element.26.grad_ref, bf16[128,512]{1,0:T(8,128)(2,1)S(1)} %collective-permute-done.16.after_ref, bf16[128,512]{1,0:T(8,128)(2,1)S(1)} %bitcast.39, ...), custom_call_target="tpu_custom_call" | custom-call | tf_op jit(solution)/shard_map/mixed_grad/pallas_call | solution.py:153
  (77 shorter events, 22.8 us)
Async XLA Ops:
  0.6 10.4 %collective-permute-start = (bf16[128,512]{1,0:T(8,128)(2,1)}, bf16[128,512]{1,0:T(8,128)(2,1)S(1)}, u32[]{:S(2)}, u32[]{:S(2)}) collective-permute-start(bf16[128,512]{1,0:T(8,128)(2,1)} %param.10), channel_id=1, source_target_pairs={{0,8},{8,0},{1,9},{9,1},{2,10},{10,2},{3,11},{11,3},{4,12},{12,4},... | collective-permute-start | bytes 393224 | tf_op jit(solution)/shard_map/ppermute | solution.py:24
  12.8 23.7 %copy-start.7 = (bf16[1,128,512]{2,1,0:T(8,128)(2,1)S(1)}, bf16[1,128,512]{2,1,0:T(8,128)(2,1)}, u32[]{:S(2)}) copy-start(bf16[1,128,512]{2,1,0:T(8,128)(2,1)} %param.7) | copy-start | bytes 393220
  12.8 23.7 %copy-start.8 = (bf16[1,128,512]{2,1,0:T(8,128)(2,1)S(1)}, bf16[1,128,512]{2,1,0:T(8,128)(2,1)}, u32[]{:S(2)}) copy-start(bf16[1,128,512]{2,1,0:T(8,128)(2,1)} %param.8) | copy-start | bytes 393220
  12.8 32.5 %copy-start.11 = (bf16[1,128,512]{2,1,0:T(8,128)(2,1)S(1)}, bf16[1,128,512]{2,1,0:T(8,128)(2,1)}, u32[]{:S(2)}) copy-start(bf16[1,128,512]{2,1,0:T(8,128)(2,1)} %param.6) | copy-start | bytes 393220
  12.8 68.1 %all-to-all-start = ((bf16[32,16,2048]{2,1,0:T(8,128)(2,1)}), bf16[32,16,2048]{2,1,0:T(8,128)(2,1)S(1)}, u32[]{:S(2)}, u32[]{:S(2)}) async-start(bf16[32,16,2048]{2,1,0:T(8,128)(2,1)} %bitcast.41), calls=%async_computation | async-start | bytes 4194304 | tf_op jit(solution)/shard_map/all_to_all | solution.py:215
  17.2 14.0 %collective-permute-start.1 = (bf16[256,512]{1,0:T(8,128)(2,1)S(1)}, bf16[256,512]{1,0:T(8,128)(2,1)}, u32[]{:S(2)}, u32[]{:S(2)}) collective-permute-start(bf16[256,512]{1,0:T(8,128)(2,1)S(1)} %bitcast.36), channel_id=1, source_target_pairs={{0,16},{16,32},{32,48},{48,256},{256,272},{272,288},{288,304},{304... | collective-permute-start | bytes 786440 | tf_op jit(solution)/shard_map/ppermute | solution.py:224
  31.2 8.7 %collective-permute-start.7 = (bf16[256,512]{1,0:T(8,128)(2,1)}, bf16[256,512]{1,0:T(8,128)(2,1)}, u32[]{:S(2)}, u32[]{:S(2)}) collective-permute-start(bf16[256,512]{1,0:T(8,128)(2,1)} %collective-permute-done.1.refs_1_), channel_id=1, source_target_pairs={{0,16},{16,32},{32,48},{48,256},{256,272},{272,288},{288,304},{304... | collective-permute-start | bytes 786440 | tf_op jit(solution)/shard_map/ppermute | solution.py:224
  36.6 8.7 %collective-permute-start.2 = (bf16[128,512]{1,0:T(8,128)(2,1)S(1)}, bf16[128,512]{1,0:T(8,128)(2,1)S(1)}, u32[]{:S(2)}, u32[]{:S(2)}) collective-permute-start(bf16[128,512]{1,0:T(8,128)(2,1)S(1)} %multiply_convert_fusion.2), channel_id=1, source_target_pairs={{0,8},{8,16},{16,24},{24,32},{32,40},{40,48},{48,56},{56,64},{64,7... | collective-permute-start | bytes 393224 | tf_op jit(solution)/shard_map/ppermute | solution.py:35
  39.9 14.9 %collective-permute-start.9 = (bf16[256,512]{1,0:T(8,128)(2,1)}, bf16[256,512]{1,0:T(8,128)(2,1)S(1)}, u32[]{:S(2)}, u32[]{:S(2)}) collective-permute-start(bf16[256,512]{1,0:T(8,128)(2,1)} %collective-permute-done.7.refs_3_), channel_id=1, source_target_pairs={{0,16},{16,32},{32,48},{48,256},{256,272},{272,288},{288,304},{304... | collective-permute-start | bytes 786440 | tf_op jit(solution)/shard_map/ppermute | solution.py:224
  45.3 19.8 %collective-permute-start.3 = (bf16[384,512]{1,0:T(8,128)(2,1)S(1)}, bf16[384,512]{1,0:T(8,128)(2,1)S(1)}, u32[]{:S(2)}, u32[]{:S(2)}) collective-permute-start(bf16[384,512]{1,0:T(8,128)(2,1)S(1)} %get-tuple-element.36), channel_id=1, source_target_pairs={{64,0},{128,64},{192,128},{0,192},{65,1},{129,65},{193,129},{1,193... | collective-permute-start | bytes 1179656 | tf_op jit(solution)/shard_map/ppermute | solution.py:206
  49.9 19.4 %collective-permute-start.4 = (bf16[384,512]{1,0:T(8,128)(2,1)S(1)}, bf16[384,512]{1,0:T(8,128)(2,1)S(1)}, u32[]{:S(2)}, u32[]{:S(2)}) collective-permute-start(bf16[384,512]{1,0:T(8,128)(2,1)S(1)} %get-tuple-element.36), channel_id=1, source_target_pairs={{128,0},{192,64},{0,128},{64,192},{129,1},{193,65},{1,129},{65,193... | collective-permute-start | bytes 1179656 | tf_op jit(solution)/shard_map/ppermute | solution.py:206
  52.4 25.3 %collective-permute-start.5 = (bf16[384,512]{1,0:T(8,128)(2,1)S(1)}, bf16[384,512]{1,0:T(8,128)(2,1)S(1)}, u32[]{:S(2)}, u32[]{:S(2)}) collective-permute-start(bf16[384,512]{1,0:T(8,128)(2,1)S(1)} %get-tuple-element.36), channel_id=1, source_target_pairs={{192,0},{0,64},{64,128},{128,192},{193,1},{1,65},{65,129},{129,193... | collective-permute-start | bytes 1179656 | tf_op jit(solution)/shard_map/ppermute | solution.py:206
  54.9 16.9 %collective-permute-start.11 = (bf16[128,512]{1,0:T(8,128)(2,1)S(1)}, bf16[128,512]{1,0:T(8,128)(2,1)}, u32[]{:S(2)}, u32[]{:S(2)}) collective-permute-start(bf16[128,512]{1,0:T(8,128)(2,1)S(1)} %slice_select_fusion), channel_id=1, source_target_pairs={{0,16},{16,32},{32,48},{48,256},{256,272},{272,288},{288,304},{304... | collective-permute-start | bytes 393224 | tf_op jit(solution)/shard_map/ppermute | solution.py:228
  57.5 23.4 %collective-permute-start.6 = (bf16[256,512]{1,0:T(8,128)(2,1)}, bf16[256,512]{1,0:T(8,128)(2,1)}, u32[]{:S(2)}, u32[]{:S(2)}) collective-permute-start(bf16[256,512]{1,0:T(8,128)(2,1)} %collective-permute-done.1.refs_1_), channel_id=1, source_target_pairs={{0,8},{8,0},{1,9},{9,1},{2,10},{10,2},{3,11},{11,3},{4,12},{12,4},... | collective-permute-start | bytes 786440 | tf_op jit(solution)/shard_map/ppermute | solution.py:24
  65.1 15.8 %collective-permute-start.8 = (bf16[256,512]{1,0:T(8,128)(2,1)}, bf16[256,512]{1,0:T(8,128)(2,1)}, u32[]{:S(2)}, u32[]{:S(2)}) collective-permute-start(bf16[256,512]{1,0:T(8,128)(2,1)} %collective-permute-done.7.refs_3_), channel_id=1, source_target_pairs={{0,8},{8,0},{1,9},{9,1},{2,10},{10,2},{3,11},{11,3},{4,12},{12,4},... | collective-permute-start | bytes 786440 | tf_op jit(solution)/shard_map/ppermute | solution.py:24
  69.3 11.6 %collective-permute-start.10 = (bf16[256,512]{1,0:T(8,128)(2,1)S(1)}, bf16[256,512]{1,0:T(8,128)(2,1)}, u32[]{:S(2)}, u32[]{:S(2)}) collective-permute-start(bf16[256,512]{1,0:T(8,128)(2,1)S(1)} %collective-permute-done.9.refs_5_), channel_id=1, source_target_pairs={{0,8},{8,0},{1,9},{9,1},{2,10},{10,2},{3,11},{11,3},{4,12},{12,4},... | collective-permute-start | bytes 786440 | tf_op jit(solution)/shard_map/ppermute | solution.py:24
  71.8 9.1 %collective-permute-start.12 = (bf16[128,512]{1,0:T(8,128)(2,1)}, bf16[128,512]{1,0:T(8,128)(2,1)}, u32[]{:S(2)}, u32[]{:S(2)}) collective-permute-start(bf16[128,512]{1,0:T(8,128)(2,1)} %collective-permute-done.11.refs_7_), channel_id=1, source_target_pairs={{0,8},{8,0},{1,9},{9,1},{2,10},{10,2},{3,11},{11,3},{4,12},{12,4},... | collective-permute-start | bytes 393224 | tf_op jit(solution)/shard_map/ppermute | solution.py:24
  85.7 23.2 %collective-permute-start.13 = (bf16[128,512]{1,0:T(8,128)(2,1)S(1)}, bf16[128,512]{1,0:T(8,128)(2,1)S(1)}, u32[]{:S(2)}, u32[]{:S(2)}) collective-permute-start(bf16[128,512]{1,0:T(8,128)(2,1)S(1)} %get-tuple-element.32), channel_id=1, source_target_pairs={{192,0},{0,64},{64,128},{128,192},{193,1},{1,65},{65,129},{129,193... | collective-permute-start | bytes 393224 | tf_op jit(solution)/shard_map/ppermute | solution.py:206
  90.6 18.3 %collective-permute-start.14 = (bf16[128,512]{1,0:T(8,128)(2,1)S(1)}, bf16[128,512]{1,0:T(8,128)(2,1)S(1)}, u32[]{:S(2)}, u32[]{:S(2)}) collective-permute-start(bf16[128,512]{1,0:T(8,128)(2,1)S(1)} %get-tuple-element.34), channel_id=1, source_target_pairs={{128,0},{192,64},{0,128},{64,192},{129,1},{193,65},{1,129},{65,193... | collective-permute-start | bytes 393224 | tf_op jit(solution)/shard_map/ppermute | solution.py:206
  94.3 14.6 %collective-permute-start.15 = (bf16[128,512]{1,0:T(8,128)(2,1)S(1)}, bf16[128,512]{1,0:T(8,128)(2,1)S(1)}, u32[]{:S(2)}, u32[]{:S(2)}) collective-permute-start(bf16[128,512]{1,0:T(8,128)(2,1)S(1)} %get-tuple-element.33), channel_id=1, source_target_pairs={{64,0},{128,64},{192,128},{0,192},{65,1},{129,65},{193,129},{1,193... | collective-permute-start | bytes 393224 | tf_op jit(solution)/shard_map/ppermute | solution.py:206
  99.8 26.8 %copy-start.9 = (bf16[1,128,512]{2,1,0:T(8,128)(2,1)S(1)}, bf16[1,128,512]{2,1,0:T(8,128)(2,1)}, u32[]{:S(2)}) copy-start(bf16[1,128,512]{2,1,0:T(8,128)(2,1)} %param.8) | copy-start | bytes 393220
  99.9 26.8 %copy-start.10 = (f32[32,256]{1,0:T(8,128)S(1)}, f32[32,256]{1,0:T(8,128)}, u32[]{:S(2)}) copy-start(f32[32,256]{1,0:T(8,128)} %concatenate.16.rows_ref) | copy-start | bytes 98308
  110.3 18.8 %all-to-all-start.2 = ((f32[8,32,128]{2,1,0:T(8,128)}), f32[8,32,128]{2,1,0:T(8,128)S(1)}, u32[]{:S(2)}, u32[]{:S(2)}) async-start(f32[8,32,128]{2,1,0:T(8,128)} %broadcast_in_dim.35), calls=%async_computation.2 | async-start | bytes 262144 | tf_op jit(solution)/shard_map/all_to_all | solution.py:41
  118.7 8.0 %collective-permute-start.16 = (bf16[128,512]{1,0:T(8,128)(2,1)S(1)}, bf16[128,512]{1,0:T(8,128)(2,1)S(1)}, u32[]{:S(2)}, u32[]{:S(2)}) collective-permute-start(bf16[128,512]{1,0:T(8,128)(2,1)S(1)} %get-tuple-element.26.grad_ref), channel_id=1, source_target_pairs={{8,0},{16,8},{24,16},{32,24},{40,32},{48,40},{56,48},{64,56},{72,6... | collective-permute-start | bytes 393224 | tf_op jit(solution)/shard_map/ppermute | solution.py:35
  (10 other events, 128.1 us)

commit v7 on v6

v7 whole, which is shorter than its diff:
```python
import math

import jax
import jax.numpy as jnp
from jax import lax
from jax.experimental import pallas as pl
from jax.experimental.pallas import tpu as pltpu
from jax.sharding import Mesh, PartitionSpec as P

GROUP = 16
TAPS = 128
LANES = 128
PER = LANES // GROUP
F32 = jnp.float32
BF16 = jnp.bfloat16

Z = ("zh", "zl")
CONTEXT = ("x", "zl", "co")
VMEM = pltpu.CompilerParams(vmem_limit_bytes=8 * 1024 * 1024)


def swap(block, axis):
    return lax.ppermute(block, axis, [(0, 1), (1, 0)])


def in_order(mine, theirs, axis):
    first = lax.axis_index(axis) == 0
    return jnp.stack([jnp.where(first, mine, theirs), jnp.where(first, theirs, mine)])


def from_behind(block, distance):
    n = lax.axis_size(CONTEXT)
    route = [(i - distance, i) for i in range(n) if 0 <= i - distance < n]
    return lax.ppermute(block, CONTEXT, route)


def sum_over(block, axes):
    n = lax.axis_size(axes)
    copies = jnp.broadcast_to(block[None], (n,) + block.shape)
    return jnp.sum(lax.all_to_all(copies, axes, split_axis=0, concat_axis=0), axis=0)


def shifted_rows(row):
    return pltpu.roll(jnp.broadcast_to(row, (TAPS, 2 * TAPS)), 0, 1, stride=1, stride_axis=0)


def lane_group(shape):
    return lax.broadcasted_iota(jnp.int32, shape, 1) >> 4


def filtered(rows_ref, window):
    owner = lane_group((TAPS, LANES))
    total = jnp.zeros((TAPS, LANES), F32)
    for g in range(PER):
        table = shifted_rows(rows_ref[g : g + 1, :]).astype(BF16)
        term = jnp.dot(table, window, preferred_element_type=F32)
        total = jnp.where(owner == g, term, total)
    return total


def conv_kernel(rows_ref, window_ref, conv_ref, turned_ref):
    window = window_ref[...]
    conv_ref[...] = filtered(rows_ref, window)
    n = window.shape[0]
    across = lax.broadcasted_iota(jnp.int32, (n, n), 0) + lax.broadcasted_iota(jnp.int32, (n, n), 1)
    turn_rows = (across == n - 1).astype(F32).astype(BF16)
    turned_ref[...] = jnp.dot(turn_rows, window, preferred_element_type=F32).astype(BF16)


def mixed_grad_kernel(rows_ref, grad_ref, after_ref, key_ref, value_ref, key_grad_ref, value_grad_ref):
    window = jnp.concatenate([grad_ref[...], after_ref[...]], 0)
    mixed_grad = filtered(rows_ref, window)
    key_grad_ref[...] = (mixed_grad * value_ref[...].astype(F32)).astype(BF16)
    value_grad_ref[...] = (mixed_grad * key_ref[...].astype(F32)).astype(BF16)


def branch_kernel(terms_ref, conv_ref, query_ref, turned_ref, query_grad_ref, conv_grad_ref, lag_ref):
    branch_grad = terms_ref[0].astype(F32)
    for x in range(1, terms_ref.shape[0]):
        branch_grad = branch_grad + terms_ref[x].astype(F32)
    query_grad_ref[...] = (branch_grad * conv_ref[...]).astype(BF16)
    conv_grad = (branch_grad * query_ref[...].astype(F32)).astype(BF16)
    conv_grad_ref[...] = conv_grad
    owner = lane_group((TAPS, LANES))
    wide = conv_grad.astype(F32)
    for g in range(PER):
        part = jnp.where(owner == g, wide, 0.0).astype(BF16)
        outer = lax.dot_general(part, turned_ref[...], (((1,), (1,)), ((), ())), preferred_element_type=F32)
        skewed = pltpu.roll(outer, 1, 1, stride=1, stride_axis=0)
        lag_ref[g : g + 1, :] = jnp.sum(skewed, axis=0, keepdims=True)[:, TAPS:]


def product_kernel(place_ref, cot_ref, *refs):
    count = (len(refs) - 3) // 2
    weights_hbm, out_ref, total_ref, weights, sems = refs[:count], refs[count], refs[count + 1], refs[count + 2 : -1], refs[-1]
    copies = [pltpu.make_async_copy(weights_hbm[i], weights[i], sems.at[i]) for i in range(count)]
    for copy in copies:
        copy.start()
    z, core = place_ref[0], place_ref[1]
    depth = weights[0].shape[0]
    pieces = [(z, 0)]
    for step in (1, 2, 3):
        below, above = lax.rem(z + 8 - step, 8), lax.rem(z + step, 8)
        pieces += [(jnp.where(core == 0, below, above), 0), (jnp.where(core == 0, above, below), 0)]
    far = lax.rem(z + 4, 8)
    pieces += [(far, jnp.where(core == 0, 0, depth // 2)), (far, jnp.where(core == 0, depth // 2, 0))]
    for i, (place, offset) in enumerate(pieces):
        copies[i].wait()
        columns = pl.ds(pl.multiple_of(place * depth + offset, LANES), weights[i].shape[0])
        for x in range(4):
            rows = slice(x * TAPS, (x + 1) * TAPS)
            term = jnp.dot(cot_ref[rows, columns], weights[i][...], preferred_element_type=F32)
            if i:
                term = total_ref[x] + term
            if i < count - 1:
                total_ref[x] = term
            else:
                out_ref[x] = term.astype(BF16)


def lane_blocks(*lead):
    return pl.BlockSpec(lead + (LANES,), lambda l: (0,) * len(lead) + (l,))


def convolve(rows, window):
    width = window.shape[1]
    return pl.pallas_call(
        conv_kernel,
        grid=(width // LANES,),
        in_specs=[pl.BlockSpec((PER, 2 * TAPS), lambda l: (l, 0)), lane_blocks(2 * TAPS)],
        out_specs=[lane_blocks(TAPS), lane_blocks(2 * TAPS)],
        out_shape=[jax.ShapeDtypeStruct((TAPS, width), F32), jax.ShapeDtypeStruct((2 * TAPS, width), BF16)],
        compiler_params=VMEM,
        name="conv",
    )(rows, window)


def mixed_gradient(rows, grad, after, keys, values):
    width = grad.shape[1]
    tile = lane_blocks(TAPS)
    return pl.pallas_call(
        mixed_grad_kernel,
        grid=(width // LANES,),
        in_specs=[pl.BlockSpec((PER, 2 * TAPS), lambda l: (l, 0)), tile, tile, tile, tile],
        out_specs=[tile, tile],
        out_shape=[jax.ShapeDtypeStruct((TAPS, width), BF16)] * 2,
        compiler_params=VMEM,
        name="mixed_grad",
    )(rows, grad, after, keys, values)


def branch_gradients(terms, conv, query, turned):
    width = query.shape[1]
    tile = lane_blocks(TAPS)
    return pl.pallas_call(
        branch_kernel,
        grid=(width // LANES,),
        in_specs=[lane_blocks(terms.shape[0], TAPS), tile, tile, lane_blocks(2 * TAPS)],
        out_specs=[tile, tile, pl.BlockSpec((PER, TAPS), lambda l: (l, 0))],
        out_shape=[jax.ShapeDtypeStruct((TAPS, width), BF16)] * 2 + [jax.ShapeDtypeStruct((width // GROUP, TAPS), F32)],
        compiler_params=VMEM,
        name="branch",
    )(terms, conv, query, turned)


def partial_products(cotangent, weights):
    width = weights[0].shape[1]
    place = jnp.stack([lax.axis_index(Z), lax.axis_index("co")]).astype(jnp.int32)
    whole = pl.BlockSpec(memory_space=pltpu.VMEM)
    return pl.pallas_call(
        product_kernel,
        in_specs=[pl.BlockSpec(memory_space=pltpu.SMEM), whole]
        + [pl.BlockSpec(memory_space=pltpu.HBM)] * len(weights),
        out_specs=whole,
        out_shape=jax.ShapeDtypeStruct((4, TAPS, width), BF16),
        scratch_shapes=[pltpu.VMEM((4, TAPS, width), F32)]
        + [pltpu.VMEM(a.shape, a.dtype) for a in weights]
        + [pltpu.SemaphoreType.DMA((len(weights),))],
        compiler_params=VMEM,
        name="product",
    )(place, cotangent, *weights)


def cotangent_columns(cotangent, after):
    rows, width = cotangent.shape
    depth = width // 64
    parts = cotangent.reshape(rows, 2, 4, 4, 2, depth).transpose(2, 0, 1, 3, 4, 5)
    parts, _ = lax.optimization_barrier((parts.reshape(4, 1, rows, 16 * depth), after))
    copies = jnp.broadcast_to(parts, (4, 8, rows, 16 * depth)).reshape(32, rows, 16 * depth)
    return lax.all_to_all(copies, ("x", "y"), split_axis=0, concat_axis=0).reshape(32 * rows, 16 * depth)


def weight_blocks(chip):
    n = lax.axis_size(Z)
    route = [(2 * i, 2 * ((i + 1) % n)) for i in range(n)] + [(2 * i + 1, 2 * ((i - 1) % n) + 1) for i in range(n)]
    blocks = [chip]
    got = chip
    for _ in range(3):
        got = lax.ppermute(got, Z + ("co",), route)
        blocks += [got, swap(got, "co")]
    half = got.shape[0] // 2
    got = jnp.where(lax.axis_index("co") == 0, got[:half], got[half:])
    got = lax.ppermute(got, Z + ("co",), route)
    return blocks + [got, swap(got, "co")]


def local(query_branch, key_branch, value_branch, cotangent, out_weight, filters):
    query, keys, values = query_branch[0], key_branch[0], value_branch[0]
    tokens, width = query.shape
    groups = filters.shape[0]
    chip = in_order(out_weight, swap(out_weight, "co"), "co").reshape(2 * out_weight.shape[0], width)
    gathered = cotangent_columns(cotangent[0], chip)
    weights = weight_blocks(chip)

    keys, _ = lax.optimization_barrier((keys, weights[1]))
    mixed = (keys.astype(F32) * values.astype(F32)).astype(BF16)
    before = from_behind(mixed, 1)
    window = jnp.concatenate([before, mixed], 0)
    taps = filters.astype(F32)
    zero = jnp.zeros((groups, TAPS), F32)
    rows = jnp.concatenate([taps, zero], 1)
    turned_rows = jnp.concatenate([zero[:, :1], taps[:, ::-1], zero[:, 1:]], 1)
    conv, turned = convolve(turned_rows, window)

    gathered, conv, turned, rows = lax.optimization_barrier((gathered, conv, turned, rows))
    partial = partial_products(gathered, weights)
    terms = lax.all_to_all(partial, "x", split_axis=0, concat_axis=0)
    query_grad, conv_grad, lags = branch_gradients(terms, conv, query, turned)
    lag_sum = sum_over(sum_over(lags, ("x", "co")), Z)
    filter_grad = lag_sum * (1.0 / math.sqrt(2 * lax.axis_size(CONTEXT) * tokens * GROUP))
    after = from_behind(conv_grad, -1)
    key_grad, value_grad = mixed_gradient(rows, conv_grad, after, keys, values)
    return (query_grad[None], key_grad[None], value_grad[None], filter_grad)


def solution(mesh):
    fine = Mesh(mesh.devices.reshape(2, 4, 4, 2, 8), ("zh", "x", "zl", "co", "y"))
    branch = P("zh", CONTEXT, "y")
    return jax.shard_map(
        local,
        mesh=fine,
        in_specs=(
            branch,
            branch,
            branch,
            P("zh", CONTEXT + ("y",), None),
            P(("zh",) + CONTEXT, "y"),
            P("y", None),
        ),
        out_specs=(branch, branch, branch, P("y", None)),
        check_vma=False,
    )
```

time: 131 us -> 117 us (0.89)
  starting transfers between devices: 79.3 us -> 59.8 us
  blocking collectives: 8.97 us -> 21.6 us
  waiting for transfers between devices: 18.2 us -> 11.5 us
  other arithmetic: 2.76 us -> 4.71 us
  Pallas kernels: 12.1 us -> 10.3 us
    ppermute x6 -> x0, starting transfers between devices: 20.6 us -> none  [turn(): lax.ppermute(block, axes, [((i + distance) % n, i) for i in range(n)])]
    all_to_all x0 -> x1, blocking collectives: none -> 12.8 us  [local(): terms = lax.all_to_all(partial, 'x', split_axis=0, concat_axis=0)]
    ppermute x6 -> x0, waiting for transfers between devices: 8.54 us -> none  [turn(): lax.ppermute(block, axes, [((i + distance) % n, i) for i in range(n)])]
    ppermute x4, starting transfers between devices: 22.9 us -> 25.9 us  [weight_blocks(): got = lax.ppermute(got, Z + ('co',), route)]
    all_to_all x1, starting transfers between devices: 8.34 us -> 5.76 us  [sum_over(): lax.all_to_all(copies, axes, split_axis=0, concat_axis=0)]
    pallas_call x2 -> x1, Pallas kernels: 5.16 us -> 2.96 us  [branch_gradients(): pl.pallas_call(branch_kernel, grid=(width // LANES,), in_specs=[lane_bloc...]
    ppermute x4, waiting for transfers between devices: 4.75 us -> 6.59 us  [weight_blocks(): got = lax.ppermute(got, Z + ('co',), route)]
    unnamed x30 -> x20, local copies, waits for them, and re-layouts: 2.69 us -> 2.16 us
  transfers between devices with their start and end apart: 19 -> 13, of which waited for: 6 -> 3; matrix products, arithmetic and copies ran while one was open for 3% -> 5% of each run, Pallas kernels for 7% -> 4%
where the time goes in v7:
time: 117 us; the launch traced here: 116 us
  starting transfers between devices  59.8 us (51%)
  blocking collectives  21.6 us (18%)
  waiting for transfers between devices  11.5 us (10%)
  Pallas kernels  10.3 us (9%)
  local copies, waits for them, and re-layouts  7.37 us (6%)
  other arithmetic  4.71 us (4%)
    ppermute x4, starting transfers between devices, weight_blocks(): got = lax.ppermute(got, Z + ('co',), route)  25.9 us
    ppermute x5, starting transfers between devices, swap(): return lax.ppermute(block, axis, [(0, 1), (1, 0)])  18.8 us
    all_to_all x1, blocking collectives, local(): terms = lax.all_to_all(partial, 'x', split_axis=0, concat_axis=0)  12.8 us
    all_to_all x1, blocking collectives, sum_over(): lax.all_to_all(copies, axes, split_axis=0, concat_axis=0)  8.77 us
    ppermute x4, waiting for transfers between devices, weight_blocks(): got = lax.ppermute(got, Z + ('co',), route)  6.59 us
    all_to_all x1, starting transfers between devices, sum_over(): lax.all_to_all(copies, axes, split_axis=0, concat_axis=0)  5.76 us
    ppermute x2, starting transfers between devices, from_behind(): return lax.ppermute(block, CONTEXT, route)  4.95 us
    ppermute x2, waiting for transfers between devices, from_behind(): return lax.ppermute(block, CONTEXT, route)  4.91 us
  transfers between devices with their start and end apart: 13, of which 3 were waited for; matrix products, arithmetic and copies ran while one was open for 5% of the time, Pallas kernels for 4%

profile of v7, /device:TPU:1, one launch (start us, length us, event | category | flops | bytes accessed | tf_op | source)
XLA Modules:
  0.0 116.2 jit_solution(16203116454532436084)
XLA Ops:
  0.6 8.8 %collective-permute-start = (bf16[128,512]{1,0:T(8,128)(2,1)}, bf16[128,512]{1,0:T(8,128)(2,1)S(1)}, u32[]{:S(2)}, u32[]{:S(2)}) collective-permute-start(bf16[128,512]{1,0:T(8,128)(2,1)} %param.10), channel_id=1, source_target_pairs={{0,8},{8,0},{1,9},{9,1},{2,10},{10,2},{3,11},{11,3},{4,12},{12,4},... | collective-permute-start | bytes 393224 | tf_op jit(solution)/shard_map/ppermute | solution.py:23
  11.9 1.6 %broadcast_in_dim.30 = bf16[4,8,16,2048]{3,2,1,0:T(8,128)(2,1)} broadcast(bf16[4,16,2048]{2,1,0:T(8,128)(2,1)S(1)} %bitcast.29), dimensions={0,2,3} | broadcast | bytes 2359296 | tf_op jit(solution)/shard_map/broadcast_in_dim | solution.py:189
  13.5 4.4 %all-to-all-start = ((bf16[32,16,2048]{2,1,0:T(8,128)(2,1)}), bf16[32,16,2048]{2,1,0:T(8,128)(2,1)S(1)}, u32[]{:S(2)}, u32[]{:S(2)}) async-start(bf16[32,16,2048]{2,1,0:T(8,128)(2,1)} %bitcast.28), calls=%async_computation | async-start | bytes 4194304 | tf_op jit(solution)/shard_map/all_to_all | solution.py:190
  17.9 10.7 %collective-permute-start.1 = (bf16[256,512]{1,0:T(8,128)(2,1)S(1)}, bf16[256,512]{1,0:T(8,128)(2,1)S(1)}, u32[]{:S(2)}, u32[]{:S(2)}) collective-permute-start(bf16[256,512]{1,0:T(8,128)(2,1)S(1)} %bitcast.22), channel_id=1, source_target_pairs={{0,16},{16,32},{32,48},{48,256},{256,272},{272,288},{288,304},{304... | collective-permute-start | bytes 786440 | tf_op jit(solution)/shard_map/ppermute | solution.py:199
  28.6 3.3 %collective-permute-done.1.refs_1_ = bf16[256,512]{1,0:T(8,128)(2,1)S(1)} collective-permute-done((bf16[256,512]{1,0:T(8,128)(2,1)S(1)}, bf16[256,512]{1,0:T(8,128)(2,1)S(1)}, u32[]{:S(2)}, u32[]{:S(2)}) %collective-permute-start.1) | collective-permute-done | bytes 262176 | tf_op jit(solution)/shard_map/ppermute | solution.py:199
  31.9 5.0 %collective-permute-start.4 = (bf16[256,512]{1,0:T(8,128)(2,1)S(1)}, bf16[256,512]{1,0:T(8,128)(2,1)S(1)}, u32[]{:S(2)}, u32[]{:S(2)}) collective-permute-start(bf16[256,512]{1,0:T(8,128)(2,1)S(1)} %collective-permute-done.1.refs_1_), channel_id=1, source_target_pairs={{0,16},{16,32},{32,48},{48,256},{256,272},{272,288},{288,304},{304... | collective-permute-start | bytes 786440 | tf_op jit(solution)/shard_map/ppermute | solution.py:199
  36.9 3.3 %collective-permute-done.4.refs_3_ = bf16[256,512]{1,0:T(8,128)(2,1)S(1)} collective-permute-done((bf16[256,512]{1,0:T(8,128)(2,1)S(1)}, bf16[256,512]{1,0:T(8,128)(2,1)S(1)}, u32[]{:S(2)}, u32[]{:S(2)}) %collective-permute-start.4) | collective-permute-done | bytes 262176 | tf_op jit(solution)/shard_map/ppermute | solution.py:199
  40.2 5.3 %collective-permute-start.6 = (bf16[256,512]{1,0:T(8,128)(2,1)S(1)}, bf16[256,512]{1,0:T(8,128)(2,1)S(1)}, u32[]{:S(2)}, u32[]{:S(2)}) collective-permute-start(bf16[256,512]{1,0:T(8,128)(2,1)S(1)} %collective-permute-done.4.refs_3_), channel_id=1, source_target_pairs={{0,16},{16,32},{32,48},{48,256},{256,272},{272,288},{288,304},{304... | collective-permute-start | bytes 786440 | tf_op jit(solution)/shard_map/ppermute | solution.py:199
  46.4 1.9 %collective-permute-start.2 = (bf16[128,512]{1,0:T(8,128)(2,1)}, bf16[128,512]{1,0:T(8,128)(2,1)}, u32[]{:S(2)}, u32[]{:S(2)}) collective-permute-start(bf16[128,512]{1,0:T(8,128)(2,1)} %multiply_convert_fusion), channel_id=1, source_target_pairs={{0,8},{8,16},{16,24},{24,32},{32,40},{40,48},{48,56},{56,64},{64,7... | collective-permute-start | bytes 393224 | tf_op jit(solution)/shard_map/ppermute | solution.py:34
  48.3 3.0 %collective-permute-start.3 = (bf16[256,512]{1,0:T(8,128)(2,1)S(1)}, bf16[256,512]{1,0:T(8,128)(2,1)}, u32[]{:S(2)}, u32[]{:S(2)}) collective-permute-start(bf16[256,512]{1,0:T(8,128)(2,1)S(1)} %collective-permute-done.1.refs_1_), channel_id=1, source_target_pairs={{0,8},{8,0},{1,9},{9,1},{2,10},{10,2},{3,11},{11,3},{4,12},{12,4},... | collective-permute-start | bytes 786440 | tf_op jit(solution)/shard_map/ppermute | solution.py:23
  51.4 1.9 %collective-permute-start.5 = (bf16[256,512]{1,0:T(8,128)(2,1)S(1)}, bf16[256,512]{1,0:T(8,128)(2,1)}, u32[]{:S(2)}, u32[]{:S(2)}) collective-permute-start(bf16[256,512]{1,0:T(8,128)(2,1)S(1)} %collective-permute-done.4.refs_3_), channel_id=1, source_target_pairs={{0,8},{8,0},{1,9},{9,1},{2,10},{10,2},{3,11},{11,3},{4,12},{12,4},... | collective-permute-start | bytes 786440 | tf_op jit(solution)/shard_map/ppermute | solution.py:23
  54.0 4.9 %collective-permute-start.8 = (bf16[128,512]{1,0:T(8,128)(2,1)}, bf16[128,512]{1,0:T(8,128)(2,1)S(1)}, u32[]{:S(2)}, u32[]{:S(2)}) collective-permute-start(bf16[128,512]{1,0:T(8,128)(2,1)} %slice_select_fusion), channel_id=1, source_target_pairs={{0,16},{16,32},{32,48},{48,256},{256,272},{272,288},{288,304},{304... | collective-permute-start | bytes 393224 | tf_op jit(solution)/shard_map/ppermute | solution.py:203
  58.9 1.9 %collective-permute-start.7 = (bf16[256,512]{1,0:T(8,128)(2,1)S(1)}, bf16[256,512]{1,0:T(8,128)(2,1)}, u32[]{:S(2)}, u32[]{:S(2)}) collective-permute-start(bf16[256,512]{1,0:T(8,128)(2,1)S(1)} %collective-permute-done.6.refs_5_), channel_id=1, source_target_pairs={{0,8},{8,0},{1,9},{9,1},{2,10},{10,2},{3,11},{11,3},{4,12},{12,4},... | collective-permute-start | bytes 786440 | tf_op jit(solution)/shard_map/ppermute | solution.py:23
  61.6 3.1 %collective-permute-start.9 = (bf16[128,512]{1,0:T(8,128)(2,1)S(1)}, bf16[128,512]{1,0:T(8,128)(2,1)}, u32[]{:S(2)}, u32[]{:S(2)}) collective-permute-start(bf16[128,512]{1,0:T(8,128)(2,1)S(1)} %collective-permute-done.8.refs_7_), channel_id=1, source_target_pairs={{0,8},{8,0},{1,9},{9,1},{2,10},{10,2},{3,11},{11,3},{4,12},{12,4},... | collective-permute-start | bytes 393224 | tf_op jit(solution)/shard_map/ppermute | solution.py:23
  64.7 1.3 %concatenate.11.rows_ref = f32[32,256]{1,0:T(8,128)} pad(bf16[32,128]{1,0:T(8,128)(2,1)} %param.11, f32[]{:T(128)} %constant.24.clone.1), padding=0_0x0_128 | pad | bytes 40964 | tf_op jit(solution)/shard_map/concatenate | solution.py:221
  67.8 1.8 %conv.1 = (f32[128,512]{1,0:T(8,128)S(1)}, bf16[256,512]{1,0:T(8,128)(2,1)S(1)}) custom-call(f32[32,256]{1,0:T(8,128)S(1)} %copy-done.8, bf16[256,512]{1,0:T(8,128)(2,1)S(1)} %pad_maximum_fusion.1.window_ref), custom_call_target="tpu_custom_call" | custom-call | tf_op jit(solution)/shard_map/conv/pallas_call | solution.py:127
  71.0 3.0 %product.1 = bf16[4,128,512]{2,1,0:T(8,128)(2,1)S(1)} custom-call(s32[2]{0:T(128)S(1)} %pad_add_fusion.place_ref, bf16[512,2048]{1,0:T(8,128)(2,1)S(1)} %bitcast.21, bf16[256,512]{1,0:T(8,128)(2,1)S(1)} %bitcast.23, bf16[256,512]{1,0:T(8,128)(2,1)S(1)} %collective-permute-done.1.refs_1_, bf16[256,512]{1,0:T(8,128)(2,1)} %collective-permute-done.3.refs_2_, ...), custom_call_target="tpu_custom_call" | custom-call | tf_op jit(solution)/shard_map/product/pallas_call | solution.py:170
  74.1 12.8 %all_to_all.20.terms_ref = bf16[4,128,512]{2,1,0:T(8,128)(2,1)S(1)} all-to-all(bf16[4,128,512]{2,1,0:T(8,128)(2,1)S(1)} %product.1), channel_id=1, replica_groups=mesh['zh'=2,'x'=4,'zl'=4,'co'=2,'y'=8] {'x'}, dimensions={0} | all-to-all | bytes 1048576 | tf_op jit(solution)/shard_map/all_to_all | solution.py:227
  86.9 3.0 %branch.1 = (bf16[128,512]{1,0:T(8,128)(2,1)}, bf16[128,512]{1,0:T(8,128)(2,1)S(1)}, f32[32,128]{1,0:T(8,128)S(1)}) custom-call(bf16[4,128,512]{2,1,0:T(8,128)(2,1)S(1)} %all_to_all.20.terms_ref, f32[128,512]{1,0:T(8,128)S(1)} %copy-done.3, bf16[128,512]{1,0:T(8,128)(2,1)S(1)} %bitcast.27, bf16[256,512]{1,0:T(8,128)(2,1)S(1)} %copy-done.5), custom_call_target="tpu_custom_call" | custom-call | tf_op jit(solution)/shard_map/branch/pallas_call | solution.py:155
  89.9 8.8 %all_to_all.21 = f32[8,32,128]{2,1,0:T(8,128)S(1)} all-to-all(f32[8,32,128]{2,1,0:T(8,128)S(1)} %broadcast_in_dim.34), channel_id=1, replica_groups=mesh['zh'=2,'x'=4,'zl'=4,'co'=2,'y'=8] {'x','co'}, dimensions={0} | all-to-all | bytes 262144 | tf_op jit(solution)/shard_map/all_to_all | solution.py:40
  99.3 5.8 %all-to-all-start.3 = ((f32[8,32,128]{2,1,0:T(8,128)}), f32[8,32,128]{2,1,0:T(8,128)S(1)}, u32[]{:S(2)}, u32[]{:S(2)}) async-start(f32[8,32,128]{2,1,0:T(8,128)} %broadcast_in_dim.35), calls=%async_computation.3 | async-start | bytes 262144 | tf_op jit(solution)/shard_map/all_to_all | solution.py:40
  105.1 3.0 %collective-permute-start.10 = (bf16[128,512]{1,0:T(8,128)(2,1)S(1)}, bf16[128,512]{1,0:T(8,128)(2,1)S(1)}, u32[]{:S(2)}, u32[]{:S(2)}) collective-permute-start(bf16[128,512]{1,0:T(8,128)(2,1)S(1)} %get-tuple-element.26.grad_ref), channel_id=1, source_target_pairs={{8,0},{16,8},{24,16},{32,24},{40,32},{48,40},{56,48},{64,56},{72,6... | collective-permute-start | bytes 393224 | tf_op jit(solution)/shard_map/ppermute | solution.py:34
  108.1 4.9 %collective-permute-done.10.after_ref = bf16[128,512]{1,0:T(8,128)(2,1)S(1)} collective-permute-done((bf16[128,512]{1,0:T(8,128)(2,1)S(1)}, bf16[128,512]{1,0:T(8,128)(2,1)S(1)}, u32[]{:S(2)}, u32[]{:S(2)}) %collective-permute-start.10) | collective-permute-done | bytes 131104 | tf_op jit(solution)/shard_map/ppermute | solution.py:34
  113.0 2.5 %mixed_grad.1 = (bf16[128,512]{1,0:T(8,128)(2,1)}, bf16[128,512]{1,0:T(8,128)(2,1)}) custom-call(f32[32,256]{1,0:T(8,128)S(1)} %copy-done.7, bf16[128,512]{1,0:T(8,128)(2,1)S(1)} %get-tuple-element.26.grad_ref, bf16[128,512]{1,0:T(8,128)(2,1)S(1)} %collective-permute-done.10.after_ref, bf16[128,512]{1,0:T(8,128)(2,1)S(1)} %bitcast.25, ...), custom_call_target="tpu_custom_call" | custom-call | tf_op jit(solution)/shard_map/mixed_grad/pallas_call | solution.py:141
  (49 shorter events, 9.2 us)
Async XLA Ops:
  0.6 10.3 %collective-permute-start = (bf16[128,512]{1,0:T(8,128)(2,1)}, bf16[128,512]{1,0:T(8,128)(2,1)S(1)}, u32[]{:S(2)}, u32[]{:S(2)}) collective-permute-start(bf16[128,512]{1,0:T(8,128)(2,1)} %param.10), channel_id=1, source_target_pairs={{0,8},{8,0},{1,9},{9,1},{2,10},{10,2},{3,11},{11,3},{4,12},{12,4},... | collective-permute-start | bytes 393224 | tf_op jit(solution)/shard_map/ppermute | solution.py:23
  13.5 32.0 %copy-start.9 = (bf16[32,128]{1,0:T(8,128)(2,1)S(1)}, bf16[32,128]{1,0:T(8,128)(2,1)}, u32[]{:S(2)}) copy-start(bf16[32,128]{1,0:T(8,128)(2,1)} %param.11) | copy-start | bytes 24580
  13.5 32.2 %copy-start = (bf16[1,128,512]{2,1,0:T(8,128)(2,1)S(1)}, bf16[1,128,512]{2,1,0:T(8,128)(2,1)}, u32[]{:S(2)}) copy-start(bf16[1,128,512]{2,1,0:T(8,128)(2,1)} %param.7) | copy-start | bytes 393220
  13.5 32.2 %copy-start.1 = (bf16[1,128,512]{2,1,0:T(8,128)(2,1)S(1)}, bf16[1,128,512]{2,1,0:T(8,128)(2,1)}, u32[]{:S(2)}) copy-start(bf16[1,128,512]{2,1,0:T(8,128)(2,1)} %param.8) | copy-start | bytes 393220
  13.5 57.5 %all-to-all-start = ((bf16[32,16,2048]{2,1,0:T(8,128)(2,1)}), bf16[32,16,2048]{2,1,0:T(8,128)(2,1)S(1)}, u32[]{:S(2)}, u32[]{:S(2)}) async-start(bf16[32,16,2048]{2,1,0:T(8,128)(2,1)} %bitcast.28), calls=%async_computation | async-start | bytes 4194304 | tf_op jit(solution)/shard_map/all_to_all | solution.py:190
  17.9 14.0 %collective-permute-start.1 = (bf16[256,512]{1,0:T(8,128)(2,1)S(1)}, bf16[256,512]{1,0:T(8,128)(2,1)S(1)}, u32[]{:S(2)}, u32[]{:S(2)}) collective-permute-start(bf16[256,512]{1,0:T(8,128)(2,1)S(1)} %bitcast.22), channel_id=1, source_target_pairs={{0,16},{16,32},{32,48},{48,256},{256,272},{272,288},{288,304},{304... | collective-permute-start | bytes 786440 | tf_op jit(solution)/shard_map/ppermute | solution.py:199
  31.9 8.3 %collective-permute-start.4 = (bf16[256,512]{1,0:T(8,128)(2,1)S(1)}, bf16[256,512]{1,0:T(8,128)(2,1)S(1)}, u32[]{:S(2)}, u32[]{:S(2)}) collective-permute-start(bf16[256,512]{1,0:T(8,128)(2,1)S(1)} %collective-permute-done.1.refs_1_), channel_id=1, source_target_pairs={{0,16},{16,32},{32,48},{48,256},{256,272},{272,288},{288,304},{304... | collective-permute-start | bytes 786440 | tf_op jit(solution)/shard_map/ppermute | solution.py:199
  40.2 13.1 %collective-permute-start.6 = (bf16[256,512]{1,0:T(8,128)(2,1)S(1)}, bf16[256,512]{1,0:T(8,128)(2,1)S(1)}, u32[]{:S(2)}, u32[]{:S(2)}) collective-permute-start(bf16[256,512]{1,0:T(8,128)(2,1)S(1)} %collective-permute-done.4.refs_3_), channel_id=1, source_target_pairs={{0,16},{16,32},{32,48},{48,256},{256,272},{272,288},{288,304},{304... | collective-permute-start | bytes 786440 | tf_op jit(solution)/shard_map/ppermute | solution.py:199
  46.4 19.6 %collective-permute-start.2 = (bf16[128,512]{1,0:T(8,128)(2,1)}, bf16[128,512]{1,0:T(8,128)(2,1)}, u32[]{:S(2)}, u32[]{:S(2)}) collective-permute-start(bf16[128,512]{1,0:T(8,128)(2,1)} %multiply_convert_fusion), channel_id=1, source_target_pairs={{0,8},{8,16},{16,24},{24,32},{32,40},{40,48},{48,56},{56,64},{64,7... | collective-permute-start | bytes 393224 | tf_op jit(solution)/shard_map/ppermute | solution.py:34
  48.3 22.7 %collective-permute-start.3 = (bf16[256,512]{1,0:T(8,128)(2,1)S(1)}, bf16[256,512]{1,0:T(8,128)(2,1)}, u32[]{:S(2)}, u32[]{:S(2)}) collective-permute-start(bf16[256,512]{1,0:T(8,128)(2,1)S(1)} %collective-permute-done.1.refs_1_), channel_id=1, source_target_pairs={{0,8},{8,0},{1,9},{9,1},{2,10},{10,2},{3,11},{11,3},{4,12},{12,4},... | collective-permute-start | bytes 786440 | tf_op jit(solution)/shard_map/ppermute | solution.py:23
  51.4 19.6 %collective-permute-start.5 = (bf16[256,512]{1,0:T(8,128)(2,1)S(1)}, bf16[256,512]{1,0:T(8,128)(2,1)}, u32[]{:S(2)}, u32[]{:S(2)}) collective-permute-start(bf16[256,512]{1,0:T(8,128)(2,1)S(1)} %collective-permute-done.4.refs_3_), channel_id=1, source_target_pairs={{0,8},{8,0},{1,9},{9,1},{2,10},{10,2},{3,11},{11,3},{4,12},{12,4},... | collective-permute-start | bytes 786440 | tf_op jit(solution)/shard_map/ppermute | solution.py:23
  54.0 7.6 %collective-permute-start.8 = (bf16[128,512]{1,0:T(8,128)(2,1)}, bf16[128,512]{1,0:T(8,128)(2,1)S(1)}, u32[]{:S(2)}, u32[]{:S(2)}) collective-permute-start(bf16[128,512]{1,0:T(8,128)(2,1)} %slice_select_fusion), channel_id=1, source_target_pairs={{0,16},{16,32},{32,48},{48,256},{256,272},{272,288},{288,304},{304... | collective-permute-start | bytes 393224 | tf_op jit(solution)/shard_map/ppermute | solution.py:203
  58.9 12.1 %collective-permute-start.7 = (bf16[256,512]{1,0:T(8,128)(2,1)S(1)}, bf16[256,512]{1,0:T(8,128)(2,1)}, u32[]{:S(2)}, u32[]{:S(2)}) collective-permute-start(bf16[256,512]{1,0:T(8,128)(2,1)S(1)} %collective-permute-done.6.refs_5_), channel_id=1, source_target_pairs={{0,8},{8,0},{1,9},{9,1},{2,10},{10,2},{3,11},{11,3},{4,12},{12,4},... | collective-permute-start | bytes 786440 | tf_op jit(solution)/shard_map/ppermute | solution.py:23
  61.6 9.4 %collective-permute-start.9 = (bf16[128,512]{1,0:T(8,128)(2,1)S(1)}, bf16[128,512]{1,0:T(8,128)(2,1)}, u32[]{:S(2)}, u32[]{:S(2)}) collective-permute-start(bf16[128,512]{1,0:T(8,128)(2,1)S(1)} %collective-permute-done.8.refs_7_), channel_id=1, source_target_pairs={{0,8},{8,0},{1,9},{9,1},{2,10},{10,2},{3,11},{11,3},{4,12},{12,4},... | collective-permute-start | bytes 393224 | tf_op jit(solution)/shard_map/ppermute | solution.py:23
  67.0 0.8 copy-start.8
  69.6 0.7 copy-start.2
  70.3 0.7 copy-start.4
  71.0 15.9 %copy-start.3 = (f32[128,512]{1,0:T(8,128)S(1)}, f32[128,512]{1,0:T(8,128)}, u32[]{:S(2)}) copy-start(f32[128,512]{1,0:T(8,128)} %copy-done.2) | copy-start | bytes 786436
  71.0 15.9 %copy-start.5 = (bf16[256,512]{1,0:T(8,128)(2,1)S(1)}, bf16[256,512]{1,0:T(8,128)(2,1)}, u32[]{:S(2)}) copy-start(bf16[256,512]{1,0:T(8,128)(2,1)} %copy-done.4) | copy-start | bytes 786436
  71.0 15.9 %copy-start.6 = (bf16[1,128,512]{2,1,0:T(8,128)(2,1)S(1)}, bf16[1,128,512]{2,1,0:T(8,128)(2,1)}, u32[]{:S(2)}) copy-start(bf16[1,128,512]{2,1,0:T(8,128)(2,1)} %param.6) | copy-start | bytes 393220
  74.0 39.0 %copy-start.7 = (f32[32,256]{1,0:T(8,128)S(1)}, f32[32,256]{1,0:T(8,128)}, u32[]{:S(2)}) copy-start(f32[32,256]{1,0:T(8,128)} %concatenate.11.rows_ref) | copy-start | bytes 98308
  99.3 16.2 %all-to-all-start.3 = ((f32[8,32,128]{2,1,0:T(8,128)}), f32[8,32,128]{2,1,0:T(8,128)S(1)}, u32[]{:S(2)}, u32[]{:S(2)}) async-start(f32[8,32,128]{2,1,0:T(8,128)} %broadcast_in_dim.35), calls=%async_computation.3 | async-start | bytes 262144 | tf_op jit(solution)/shard_map/all_to_all | solution.py:40
  105.1 8.0 %collective-permute-start.10 = (bf16[128,512]{1,0:T(8,128)(2,1)S(1)}, bf16[128,512]{1,0:T(8,128)(2,1)S(1)}, u32[]{:S(2)}, u32[]{:S(2)}) collective-permute-start(bf16[128,512]{1,0:T(8,128)(2,1)S(1)} %get-tuple-element.26.grad_ref), channel_id=1, source_target_pairs={{8,0},{16,8},{24,16},{32,24},{40,32},{48,40},{56,48},{64,56},{72,6... | collective-permute-start | bytes 393224 | tf_op jit(solution)/shard_map/ppermute | solution.py:34

commit v8 on v7

--- a/solution.py
+++ b/solution.py
@@ -34,12 +34,6 @@
     return lax.ppermute(block, CONTEXT, route)
 
 
-def sum_over(block, axes):
-    n = lax.axis_size(axes)
-    copies = jnp.broadcast_to(block[None], (n,) + block.shape)
-    return jnp.sum(lax.all_to_all(copies, axes, split_axis=0, concat_axis=0), axis=0)
-
-
 def shifted_rows(row):
     return pltpu.roll(jnp.broadcast_to(row, (TAPS, 2 * TAPS)), 0, 1, stride=1, stride_axis=0)
 
@@ -48,30 +42,48 @@
     return lax.broadcasted_iota(jnp.int32, shape, 1) >> 4
 
 
-def filtered(rows_ref, window):
+def filtered(rows, window):
     owner = lane_group((TAPS, LANES))
     total = jnp.zeros((TAPS, LANES), F32)
     for g in range(PER):
-        table = shifted_rows(rows_ref[g : g + 1, :]).astype(BF16)
+        table = shifted_rows(rows[g : g + 1, :]).astype(BF16)
         term = jnp.dot(table, window, preferred_element_type=F32)
         total = jnp.where(owner == g, term, total)
     return total
 
 
-def conv_kernel(rows_ref, window_ref, conv_ref, turned_ref):
-    window = window_ref[...]
-    conv_ref[...] = filtered(rows_ref, window)
-    n = window.shape[0]
-    across = lax.broadcasted_iota(jnp.int32, (n, n), 0) + lax.broadcasted_iota(jnp.int32, (n, n), 1)
-    turn_rows = (across == n - 1).astype(F32).astype(BF16)
-    turned_ref[...] = jnp.dot(turn_rows, window, preferred_element_type=F32).astype(BF16)
-
-
-def mixed_grad_kernel(rows_ref, grad_ref, after_ref, key_ref, value_ref, key_grad_ref, value_grad_ref):
+def antidiagonal(rows, columns, total):
+    across = lax.broadcasted_iota(jnp.int32, (rows, columns), 0) + lax.broadcasted_iota(jnp.int32, (rows, columns), 1)
+    return (across == total).astype(F32).astype(BF16)
+
+
+def conv_kernel(filters_ref, before_ref, mixed_ref, conv_ref, turned_ref):
+    window = jnp.concatenate([before_ref[...], mixed_ref[...]], 0)
+    n = 2 * TAPS
+    rows = jnp.dot(filters_ref[...], antidiagonal(TAPS, n, TAPS), preferred_element_type=F32)
+    conv_ref[...] = filtered(rows, window)
+    turned_ref[...] = jnp.dot(antidiagonal(n, n, n - 1), window, preferred_element_type=F32).astype(BF16)
+
+
+def mixed_grad_kernel(filters_ref, grad_ref, after_ref, key_ref, value_ref, key_grad_ref, value_grad_ref):
     window = jnp.concatenate([grad_ref[...], after_ref[...]], 0)
-    mixed_grad = filtered(rows_ref, window)
+    taps = filters_ref[...].astype(F32)
+    mixed_grad = filtered(jnp.concatenate([taps, jnp.zeros(taps.shape, F32)], 1), window)
     key_grad_ref[...] = (mixed_grad * value_ref[...].astype(F32)).astype(BF16)
     value_grad_ref[...] = (mixed_grad * key_ref[...].astype(F32)).astype(BF16)
+
+
+def spread_kernel(cot_ref, out_ref):
+    size = cot_ref.shape[1] // 8
+    for x in range(4):
+        for zh in range(2):
+            out_ref[x, 0, :, zh * size : (zh + 1) * size] = cot_ref[:, (4 * zh + x) * size : (4 * zh + x + 1) * size]
+
+
+def sum_kernel(parts_ref, out_ref):
+    total = jnp.sum(parts_ref[...], axis=0)
+    for i in range(out_ref.shape[0]):
+        out_ref[i] = total
 
 
 def branch_kernel(terms_ref, conv_ref, query_ref, turned_ref, query_grad_ref, conv_grad_ref, lag_ref):
@@ -87,7 +99,9 @@
         part = jnp.where(owner == g, wide, 0.0).astype(BF16)
         outer = lax.dot_general(part, turned_ref[...], (((1,), (1,)), ((), ())), preferred_element_type=F32)
         skewed = pltpu.roll(outer, 1, 1, stride=1, stride_axis=0)
-        lag_ref[g : g + 1, :] = jnp.sum(skewed, axis=0, keepdims=True)[:, TAPS:]
+        sums = jnp.sum(skewed, axis=0, keepdims=True)[:, TAPS:]
+        for copy in range(lag_ref.shape[0]):
+            lag_ref[copy, g : g + 1, :] = sums
 
 
 def product_kernel(place_ref, cot_ref, *refs):
@@ -122,31 +136,57 @@
     return pl.BlockSpec(lead + (LANES,), lambda l: (0,) * len(lead) + (l,))
 
 
-def convolve(rows, window):
-    width = window.shape[1]
+FILTER_BLOCK = pl.BlockSpec((PER, TAPS), lambda l: (l, 0))
+
+
+def spread(cotangent):
+    rows, width = cotangent.shape
+    return pl.pallas_call(
+        spread_kernel,
+        grid=(8,),
+        in_specs=[pl.BlockSpec((rows, width), lambda i: (0, 0))],
+        out_specs=pl.BlockSpec((4, 1, rows, width // 4), lambda i: (0, i, 0, 0)),
+        out_shape=jax.ShapeDtypeStruct((4, 8, rows, width // 4), cotangent.dtype),
+        compiler_params=VMEM,
+        name="spread",
+    )(cotangent)
+
+
+def summed_copies(parts):
+    return pl.pallas_call(
+        sum_kernel,
+        out_shape=jax.ShapeDtypeStruct(parts.shape, parts.dtype),
+        compiler_params=VMEM,
+        name="sums",
+    )(parts)
+
+
+def convolve(filters, before, mixed):
+    width = mixed.shape[1]
+    tile = lane_blocks(TAPS)
     return pl.pallas_call(
         conv_kernel,
         grid=(width // LANES,),
-        in_specs=[pl.BlockSpec((PER, 2 * TAPS), lambda l: (l, 0)), lane_blocks(2 * TAPS)],
-        out_specs=[lane_blocks(TAPS), lane_blocks(2 * TAPS)],
+        in_specs=[FILTER_BLOCK, tile, tile],
+        out_specs=[tile, lane_blocks(2 * TAPS)],
         out_shape=[jax.ShapeDtypeStruct((TAPS, width), F32), jax.ShapeDtypeStruct((2 * TAPS, width), BF16)],
         compiler_params=VMEM,
         name="conv",
-    )(rows, window)
-
-
-def mixed_gradient(rows, grad, after, keys, values):
+    )(filters, before, mixed)
+
+
+def mixed_gradient(filters, grad, after, keys, values):
     width = grad.shape[1]
     tile = lane_blocks(TAPS)
     return pl.pallas_call(
         mixed_grad_kernel,
         grid=(width // LANES,),
-        in_specs=[pl.BlockSpec((PER, 2 * TAPS), lambda l: (l, 0)), tile, tile, tile, tile],
+        in_specs=[FILTER_BLOCK, tile, tile, tile, tile],
         out_specs=[tile, tile],
         out_shape=[jax.ShapeDtypeStruct((TAPS, width), BF16)] * 2,
         compiler_params=VMEM,
         name="mixed_grad",
-    )(rows, grad, after, keys, values)
+    )(filters, grad, after, keys, values)
 
 
 def branch_gradients(terms, conv, query, turned):
@@ -156,8 +196,9 @@
         branch_kernel,
         grid=(width // LANES,),
         in_specs=[lane_blocks(terms.shape[0], TAPS), tile, tile, lane_blocks(2 * TAPS)],
-        out_specs=[tile, tile, pl.BlockSpec((PER, TAPS), lambda l: (l, 0))],
-        out_shape=[jax.ShapeDtypeStruct((TAPS, width), BF16)] * 2 + [jax.ShapeDtypeStruct((width // GROUP, TAPS), F32)],
+        out_specs=[tile, tile, pl.BlockSpec((8, PER, TAPS), lambda l: (0, l, 0))],
+        out_shape=[jax.ShapeDtypeStruct((TAPS, width), BF16)] * 2
+        + [jax.ShapeDtypeStruct((8, width // GROUP, TAPS), F32)],
         compiler_params=VMEM,
         name="branch",
     )(terms, conv, query, turned)
@@ -181,16 +222,11 @@
     )(place, cotangent, *weights)
 
 
-def cotangent_columns(cotangent, after):
-    rows, width = cotangent.shape
-    depth = width // 64
-    parts = cotangent.reshape(rows, 2, 4, 4, 2, depth).transpose(2, 0, 1, 3, 4, 5)
-    parts, _ = lax.optimization_barrier((parts.reshape(4, 1, rows, 16 * depth), after))
-    copies = jnp.broadcast_to(parts, (4, 8, rows, 16 * depth)).reshape(32, rows, 16 * depth)
-    return lax.all_to_all(copies, ("x", "y"), split_axis=0, concat_axis=0).reshape(32 * rows, 16 * depth)
-
-
-def weight_blocks(chip):
+def exchange(copies, axes):
+    return lax.all_to_all(copies, axes, split_axis=0, concat_axis=0)
+
+
+def weight_blocks(chip, beside):
     n = lax.axis_size(Z)
     route = [(2 * i, 2 * ((i + 1) % n)) for i in range(n)] + [(2 * i + 1, 2 * ((i - 1) % n) + 1) for i in range(n)]
     blocks = [chip]
@@ -200,6 +236,7 @@
         blocks += [got, swap(got, "co")]
     half = got.shape[0] // 2
     got = jnp.where(lax.axis_index("co") == 0, got[:half], got[half:])
+    got, _ = lax.optimization_barrier((got, beside))
     got = lax.ppermute(got, Z + ("co",), route)
     return blocks + [got, swap(got, "co")]
 
@@ -207,29 +244,24 @@
 def local(query_branch, key_branch, value_branch, cotangent, out_weight, filters):
     query, keys, values = query_branch[0], key_branch[0], value_branch[0]
     tokens, width = query.shape
-    groups = filters.shape[0]
     chip = in_order(out_weight, swap(out_weight, "co"), "co").reshape(2 * out_weight.shape[0], width)
-    gathered = cotangent_columns(cotangent[0], chip)
-    weights = weight_blocks(chip)
-
-    keys, _ = lax.optimization_barrier((keys, weights[1]))
+    copies, chip = lax.optimization_barrier((spread(cotangent[0]), chip))
+    gathered = exchange(copies.reshape((32,) + copies.shape[2:]), ("x", "y")).reshape(4 * TAPS, -1)
+
+    keys, values, chip = lax.optimization_barrier((keys, values, chip))
     mixed = (keys.astype(F32) * values.astype(F32)).astype(BF16)
-    before = from_behind(mixed, 1)
-    window = jnp.concatenate([before, mixed], 0)
-    taps = filters.astype(F32)
-    zero = jnp.zeros((groups, TAPS), F32)
-    rows = jnp.concatenate([taps, zero], 1)
-    turned_rows = jnp.concatenate([zero[:, :1], taps[:, ::-1], zero[:, 1:]], 1)
-    conv, turned = convolve(turned_rows, window)
-
-    gathered, conv, turned, rows = lax.optimization_barrier((gathered, conv, turned, rows))
-    partial = partial_products(gathered, weights)
-    terms = lax.all_to_all(partial, "x", split_axis=0, concat_axis=0)
+    conv, turned = convolve(filters, from_behind(mixed, 1), mixed)
+    weights = weight_blocks(chip, conv)
+
+    gathered, conv, turned = lax.optimization_barrier((gathered, conv, turned))
+    terms = exchange(partial_products(gathered, weights), "x")
     query_grad, conv_grad, lags = branch_gradients(terms, conv, query, turned)
-    lag_sum = sum_over(sum_over(lags, ("x", "co")), Z)
-    filter_grad = lag_sum * (1.0 / math.sqrt(2 * lax.axis_size(CONTEXT) * tokens * GROUP))
+    lags = summed_copies(exchange(lags, ("x", "co")))
     after = from_behind(conv_grad, -1)
-    key_grad, value_grad = mixed_gradient(rows, conv_grad, after, keys, values)
+    lags, after = lax.optimization_barrier((lags, after))
+    scale = 1.0 / math.sqrt(2 * lax.axis_size(CONTEXT) * tokens * GROUP)
+    filter_grad = jnp.sum(exchange(lags, Z), axis=0) * scale
+    key_grad, value_grad = mixed_gradient(filters, conv_grad, after, keys, values)
     return (query_grad[None], key_grad[None], value_grad[None], filter_grad)
 
 

time: 117 us -> 119 us (1.017)
  the two profiles are of different devices: /device:TPU:1 before, /device:TPU:24 now
where the time goes in v8:
time: 119 us; the launch traced here: 118 us
  starting transfers between devices  45.7 us (38%)
  waiting for transfers between devices  28.7 us (24%)
  blocking collectives  26.4 us (22%)
  Pallas kernels  11.8 us (10%)
  local copies, waits for them, and re-layouts  3.69 us (3%)
    all_to_all x2, blocking collectives, exchange(): return lax.all_to_all(copies, axes, split_axis=0, concat_axis=0)  26.4 us
    ppermute x4, waiting for transfers between devices, weight_blocks(): got = lax.ppermute(got, Z + ('co',), route)  19.8 us
    all_to_all x2, starting transfers between devices, exchange(): return lax.all_to_all(copies, axes, split_axis=0, concat_axis=0)  16.1 us
    ppermute x4, starting transfers between devices, weight_blocks(): got = lax.ppermute(got, Z + ('co',), route)  12.9 us
    ppermute x5, starting transfers between devices, swap(): return lax.ppermute(block, axis, [(0, 1), (1, 0)])  12.4 us
    all_to_all x2, waiting for transfers between devices, exchange(): return lax.all_to_all(copies, axes, split_axis=0, concat_axis=0)  6.56 us
    ppermute x2, starting transfers between devices, from_behind(): return lax.ppermute(block, CONTEXT, route)  4.34 us
    unnamed x22, local copies, waits for them, and re-layouts  3.69 us
  transfers between devices with their start and end apart: 13, of which 6 were waited for; matrix products, arithmetic and copies ran while one was open for 0% of the time, Pallas kernels for 5%

profile of v8, /device:TPU:24, one launch (start us, length us, event | category | flops | bytes accessed | tf_op | source)
XLA Modules:
  0.0 118.0 jit_solution(16255821678754536156)
XLA Ops:
  0.6 1.9 %collective-permute-start = (bf16[128,512]{1,0:T(8,128)(2,1)}, bf16[128,512]{1,0:T(8,128)(2,1)S(1)}, u32[]{:S(2)}, u32[]{:S(2)}) collective-permute-start(bf16[128,512]{1,0:T(8,128)(2,1)} %param.10), channel_id=1, source_target_pairs={{0,8},{8,0},{1,9},{9,1},{2,10},{10,2},{3,11},{11,3},{4,12},{12,4},... | collective-permute-start | bytes 393224 | tf_op jit(solution)/shard_map/ppermute | solution.py:23
  3.9 1.3 %copy-done = bf16[4,8,16,2048]{3,2,1,0:T(8,128)(2,1)} copy-done((bf16[4,8,16,2048]{3,2,1,0:T(8,128)(2,1)}, bf16[4,8,16,2048]{3,2,1,0:T(8,128)(2,1)S(1)}, u32[]{:S(2)}) %copy-start) | copy-done | bytes 2097176
  5.3 10.1 %all-to-all-start = ((bf16[32,16,2048]{2,1,0:T(8,128)(2,1)}), bf16[32,16,2048]{2,1,0:T(8,128)(2,1)S(1)}, u32[]{:S(2)}, u32[]{:S(2)}) async-start(bf16[32,16,2048]{2,1,0:T(8,128)(2,1)} %bitcast.17), calls=%async_computation | async-start | bytes 4194304 | tf_op jit(solution)/shard_map/all_to_all | solution.py:226
  15.4 4.3 %collective-permute-start.2 = (bf16[256,512]{1,0:T(8,128)(2,1)S(1)}, bf16[256,512]{1,0:T(8,128)(2,1)S(1)}, u32[]{:S(2)}, u32[]{:S(2)}) collective-permute-start(bf16[256,512]{1,0:T(8,128)(2,1)S(1)} %bitcast.18), channel_id=1, source_target_pairs={{0,16},{16,32},{32,48},{48,256},{256,272},{272,288},{288,304},{304... | collective-permute-start | bytes 786440 | tf_op jit(solution)/shard_map/ppermute | solution.py:235
  19.7 11.0 %collective-permute-done.2.refs_1_ = bf16[256,512]{1,0:T(8,128)(2,1)S(1)} collective-permute-done((bf16[256,512]{1,0:T(8,128)(2,1)S(1)}, bf16[256,512]{1,0:T(8,128)(2,1)S(1)}, u32[]{:S(2)}, u32[]{:S(2)}) %collective-permute-start.2) | collective-permute-done | bytes 262176 | tf_op jit(solution)/shard_map/ppermute | solution.py:235
  30.7 1.9 %collective-permute-start.4 = (bf16[256,512]{1,0:T(8,128)(2,1)S(1)}, bf16[256,512]{1,0:T(8,128)(2,1)S(1)}, u32[]{:S(2)}, u32[]{:S(2)}) collective-permute-start(bf16[256,512]{1,0:T(8,128)(2,1)S(1)} %collective-permute-done.2.refs_1_), channel_id=1, source_target_pairs={{0,16},{16,32},{32,48},{48,256},{256,272},{272,288},{288,304},{304... | collective-permute-start | bytes 786440 | tf_op jit(solution)/shard_map/ppermute | solution.py:235
  32.6 7.5 %collective-permute-done.4.refs_3_ = bf16[256,512]{1,0:T(8,128)(2,1)S(1)} collective-permute-done((bf16[256,512]{1,0:T(8,128)(2,1)S(1)}, bf16[256,512]{1,0:T(8,128)(2,1)S(1)}, u32[]{:S(2)}, u32[]{:S(2)}) %collective-permute-start.4) | collective-permute-done | bytes 262176 | tf_op jit(solution)/shard_map/ppermute | solution.py:235
  40.2 1.9 %collective-permute-start.6 = (bf16[256,512]{1,0:T(8,128)(2,1)S(1)}, bf16[256,512]{1,0:T(8,128)(2,1)S(1)}, u32[]{:S(2)}, u32[]{:S(2)}) collective-permute-start(bf16[256,512]{1,0:T(8,128)(2,1)S(1)} %collective-permute-done.4.refs_3_), channel_id=1, source_target_pairs={{0,16},{16,32},{32,48},{48,256},{256,272},{272,288},{288,304},{304... | collective-permute-start | bytes 786440 | tf_op jit(solution)/shard_map/ppermute | solution.py:235
  42.1 3.1 %collective-permute-start.1 = (bf16[128,512]{1,0:T(8,128)(2,1)S(1)}, bf16[128,512]{1,0:T(8,128)(2,1)S(1)}, u32[]{:S(2)}, u32[]{:S(2)}) collective-permute-start(bf16[128,512]{1,0:T(8,128)(2,1)S(1)} %multiply_convert_fusion.mixed_ref), channel_id=1, source_target_pairs={{0,8},{8,16},{16,24},{24,32},{32,40},{40,48},{48,56},{56,64},{64,7... | collective-permute-start | bytes 393224 | tf_op jit(solution)/shard_map/ppermute | solution.py:34
  46.2 2.3 %conv.1 = (f32[128,512]{1,0:T(8,128)S(1)}, bf16[256,512]{1,0:T(8,128)(2,1)S(1)}) custom-call(bf16[32,128]{1,0:T(8,128)(2,1)S(1)} %copy-done.9, bf16[128,512]{1,0:T(8,128)(2,1)S(1)} %collective-permute-done.1.before_ref, bf16[128,512]{1,0:T(8,128)(2,1)S(1)} %multiply_convert_fusion.mixed_ref), custom_call_target="tpu_custom_call" | custom-call | tf_op jit(solution)/shard_map/conv/pallas_call | solution.py:167
  49.9 3.2 %collective-permute-start.3 = (bf16[256,512]{1,0:T(8,128)(2,1)S(1)}, bf16[256,512]{1,0:T(8,128)(2,1)}, u32[]{:S(2)}, u32[]{:S(2)}) collective-permute-start(bf16[256,512]{1,0:T(8,128)(2,1)S(1)} %collective-permute-done.2.refs_1_), channel_id=1, source_target_pairs={{0,8},{8,0},{1,9},{9,1},{2,10},{10,2},{3,11},{11,3},{4,12},{12,4},... | collective-permute-start | bytes 786440 | tf_op jit(solution)/shard_map/ppermute | solution.py:23
  53.1 1.9 %collective-permute-start.5 = (bf16[256,512]{1,0:T(8,128)(2,1)S(1)}, bf16[256,512]{1,0:T(8,128)(2,1)}, u32[]{:S(2)}, u32[]{:S(2)}) collective-permute-start(bf16[256,512]{1,0:T(8,128)(2,1)S(1)} %collective-permute-done.4.refs_3_), channel_id=1, source_target_pairs={{0,8},{8,0},{1,9},{9,1},{2,10},{10,2},{3,11},{11,3},{4,12},{12,4},... | collective-permute-start | bytes 786440 | tf_op jit(solution)/shard_map/ppermute | solution.py:23
  55.1 4.8 %collective-permute-start.8 = (bf16[128,512]{1,0:T(8,128)(2,1)S(1)}, bf16[128,512]{1,0:T(8,128)(2,1)S(1)}, u32[]{:S(2)}, u32[]{:S(2)}) collective-permute-start(bf16[128,512]{1,0:T(8,128)(2,1)S(1)} %slice_select_fusion), channel_id=1, source_target_pairs={{0,16},{16,32},{32,48},{48,256},{256,272},{272,288},{288,304},{304... | collective-permute-start | bytes 393224 | tf_op jit(solution)/shard_map/ppermute | solution.py:240
  59.9 3.5 %collective-permute-start.7 = (bf16[256,512]{1,0:T(8,128)(2,1)S(1)}, bf16[256,512]{1,0:T(8,128)(2,1)}, u32[]{:S(2)}, u32[]{:S(2)}) collective-permute-start(bf16[256,512]{1,0:T(8,128)(2,1)S(1)} %collective-permute-done.6.refs_5_), channel_id=1, source_target_pairs={{0,8},{8,0},{1,9},{9,1},{2,10},{10,2},{3,11},{11,3},{4,12},{12,4},... | collective-permute-start | bytes 786440 | tf_op jit(solution)/shard_map/ppermute | solution.py:23
  63.3 1.3 %collective-permute-done.8.refs_7_ = bf16[128,512]{1,0:T(8,128)(2,1)S(1)} collective-permute-done((bf16[128,512]{1,0:T(8,128)(2,1)S(1)}, bf16[128,512]{1,0:T(8,128)(2,1)S(1)}, u32[]{:S(2)}, u32[]{:S(2)}) %collective-permute-start.8) | collective-permute-done | bytes 131104 | tf_op jit(solution)/shard_map/ppermute | solution.py:240
  64.6 1.9 %collective-permute-start.9 = (bf16[128,512]{1,0:T(8,128)(2,1)S(1)}, bf16[128,512]{1,0:T(8,128)(2,1)}, u32[]{:S(2)}, u32[]{:S(2)}) collective-permute-start(bf16[128,512]{1,0:T(8,128)(2,1)S(1)} %collective-permute-done.8.refs_7_), channel_id=1, source_target_pairs={{0,8},{8,0},{1,9},{9,1},{2,10},{10,2},{3,11},{11,3},{4,12},{12,4},... | collective-permute-start | bytes 393224 | tf_op jit(solution)/shard_map/ppermute | solution.py:23
  66.7 1.3 %collective-permute-done.9.refs_8_ = bf16[128,512]{1,0:T(8,128)(2,1)} collective-permute-done((bf16[128,512]{1,0:T(8,128)(2,1)S(1)}, bf16[128,512]{1,0:T(8,128)(2,1)}, u32[]{:S(2)}, u32[]{:S(2)}) %collective-permute-start.9) | collective-permute-done | bytes 131104 | tf_op jit(solution)/shard_map/ppermute | solution.py:23
  68.0 3.0 %product.1 = bf16[4,128,512]{2,1,0:T(8,128)(2,1)S(1)} custom-call(s32[2]{0:T(128)S(1)} %pad_add_fusion.place_ref, bf16[512,2048]{1,0:T(8,128)(2,1)S(1)} %bitcast.16, bf16[256,512]{1,0:T(8,128)(2,1)S(1)} %bitcast.19, bf16[256,512]{1,0:T(8,128)(2,1)S(1)} %collective-permute-done.2.refs_1_, bf16[256,512]{1,0:T(8,128)(2,1)} %collective-permute-done.3.refs_2_, ...), custom_call_target="tpu_custom_call" | custom-call | tf_op jit(solution)/shard_map/product/pallas_call | solution.py:211
  71.0 17.3 %all_to_all.20.terms_ref = bf16[4,128,512]{2,1,0:T(8,128)(2,1)S(1)} all-to-all(bf16[4,128,512]{2,1,0:T(8,128)(2,1)S(1)} %product.1), channel_id=1, replica_groups=mesh['zh'=2,'x'=4,'zl'=4,'co'=2,'y'=8] {'x'}, dimensions={0} | all-to-all | bytes 1048576 | tf_op jit(solution)/shard_map/all_to_all | solution.py:226
  88.3 2.9 %branch.1 = (bf16[128,512]{1,0:T(8,128)(2,1)}, bf16[128,512]{1,0:T(8,128)(2,1)S(1)}, f32[8,32,128]{2,1,0:T(8,128)S(1)}) custom-call(bf16[4,128,512]{2,1,0:T(8,128)(2,1)S(1)} %all_to_all.20.terms_ref, f32[128,512]{1,0:T(8,128)S(1)} %copy-done.5, bf16[128,512]{1,0:T(8,128)(2,1)S(1)} %bitcast.25, bf16[256,512]{1,0:T(8,128)(2,1)S(1)} %copy-done.7), custom_call_target="tpu_custom_call" | custom-call | tf_op jit(solution)/shard_map/branch/pallas_call | solution.py:195
  92.5 9.1 %all_to_all.21.parts_ref = f32[8,32,128]{2,1,0:T(8,128)S(1)} all-to-all(f32[8,32,128]{2,1,0:T(8,128)S(1)} %get-tuple-element.35), channel_id=1, replica_groups=mesh['zh'=2,'x'=4,'zl'=4,'co'=2,'y'=8] {'x','co'}, dimensions={0} | all-to-all | bytes 262144 | tf_op jit(solution)/shard_map/all_to_all | solution.py:226
  102.3 6.0 %all-to-all-start.3 = ((f32[8,32,128]{2,1,0:T(8,128)}), f32[8,32,128]{2,1,0:T(8,128)S(1)}, u32[]{:S(2)}, u32[]{:S(2)}) async-start(f32[8,32,128]{2,1,0:T(8,128)} %sums.1), calls=%async_computation.3 | async-start | bytes 262144 | tf_op jit(solution)/shard_map/all_to_all | solution.py:226
  108.3 2.5 %mixed_grad.1 = (bf16[128,512]{1,0:T(8,128)(2,1)}, bf16[128,512]{1,0:T(8,128)(2,1)}) custom-call(bf16[32,128]{1,0:T(8,128)(2,1)S(1)} %copy-done.9, bf16[128,512]{1,0:T(8,128)(2,1)S(1)} %get-tuple-element.34.grad_ref, bf16[128,512]{1,0:T(8,128)(2,1)S(1)} %collective-permute-done.10.after_ref, bf16[128,512]{1,0:T(8,128)(2,1)S(1)} %bitcast.23, ...), custom_call_target="tpu_custom_call" | custom-call | tf_op jit(solution)/shard_map/mixed_grad/pallas_call | solution.py:181
  110.9 6.6 %all-to-all-done.3 = f32[8,32,128]{2,1,0:T(8,128)S(1)} async-done(((f32[8,32,128]{2,1,0:T(8,128)}), f32[8,32,128]{2,1,0:T(8,128)S(1)}, u32[]{:S(2)}, u32[]{:S(2)}) %all-to-all-start.3) | async-done | bytes 131104 | tf_op jit(solution)/shard_map/all_to_all | solution.py:226
  (39 shorter events, 6.5 us)
Async XLA Ops:
  0.6 4.6 %collective-permute-start = (bf16[128,512]{1,0:T(8,128)(2,1)}, bf16[128,512]{1,0:T(8,128)(2,1)S(1)}, u32[]{:S(2)}, u32[]{:S(2)}) collective-permute-start(bf16[128,512]{1,0:T(8,128)(2,1)} %param.10), channel_id=1, source_target_pairs={{0,8},{8,0},{1,9},{9,1},{2,10},{10,2},{3,11},{11,3},{4,12},{12,4},... | collective-permute-start | bytes 393224 | tf_op jit(solution)/shard_map/ppermute | solution.py:23
  2.6 1.0 copy-start.3
  3.5 1.7 %copy-start.10 = (bf16[128,512]{1,0:T(8,128)(2,1)S(1)}, bf16[128,512]{1,0:T(8,128)(2,1)}, u32[]{:S(2)}) copy-start(bf16[128,512]{1,0:T(8,128)(2,1)} %param.10) | copy-start | bytes 393220
  3.9 1.3 %copy-start = (bf16[4,8,16,2048]{3,2,1,0:T(8,128)(2,1)}, bf16[4,8,16,2048]{3,2,1,0:T(8,128)(2,1)S(1)}, u32[]{:S(2)}) copy-start(bf16[4,8,16,2048]{3,2,1,0:T(8,128)(2,1)S(1)} %spread.1) | copy-start | bytes 6291460
  5.3 36.8 %copy-start.1 = (bf16[1,128,512]{2,1,0:T(8,128)(2,1)S(1)}, bf16[1,128,512]{2,1,0:T(8,128)(2,1)}, u32[]{:S(2)}) copy-start(bf16[1,128,512]{2,1,0:T(8,128)(2,1)} %param.8) | copy-start | bytes 393220
  5.3 36.8 %copy-start.2 = (bf16[1,128,512]{2,1,0:T(8,128)(2,1)S(1)}, bf16[1,128,512]{2,1,0:T(8,128)(2,1)}, u32[]{:S(2)}) copy-start(bf16[1,128,512]{2,1,0:T(8,128)(2,1)} %param.7) | copy-start | bytes 393220
  5.3 40.9 %copy-start.9 = (bf16[32,128]{1,0:T(8,128)(2,1)S(1)}, bf16[32,128]{1,0:T(8,128)(2,1)}, u32[]{:S(2)}) copy-start(bf16[32,128]{1,0:T(8,128)(2,1)} %filters_ref.3) | copy-start | bytes 24580
  5.3 61.3 %all-to-all-start = ((bf16[32,16,2048]{2,1,0:T(8,128)(2,1)}), bf16[32,16,2048]{2,1,0:T(8,128)(2,1)S(1)}, u32[]{:S(2)}, u32[]{:S(2)}) async-start(bf16[32,16,2048]{2,1,0:T(8,128)(2,1)} %bitcast.17), calls=%async_computation | async-start | bytes 4194304 | tf_op jit(solution)/shard_map/all_to_all | solution.py:226
  15.4 15.3 %collective-permute-start.2 = (bf16[256,512]{1,0:T(8,128)(2,1)S(1)}, bf16[256,512]{1,0:T(8,128)(2,1)S(1)}, u32[]{:S(2)}, u32[]{:S(2)}) collective-permute-start(bf16[256,512]{1,0:T(8,128)(2,1)S(1)} %bitcast.18), channel_id=1, source_target_pairs={{0,16},{16,32},{32,48},{48,256},{256,272},{272,288},{288,304},{304... | collective-permute-start | bytes 786440 | tf_op jit(solution)/shard_map/ppermute | solution.py:235
  30.7 9.5 %collective-permute-start.4 = (bf16[256,512]{1,0:T(8,128)(2,1)S(1)}, bf16[256,512]{1,0:T(8,128)(2,1)S(1)}, u32[]{:S(2)}, u32[]{:S(2)}) collective-permute-start(bf16[256,512]{1,0:T(8,128)(2,1)S(1)} %collective-permute-done.2.refs_1_), channel_id=1, source_target_pairs={{0,16},{16,32},{32,48},{48,256},{256,272},{272,288},{288,304},{304... | collective-permute-start | bytes 786440 | tf_op jit(solution)/shard_map/ppermute | solution.py:235
  40.2 14.9 %collective-permute-start.6 = (bf16[256,512]{1,0:T(8,128)(2,1)S(1)}, bf16[256,512]{1,0:T(8,128)(2,1)S(1)}, u32[]{:S(2)}, u32[]{:S(2)}) collective-permute-start(bf16[256,512]{1,0:T(8,128)(2,1)S(1)} %collective-permute-done.4.refs_3_), channel_id=1, source_target_pairs={{0,16},{16,32},{32,48},{48,256},{256,272},{272,288},{288,304},{304... | collective-permute-start | bytes 786440 | tf_op jit(solution)/shard_map/ppermute | solution.py:235
  42.1 4.0 %collective-permute-start.1 = (bf16[128,512]{1,0:T(8,128)(2,1)S(1)}, bf16[128,512]{1,0:T(8,128)(2,1)S(1)}, u32[]{:S(2)}, u32[]{:S(2)}) collective-permute-start(bf16[128,512]{1,0:T(8,128)(2,1)S(1)} %multiply_convert_fusion.mixed_ref), channel_id=1, source_target_pairs={{0,8},{8,16},{16,24},{24,32},{32,40},{40,48},{48,56},{56,64},{64,7... | collective-permute-start | bytes 393224 | tf_op jit(solution)/shard_map/ppermute | solution.py:34
  48.5 0.7 copy-start.4
  49.2 0.7 copy-start.6
  49.9 16.7 %collective-permute-start.3 = (bf16[256,512]{1,0:T(8,128)(2,1)S(1)}, bf16[256,512]{1,0:T(8,128)(2,1)}, u32[]{:S(2)}, u32[]{:S(2)}) collective-permute-start(bf16[256,512]{1,0:T(8,128)(2,1)S(1)} %collective-permute-done.2.refs_1_), channel_id=1, source_target_pairs={{0,8},{8,0},{1,9},{9,1},{2,10},{10,2},{3,11},{11,3},{4,12},{12,4},... | collective-permute-start | bytes 786440 | tf_op jit(solution)/shard_map/ppermute | solution.py:23
  53.1 13.5 %collective-permute-start.5 = (bf16[256,512]{1,0:T(8,128)(2,1)S(1)}, bf16[256,512]{1,0:T(8,128)(2,1)}, u32[]{:S(2)}, u32[]{:S(2)}) collective-permute-start(bf16[256,512]{1,0:T(8,128)(2,1)S(1)} %collective-permute-done.4.refs_3_), channel_id=1, source_target_pairs={{0,8},{8,0},{1,9},{9,1},{2,10},{10,2},{3,11},{11,3},{4,12},{12,4},... | collective-permute-start | bytes 786440 | tf_op jit(solution)/shard_map/ppermute | solution.py:23
  55.1 9.5 %collective-permute-start.8 = (bf16[128,512]{1,0:T(8,128)(2,1)S(1)}, bf16[128,512]{1,0:T(8,128)(2,1)S(1)}, u32[]{:S(2)}, u32[]{:S(2)}) collective-permute-start(bf16[128,512]{1,0:T(8,128)(2,1)S(1)} %slice_select_fusion), channel_id=1, source_target_pairs={{0,16},{16,32},{32,48},{48,256},{256,272},{272,288},{288,304},{304... | collective-permute-start | bytes 393224 | tf_op jit(solution)/shard_map/ppermute | solution.py:240
  59.9 8.1 %collective-permute-start.7 = (bf16[256,512]{1,0:T(8,128)(2,1)S(1)}, bf16[256,512]{1,0:T(8,128)(2,1)}, u32[]{:S(2)}, u32[]{:S(2)}) collective-permute-start(bf16[256,512]{1,0:T(8,128)(2,1)S(1)} %collective-permute-done.6.refs_5_), channel_id=1, source_target_pairs={{0,8},{8,0},{1,9},{9,1},{2,10},{10,2},{3,11},{11,3},{4,12},{12,4},... | collective-permute-start | bytes 786440 | tf_op jit(solution)/shard_map/ppermute | solution.py:23
  64.6 3.4 %collective-permute-start.9 = (bf16[128,512]{1,0:T(8,128)(2,1)S(1)}, bf16[128,512]{1,0:T(8,128)(2,1)}, u32[]{:S(2)}, u32[]{:S(2)}) collective-permute-start(bf16[128,512]{1,0:T(8,128)(2,1)S(1)} %collective-permute-done.8.refs_7_), channel_id=1, source_target_pairs={{0,8},{8,0},{1,9},{9,1},{2,10},{10,2},{3,11},{11,3},{4,12},{12,4},... | collective-permute-start | bytes 393224 | tf_op jit(solution)/shard_map/ppermute | solution.py:23
  66.6 21.7 %copy-start.5 = (f32[128,512]{1,0:T(8,128)S(1)}, f32[128,512]{1,0:T(8,128)}, u32[]{:S(2)}) copy-start(f32[128,512]{1,0:T(8,128)} %copy-done.4) | copy-start | bytes 786436
  66.6 21.7 %copy-start.7 = (bf16[256,512]{1,0:T(8,128)(2,1)S(1)}, bf16[256,512]{1,0:T(8,128)(2,1)}, u32[]{:S(2)}) copy-start(bf16[256,512]{1,0:T(8,128)(2,1)} %copy-done.6) | copy-start | bytes 786436
  66.6 21.7 %copy-start.8 = (bf16[1,128,512]{2,1,0:T(8,128)(2,1)S(1)}, bf16[1,128,512]{2,1,0:T(8,128)(2,1)}, u32[]{:S(2)}) copy-start(bf16[1,128,512]{2,1,0:T(8,128)(2,1)} %param.6) | copy-start | bytes 393220
  91.2 11.1 %collective-permute-start.10 = (bf16[128,512]{1,0:T(8,128)(2,1)S(1)}, bf16[128,512]{1,0:T(8,128)(2,1)S(1)}, u32[]{:S(2)}, u32[]{:S(2)}) collective-permute-start(bf16[128,512]{1,0:T(8,128)(2,1)S(1)} %get-tuple-element.34.grad_ref), channel_id=1, source_target_pairs={{8,0},{16,8},{24,16},{32,24},{40,32},{48,40},{56,48},{64,56},{72,6... | collective-permute-start | bytes 393224 | tf_op jit(solution)/shard_map/ppermute | solution.py:34
  102.3 15.1 %all-to-all-start.3 = ((f32[8,32,128]{2,1,0:T(8,128)}), f32[8,32,128]{2,1,0:T(8,128)S(1)}, u32[]{:S(2)}, u32[]{:S(2)}) async-start(f32[8,32,128]{2,1,0:T(8,128)} %sums.1), calls=%async_computation.3 | async-start | bytes 262144 | tf_op jit(solution)/shard_map/all_to_all | solution.py:226

commit v9 on v8

--- a/solution.py
+++ b/solution.py
@@ -112,15 +112,14 @@
         copy.start()
     z, core = place_ref[0], place_ref[1]
     depth = weights[0].shape[0]
-    pieces = [(z, 0)]
+    pieces = [z]
     for step in (1, 2, 3):
         below, above = lax.rem(z + 8 - step, 8), lax.rem(z + step, 8)
-        pieces += [(jnp.where(core == 0, below, above), 0), (jnp.where(core == 0, above, below), 0)]
-    far = lax.rem(z + 4, 8)
-    pieces += [(far, jnp.where(core == 0, 0, depth // 2)), (far, jnp.where(core == 0, depth // 2, 0))]
-    for i, (place, offset) in enumerate(pieces):
+        pieces += [jnp.where(core == 0, below, above), jnp.where(core == 0, above, below)]
+    pieces.append(lax.rem(z + 4, 8))
+    for i, place in enumerate(pieces):
         copies[i].wait()
-        columns = pl.ds(pl.multiple_of(place * depth + offset, LANES), weights[i].shape[0])
+        columns = pl.ds(pl.multiple_of(place * depth, LANES), depth)
         for x in range(4):
             rows = slice(x * TAPS, (x + 1) * TAPS)
             term = jnp.dot(cot_ref[rows, columns], weights[i][...], preferred_element_type=F32)
@@ -231,21 +230,19 @@
     route = [(2 * i, 2 * ((i + 1) % n)) for i in range(n)] + [(2 * i + 1, 2 * ((i - 1) % n) + 1) for i in range(n)]
     blocks = [chip]
     got = chip
-    for _ in range(3):
+    for _ in range(n // 2 - 1):
         got = lax.ppermute(got, Z + ("co",), route)
-        blocks += [got, swap(got, "co")]
-    half = got.shape[0] // 2
-    got = jnp.where(lax.axis_index("co") == 0, got[:half], got[half:])
-    got, _ = lax.optimization_barrier((got, beside))
-    got = lax.ppermute(got, Z + ("co",), route)
-    return blocks + [got, swap(got, "co")]
+        got, beside = lax.optimization_barrier((got, beside))
+        beside = swap(got, "co")
+        blocks += [got, beside]
+    return blocks + [lax.ppermute(got, Z + ("co",), route)]
 
 
 def local(query_branch, key_branch, value_branch, cotangent, out_weight, filters):
     query, keys, values = query_branch[0], key_branch[0], value_branch[0]
     tokens, width = query.shape
     chip = in_order(out_weight, swap(out_weight, "co"), "co").reshape(2 * out_weight.shape[0], width)
-    copies, chip = lax.optimization_barrier((spread(cotangent[0]), chip))
+    copies = spread(cotangent[0])
     gathered = exchange(copies.reshape((32,) + copies.shape[2:]), ("x", "y")).reshape(4 * TAPS, -1)
 
     keys, values, chip = lax.optimization_barrier((keys, values, chip))

time: 119 us -> 119 us (level)
  the two profiles are of different devices: /device:TPU:24 before, /device:TPU:1 now
where the time goes in v9:
time: 119 us; the launch traced here: 117 us
  starting transfers between devices  57.4 us (48%)
  blocking collectives  23.1 us (19%)
  waiting for transfers between devices  18.6 us (16%)
  Pallas kernels  11.2 us (9%)
  local copies, waits for them, and re-layouts  5.38 us (5%)
    all_to_all x2, blocking collectives, exchange(): return lax.all_to_all(copies, axes, split_axis=0, concat_axis=0)  23.1 us
    ppermute x3, starting transfers between devices, weight_blocks(): got = lax.ppermute(got, Z + ('co',), route)  20.8 us
    all_to_all x2, starting transfers between devices, exchange(): return lax.all_to_all(copies, axes, split_axis=0, concat_axis=0)  14.1 us
    ppermute x4, starting transfers between devices, swap(): return lax.ppermute(block, axis, [(0, 1), (1, 0)])  12 us
    ppermute x2, starting transfers between devices, from_behind(): return lax.ppermute(block, CONTEXT, route)  7.3 us
    ppermute x3, waiting for transfers between devices, weight_blocks(): got = lax.ppermute(got, Z + ('co',), route)  6.06 us
    unnamed x26, local copies, waits for them, and re-layouts  5.38 us
    all_to_all x2, waiting for transfers between devices, exchange(): return lax.all_to_all(copies, axes, split_axis=0, concat_axis=0)  5.33 us
  transfers between devices with their start and end apart: 12, of which 6 were waited for; matrix products, arithmetic and copies ran while one was open for 0% of the time, Pallas kernels for 5%

profile of v9, /device:TPU:1, one launch (start us, length us, event | category | flops | bytes accessed | tf_op | source)
XLA Modules:
  0.0 117.4 jit_solution(4641866468191879530)
XLA Ops:
  2.0 1.3 %copy-done = bf16[4,8,16,2048]{3,2,1,0:T(8,128)(2,1)} copy-done((bf16[4,8,16,2048]{3,2,1,0:T(8,128)(2,1)}, bf16[4,8,16,2048]{3,2,1,0:T(8,128)(2,1)S(1)}, u32[]{:S(2)}) %copy-start) | copy-done | bytes 2097176
  3.3 10.6 %all-to-all-start = ((bf16[32,16,2048]{2,1,0:T(8,128)(2,1)}), bf16[32,16,2048]{2,1,0:T(8,128)(2,1)S(1)}, u32[]{:S(2)}, u32[]{:S(2)}) async-start(bf16[32,16,2048]{2,1,0:T(8,128)(2,1)} %bitcast.17), calls=%async_computation | async-start | bytes 4194304 | tf_op jit(solution)/shard_map/all_to_all | solution.py:225
  14.0 2.9 %collective-permute-start = (bf16[128,512]{1,0:T(8,128)(2,1)S(1)}, bf16[128,512]{1,0:T(8,128)(2,1)S(1)}, u32[]{:S(2)}, u32[]{:S(2)}) collective-permute-start(bf16[128,512]{1,0:T(8,128)(2,1)S(1)} %copy-done.12), channel_id=1, source_target_pairs={{0,8},{8,0},{1,9},{9,1},{2,10},{10,2},{3,11},{11,3},{4,12},{12,4},... | collective-permute-start | bytes 393224 | tf_op jit(solution)/shard_map/ppermute | solution.py:23
  17.9 10.7 %collective-permute-start.2 = (bf16[256,512]{1,0:T(8,128)(2,1)S(1)}, bf16[256,512]{1,0:T(8,128)(2,1)S(1)}, u32[]{:S(2)}, u32[]{:S(2)}) collective-permute-start(bf16[256,512]{1,0:T(8,128)(2,1)S(1)} %bitcast.18), channel_id=1, source_target_pairs={{0,16},{16,32},{32,48},{48,256},{256,272},{272,288},{288,304},{304... | collective-permute-start | bytes 786440 | tf_op jit(solution)/shard_map/ppermute | solution.py:234
  28.6 1.9 %collective-permute-start.1 = (bf16[128,512]{1,0:T(8,128)(2,1)S(1)}, bf16[128,512]{1,0:T(8,128)(2,1)S(1)}, u32[]{:S(2)}, u32[]{:S(2)}) collective-permute-start(bf16[128,512]{1,0:T(8,128)(2,1)S(1)} %multiply_convert_fusion.mixed_ref), channel_id=1, source_target_pairs={{0,8},{8,16},{16,24},{24,32},{32,40},{40,48},{48,56},{56,64},{64,7... | collective-permute-start | bytes 393224 | tf_op jit(solution)/shard_map/ppermute | solution.py:34
  30.5 1.9 %collective-permute-done.1.before_ref = bf16[128,512]{1,0:T(8,128)(2,1)S(1)} collective-permute-done((bf16[128,512]{1,0:T(8,128)(2,1)S(1)}, bf16[128,512]{1,0:T(8,128)(2,1)S(1)}, u32[]{:S(2)}, u32[]{:S(2)}) %collective-permute-start.1) | collective-permute-done | bytes 131104 | tf_op jit(solution)/shard_map/ppermute | solution.py:34
  32.5 2.3 %conv.1 = (f32[128,512]{1,0:T(8,128)S(1)}, bf16[256,512]{1,0:T(8,128)(2,1)S(1)}) custom-call(bf16[32,128]{1,0:T(8,128)(2,1)S(1)} %copy-done.11, bf16[128,512]{1,0:T(8,128)(2,1)S(1)} %collective-permute-done.1.before_ref, bf16[128,512]{1,0:T(8,128)(2,1)S(1)} %multiply_convert_fusion.mixed_ref), custom_call_target="tpu_custom_call" | custom-call | tf_op jit(solution)/shard_map/conv/pallas_call | solution.py:166
  36.2 1.9 %collective-permute-start.3 = (bf16[256,512]{1,0:T(8,128)(2,1)S(1)}, bf16[256,512]{1,0:T(8,128)(2,1)S(1)}, u32[]{:S(2)}, u32[]{:S(2)}) collective-permute-start(bf16[256,512]{1,0:T(8,128)(2,1)S(1)} %collective-permute-done.2.refs_1_), channel_id=1, source_target_pairs={{0,8},{8,0},{1,9},{9,1},{2,10},{10,2},{3,11},{11,3},{4,12},{12,4},... | collective-permute-start | bytes 786440 | tf_op jit(solution)/shard_map/ppermute | solution.py:23
  38.1 6.1 %collective-permute-start.4 = (bf16[256,512]{1,0:T(8,128)(2,1)S(1)}, bf16[256,512]{1,0:T(8,128)(2,1)S(1)}, u32[]{:S(2)}, u32[]{:S(2)}) collective-permute-start(bf16[256,512]{1,0:T(8,128)(2,1)S(1)} %collective-permute-done.2.refs_1_), channel_id=1, source_target_pairs={{0,16},{16,32},{32,48},{48,256},{256,272},{272,288},{288,304},{304... | collective-permute-start | bytes 786440 | tf_op jit(solution)/shard_map/ppermute | solution.py:234
  44.2 3.3 %collective-permute-done.4.refs_3_ = bf16[256,512]{1,0:T(8,128)(2,1)S(1)} collective-permute-done((bf16[256,512]{1,0:T(8,128)(2,1)S(1)}, bf16[256,512]{1,0:T(8,128)(2,1)S(1)}, u32[]{:S(2)}, u32[]{:S(2)}) %collective-permute-start.4) | collective-permute-done | bytes 262176 | tf_op jit(solution)/shard_map/ppermute | solution.py:234
  47.5 3.2 %collective-permute-start.5 = (bf16[256,512]{1,0:T(8,128)(2,1)S(1)}, bf16[256,512]{1,0:T(8,128)(2,1)S(1)}, u32[]{:S(2)}, u32[]{:S(2)}) collective-permute-start(bf16[256,512]{1,0:T(8,128)(2,1)S(1)} %collective-permute-done.4.refs_3_), channel_id=1, source_target_pairs={{0,8},{8,0},{1,9},{9,1},{2,10},{10,2},{3,11},{11,3},{4,12},{12,4},... | collective-permute-start | bytes 786440 | tf_op jit(solution)/shard_map/ppermute | solution.py:23
  50.8 4.0 %collective-permute-start.6 = (bf16[256,512]{1,0:T(8,128)(2,1)S(1)}, bf16[256,512]{1,0:T(8,128)(2,1)}, u32[]{:S(2)}, u32[]{:S(2)}) collective-permute-start(bf16[256,512]{1,0:T(8,128)(2,1)S(1)} %collective-permute-done.4.refs_3_), channel_id=1, source_target_pairs={{0,16},{16,32},{32,48},{48,256},{256,272},{272,288},{288,304},{304... | collective-permute-start | bytes 786440 | tf_op jit(solution)/shard_map/ppermute | solution.py:234
  55.5 2.8 %collective-permute-done.6.refs_5_ = bf16[256,512]{1,0:T(8,128)(2,1)} collective-permute-done((bf16[256,512]{1,0:T(8,128)(2,1)S(1)}, bf16[256,512]{1,0:T(8,128)(2,1)}, u32[]{:S(2)}, u32[]{:S(2)}) %collective-permute-start.6) | collective-permute-done | bytes 262176 | tf_op jit(solution)/shard_map/ppermute | solution.py:234
  58.3 4.0 %collective-permute-start.7 = (bf16[256,512]{1,0:T(8,128)(2,1)}, bf16[256,512]{1,0:T(8,128)(2,1)}, u32[]{:S(2)}, u32[]{:S(2)}) collective-permute-start(bf16[256,512]{1,0:T(8,128)(2,1)} %collective-permute-done.6.refs_5_), channel_id=1, source_target_pairs={{0,8},{8,0},{1,9},{9,1},{2,10},{10,2},{3,11},{11,3},{4,12},{12,4},... | collective-permute-start | bytes 786440 | tf_op jit(solution)/shard_map/ppermute | solution.py:23
  62.3 3.3 %collective-permute-start.8 = (bf16[256,512]{1,0:T(8,128)(2,1)}, bf16[256,512]{1,0:T(8,128)(2,1)}, u32[]{:S(2)}, u32[]{:S(2)}) collective-permute-start(bf16[256,512]{1,0:T(8,128)(2,1)} %collective-permute-done.6.refs_5_), channel_id=1, source_target_pairs={{0,16},{16,32},{32,48},{48,256},{256,272},{272,288},{288,304},{304... | collective-permute-start | bytes 786440 | tf_op jit(solution)/shard_map/ppermute | solution.py:238
  65.6 4.4 %collective-permute-done.8.refs_7_ = bf16[256,512]{1,0:T(8,128)(2,1)} collective-permute-done((bf16[256,512]{1,0:T(8,128)(2,1)}, bf16[256,512]{1,0:T(8,128)(2,1)}, u32[]{:S(2)}, u32[]{:S(2)}) %collective-permute-start.8) | collective-permute-done | bytes 262176 | tf_op jit(solution)/shard_map/ppermute | solution.py:238
  70.9 2.4 %product.1 = bf16[4,128,512]{2,1,0:T(8,128)(2,1)S(1)} custom-call(s32[2]{0:T(128)S(1)} %pad_add_fusion.place_ref, bf16[512,2048]{1,0:T(8,128)(2,1)S(1)} %bitcast.16, bf16[256,512]{1,0:T(8,128)(2,1)S(1)} %bitcast.19, bf16[256,512]{1,0:T(8,128)(2,1)S(1)} %collective-permute-done.2.refs_1_, bf16[256,512]{1,0:T(8,128)(2,1)S(1)} %collective-permute-done.3.refs_2_, ...), custom_call_target="tpu_custom_call" | custom-call | tf_op jit(solution)/shard_map/product/pallas_call | solution.py:210
  73.4 11.1 %all_to_all.20.terms_ref = bf16[4,128,512]{2,1,0:T(8,128)(2,1)S(1)} all-to-all(bf16[4,128,512]{2,1,0:T(8,128)(2,1)S(1)} %product.1), channel_id=1, replica_groups=mesh['zh'=2,'x'=4,'zl'=4,'co'=2,'y'=8] {'x'}, dimensions={0} | all-to-all | bytes 1048576 | tf_op jit(solution)/shard_map/all_to_all | solution.py:225
  84.4 2.9 %branch.1 = (bf16[128,512]{1,0:T(8,128)(2,1)}, bf16[128,512]{1,0:T(8,128)(2,1)S(1)}, f32[8,32,128]{2,1,0:T(8,128)S(1)}) custom-call(bf16[4,128,512]{2,1,0:T(8,128)(2,1)S(1)} %all_to_all.20.terms_ref, f32[128,512]{1,0:T(8,128)S(1)} %copy-done.7, bf16[128,512]{1,0:T(8,128)(2,1)S(1)} %bitcast.25, bf16[256,512]{1,0:T(8,128)(2,1)S(1)} %copy-done.9), custom_call_target="tpu_custom_call" | custom-call | tf_op jit(solution)/shard_map/branch/pallas_call | solution.py:194
  87.3 5.4 %collective-permute-start.9 = (bf16[128,512]{1,0:T(8,128)(2,1)S(1)}, bf16[128,512]{1,0:T(8,128)(2,1)S(1)}, u32[]{:S(2)}, u32[]{:S(2)}) collective-permute-start(bf16[128,512]{1,0:T(8,128)(2,1)S(1)} %get-tuple-element.34.grad_ref), channel_id=1, source_target_pairs={{8,0},{16,8},{24,16},{32,24},{40,32},{48,40},{56,48},{64,56},{72,6... | collective-permute-start | bytes 393224 | tf_op jit(solution)/shard_map/ppermute | solution.py:34
  92.7 12.1 %all_to_all.21.parts_ref = f32[8,32,128]{2,1,0:T(8,128)S(1)} all-to-all(f32[8,32,128]{2,1,0:T(8,128)S(1)} %get-tuple-element.35), channel_id=1, replica_groups=mesh['zh'=2,'x'=4,'zl'=4,'co'=2,'y'=8] {'x','co'}, dimensions={0} | all-to-all | bytes 262144 | tf_op jit(solution)/shard_map/all_to_all | solution.py:225
  105.5 3.5 %all-to-all-start.3 = ((f32[8,32,128]{2,1,0:T(8,128)}), f32[8,32,128]{2,1,0:T(8,128)S(1)}, u32[]{:S(2)}, u32[]{:S(2)}) async-start(f32[8,32,128]{2,1,0:T(8,128)} %sums.1), calls=%async_computation.3 | async-start | bytes 262144 | tf_op jit(solution)/shard_map/all_to_all | solution.py:225
  108.9 2.5 %mixed_grad.1 = (bf16[128,512]{1,0:T(8,128)(2,1)}, bf16[128,512]{1,0:T(8,128)(2,1)}) custom-call(bf16[32,128]{1,0:T(8,128)(2,1)S(1)} %copy-done.11, bf16[128,512]{1,0:T(8,128)(2,1)S(1)} %get-tuple-element.34.grad_ref, bf16[128,512]{1,0:T(8,128)(2,1)S(1)} %collective-permute-done.9.after_ref, bf16[128,512]{1,0:T(8,128)(2,1)S(1)} %bitcast.23, ...), custom_call_target="tpu_custom_call" | custom-call | tf_op jit(solution)/shard_map/mixed_grad/pallas_call | solution.py:180
  111.5 5.3 %all-to-all-done.3 = f32[8,32,128]{2,1,0:T(8,128)S(1)} async-done(((f32[8,32,128]{2,1,0:T(8,128)}), f32[8,32,128]{2,1,0:T(8,128)S(1)}, u32[]{:S(2)}, u32[]{:S(2)}) %all-to-all-start.3) | async-done | bytes 131104 | tf_op jit(solution)/shard_map/all_to_all | solution.py:225
  (40 shorter events, 6.8 us)
Async XLA Ops:
  0.6 1.0 copy-start.3
  1.9 1.3 %copy-start = (bf16[4,8,16,2048]{3,2,1,0:T(8,128)(2,1)}, bf16[4,8,16,2048]{3,2,1,0:T(8,128)(2,1)S(1)}, u32[]{:S(2)}) copy-start(bf16[4,8,16,2048]{3,2,1,0:T(8,128)(2,1)S(1)} %spread.1) | copy-start | bytes 6291460
  3.3 10.7 %copy-start.12 = (bf16[128,512]{1,0:T(8,128)(2,1)S(1)}, bf16[128,512]{1,0:T(8,128)(2,1)}, u32[]{:S(2)}) copy-start(bf16[128,512]{1,0:T(8,128)(2,1)} %param.10) | copy-start | bytes 393220
  3.3 25.2 %copy-start.1 = (bf16[1,128,512]{2,1,0:T(8,128)(2,1)S(1)}, bf16[1,128,512]{2,1,0:T(8,128)(2,1)}, u32[]{:S(2)}) copy-start(bf16[1,128,512]{2,1,0:T(8,128)(2,1)} %param.8) | copy-start | bytes 393220
  3.3 25.3 %copy-start.2 = (bf16[1,128,512]{2,1,0:T(8,128)(2,1)S(1)}, bf16[1,128,512]{2,1,0:T(8,128)(2,1)}, u32[]{:S(2)}) copy-start(bf16[1,128,512]{2,1,0:T(8,128)(2,1)} %param.7) | copy-start | bytes 393220
  3.3 29.2 %copy-start.11 = (bf16[32,128]{1,0:T(8,128)(2,1)S(1)}, bf16[32,128]{1,0:T(8,128)(2,1)}, u32[]{:S(2)}) copy-start(bf16[32,128]{1,0:T(8,128)(2,1)} %filters_ref.3) | copy-start | bytes 24580
  3.3 62.3 %all-to-all-start = ((bf16[32,16,2048]{2,1,0:T(8,128)(2,1)}), bf16[32,16,2048]{2,1,0:T(8,128)(2,1)S(1)}, u32[]{:S(2)}, u32[]{:S(2)}) async-start(bf16[32,16,2048]{2,1,0:T(8,128)(2,1)} %bitcast.17), calls=%async_computation | async-start | bytes 4194304 | tf_op jit(solution)/shard_map/all_to_all | solution.py:225
  14.0 3.8 %collective-permute-start = (bf16[128,512]{1,0:T(8,128)(2,1)S(1)}, bf16[128,512]{1,0:T(8,128)(2,1)S(1)}, u32[]{:S(2)}, u32[]{:S(2)}) collective-permute-start(bf16[128,512]{1,0:T(8,128)(2,1)S(1)} %copy-done.12), channel_id=1, source_target_pairs={{0,8},{8,0},{1,9},{9,1},{2,10},{10,2},{3,11},{11,3},{4,12},{12,4},... | collective-permute-start | bytes 393224 | tf_op jit(solution)/shard_map/ppermute | solution.py:23
  17.9 18.3 %collective-permute-start.2 = (bf16[256,512]{1,0:T(8,128)(2,1)S(1)}, bf16[256,512]{1,0:T(8,128)(2,1)S(1)}, u32[]{:S(2)}, u32[]{:S(2)}) collective-permute-start(bf16[256,512]{1,0:T(8,128)(2,1)S(1)} %bitcast.18), channel_id=1, source_target_pairs={{0,16},{16,32},{32,48},{48,256},{256,272},{272,288},{288,304},{304... | collective-permute-start | bytes 786440 | tf_op jit(solution)/shard_map/ppermute | solution.py:234
  28.6 3.9 %collective-permute-start.1 = (bf16[128,512]{1,0:T(8,128)(2,1)S(1)}, bf16[128,512]{1,0:T(8,128)(2,1)S(1)}, u32[]{:S(2)}, u32[]{:S(2)}) collective-permute-start(bf16[128,512]{1,0:T(8,128)(2,1)S(1)} %multiply_convert_fusion.mixed_ref), channel_id=1, source_target_pairs={{0,8},{8,16},{16,24},{24,32},{32,40},{40,48},{48,56},{56,64},{64,7... | collective-permute-start | bytes 393224 | tf_op jit(solution)/shard_map/ppermute | solution.py:34
  35.5 0.7 copy-start.8
  36.2 8.0 %collective-permute-start.3 = (bf16[256,512]{1,0:T(8,128)(2,1)S(1)}, bf16[256,512]{1,0:T(8,128)(2,1)S(1)}, u32[]{:S(2)}, u32[]{:S(2)}) collective-permute-start(bf16[256,512]{1,0:T(8,128)(2,1)S(1)} %collective-permute-done.2.refs_1_), channel_id=1, source_target_pairs={{0,8},{8,0},{1,9},{9,1},{2,10},{10,2},{3,11},{11,3},{4,12},{12,4},... | collective-permute-start | bytes 786440 | tf_op jit(solution)/shard_map/ppermute | solution.py:23
  38.1 9.4 %collective-permute-start.4 = (bf16[256,512]{1,0:T(8,128)(2,1)S(1)}, bf16[256,512]{1,0:T(8,128)(2,1)S(1)}, u32[]{:S(2)}, u32[]{:S(2)}) collective-permute-start(bf16[256,512]{1,0:T(8,128)(2,1)S(1)} %collective-permute-done.2.refs_1_), channel_id=1, source_target_pairs={{0,16},{16,32},{32,48},{48,256},{256,272},{272,288},{288,304},{304... | collective-permute-start | bytes 786440 | tf_op jit(solution)/shard_map/ppermute | solution.py:234
  47.5 7.2 %collective-permute-start.5 = (bf16[256,512]{1,0:T(8,128)(2,1)S(1)}, bf16[256,512]{1,0:T(8,128)(2,1)S(1)}, u32[]{:S(2)}, u32[]{:S(2)}) collective-permute-start(bf16[256,512]{1,0:T(8,128)(2,1)S(1)} %collective-permute-done.4.refs_3_), channel_id=1, source_target_pairs={{0,8},{8,0},{1,9},{9,1},{2,10},{10,2},{3,11},{11,3},{4,12},{12,4},... | collective-permute-start | bytes 786440 | tf_op jit(solution)/shard_map/ppermute | solution.py:23
  50.8 7.5 %collective-permute-start.6 = (bf16[256,512]{1,0:T(8,128)(2,1)S(1)}, bf16[256,512]{1,0:T(8,128)(2,1)}, u32[]{:S(2)}, u32[]{:S(2)}) collective-permute-start(bf16[256,512]{1,0:T(8,128)(2,1)S(1)} %collective-permute-done.4.refs_3_), channel_id=1, source_target_pairs={{0,16},{16,32},{32,48},{48,256},{256,272},{272,288},{288,304},{304... | collective-permute-start | bytes 786440 | tf_op jit(solution)/shard_map/ppermute | solution.py:234
  54.8 0.7 copy-start.4
  58.3 7.4 %collective-permute-start.7 = (bf16[256,512]{1,0:T(8,128)(2,1)}, bf16[256,512]{1,0:T(8,128)(2,1)}, u32[]{:S(2)}, u32[]{:S(2)}) collective-permute-start(bf16[256,512]{1,0:T(8,128)(2,1)} %collective-permute-done.6.refs_5_), channel_id=1, source_target_pairs={{0,8},{8,0},{1,9},{9,1},{2,10},{10,2},{3,11},{11,3},{4,12},{12,4},... | collective-permute-start | bytes 786440 | tf_op jit(solution)/shard_map/ppermute | solution.py:23
  62.3 7.7 %collective-permute-start.8 = (bf16[256,512]{1,0:T(8,128)(2,1)}, bf16[256,512]{1,0:T(8,128)(2,1)}, u32[]{:S(2)}, u32[]{:S(2)}) collective-permute-start(bf16[256,512]{1,0:T(8,128)(2,1)} %collective-permute-done.6.refs_5_), channel_id=1, source_target_pairs={{0,16},{16,32},{32,48},{48,256},{256,272},{272,288},{288,304},{304... | collective-permute-start | bytes 786440 | tf_op jit(solution)/shard_map/ppermute | solution.py:238
  70.0 1.0 copy-start.5
  70.9 13.5 %copy-start.7 = (f32[128,512]{1,0:T(8,128)S(1)}, f32[128,512]{1,0:T(8,128)}, u32[]{:S(2)}) copy-start(f32[128,512]{1,0:T(8,128)} %copy-done.6) | copy-start | bytes 786436
  70.9 13.5 %copy-start.9 = (bf16[256,512]{1,0:T(8,128)(2,1)S(1)}, bf16[256,512]{1,0:T(8,128)(2,1)}, u32[]{:S(2)}) copy-start(bf16[256,512]{1,0:T(8,128)(2,1)} %copy-done.8) | copy-start | bytes 786436
  70.9 13.5 %copy-start.10 = (bf16[1,128,512]{2,1,0:T(8,128)(2,1)S(1)}, bf16[1,128,512]{2,1,0:T(8,128)(2,1)}, u32[]{:S(2)}) copy-start(bf16[1,128,512]{2,1,0:T(8,128)(2,1)} %param.6) | copy-start | bytes 393220
  87.3 18.1 %collective-permute-start.9 = (bf16[128,512]{1,0:T(8,128)(2,1)S(1)}, bf16[128,512]{1,0:T(8,128)(2,1)S(1)}, u32[]{:S(2)}, u32[]{:S(2)}) collective-permute-start(bf16[128,512]{1,0:T(8,128)(2,1)S(1)} %get-tuple-element.34.grad_ref), channel_id=1, source_target_pairs={{8,0},{16,8},{24,16},{32,24},{40,32},{48,40},{56,48},{64,56},{72,6... | collective-permute-start | bytes 393224 | tf_op jit(solution)/shard_map/ppermute | solution.py:34
  105.5 11.3 %all-to-all-start.3 = ((f32[8,32,128]{2,1,0:T(8,128)}), f32[8,32,128]{2,1,0:T(8,128)S(1)}, u32[]{:S(2)}, u32[]{:S(2)}) async-start(f32[8,32,128]{2,1,0:T(8,128)} %sums.1), calls=%async_computation.3 | async-start | bytes 262144 | tf_op jit(solution)/shard_map/all_to_all | solution.py:225
  (1 other events, 0.7 us)

commit v10 on v9

--- a/solution.py
+++ b/solution.py
@@ -16,6 +16,7 @@
 
 Z = ("zh", "zl")
 CONTEXT = ("x", "zl", "co")
+Y = ("yq", "yp")
 VMEM = pltpu.CompilerParams(vmem_limit_bytes=8 * 1024 * 1024)
 
 
@@ -104,31 +105,35 @@
             lag_ref[copy, g : g + 1, :] = sums
 
 
-def product_kernel(place_ref, cot_ref, *refs):
+def product_kernel(place_ref, own_ref, low_ref, high_ref, *refs):
     count = (len(refs) - 3) // 2
     weights_hbm, out_ref, total_ref, weights, sems = refs[:count], refs[count], refs[count + 1], refs[count + 2 : -1], refs[-1]
     copies = [pltpu.make_async_copy(weights_hbm[i], weights[i], sems.at[i]) for i in range(count)]
     for copy in copies:
         copy.start()
-    z, core = place_ref[0], place_ref[1]
+    z, core, odd = place_ref[0], place_ref[1], place_ref[2]
     depth = weights[0].shape[0]
     pieces = [z]
     for step in (1, 2, 3):
         below, above = lax.rem(z + 8 - step, 8), lax.rem(z + step, 8)
         pieces += [jnp.where(core == 0, below, above), jnp.where(core == 0, above, below)]
     pieces.append(lax.rem(z + 4, 8))
+    half = own_ref.shape[0] // 2
+    parts = ((own_ref, 0), (own_ref, half), (low_ref, 0), (high_ref, 0))
     for i, place in enumerate(pieces):
         copies[i].wait()
         columns = pl.ds(pl.multiple_of(place * depth, LANES), depth)
-        for x in range(4):
-            rows = slice(x * TAPS, (x + 1) * TAPS)
-            term = jnp.dot(cot_ref[rows, columns], weights[i][...], preferred_element_type=F32)
+        for j, (cot_ref, first) in enumerate(parts):
+            term = jnp.dot(cot_ref[first : first + half, columns], weights[i][...], preferred_element_type=F32)
             if i:
-                term = total_ref[x] + term
+                term = total_ref[j] + term
             if i < count - 1:
-                total_ref[x] = term
-            else:
-                out_ref[x] = term.astype(BF16)
+                total_ref[j] = term
+                continue
+            term = term.astype(BF16).reshape(2, 4, 16, term.shape[1])
+            for x in range(2):
+                for pair in range(4):
+                    out_ref[2 * (j % 2) + x, pair, odd if j < 2 else 1 - odd] = term[x, pair]
 
 
 def lane_blocks(*lead):
@@ -142,10 +147,10 @@
     rows, width = cotangent.shape
     return pl.pallas_call(
         spread_kernel,
-        grid=(8,),
+        grid=(4,),
         in_specs=[pl.BlockSpec((rows, width), lambda i: (0, 0))],
         out_specs=pl.BlockSpec((4, 1, rows, width // 4), lambda i: (0, i, 0, 0)),
-        out_shape=jax.ShapeDtypeStruct((4, 8, rows, width // 4), cotangent.dtype),
+        out_shape=jax.ShapeDtypeStruct((4, 4, rows, width // 4), cotangent.dtype),
         compiler_params=VMEM,
         name="spread",
     )(cotangent)
@@ -203,55 +208,69 @@
     )(terms, conv, query, turned)
 
 
-def partial_products(cotangent, weights):
+def partial_products(parts, weights):
     width = weights[0].shape[1]
-    place = jnp.stack([lax.axis_index(Z), lax.axis_index("co")]).astype(jnp.int32)
+    place = jnp.stack([lax.axis_index(Z), lax.axis_index("co"), lax.axis_index("yp")]).astype(jnp.int32)
     whole = pl.BlockSpec(memory_space=pltpu.VMEM)
-    return pl.pallas_call(
+    out = pl.pallas_call(
         product_kernel,
-        in_specs=[pl.BlockSpec(memory_space=pltpu.SMEM), whole]
+        in_specs=[pl.BlockSpec(memory_space=pltpu.SMEM)]
+        + [whole] * 3
         + [pl.BlockSpec(memory_space=pltpu.HBM)] * len(weights),
         out_specs=whole,
-        out_shape=jax.ShapeDtypeStruct((4, TAPS, width), BF16),
+        out_shape=jax.ShapeDtypeStruct((4, 4, 2, 16, width), BF16),
         scratch_shapes=[pltpu.VMEM((4, TAPS, width), F32)]
         + [pltpu.VMEM(a.shape, a.dtype) for a in weights]
         + [pltpu.SemaphoreType.DMA((len(weights),))],
         compiler_params=VMEM,
         name="product",
-    )(place, cotangent, *weights)
+    )(place, *parts, *weights)
+    return out.reshape(4, TAPS, width)
 
 
 def exchange(copies, axes):
     return lax.all_to_all(copies, axes, split_axis=0, concat_axis=0)
 
 
-def weight_blocks(chip, beside):
+def ahead(block, axes, distance):
+    n = lax.axis_size(axes)
+    return lax.ppermute(block, axes, [((i + distance) % n, i) for i in range(n)])
+
+
+def along_z(block, steps):
     n = lax.axis_size(Z)
-    route = [(2 * i, 2 * ((i + 1) % n)) for i in range(n)] + [(2 * i + 1, 2 * ((i - 1) % n) + 1) for i in range(n)]
-    blocks = [chip]
-    got = chip
-    for _ in range(n // 2 - 1):
-        got = lax.ppermute(got, Z + ("co",), route)
-        got, beside = lax.optimization_barrier((got, beside))
-        beside = swap(got, "co")
-        blocks += [got, beside]
-    return blocks + [lax.ppermute(got, Z + ("co",), route)]
+    route = [(2 * i, 2 * ((i + steps) % n)) for i in range(n)]
+    route += [(2 * i + 1, 2 * ((i - steps) % n) + 1) for i in range(n)]
+    return lax.ppermute(block, Z + ("co",), route)
+
+
+def weight_blocks(chip):
+    one, two = along_z(chip, 1), along_z(chip, 2)
+    three, four = along_z(two, 1), along_z(two, 2)
+    return [chip, one, swap(one, "co"), two, swap(two, "co"), three, swap(three, "co"), four]
+
+
+def cotangent_parts(cotangent):
+    copies = spread(cotangent)
+    rows, width = copies.shape[2:]
+    own = exchange(copies.reshape(16, rows, width), ("x", "yq"))
+    low, high = ahead(own[:8], Y, -1), ahead(own[8:], Y, 1)
+    return [part.reshape(-1, width) for part in (own, low, high)]
 
 
 def local(query_branch, key_branch, value_branch, cotangent, out_weight, filters):
     query, keys, values = query_branch[0], key_branch[0], value_branch[0]
     tokens, width = query.shape
     chip = in_order(out_weight, swap(out_weight, "co"), "co").reshape(2 * out_weight.shape[0], width)
-    copies = spread(cotangent[0])
-    gathered = exchange(copies.reshape((32,) + copies.shape[2:]), ("x", "y")).reshape(4 * TAPS, -1)
+    parts = cotangent_parts(cotangent[0])
 
     keys, values, chip = lax.optimization_barrier((keys, values, chip))
     mixed = (keys.astype(F32) * values.astype(F32)).astype(BF16)
     conv, turned = convolve(filters, from_behind(mixed, 1), mixed)
-    weights = weight_blocks(chip, conv)
-
-    gathered, conv, turned = lax.optimization_barrier((gathered, conv, turned))
-    terms = exchange(partial_products(gathered, weights), "x")
+    weights = weight_blocks(chip)
+
+    parts, conv, turned = lax.optimization_barrier((parts, conv, turned))
+    terms = exchange(partial_products(parts, weights), "x")
     query_grad, conv_grad, lags = branch_gradients(terms, conv, query, turned)
     lags = summed_copies(exchange(lags, ("x", "co")))
     after = from_behind(conv_grad, -1)
@@ -263,8 +282,8 @@
 
 
 def solution(mesh):
-    fine = Mesh(mesh.devices.reshape(2, 4, 4, 2, 8), ("zh", "x", "zl", "co", "y"))
-    branch = P("zh", CONTEXT, "y")
+    fine = Mesh(mesh.devices.reshape(2, 4, 4, 2, 4, 2), ("zh", "x", "zl", "co", "yq", "yp"))
+    branch = P("zh", CONTEXT, Y)
     return jax.shard_map(
         local,
         mesh=fine,
@@ -272,10 +291,10 @@
             branch,
             branch,
             branch,
-            P("zh", CONTEXT + ("y",), None),
-            P(("zh",) + CONTEXT, "y"),
-            P("y", None),
+            P("zh", CONTEXT + Y, None),
+            P(("zh",) + CONTEXT, Y),
+            P(Y, None),
         ),
-        out_specs=(branch, branch, branch, P("y", None)),
+        out_specs=(branch, branch, branch, P(Y, None)),
         check_vma=False,
     )

time: 119 us -> 130 us (1.092)
  starting transfers between devices: 57.4 us -> 66.9 us
  waiting for transfers between devices: 18.6 us -> 20.9 us
  Pallas kernels: 11.2 us -> 12.9 us
  local copies, waits for them, and re-layouts: 5.38 us -> 4.03 us
    all_to_all x2, waiting for transfers between devices: 5.33 us -> 18 us  [exchange(): return lax.all_to_all(copies, axes, split_axis=0, concat_axis=0)]
    ppermute x4 -> x6, starting transfers between devices: 24 us -> 35.1 us  [the longest x4 28.7 us: along_z(): return lax.ppermute(block, Z + ('co',), route)]
    ppermute x4 -> x6, waiting for transfers between devices: 10.4 us -> 0.02 us  [the longest x4 0.01 us: along_z(): return lax.ppermute(block, Z + ('co',), route)]
    unnamed x26 -> x16, local copies, waits for them, and re-layouts: 5.38 us -> 3.14 us
  transfers between devices with their start and end apart: 12 -> 14, of which waited for: 6 -> 4; matrix products, arithmetic and copies ran while one was open for 0% -> 1% of each run, Pallas kernels for 5% -> 4%
where the time goes in v10:
time: 130 us; the launch traced here: 129 us
  starting transfers between devices  66.9 us (51%)
  blocking collectives  22.6 us (17%)
  waiting for transfers between devices  20.9 us (16%)
  Pallas kernels  12.9 us (10%)
  local copies, waits for them, and re-layouts  4.03 us (3%)
    ppermute x4, starting transfers between devices, along_z(): return lax.ppermute(block, Z + ('co',), route)  28.7 us
    all_to_all x2, blocking collectives, exchange(): return lax.all_to_all(copies, axes, split_axis=0, concat_axis=0)  22.6 us
    all_to_all x2, waiting for transfers between devices, exchange(): return lax.all_to_all(copies, axes, split_axis=0, concat_axis=0)  18 us
    all_to_all x2, starting transfers between devices, exchange(): return lax.all_to_all(copies, axes, split_axis=0, concat_axis=0)  13.7 us
    ppermute x4, starting transfers between devices, swap(): return lax.ppermute(block, axis, [(0, 1), (1, 0)])  11.8 us
    ppermute x2, starting transfers between devices, ahead(): lax.ppermute(block, axes, [((i + distance) % n, i) for i in range(n)])  6.48 us
    ppermute x2, starting transfers between devices, from_behind(): return lax.ppermute(block, CONTEXT, route)  6.23 us
    unnamed x16, local copies, waits for them, and re-layouts  3.14 us
  transfers between devices with their start and end apart: 14, of which 4 were waited for; matrix products, arithmetic and copies ran while one was open for 1% of the time, Pallas kernels for 4%

profile of v10, /device:TPU:1, one launch (start us, length us, event | category | flops | bytes accessed | tf_op | source)
XLA Modules:
  0.0 129.1 jit_solution(14292541937869886024)
XLA Ops:
  1.6 1.6 %spread.1 = bf16[4,4,16,2048]{3,2,1,0:T(8,128)(2,1)} custom-call(bf16[16,8192]{1,0:T(8,128)(2,1)S(1)} %bitcast.31), custom_call_target="tpu_custom_call" | custom-call | tf_op jit(solution)/shard_map/spread/pallas_call | solution.py:148
  3.2 10.3 %all-to-all-start = ((bf16[16,16,2048]{2,1,0:T(8,128)(2,1)}), bf16[16,16,2048]{2,1,0:T(8,128)(2,1)S(1)}, u32[]{:S(2)}, u32[]{:S(2)}) async-start(bf16[16,16,2048]{2,1,0:T(8,128)(2,1)} %bitcast.4), calls=%async_computation | async-start | bytes 2097152 | tf_op jit(solution)/shard_map/all_to_all | solution.py:232
  13.5 2.9 %collective-permute-start.2 = (bf16[128,512]{1,0:T(8,128)(2,1)S(1)}, bf16[128,512]{1,0:T(8,128)(2,1)S(1)}, u32[]{:S(2)}, u32[]{:S(2)}) collective-permute-start(bf16[128,512]{1,0:T(8,128)(2,1)S(1)} %copy-done.7), channel_id=1, source_target_pairs={{0,8},{8,0},{1,9},{9,1},{2,10},{10,2},{3,11},{11,3},{4,12},{12,4},... | collective-permute-start | bytes 393224 | tf_op jit(solution)/shard_map/ppermute | solution.py:24
  17.5 10.8 %collective-permute-start.6 = (bf16[256,512]{1,0:T(8,128)(2,1)S(1)}, bf16[256,512]{1,0:T(8,128)(2,1)S(1)}, u32[]{:S(2)}, u32[]{:S(2)}) collective-permute-start(bf16[256,512]{1,0:T(8,128)(2,1)S(1)} %bitcast.22), channel_id=1, source_target_pairs={{0,32},{16,48},{32,256},{48,272},{256,288},{272,304},{288,0},{304,... | collective-permute-start | bytes 786440 | tf_op jit(solution)/shard_map/ppermute | solution.py:244
  28.2 12.9 %all-to-all-done = bf16[16,16,2048]{2,1,0:T(8,128)(2,1)S(1)} async-done(((bf16[16,16,2048]{2,1,0:T(8,128)(2,1)}), bf16[16,16,2048]{2,1,0:T(8,128)(2,1)S(1)}, u32[]{:S(2)}, u32[]{:S(2)}) %all-to-all-start) | async-done | bytes 1048608 | tf_op jit(solution)/shard_map/all_to_all | solution.py:232
  42.0 1.9 %collective-permute-start = (bf16[8,16,2048]{2,1,0:T(8,128)(2,1)S(1)}, bf16[8,16,2048]{2,1,0:T(8,128)(2,1)S(1)}, u32[]{:S(2)}, u32[]{:S(2)}) collective-permute-start(bf16[8,16,2048]{2,1,0:T(8,128)(2,1)S(1)} %get-tuple-element.39), channel_id=1, source_target_pairs={{7,0},{0,1},{1,2},{2,3},{3,4},{4,5},{5,6},{6,7},{15,8},{8,9},{9,10... | collective-permute-start | bytes 1572872 | tf_op jit(solution)/shard_map/ppermute | solution.py:237
  43.9 10.7 %collective-permute-start.4 = (bf16[256,512]{1,0:T(8,128)(2,1)S(1)}, bf16[256,512]{1,0:T(8,128)(2,1)S(1)}, u32[]{:S(2)}, u32[]{:S(2)}) collective-permute-start(bf16[256,512]{1,0:T(8,128)(2,1)S(1)} %bitcast.23), channel_id=1, source_target_pairs={{0,16},{16,32},{32,48},{48,256},{256,272},{272,288},{288,304},{304... | collective-permute-start | bytes 786440 | tf_op jit(solution)/shard_map/ppermute | solution.py:244
  54.6 2.2 %collective-permute-start.8 = (bf16[256,512]{1,0:T(8,128)(2,1)S(1)}, bf16[256,512]{1,0:T(8,128)(2,1)S(1)}, u32[]{:S(2)}, u32[]{:S(2)}) collective-permute-start(bf16[256,512]{1,0:T(8,128)(2,1)S(1)} %collective-permute-done.6.refs_3_), channel_id=1, source_target_pairs={{0,16},{16,32},{32,48},{48,256},{256,272},{272,288},{288,304},{304... | collective-permute-start | bytes 786440 | tf_op jit(solution)/shard_map/ppermute | solution.py:244
  56.8 4.6 %collective-permute-start.1 = (bf16[8,16,2048]{2,1,0:T(8,128)(2,1)}, bf16[8,16,2048]{2,1,0:T(8,128)(2,1)S(1)}, u32[]{:S(2)}, u32[]{:S(2)}) collective-permute-start(bf16[8,16,2048]{2,1,0:T(8,128)(2,1)} %get-tuple-element.38), channel_id=1, source_target_pairs={{1,0},{2,1},{3,2},{4,3},{5,4},{6,5},{7,6},{0,7},{9,8},{10,9},{11,1... | collective-permute-start | bytes 1572872 | tf_op jit(solution)/shard_map/ppermute | solution.py:237
  61.4 3.2 %collective-permute-start.3 = (bf16[128,512]{1,0:T(8,128)(2,1)S(1)}, bf16[128,512]{1,0:T(8,128)(2,1)S(1)}, u32[]{:S(2)}, u32[]{:S(2)}) collective-permute-start(bf16[128,512]{1,0:T(8,128)(2,1)S(1)} %multiply_convert_fusion.mixed_ref), channel_id=1, source_target_pairs={{0,8},{8,16},{16,24},{24,32},{32,40},{40,48},{48,56},{56,64},{64,7... | collective-permute-start | bytes 393224 | tf_op jit(solution)/shard_map/ppermute | solution.py:35
  64.7 1.9 %collective-permute-done.3.before_ref = bf16[128,512]{1,0:T(8,128)(2,1)S(1)} collective-permute-done((bf16[128,512]{1,0:T(8,128)(2,1)S(1)}, bf16[128,512]{1,0:T(8,128)(2,1)S(1)}, u32[]{:S(2)}, u32[]{:S(2)}) %collective-permute-start.3) | collective-permute-done | bytes 131104 | tf_op jit(solution)/shard_map/ppermute | solution.py:35
  67.3 5.0 %collective-permute-start.10 = (bf16[256,512]{1,0:T(8,128)(2,1)S(1)}, bf16[256,512]{1,0:T(8,128)(2,1)}, u32[]{:S(2)}, u32[]{:S(2)}) collective-permute-start(bf16[256,512]{1,0:T(8,128)(2,1)S(1)} %collective-permute-done.6.refs_3_), channel_id=1, source_target_pairs={{0,32},{16,48},{32,256},{48,272},{256,288},{272,304},{288,0},{304,... | collective-permute-start | bytes 786440 | tf_op jit(solution)/shard_map/ppermute | solution.py:244
  72.3 4.6 %collective-permute-start.7 = (bf16[256,512]{1,0:T(8,128)(2,1)S(1)}, bf16[256,512]{1,0:T(8,128)(2,1)}, u32[]{:S(2)}, u32[]{:S(2)}) collective-permute-start(bf16[256,512]{1,0:T(8,128)(2,1)S(1)} %collective-permute-done.6.refs_3_), channel_id=1, source_target_pairs={{0,8},{8,0},{1,9},{9,1},{2,10},{10,2},{3,11},{11,3},{4,12},{12,4},... | collective-permute-start | bytes 786440 | tf_op jit(solution)/shard_map/ppermute | solution.py:24
  77.0 1.9 %collective-permute-start.5 = (bf16[256,512]{1,0:T(8,128)(2,1)S(1)}, bf16[256,512]{1,0:T(8,128)(2,1)}, u32[]{:S(2)}, u32[]{:S(2)}) collective-permute-start(bf16[256,512]{1,0:T(8,128)(2,1)S(1)} %collective-permute-done.4.refs_1_), channel_id=1, source_target_pairs={{0,8},{8,0},{1,9},{9,1},{2,10},{10,2},{3,11},{11,3},{4,12},{12,4},... | collective-permute-start | bytes 786440 | tf_op jit(solution)/shard_map/ppermute | solution.py:24
  78.9 2.4 %collective-permute-start.9 = (bf16[256,512]{1,0:T(8,128)(2,1)S(1)}, bf16[256,512]{1,0:T(8,128)(2,1)}, u32[]{:S(2)}, u32[]{:S(2)}) collective-permute-start(bf16[256,512]{1,0:T(8,128)(2,1)S(1)} %collective-permute-done.8.refs_5_), channel_id=1, source_target_pairs={{0,8},{8,0},{1,9},{9,1},{2,10},{10,2},{3,11},{11,3},{4,12},{12,4},... | collective-permute-start | bytes 786440 | tf_op jit(solution)/shard_map/ppermute | solution.py:24
  82.9 2.3 %conv.1 = (f32[128,512]{1,0:T(8,128)S(1)}, bf16[256,512]{1,0:T(8,128)(2,1)S(1)}) custom-call(bf16[32,128]{1,0:T(8,128)(2,1)S(1)} %copy-done.6, bf16[128,512]{1,0:T(8,128)(2,1)S(1)} %copy-done.5, bf16[128,512]{1,0:T(8,128)(2,1)S(1)} %multiply_convert_fusion.mixed_ref), custom_call_target="tpu_custom_call" | custom-call | tf_op jit(solution)/shard_map/conv/pallas_call | solution.py:171
  85.3 2.9 %product.1 = bf16[4,4,2,16,512]{4,3,2,1,0:T(8,128)(2,1)S(1)} custom-call(s32[3]{0:T(128)S(1)} %pad_add_fusion.place_ref, bf16[256,2048]{1,0:T(8,128)(2,1)S(1)} %bitcast.20, bf16[128,2048]{1,0:T(8,128)(2,1)S(1)} %bitcast.25, bf16[128,2048]{1,0:T(8,128)(2,1)S(1)} %bitcast.26, bf16[256,512]{1,0:T(8,128)(2,1)S(1)} %bitcast.24, ...), custom_call_target="tpu_custom_call" | custom-call | tf_op jit(solution)/shard_map/product/pallas_call | solution.py:215
  88.2 11.9 %all_to_all.20.terms_ref = bf16[4,128,512]{2,1,0:T(8,128)(2,1)S(1)} all-to-all(bf16[4,128,512]{2,1,0:T(8,128)(2,1)S(1)} %bitcast.21), channel_id=1, replica_groups=mesh['zh'=2,'x'=4,'zl'=4,'co'=2,'yq'=4,'yp'=2] {'x'}, dimensions={0} | all-to-all | bytes 1048576 | tf_op jit(solution)/shard_map/all_to_all | solution.py:232
  100.1 2.9 %branch.1 = (bf16[128,512]{1,0:T(8,128)(2,1)}, bf16[128,512]{1,0:T(8,128)(2,1)S(1)}, f32[8,32,128]{2,1,0:T(8,128)S(1)}) custom-call(bf16[4,128,512]{2,1,0:T(8,128)(2,1)S(1)} %all_to_all.20.terms_ref, f32[128,512]{1,0:T(8,128)S(1)} %get-tuple-element.29.conv_ref, bf16[128,512]{1,0:T(8,128)(2,1)S(1)} %bitcast.32, bf16[256,512]{1,0:T(8,128)(2,1)S(1)} %get-tuple-element.30.turned_ref), custom_call_target="tpu_custom_call" | custom-call | tf_op jit(solution)/shard_map/branch/pallas_call | solution.py:199
  103.0 3.0 %collective-permute-start.11 = (bf16[128,512]{1,0:T(8,128)(2,1)S(1)}, bf16[128,512]{1,0:T(8,128)(2,1)S(1)}, u32[]{:S(2)}, u32[]{:S(2)}) collective-permute-start(bf16[128,512]{1,0:T(8,128)(2,1)S(1)} %get-tuple-element.32.grad_ref), channel_id=1, source_target_pairs={{8,0},{16,8},{24,16},{32,24},{40,32},{48,40},{56,48},{64,56},{72,6... | collective-permute-start | bytes 393224 | tf_op jit(solution)/shard_map/ppermute | solution.py:35
  106.0 10.7 %all_to_all.21.parts_ref = f32[8,32,128]{2,1,0:T(8,128)S(1)} all-to-all(f32[8,32,128]{2,1,0:T(8,128)S(1)} %get-tuple-element.33), channel_id=1, replica_groups=mesh['zh'=2,'x'=4,'zl'=4,'co'=2,'yq'=4,'yp'=2] {'x','co'}, dimensions={0} | all-to-all | bytes 262144 | tf_op jit(solution)/shard_map/all_to_all | solution.py:232
  117.4 3.4 %all-to-all-start.3 = ((f32[8,32,128]{2,1,0:T(8,128)}), f32[8,32,128]{2,1,0:T(8,128)S(1)}, u32[]{:S(2)}, u32[]{:S(2)}) async-start(f32[8,32,128]{2,1,0:T(8,128)} %sums.1), calls=%async_computation.3 | async-start | bytes 262144 | tf_op jit(solution)/shard_map/all_to_all | solution.py:232
  120.8 2.5 %mixed_grad.1 = (bf16[128,512]{1,0:T(8,128)(2,1)}, bf16[128,512]{1,0:T(8,128)(2,1)}) custom-call(bf16[32,128]{1,0:T(8,128)(2,1)S(1)} %copy-done.6, bf16[128,512]{1,0:T(8,128)(2,1)S(1)} %get-tuple-element.32.grad_ref, bf16[128,512]{1,0:T(8,128)(2,1)S(1)} %collective-permute-done.11.after_ref, bf16[128,512]{1,0:T(8,128)(2,1)S(1)} %bitcast.30, ...), custom_call_target="tpu_custom_call" | custom-call | tf_op jit(solution)/shard_map/mixed_grad/pallas_call | solution.py:185
  123.3 5.1 %all-to-all-done.3 = f32[8,32,128]{2,1,0:T(8,128)S(1)} async-done(((f32[8,32,128]{2,1,0:T(8,128)}), f32[8,32,128]{2,1,0:T(8,128)S(1)}, u32[]{:S(2)}, u32[]{:S(2)}) %all-to-all-start.3) | async-done | bytes 131104 | tf_op jit(solution)/shard_map/all_to_all | solution.py:232
  (35 shorter events, 6.5 us)
Async XLA Ops:
  0.6 1.0 copy-start.2
  3.2 10.4 %copy-start.7 = (bf16[128,512]{1,0:T(8,128)(2,1)S(1)}, bf16[128,512]{1,0:T(8,128)(2,1)}, u32[]{:S(2)}) copy-start(bf16[128,512]{1,0:T(8,128)(2,1)} %param.10) | copy-start | bytes 393220
  3.2 38.0 %all-to-all-start = ((bf16[16,16,2048]{2,1,0:T(8,128)(2,1)}), bf16[16,16,2048]{2,1,0:T(8,128)(2,1)S(1)}, u32[]{:S(2)}, u32[]{:S(2)}) async-start(bf16[16,16,2048]{2,1,0:T(8,128)(2,1)} %bitcast.4), calls=%async_computation | async-start | bytes 2097152 | tf_op jit(solution)/shard_map/all_to_all | solution.py:232
  13.5 3.8 %collective-permute-start.2 = (bf16[128,512]{1,0:T(8,128)(2,1)S(1)}, bf16[128,512]{1,0:T(8,128)(2,1)S(1)}, u32[]{:S(2)}, u32[]{:S(2)}) collective-permute-start(bf16[128,512]{1,0:T(8,128)(2,1)S(1)} %copy-done.7), channel_id=1, source_target_pairs={{0,8},{8,0},{1,9},{9,1},{2,10},{10,2},{3,11},{11,3},{4,12},{12,4},... | collective-permute-start | bytes 393224 | tf_op jit(solution)/shard_map/ppermute | solution.py:24
  17.4 44.0 %copy-start = (bf16[1,128,512]{2,1,0:T(8,128)(2,1)S(1)}, bf16[1,128,512]{2,1,0:T(8,128)(2,1)}, u32[]{:S(2)}) copy-start(bf16[1,128,512]{2,1,0:T(8,128)(2,1)} %param.8) | copy-start | bytes 393220
  17.4 44.0 %copy-start.1 = (bf16[1,128,512]{2,1,0:T(8,128)(2,1)S(1)}, bf16[1,128,512]{2,1,0:T(8,128)(2,1)}, u32[]{:S(2)}) copy-start(bf16[1,128,512]{2,1,0:T(8,128)(2,1)} %param.7) | copy-start | bytes 393220
  17.5 37.2 %collective-permute-start.6 = (bf16[256,512]{1,0:T(8,128)(2,1)S(1)}, bf16[256,512]{1,0:T(8,128)(2,1)S(1)}, u32[]{:S(2)}, u32[]{:S(2)}) collective-permute-start(bf16[256,512]{1,0:T(8,128)(2,1)S(1)} %bitcast.22), channel_id=1, source_target_pairs={{0,32},{16,48},{32,256},{48,272},{256,288},{272,304},{288,0},{304,... | collective-permute-start | bytes 786440 | tf_op jit(solution)/shard_map/ppermute | solution.py:244
  42.0 36.9 %collective-permute-start = (bf16[8,16,2048]{2,1,0:T(8,128)(2,1)S(1)}, bf16[8,16,2048]{2,1,0:T(8,128)(2,1)S(1)}, u32[]{:S(2)}, u32[]{:S(2)}) collective-permute-start(bf16[8,16,2048]{2,1,0:T(8,128)(2,1)S(1)} %get-tuple-element.39), channel_id=1, source_target_pairs={{7,0},{0,1},{1,2},{2,3},{3,4},{4,5},{5,6},{6,7},{15,8},{8,9},{9,10... | collective-permute-start | bytes 1572872 | tf_op jit(solution)/shard_map/ppermute | solution.py:237
  43.9 28.4 %collective-permute-start.4 = (bf16[256,512]{1,0:T(8,128)(2,1)S(1)}, bf16[256,512]{1,0:T(8,128)(2,1)S(1)}, u32[]{:S(2)}, u32[]{:S(2)}) collective-permute-start(bf16[256,512]{1,0:T(8,128)(2,1)S(1)} %bitcast.23), channel_id=1, source_target_pairs={{0,16},{16,32},{32,48},{48,256},{256,272},{272,288},{288,304},{304... | collective-permute-start | bytes 786440 | tf_op jit(solution)/shard_map/ppermute | solution.py:244
  54.6 22.3 %collective-permute-start.8 = (bf16[256,512]{1,0:T(8,128)(2,1)S(1)}, bf16[256,512]{1,0:T(8,128)(2,1)S(1)}, u32[]{:S(2)}, u32[]{:S(2)}) collective-permute-start(bf16[256,512]{1,0:T(8,128)(2,1)S(1)} %collective-permute-done.6.refs_3_), channel_id=1, source_target_pairs={{0,16},{16,32},{32,48},{48,256},{256,272},{272,288},{288,304},{304... | collective-permute-start | bytes 786440 | tf_op jit(solution)/shard_map/ppermute | solution.py:244
  56.8 28.5 %collective-permute-start.1 = (bf16[8,16,2048]{2,1,0:T(8,128)(2,1)}, bf16[8,16,2048]{2,1,0:T(8,128)(2,1)S(1)}, u32[]{:S(2)}, u32[]{:S(2)}) collective-permute-start(bf16[8,16,2048]{2,1,0:T(8,128)(2,1)} %get-tuple-element.38), channel_id=1, source_target_pairs={{1,0},{2,1},{3,2},{4,3},{5,4},{6,5},{7,6},{0,7},{9,8},{10,9},{11,1... | collective-permute-start | bytes 1572872 | tf_op jit(solution)/shard_map/ppermute | solution.py:237
  61.4 5.2 %collective-permute-start.3 = (bf16[128,512]{1,0:T(8,128)(2,1)S(1)}, bf16[128,512]{1,0:T(8,128)(2,1)S(1)}, u32[]{:S(2)}, u32[]{:S(2)}) collective-permute-start(bf16[128,512]{1,0:T(8,128)(2,1)S(1)} %multiply_convert_fusion.mixed_ref), channel_id=1, source_target_pairs={{0,8},{8,16},{16,24},{24,32},{32,40},{40,48},{48,56},{56,64},{64,7... | collective-permute-start | bytes 393224 | tf_op jit(solution)/shard_map/ppermute | solution.py:35
  66.6 0.7 copy-start.4
  67.3 18.0 %collective-permute-start.10 = (bf16[256,512]{1,0:T(8,128)(2,1)S(1)}, bf16[256,512]{1,0:T(8,128)(2,1)}, u32[]{:S(2)}, u32[]{:S(2)}) collective-permute-start(bf16[256,512]{1,0:T(8,128)(2,1)S(1)} %collective-permute-done.6.refs_3_), channel_id=1, source_target_pairs={{0,32},{16,48},{32,256},{48,272},{256,288},{272,304},{288,0},{304,... | collective-permute-start | bytes 786440 | tf_op jit(solution)/shard_map/ppermute | solution.py:244
  72.3 13.0 %collective-permute-start.7 = (bf16[256,512]{1,0:T(8,128)(2,1)S(1)}, bf16[256,512]{1,0:T(8,128)(2,1)}, u32[]{:S(2)}, u32[]{:S(2)}) collective-permute-start(bf16[256,512]{1,0:T(8,128)(2,1)S(1)} %collective-permute-done.6.refs_3_), channel_id=1, source_target_pairs={{0,8},{8,0},{1,9},{9,1},{2,10},{10,2},{3,11},{11,3},{4,12},{12,4},... | collective-permute-start | bytes 786440 | tf_op jit(solution)/shard_map/ppermute | solution.py:24
  77.0 8.3 %collective-permute-start.5 = (bf16[256,512]{1,0:T(8,128)(2,1)S(1)}, bf16[256,512]{1,0:T(8,128)(2,1)}, u32[]{:S(2)}, u32[]{:S(2)}) collective-permute-start(bf16[256,512]{1,0:T(8,128)(2,1)S(1)} %collective-permute-done.4.refs_1_), channel_id=1, source_target_pairs={{0,8},{8,0},{1,9},{9,1},{2,10},{10,2},{3,11},{11,3},{4,12},{12,4},... | collective-permute-start | bytes 786440 | tf_op jit(solution)/shard_map/ppermute | solution.py:24
  78.9 6.4 %collective-permute-start.9 = (bf16[256,512]{1,0:T(8,128)(2,1)S(1)}, bf16[256,512]{1,0:T(8,128)(2,1)}, u32[]{:S(2)}, u32[]{:S(2)}) collective-permute-start(bf16[256,512]{1,0:T(8,128)(2,1)S(1)} %collective-permute-done.8.refs_5_), channel_id=1, source_target_pairs={{0,8},{8,0},{1,9},{9,1},{2,10},{10,2},{3,11},{11,3},{4,12},{12,4},... | collective-permute-start | bytes 786440 | tf_op jit(solution)/shard_map/ppermute | solution.py:24
  81.3 0.7 copy-start.6
  82.0 0.9 copy-start.5
  88.2 11.9 %copy-start.3 = (bf16[1,128,512]{2,1,0:T(8,128)(2,1)S(1)}, bf16[1,128,512]{2,1,0:T(8,128)(2,1)}, u32[]{:S(2)}) copy-start(bf16[1,128,512]{2,1,0:T(8,128)(2,1)} %param.6) | copy-start | bytes 393220
  103.0 14.4 %collective-permute-start.11 = (bf16[128,512]{1,0:T(8,128)(2,1)S(1)}, bf16[128,512]{1,0:T(8,128)(2,1)S(1)}, u32[]{:S(2)}, u32[]{:S(2)}) collective-permute-start(bf16[128,512]{1,0:T(8,128)(2,1)S(1)} %get-tuple-element.32.grad_ref), channel_id=1, source_target_pairs={{8,0},{16,8},{24,16},{32,24},{40,32},{48,40},{56,48},{64,56},{72,6... | collective-permute-start | bytes 393224 | tf_op jit(solution)/shard_map/ppermute | solution.py:35
  117.4 11.1 %all-to-all-start.3 = ((f32[8,32,128]{2,1,0:T(8,128)}), f32[8,32,128]{2,1,0:T(8,128)S(1)}, u32[]{:S(2)}, u32[]{:S(2)}) async-start(f32[8,32,128]{2,1,0:T(8,128)} %sums.1), calls=%async_computation.3 | async-start | bytes 262144 | tf_op jit(solution)/shard_map/all_to_all | solution.py:232

commit v11 on v10

--- a/solution.py
+++ b/solution.py
@@ -36,7 +36,17 @@
 
 
 def shifted_rows(row):
-    return pltpu.roll(jnp.broadcast_to(row, (TAPS, 2 * TAPS)), 0, 1, stride=1, stride_axis=0)
+    rows = pltpu.roll(jnp.broadcast_to(row, (8, 2 * TAPS)), 0, 1, stride=1, stride_axis=0)
+    while rows.shape[0] < TAPS:
+        rows = jnp.concatenate([rows, pltpu.roll(rows, rows.shape[0], 1)], 0)
+    return rows
+
+
+def skewed_sum(rows):
+    while rows.shape[0] > 8:
+        half = rows.shape[0] // 2
+        rows = rows[:half] + pltpu.roll(rows[half:], half, 1)
+    return jnp.sum(pltpu.roll(rows, 1, 1, stride=1, stride_axis=0), axis=0, keepdims=True)
 
 
 def lane_group(shape):
@@ -99,8 +109,7 @@
     for g in range(PER):
         part = jnp.where(owner == g, wide, 0.0).astype(BF16)
         outer = lax.dot_general(part, turned_ref[...], (((1,), (1,)), ((), ())), preferred_element_type=F32)
-        skewed = pltpu.roll(outer, 1, 1, stride=1, stride_axis=0)
-        sums = jnp.sum(skewed, axis=0, keepdims=True)[:, TAPS:]
+        sums = skewed_sum(outer)[:, TAPS:]
         for copy in range(lag_ref.shape[0]):
             lag_ref[copy, g : g + 1, :] = sums
 
@@ -113,21 +122,23 @@
         copy.start()
     z, core, odd = place_ref[0], place_ref[1], place_ref[2]
     depth = weights[0].shape[0]
-    pieces = [z]
-    for step in (1, 2, 3):
-        below, above = lax.rem(z + 8 - step, 8), lax.rem(z + step, 8)
-        pieces += [jnp.where(core == 0, below, above), jnp.where(core == 0, above, below)]
-    pieces.append(lax.rem(z + 4, 8))
+    below, above = [lax.rem(z + 8 - i, 8) for i in range(4)], [lax.rem(z + i, 8) for i in range(4)]
+    mine = [jnp.where(core == 0, b, a) for b, a in zip(below, above)]
+    theirs = [jnp.where(core == 0, a, b) for b, a in zip(below, above)]
+    pieces = [(0, 0, z), (1, 0, mine[1]), (2, 0, theirs[1]), (3, 0, lax.rem(z + 4, 8))]
+    pieces += [(4, 0, mine[2]), (4, depth, mine[3]), (5, 0, theirs[2]), (5, depth, theirs[3])]
     half = own_ref.shape[0] // 2
     parts = ((own_ref, 0), (own_ref, half), (low_ref, 0), (high_ref, 0))
-    for i, place in enumerate(pieces):
-        copies[i].wait()
+    for n, (i, offset, place) in enumerate(pieces):
+        if offset == 0:
+            copies[i].wait()
+        weight = weights[i][offset : offset + depth, :]
         columns = pl.ds(pl.multiple_of(place * depth, LANES), depth)
         for j, (cot_ref, first) in enumerate(parts):
-            term = jnp.dot(cot_ref[first : first + half, columns], weights[i][...], preferred_element_type=F32)
-            if i:
+            term = jnp.dot(cot_ref[first : first + half, columns], weight, preferred_element_type=F32)
+            if n:
                 term = total_ref[j] + term
-            if i < count - 1:
+            if n < len(pieces) - 1:
                 total_ref[j] = term
                 continue
             term = term.astype(BF16).reshape(2, 4, 16, term.shape[1])
@@ -245,30 +256,27 @@
 
 
 def weight_blocks(chip):
-    one, two = along_z(chip, 1), along_z(chip, 2)
-    three, four = along_z(two, 1), along_z(two, 2)
-    return [chip, one, swap(one, "co"), two, swap(two, "co"), three, swap(three, "co"), four]
-
-
-def cotangent_parts(cotangent):
-    copies = spread(cotangent)
-    rows, width = copies.shape[2:]
-    own = exchange(copies.reshape(16, rows, width), ("x", "yq"))
-    low, high = ahead(own[:8], Y, -1), ahead(own[8:], Y, 1)
-    return [part.reshape(-1, width) for part in (own, low, high)]
+    one, four = along_z(chip, 1), along_z(chip, 4)
+    pair = along_z(jnp.concatenate([chip, one], 0), 2)
+    return [chip, one, swap(one, "co"), four, pair, swap(pair, "co")]
 
 
 def local(query_branch, key_branch, value_branch, cotangent, out_weight, filters):
     query, keys, values = query_branch[0], key_branch[0], value_branch[0]
     tokens, width = query.shape
     chip = in_order(out_weight, swap(out_weight, "co"), "co").reshape(2 * out_weight.shape[0], width)
-    parts = cotangent_parts(cotangent[0])
-
-    keys, values, chip = lax.optimization_barrier((keys, values, chip))
+    weights = weight_blocks(chip)
+
+    copies = spread(cotangent[0])
+    rows, columns = copies.shape[2:]
+    own = exchange(copies.reshape(16, rows, columns), ("x", "yq"))
+    own, weights[2], weights[3] = lax.optimization_barrier((own, weights[2], weights[3]))
+    low, high = ahead(own[:8], Y, -1), ahead(own[8:], Y, 1)
+    parts = [part.reshape(-1, columns) for part in (own, low, high)]
+
+    keys, values, own = lax.optimization_barrier((keys, values, own))
     mixed = (keys.astype(F32) * values.astype(F32)).astype(BF16)
     conv, turned = convolve(filters, from_behind(mixed, 1), mixed)
-    weights = weight_blocks(chip)
-
     parts, conv, turned = lax.optimization_barrier((parts, conv, turned))
     terms = exchange(partial_products(parts, weights), "x")
     query_grad, conv_grad, lags = branch_gradients(terms, conv, query, turned)

time: 130 us -> 119 us (0.915)
  waiting for transfers between devices: 20.9 us -> 9.65 us
  Pallas kernels: 12.9 us -> 16 us
  blocking collectives: 22.6 us -> 20.6 us
    all_to_all x2, waiting for transfers between devices: 18 us -> 4.37 us  [exchange(): return lax.all_to_all(copies, axes, split_axis=0, concat_axis=0)]
    ppermute x4 -> x3, starting transfers between devices: 28.7 us -> 22.4 us  [along_z(): return lax.ppermute(block, Z + ('co',), route)]
    ppermute x2, starting transfers between devices: 6.23 us -> 11 us  [from_behind(): return lax.ppermute(block, CONTEXT, route)]
    ppermute x4 -> x3, waiting for transfers between devices: 0.01 us -> 2.49 us  [along_z(): return lax.ppermute(block, Z + ('co',), route)]
    all_to_all x2, starting transfers between devices: 13.7 us -> 16.1 us  [exchange(): return lax.all_to_all(copies, axes, split_axis=0, concat_axis=0)]
    ppermute x4 -> x3, starting transfers between devices: 11.8 us -> 9.52 us  [swap(): return lax.ppermute(block, axis, [(0, 1), (1, 0)])]
    pallas_call x1, Pallas kernels: 2.32 us -> 4.47 us  [convolve(): pl.pallas_call(conv_kernel, grid=(width // LANES,), in_specs=[FILTER_BLOC...]
    all_to_all x2, blocking collectives: 22.6 us -> 20.6 us  [exchange(): return lax.all_to_all(copies, axes, split_axis=0, concat_axis=0)]
  transfers between devices with their start and end apart: 14 -> 12, of which waited for: 4 -> 5; matrix products, arithmetic and copies ran while one was open for 1% -> 2% of each run, Pallas kernels for 4% -> 7%
where the time goes in v11:
time: 119 us; the launch traced here: 118 us
  starting transfers between devices  65.8 us (55%)
  blocking collectives  20.6 us (17%)
  Pallas kernels  16 us (13%)
  waiting for transfers between devices  9.65 us (8%)
  local copies, waits for them, and re-layouts  3.01 us (3%)
  other arithmetic  1.62 us (1%)
    ppermute x3, starting transfers between devices, along_z(): return lax.ppermute(block, Z + ('co',), route)  22.4 us
    all_to_all x2, blocking collectives, exchange(): return lax.all_to_all(copies, axes, split_axis=0, concat_axis=0)  20.6 us
    all_to_all x2, starting transfers between devices, exchange(): return lax.all_to_all(copies, axes, split_axis=0, concat_axis=0)  16.1 us
    ppermute x2, starting transfers between devices, from_behind(): return lax.ppermute(block, CONTEXT, route)  11 us
    ppermute x3, starting transfers between devices, swap(): return lax.ppermute(block, axis, [(0, 1), (1, 0)])  9.52 us
    ppermute x2, starting transfers between devices, ahead(): lax.ppermute(block, axes, [((i + distance) % n, i) for i in range(n)])  6.78 us
    pallas_call x1, Pallas kernels, convolve(): pl.pallas_call(conv_kernel, grid=(width // LANES,), in_specs=[FILTER_BLOC...  4.47 us
    all_to_all x2, waiting for transfers between devices, exchange(): return lax.all_to_all(copies, axes, split_axis=0, concat_axis=0)  4.37 us
  transfers between devices with their start and end apart: 12, of which 5 were waited for; matrix products, arithmetic and copies ran while one was open for 2% of the time, Pallas kernels for 7%

profile of v11, /device:TPU:1, one launch (start us, length us, event | category | flops | bytes accessed | tf_op | source)
XLA Modules:
  0.0 117.6 jit_solution(15832627803896052493)
XLA Ops:
  1.6 1.6 %spread.1 = bf16[4,4,16,2048]{3,2,1,0:T(8,128)(2,1)} custom-call(bf16[16,8192]{1,0:T(8,128)(2,1)S(1)} %bitcast.32), custom_call_target="tpu_custom_call" | custom-call | tf_op jit(solution)/shard_map/spread/pallas_call | solution.py:159
  3.2 10.3 %all-to-all-start = ((bf16[16,16,2048]{2,1,0:T(8,128)(2,1)}), bf16[16,16,2048]{2,1,0:T(8,128)(2,1)S(1)}, u32[]{:S(2)}, u32[]{:S(2)}) async-start(bf16[16,16,2048]{2,1,0:T(8,128)(2,1)} %bitcast.4), calls=%async_computation | async-start | bytes 2097152 | tf_op jit(solution)/shard_map/all_to_all | solution.py:243
  13.5 2.9 %collective-permute-start = (bf16[128,512]{1,0:T(8,128)(2,1)S(1)}, bf16[128,512]{1,0:T(8,128)(2,1)S(1)}, u32[]{:S(2)}, u32[]{:S(2)}) collective-permute-start(bf16[128,512]{1,0:T(8,128)(2,1)S(1)} %copy-done.9), channel_id=1, source_target_pairs={{0,8},{8,0},{1,9},{9,1},{2,10},{10,2},{3,11},{11,3},{4,12},{12,4},... | collective-permute-start | bytes 393224 | tf_op jit(solution)/shard_map/ppermute | solution.py:24
  17.4 10.7 %collective-permute-start.1 = (bf16[256,512]{1,0:T(8,128)(2,1)S(1)}, bf16[256,512]{1,0:T(8,128)(2,1)S(1)}, u32[]{:S(2)}, u32[]{:S(2)}) collective-permute-start(bf16[256,512]{1,0:T(8,128)(2,1)S(1)} %bitcast.21), channel_id=1, source_target_pairs={{0,16},{16,32},{32,48},{48,256},{256,272},{272,288},{288,304},{304... | collective-permute-start | bytes 786440 | tf_op jit(solution)/shard_map/ppermute | solution.py:255
  28.1 1.9 %collective-permute-start.3 = (bf16[256,512]{1,0:T(8,128)(2,1)S(1)}, bf16[256,512]{1,0:T(8,128)(2,1)S(1)}, u32[]{:S(2)}, u32[]{:S(2)}) collective-permute-start(bf16[256,512]{1,0:T(8,128)(2,1)S(1)} %bitcast.22), channel_id=1, source_target_pairs={{0,256},{16,272},{32,288},{48,304},{256,0},{272,16},{288,32},{304,... | collective-permute-start | bytes 786440 | tf_op jit(solution)/shard_map/ppermute | solution.py:255
  30.0 1.4 %collective-permute-done.1.refs_1_ = bf16[256,512]{1,0:T(8,128)(2,1)S(1)} collective-permute-done((bf16[256,512]{1,0:T(8,128)(2,1)S(1)}, bf16[256,512]{1,0:T(8,128)(2,1)S(1)}, u32[]{:S(2)}, u32[]{:S(2)}) %collective-permute-start.1) | collective-permute-done | bytes 262176 | tf_op jit(solution)/shard_map/ppermute | solution.py:255
  31.4 4.7 %collective-permute-start.2 = (bf16[256,512]{1,0:T(8,128)(2,1)S(1)}, bf16[256,512]{1,0:T(8,128)(2,1)S(1)}, u32[]{:S(2)}, u32[]{:S(2)}) collective-permute-start(bf16[256,512]{1,0:T(8,128)(2,1)S(1)} %collective-permute-done.1.refs_1_), channel_id=1, source_target_pairs={{0,8},{8,0},{1,9},{9,1},{2,10},{10,2},{3,11},{11,3},{4,12},{12,4},... | collective-permute-start | bytes 786440 | tf_op jit(solution)/shard_map/ppermute | solution.py:24
  37.0 9.8 %collective-permute-start.7 = (bf16[512,512]{1,0:T(8,128)(2,1)}, bf16[512,512]{1,0:T(8,128)(2,1)S(1)}, u32[]{:S(2)}, u32[]{:S(2)}) collective-permute-start(bf16[512,512]{1,0:T(8,128)(2,1)} %pad_maximum_fusion), channel_id=1, source_target_pairs={{0,32},{16,48},{32,256},{48,272},{256,288},{272,304},{288,0},{304,... | collective-permute-start | bytes 1572872 | tf_op jit(solution)/shard_map/ppermute | solution.py:255
  46.9 1.1 fusion
  48.0 4.9 %collective-permute-start.5 = (bf16[8,16,2048]{2,1,0:T(8,128)(2,1)}, bf16[8,16,2048]{2,1,0:T(8,128)(2,1)S(1)}, u32[]{:S(2)}, u32[]{:S(2)}) collective-permute-start(bf16[8,16,2048]{2,1,0:T(8,128)(2,1)} %get-tuple-element.42), channel_id=1, source_target_pairs={{1,0},{2,1},{3,2},{4,3},{5,4},{6,5},{7,6},{0,7},{9,8},{10,9},{11,1... | collective-permute-start | bytes 1572872 | tf_op jit(solution)/shard_map/ppermute | solution.py:248
  52.8 1.9 %collective-permute-start.4 = (bf16[8,16,2048]{2,1,0:T(8,128)(2,1)}, bf16[8,16,2048]{2,1,0:T(8,128)(2,1)S(1)}, u32[]{:S(2)}, u32[]{:S(2)}) collective-permute-start(bf16[8,16,2048]{2,1,0:T(8,128)(2,1)} %get-tuple-element.43), channel_id=1, source_target_pairs={{7,0},{0,1},{1,2},{2,3},{3,4},{4,5},{5,6},{6,7},{15,8},{8,9},{9,10... | collective-permute-start | bytes 1572872 | tf_op jit(solution)/shard_map/ppermute | solution.py:248
  54.8 1.1 collective-permute-done.7.refs_4_
  55.9 1.9 %collective-permute-start.8 = (bf16[512,512]{1,0:T(8,128)(2,1)S(1)}, bf16[512,512]{1,0:T(8,128)(2,1)}, u32[]{:S(2)}, u32[]{:S(2)}) collective-permute-start(bf16[512,512]{1,0:T(8,128)(2,1)S(1)} %collective-permute-done.7.refs_4_), channel_id=1, source_target_pairs={{0,8},{8,0},{1,9},{9,1},{2,10},{10,2},{3,11},{11,3},{4,12},{12,4},... | collective-permute-start | bytes 1572872 | tf_op jit(solution)/shard_map/ppermute | solution.py:24
  57.9 7.2 %collective-permute-start.6 = (bf16[128,512]{1,0:T(8,128)(2,1)S(1)}, bf16[128,512]{1,0:T(8,128)(2,1)}, u32[]{:S(2)}, u32[]{:S(2)}) collective-permute-start(bf16[128,512]{1,0:T(8,128)(2,1)S(1)} %multiply_convert_fusion.mixed_ref), channel_id=1, source_target_pairs={{0,8},{8,16},{16,24},{24,32},{32,40},{40,48},{48,56},{56,64},{64,7... | collective-permute-start | bytes 393224 | tf_op jit(solution)/shard_map/ppermute | solution.py:35
  65.2 1.8 %collective-permute-done.6.before_ref = bf16[128,512]{1,0:T(8,128)(2,1)} collective-permute-done((bf16[128,512]{1,0:T(8,128)(2,1)S(1)}, bf16[128,512]{1,0:T(8,128)(2,1)}, u32[]{:S(2)}, u32[]{:S(2)}) %collective-permute-start.6) | collective-permute-done | bytes 131104 | tf_op jit(solution)/shard_map/ppermute | solution.py:35
  67.0 4.5 %conv.1 = (f32[128,512]{1,0:T(8,128)S(1)}, bf16[256,512]{1,0:T(8,128)(2,1)S(1)}) custom-call(bf16[32,128]{1,0:T(8,128)(2,1)S(1)} %copy-done.8, bf16[128,512]{1,0:T(8,128)(2,1)} %collective-permute-done.6.before_ref, bf16[128,512]{1,0:T(8,128)(2,1)S(1)} %multiply_convert_fusion.mixed_ref), custom_call_target="tpu_custom_call" | custom-call | tf_op jit(solution)/shard_map/conv/pallas_call | solution.py:182
  72.5 2.3 %product.1 = bf16[4,4,2,16,512]{4,3,2,1,0:T(8,128)(2,1)S(1)} custom-call(s32[3]{0:T(128)S(1)} %pad_add_fusion.place_ref, bf16[256,2048]{1,0:T(8,128)(2,1)S(1)} %bitcast.20, bf16[128,2048]{1,0:T(8,128)(2,1)S(1)} %bitcast.27, bf16[128,2048]{1,0:T(8,128)(2,1)S(1)} %bitcast.26, bf16[256,512]{1,0:T(8,128)(2,1)S(1)} %bitcast.24, ...), custom_call_target="tpu_custom_call" | custom-call | tf_op jit(solution)/shard_map/product/pallas_call | solution.py:226
  74.8 12.9 %all_to_all.20.terms_ref = bf16[4,128,512]{2,1,0:T(8,128)(2,1)S(1)} all-to-all(bf16[4,128,512]{2,1,0:T(8,128)(2,1)S(1)} %bitcast.25), channel_id=1, replica_groups=mesh['zh'=2,'x'=4,'zl'=4,'co'=2,'yq'=4,'yp'=2] {'x'}, dimensions={0} | all-to-all | bytes 1048576 | tf_op jit(solution)/shard_map/all_to_all | solution.py:243
  87.7 3.6 %branch.1 = (bf16[128,512]{1,0:T(8,128)(2,1)}, bf16[128,512]{1,0:T(8,128)(2,1)S(1)}, f32[8,32,128]{2,1,0:T(8,128)S(1)}) custom-call(bf16[4,128,512]{2,1,0:T(8,128)(2,1)S(1)} %all_to_all.20.terms_ref, f32[128,512]{1,0:T(8,128)S(1)} %get-tuple-element.33.conv_ref, bf16[128,512]{1,0:T(8,128)(2,1)S(1)} %bitcast.33, bf16[256,512]{1,0:T(8,128)(2,1)S(1)} %get-tuple-element.34.turned_ref), custom_call_target="tpu_custom_call" | custom-call | tf_op jit(solution)/shard_map/branch/pallas_call | solution.py:210
  91.3 3.7 %collective-permute-start.9 = (bf16[128,512]{1,0:T(8,128)(2,1)S(1)}, bf16[128,512]{1,0:T(8,128)(2,1)S(1)}, u32[]{:S(2)}, u32[]{:S(2)}) collective-permute-start(bf16[128,512]{1,0:T(8,128)(2,1)S(1)} %get-tuple-element.36.grad_ref), channel_id=1, source_target_pairs={{8,0},{16,8},{24,16},{32,24},{40,32},{48,40},{56,48},{64,56},{72,6... | collective-permute-start | bytes 393224 | tf_op jit(solution)/shard_map/ppermute | solution.py:35
  95.1 7.6 %all_to_all.21.parts_ref = f32[8,32,128]{2,1,0:T(8,128)S(1)} all-to-all(f32[8,32,128]{2,1,0:T(8,128)S(1)} %get-tuple-element.37), channel_id=1, replica_groups=mesh['zh'=2,'x'=4,'zl'=4,'co'=2,'yq'=4,'yp'=2] {'x','co'}, dimensions={0} | all-to-all | bytes 262144 | tf_op jit(solution)/shard_map/all_to_all | solution.py:243
  103.4 5.8 %all-to-all-start.3 = ((f32[8,32,128]{2,1,0:T(8,128)}), f32[8,32,128]{2,1,0:T(8,128)S(1)}, u32[]{:S(2)}, u32[]{:S(2)}) async-start(f32[8,32,128]{2,1,0:T(8,128)} %sums.1), calls=%async_computation.3 | async-start | bytes 262144 | tf_op jit(solution)/shard_map/all_to_all | solution.py:243
  109.1 3.5 %mixed_grad.1 = (bf16[128,512]{1,0:T(8,128)(2,1)}, bf16[128,512]{1,0:T(8,128)(2,1)}) custom-call(bf16[32,128]{1,0:T(8,128)(2,1)S(1)} %copy-done.8, bf16[128,512]{1,0:T(8,128)(2,1)S(1)} %get-tuple-element.36.grad_ref, bf16[128,512]{1,0:T(8,128)(2,1)S(1)} %collective-permute-done.9.after_ref, bf16[128,512]{1,0:T(8,128)(2,1)S(1)} %bitcast.31, ...), custom_call_target="tpu_custom_call" | custom-call | tf_op jit(solution)/shard_map/mixed_grad/pallas_call | solution.py:196
  112.6 4.4 %all-to-all-done.3 = f32[8,32,128]{2,1,0:T(8,128)S(1)} async-done(((f32[8,32,128]{2,1,0:T(8,128)}), f32[8,32,128]{2,1,0:T(8,128)S(1)}, u32[]{:S(2)}, u32[]{:S(2)}) %all-to-all-start.3) | async-done | bytes 131104 | tf_op jit(solution)/shard_map/all_to_all | solution.py:243
  (36 shorter events, 5.2 us)
Async XLA Ops:
  0.6 1.0 copy-start.2
  3.2 10.4 %copy-start.9 = (bf16[128,512]{1,0:T(8,128)(2,1)S(1)}, bf16[128,512]{1,0:T(8,128)(2,1)}, u32[]{:S(2)}) copy-start(bf16[128,512]{1,0:T(8,128)(2,1)} %param.10) | copy-start | bytes 393220
  3.2 43.7 %all-to-all-start = ((bf16[16,16,2048]{2,1,0:T(8,128)(2,1)}), bf16[16,16,2048]{2,1,0:T(8,128)(2,1)S(1)}, u32[]{:S(2)}, u32[]{:S(2)}) async-start(bf16[16,16,2048]{2,1,0:T(8,128)(2,1)} %bitcast.4), calls=%async_computation | async-start | bytes 2097152 | tf_op jit(solution)/shard_map/all_to_all | solution.py:243
  13.5 3.8 %collective-permute-start = (bf16[128,512]{1,0:T(8,128)(2,1)S(1)}, bf16[128,512]{1,0:T(8,128)(2,1)S(1)}, u32[]{:S(2)}, u32[]{:S(2)}) collective-permute-start(bf16[128,512]{1,0:T(8,128)(2,1)S(1)} %copy-done.9), channel_id=1, source_target_pairs={{0,8},{8,0},{1,9},{9,1},{2,10},{10,2},{3,11},{11,3},{4,12},{12,4},... | collective-permute-start | bytes 393224 | tf_op jit(solution)/shard_map/ppermute | solution.py:24
  17.4 14.0 %collective-permute-start.1 = (bf16[256,512]{1,0:T(8,128)(2,1)S(1)}, bf16[256,512]{1,0:T(8,128)(2,1)S(1)}, u32[]{:S(2)}, u32[]{:S(2)}) collective-permute-start(bf16[256,512]{1,0:T(8,128)(2,1)S(1)} %bitcast.21), channel_id=1, source_target_pairs={{0,16},{16,32},{32,48},{48,256},{256,272},{272,288},{288,304},{304... | collective-permute-start | bytes 786440 | tf_op jit(solution)/shard_map/ppermute | solution.py:255
  28.1 18.7 %collective-permute-start.3 = (bf16[256,512]{1,0:T(8,128)(2,1)S(1)}, bf16[256,512]{1,0:T(8,128)(2,1)S(1)}, u32[]{:S(2)}, u32[]{:S(2)}) collective-permute-start(bf16[256,512]{1,0:T(8,128)(2,1)S(1)} %bitcast.22), channel_id=1, source_target_pairs={{0,256},{16,272},{32,288},{48,304},{256,0},{272,16},{288,32},{304,... | collective-permute-start | bytes 786440 | tf_op jit(solution)/shard_map/ppermute | solution.py:255
  31.4 15.4 %collective-permute-start.2 = (bf16[256,512]{1,0:T(8,128)(2,1)S(1)}, bf16[256,512]{1,0:T(8,128)(2,1)S(1)}, u32[]{:S(2)}, u32[]{:S(2)}) collective-permute-start(bf16[256,512]{1,0:T(8,128)(2,1)S(1)} %collective-permute-done.1.refs_1_), channel_id=1, source_target_pairs={{0,8},{8,0},{1,9},{9,1},{2,10},{10,2},{3,11},{11,3},{4,12},{12,4},... | collective-permute-start | bytes 786440 | tf_op jit(solution)/shard_map/ppermute | solution.py:24
  37.0 20.8 %copy-start = (bf16[1,128,512]{2,1,0:T(8,128)(2,1)S(1)}, bf16[1,128,512]{2,1,0:T(8,128)(2,1)}, u32[]{:S(2)}) copy-start(bf16[1,128,512]{2,1,0:T(8,128)(2,1)} %param.8) | copy-start | bytes 393220
  37.0 20.8 %copy-start.1 = (bf16[1,128,512]{2,1,0:T(8,128)(2,1)S(1)}, bf16[1,128,512]{2,1,0:T(8,128)(2,1)}, u32[]{:S(2)}) copy-start(bf16[1,128,512]{2,1,0:T(8,128)(2,1)} %param.7) | copy-start | bytes 393220
  37.0 18.9 %collective-permute-start.7 = (bf16[512,512]{1,0:T(8,128)(2,1)}, bf16[512,512]{1,0:T(8,128)(2,1)S(1)}, u32[]{:S(2)}, u32[]{:S(2)}) collective-permute-start(bf16[512,512]{1,0:T(8,128)(2,1)} %pad_maximum_fusion), channel_id=1, source_target_pairs={{0,32},{16,48},{32,256},{48,272},{256,288},{272,304},{288,0},{304,... | collective-permute-start | bytes 1572872 | tf_op jit(solution)/shard_map/ppermute | solution.py:255
  46.8 1.1 copy-start.3
  46.9 1.1 copy-start.5
  48.0 23.6 %collective-permute-start.5 = (bf16[8,16,2048]{2,1,0:T(8,128)(2,1)}, bf16[8,16,2048]{2,1,0:T(8,128)(2,1)S(1)}, u32[]{:S(2)}, u32[]{:S(2)}) collective-permute-start(bf16[8,16,2048]{2,1,0:T(8,128)(2,1)} %get-tuple-element.42), channel_id=1, source_target_pairs={{1,0},{2,1},{3,2},{4,3},{5,4},{6,5},{7,6},{0,7},{9,8},{10,9},{11,1... | collective-permute-start | bytes 1572872 | tf_op jit(solution)/shard_map/ppermute | solution.py:248
  52.8 18.7 %collective-permute-start.4 = (bf16[8,16,2048]{2,1,0:T(8,128)(2,1)}, bf16[8,16,2048]{2,1,0:T(8,128)(2,1)S(1)}, u32[]{:S(2)}, u32[]{:S(2)}) collective-permute-start(bf16[8,16,2048]{2,1,0:T(8,128)(2,1)} %get-tuple-element.43), channel_id=1, source_target_pairs={{7,0},{0,1},{1,2},{2,3},{3,4},{4,5},{5,6},{6,7},{15,8},{8,9},{9,10... | collective-permute-start | bytes 1572872 | tf_op jit(solution)/shard_map/ppermute | solution.py:248
  55.9 15.7 %collective-permute-start.8 = (bf16[512,512]{1,0:T(8,128)(2,1)S(1)}, bf16[512,512]{1,0:T(8,128)(2,1)}, u32[]{:S(2)}, u32[]{:S(2)}) collective-permute-start(bf16[512,512]{1,0:T(8,128)(2,1)S(1)} %collective-permute-done.7.refs_4_), channel_id=1, source_target_pairs={{0,8},{8,0},{1,9},{9,1},{2,10},{10,2},{3,11},{11,3},{4,12},{12,4},... | collective-permute-start | bytes 1572872 | tf_op jit(solution)/shard_map/ppermute | solution.py:24
  57.9 9.2 %collective-permute-start.6 = (bf16[128,512]{1,0:T(8,128)(2,1)S(1)}, bf16[128,512]{1,0:T(8,128)(2,1)}, u32[]{:S(2)}, u32[]{:S(2)}) collective-permute-start(bf16[128,512]{1,0:T(8,128)(2,1)S(1)} %multiply_convert_fusion.mixed_ref), channel_id=1, source_target_pairs={{0,8},{8,16},{16,24},{24,32},{32,40},{40,48},{48,56},{56,64},{64,7... | collective-permute-start | bytes 393224 | tf_op jit(solution)/shard_map/ppermute | solution.py:35
  65.1 1.9 %copy-start.8 = (bf16[32,128]{1,0:T(8,128)(2,1)S(1)}, bf16[32,128]{1,0:T(8,128)(2,1)}, u32[]{:S(2)}) copy-start(bf16[32,128]{1,0:T(8,128)(2,1)} %filters_ref.3) | copy-start | bytes 24580
  65.1 6.4 %copy-start.4 = (bf16[256,512]{1,0:T(8,128)(2,1)S(1)}, bf16[256,512]{1,0:T(8,128)(2,1)}, u32[]{:S(2)}) copy-start(bf16[256,512]{1,0:T(8,128)(2,1)} %copy-done.3) | copy-start | bytes 786436
  71.6 1.0 copy-start.6
  74.8 12.9 %copy-start.7 = (bf16[1,128,512]{2,1,0:T(8,128)(2,1)S(1)}, bf16[1,128,512]{2,1,0:T(8,128)(2,1)}, u32[]{:S(2)}) copy-start(bf16[1,128,512]{2,1,0:T(8,128)(2,1)} %param.6) | copy-start | bytes 393220
  91.3 12.1 %collective-permute-start.9 = (bf16[128,512]{1,0:T(8,128)(2,1)S(1)}, bf16[128,512]{1,0:T(8,128)(2,1)S(1)}, u32[]{:S(2)}, u32[]{:S(2)}) collective-permute-start(bf16[128,512]{1,0:T(8,128)(2,1)S(1)} %get-tuple-element.36.grad_ref), channel_id=1, source_target_pairs={{8,0},{16,8},{24,16},{32,24},{40,32},{48,40},{56,48},{64,56},{72,6... | collective-permute-start | bytes 393224 | tf_op jit(solution)/shard_map/ppermute | solution.py:35
  103.4 13.6 %all-to-all-start.3 = ((f32[8,32,128]{2,1,0:T(8,128)}), f32[8,32,128]{2,1,0:T(8,128)S(1)}, u32[]{:S(2)}, u32[]{:S(2)}) async-start(f32[8,32,128]{2,1,0:T(8,128)} %sums.1), calls=%async_computation.3 | async-start | bytes 262144 | tf_op jit(solution)/shard_map/all_to_all | solution.py:243

commit v12 on v11

--- a/solution.py
+++ b/solution.py
@@ -36,16 +36,10 @@
 
 
 def shifted_rows(row):
-    rows = pltpu.roll(jnp.broadcast_to(row, (8, 2 * TAPS)), 0, 1, stride=1, stride_axis=0)
-    while rows.shape[0] < TAPS:
-        rows = jnp.concatenate([rows, pltpu.roll(rows, rows.shape[0], 1)], 0)
-    return rows
+    return pltpu.roll(jnp.broadcast_to(row, (TAPS, 2 * TAPS)), 0, 1, stride=1, stride_axis=0)
 
 
 def skewed_sum(rows):
-    while rows.shape[0] > 8:
-        half = rows.shape[0] // 2
-        rows = rows[:half] + pltpu.roll(rows[half:], half, 1)
     return jnp.sum(pltpu.roll(rows, 1, 1, stride=1, stride_axis=0), axis=0, keepdims=True)
 
 
@@ -276,9 +270,9 @@
 
     keys, values, own = lax.optimization_barrier((keys, values, own))
     mixed = (keys.astype(F32) * values.astype(F32)).astype(BF16)
-    conv, turned = convolve(filters, from_behind(mixed, 1), mixed)
-    parts, conv, turned = lax.optimization_barrier((parts, conv, turned))
+    parts, before = lax.optimization_barrier((parts, from_behind(mixed, 1)))
     terms = exchange(partial_products(parts, weights), "x")
+    conv, turned = convolve(filters, before, mixed)
     query_grad, conv_grad, lags = branch_gradients(terms, conv, query, turned)
     lags = summed_copies(exchange(lags, ("x", "co")))
     after = from_behind(conv_grad, -1)

time: 119 us -> 116 us (0.975)
  blocking collectives: 20.6 us -> 7.62 us
  waiting for transfers between devices: 9.65 us -> 16.5 us
  starting transfers between devices: 65.8 us -> 69.7 us
  Pallas kernels: 16 us -> 14 us
    all_to_all x2 -> x1, blocking collectives: 20.6 us -> 7.62 us  [exchange(): return lax.all_to_all(copies, axes, split_axis=0, concat_axis=0)]
    all_to_all x2 -> x3, waiting for transfers between devices: 4.37 us -> 11.2 us  [exchange(): return lax.all_to_all(copies, axes, split_axis=0, concat_axis=0)]
    all_to_all x2 -> x3, starting transfers between devices: 16.1 us -> 20.5 us  [exchange(): return lax.all_to_all(copies, axes, split_axis=0, concat_axis=0)]
    pallas_call x1, Pallas kernels: 4.47 us -> 3.26 us  [convolve(): pl.pallas_call(conv_kernel, grid=(width // LANES,), in_specs=[FILTER_BLOC...]
  transfers between devices with their start and end apart: 12 -> 13, of which waited for: 5 -> 6; matrix products, arithmetic and copies ran while one was open for 2% -> 2% of each run, Pallas kernels for 7% -> 6%
where the time goes in v12:
time: 116 us; the launch traced here: 114 us
  starting transfers between devices  69.7 us (60%)
  waiting for transfers between devices  16.5 us (14%)
  Pallas kernels  14 us (12%)
  blocking collectives  7.62 us (7%)
  local copies, waits for them, and re-layouts  3.94 us (3%)
  other arithmetic  1.63 us (1%)
    ppermute x3, starting transfers between devices, along_z(): return lax.ppermute(block, Z + ('co',), route)  22.4 us
    all_to_all x3, starting transfers between devices, exchange(): return lax.all_to_all(copies, axes, split_axis=0, concat_axis=0)  20.5 us
    all_to_all x3, waiting for transfers between devices, exchange(): return lax.all_to_all(copies, axes, split_axis=0, concat_axis=0)  11.2 us
    ppermute x2, starting transfers between devices, from_behind(): return lax.ppermute(block, CONTEXT, route)  10.4 us
    ppermute x3, starting transfers between devices, swap(): return lax.ppermute(block, axis, [(0, 1), (1, 0)])  9.52 us
    all_to_all x1, blocking collectives, exchange(): return lax.all_to_all(copies, axes, split_axis=0, concat_axis=0)  7.62 us
    ppermute x2, starting transfers between devices, ahead(): lax.ppermute(block, axes, [((i + distance) % n, i) for i in range(n)])  6.78 us
    pallas_call x1, Pallas kernels, convolve(): pl.pallas_call(conv_kernel, grid=(width // LANES,), in_specs=[FILTER_BLOC...  3.26 us
  transfers between devices with their start and end apart: 13, of which 6 were waited for; matrix products, arithmetic and copies ran while one was open for 2% of the time, Pallas kernels for 6%

profile of v12, /device:TPU:1, one launch (start us, length us, event | category | flops | bytes accessed | tf_op | source)
XLA Modules:
  0.0 114.2 jit_solution(9239684677656384499)
XLA Ops:
  1.6 1.6 %spread.1 = bf16[4,4,16,2048]{3,2,1,0:T(8,128)(2,1)} custom-call(bf16[16,8192]{1,0:T(8,128)(2,1)S(1)} %bitcast.31), custom_call_target="tpu_custom_call" | custom-call | tf_op jit(solution)/shard_map/spread/pallas_call | solution.py:153
  3.1 10.3 %all-to-all-start = ((bf16[16,16,2048]{2,1,0:T(8,128)(2,1)}), bf16[16,16,2048]{2,1,0:T(8,128)(2,1)S(1)}, u32[]{:S(2)}, u32[]{:S(2)}) async-start(bf16[16,16,2048]{2,1,0:T(8,128)(2,1)} %bitcast.4), calls=%async_computation | async-start | bytes 2097152 | tf_op jit(solution)/shard_map/all_to_all | solution.py:237
  13.5 2.9 %collective-permute-start = (bf16[128,512]{1,0:T(8,128)(2,1)S(1)}, bf16[128,512]{1,0:T(8,128)(2,1)S(1)}, u32[]{:S(2)}, u32[]{:S(2)}) collective-permute-start(bf16[128,512]{1,0:T(8,128)(2,1)S(1)} %copy-done.9), channel_id=1, source_target_pairs={{0,8},{8,0},{1,9},{9,1},{2,10},{10,2},{3,11},{11,3},{4,12},{12,4},... | collective-permute-start | bytes 393224 | tf_op jit(solution)/shard_map/ppermute | solution.py:24
  17.4 10.7 %collective-permute-start.1 = (bf16[256,512]{1,0:T(8,128)(2,1)S(1)}, bf16[256,512]{1,0:T(8,128)(2,1)S(1)}, u32[]{:S(2)}, u32[]{:S(2)}) collective-permute-start(bf16[256,512]{1,0:T(8,128)(2,1)S(1)} %bitcast.21), channel_id=1, source_target_pairs={{0,16},{16,32},{32,48},{48,256},{256,272},{272,288},{288,304},{304... | collective-permute-start | bytes 786440 | tf_op jit(solution)/shard_map/ppermute | solution.py:249
  28.1 1.9 %collective-permute-start.3 = (bf16[256,512]{1,0:T(8,128)(2,1)S(1)}, bf16[256,512]{1,0:T(8,128)(2,1)S(1)}, u32[]{:S(2)}, u32[]{:S(2)}) collective-permute-start(bf16[256,512]{1,0:T(8,128)(2,1)S(1)} %bitcast.22), channel_id=1, source_target_pairs={{0,256},{16,272},{32,288},{48,304},{256,0},{272,16},{288,32},{304,... | collective-permute-start | bytes 786440 | tf_op jit(solution)/shard_map/ppermute | solution.py:249
  30.0 1.4 %collective-permute-done.1.refs_1_ = bf16[256,512]{1,0:T(8,128)(2,1)S(1)} collective-permute-done((bf16[256,512]{1,0:T(8,128)(2,1)S(1)}, bf16[256,512]{1,0:T(8,128)(2,1)S(1)}, u32[]{:S(2)}, u32[]{:S(2)}) %collective-permute-start.1) | collective-permute-done | bytes 262176 | tf_op jit(solution)/shard_map/ppermute | solution.py:249
  31.4 4.7 %collective-permute-start.2 = (bf16[256,512]{1,0:T(8,128)(2,1)S(1)}, bf16[256,512]{1,0:T(8,128)(2,1)S(1)}, u32[]{:S(2)}, u32[]{:S(2)}) collective-permute-start(bf16[256,512]{1,0:T(8,128)(2,1)S(1)} %collective-permute-done.1.refs_1_), channel_id=1, source_target_pairs={{0,8},{8,0},{1,9},{9,1},{2,10},{10,2},{3,11},{11,3},{4,12},{12,4},... | collective-permute-start | bytes 786440 | tf_op jit(solution)/shard_map/ppermute | solution.py:24
  37.0 9.8 %collective-permute-start.7 = (bf16[512,512]{1,0:T(8,128)(2,1)}, bf16[512,512]{1,0:T(8,128)(2,1)S(1)}, u32[]{:S(2)}, u32[]{:S(2)}) collective-permute-start(bf16[512,512]{1,0:T(8,128)(2,1)} %pad_maximum_fusion), channel_id=1, source_target_pairs={{0,32},{16,48},{32,256},{48,272},{256,288},{272,304},{288,0},{304,... | collective-permute-start | bytes 1572872 | tf_op jit(solution)/shard_map/ppermute | solution.py:249
  47.9 2.3 %collective-permute-start.4 = (bf16[8,16,2048]{2,1,0:T(8,128)(2,1)}, bf16[8,16,2048]{2,1,0:T(8,128)(2,1)S(1)}, u32[]{:S(2)}, u32[]{:S(2)}) collective-permute-start(bf16[8,16,2048]{2,1,0:T(8,128)(2,1)} %get-tuple-element.41), channel_id=1, source_target_pairs={{7,0},{0,1},{1,2},{2,3},{3,4},{4,5},{5,6},{6,7},{15,8},{8,9},{9,10... | collective-permute-start | bytes 1572872 | tf_op jit(solution)/shard_map/ppermute | solution.py:242
  50.2 4.5 %collective-permute-start.5 = (bf16[8,16,2048]{2,1,0:T(8,128)(2,1)}, bf16[8,16,2048]{2,1,0:T(8,128)(2,1)S(1)}, u32[]{:S(2)}, u32[]{:S(2)}) collective-permute-start(bf16[8,16,2048]{2,1,0:T(8,128)(2,1)} %get-tuple-element.40), channel_id=1, source_target_pairs={{1,0},{2,1},{3,2},{4,3},{5,4},{6,5},{7,6},{0,7},{9,8},{10,9},{11,1... | collective-permute-start | bytes 1572872 | tf_op jit(solution)/shard_map/ppermute | solution.py:242
  54.7 1.1 collective-permute-done.7.refs_4_
  55.9 1.9 %collective-permute-start.8 = (bf16[512,512]{1,0:T(8,128)(2,1)S(1)}, bf16[512,512]{1,0:T(8,128)(2,1)}, u32[]{:S(2)}, u32[]{:S(2)}) collective-permute-start(bf16[512,512]{1,0:T(8,128)(2,1)S(1)} %collective-permute-done.7.refs_4_), channel_id=1, source_target_pairs={{0,8},{8,0},{1,9},{9,1},{2,10},{10,2},{3,11},{11,3},{4,12},{12,4},... | collective-permute-start | bytes 1572872 | tf_op jit(solution)/shard_map/ppermute | solution.py:24
  57.8 7.2 %collective-permute-start.6 = (bf16[128,512]{1,0:T(8,128)(2,1)S(1)}, bf16[128,512]{1,0:T(8,128)(2,1)}, u32[]{:S(2)}, u32[]{:S(2)}) collective-permute-start(bf16[128,512]{1,0:T(8,128)(2,1)S(1)} %multiply_convert_fusion.mixed_ref), channel_id=1, source_target_pairs={{0,8},{8,16},{16,24},{24,32},{32,40},{40,48},{48,56},{56,64},{64,7... | collective-permute-start | bytes 393224 | tf_op jit(solution)/shard_map/ppermute | solution.py:35
  65.2 1.8 %collective-permute-done.6.before_ref = bf16[128,512]{1,0:T(8,128)(2,1)} collective-permute-done((bf16[128,512]{1,0:T(8,128)(2,1)S(1)}, bf16[128,512]{1,0:T(8,128)(2,1)}, u32[]{:S(2)}, u32[]{:S(2)}) %collective-permute-start.6) | collective-permute-done | bytes 131104 | tf_op jit(solution)/shard_map/ppermute | solution.py:35
  68.9 3.1 %product.1 = bf16[4,4,2,16,512]{4,3,2,1,0:T(8,128)(2,1)} custom-call(s32[3]{0:T(128)S(1)} %pad_add_fusion.place_ref, bf16[256,2048]{1,0:T(8,128)(2,1)S(1)} %bitcast.20, bf16[128,2048]{1,0:T(8,128)(2,1)S(1)} %bitcast.25, bf16[128,2048]{1,0:T(8,128)(2,1)S(1)} %bitcast.26, bf16[256,512]{1,0:T(8,128)(2,1)S(1)} %bitcast.24, ...), custom_call_target="tpu_custom_call" | custom-call | tf_op jit(solution)/shard_map/product/pallas_call | solution.py:220
  72.0 4.4 %all-to-all-start.1 = ((bf16[4,128,512]{2,1,0:T(8,128)(2,1)}), bf16[4,128,512]{2,1,0:T(8,128)(2,1)S(1)}, u32[]{:S(2)}, u32[]{:S(2)}) async-start(bf16[4,128,512]{2,1,0:T(8,128)(2,1)} %bitcast.13), calls=%async_computation.1 | async-start | bytes 1048576 | tf_op jit(solution)/shard_map/all_to_all | solution.py:237
  76.5 3.3 %conv.1 = (f32[128,512]{1,0:T(8,128)S(1)}, bf16[256,512]{1,0:T(8,128)(2,1)S(1)}) custom-call(bf16[32,128]{1,0:T(8,128)(2,1)S(1)} %copy-done.8, bf16[128,512]{1,0:T(8,128)(2,1)} %collective-permute-done.6.before_ref, bf16[128,512]{1,0:T(8,128)(2,1)S(1)} %multiply_convert_fusion.mixed_ref), custom_call_target="tpu_custom_call" | custom-call | tf_op jit(solution)/shard_map/conv/pallas_call | solution.py:176
  79.7 5.9 %all-to-all-done.1.terms_ref = bf16[4,128,512]{2,1,0:T(8,128)(2,1)S(1)} async-done(((bf16[4,128,512]{2,1,0:T(8,128)(2,1)}), bf16[4,128,512]{2,1,0:T(8,128)(2,1)S(1)}, u32[]{:S(2)}, u32[]{:S(2)}) %all-to-all-start.1) | async-done | bytes 524320 | tf_op jit(solution)/shard_map/all_to_all | solution.py:237
  85.6 2.9 %branch.1 = (bf16[128,512]{1,0:T(8,128)(2,1)}, bf16[128,512]{1,0:T(8,128)(2,1)S(1)}, f32[8,32,128]{2,1,0:T(8,128)S(1)}) custom-call(bf16[4,128,512]{2,1,0:T(8,128)(2,1)S(1)} %all-to-all-done.1.terms_ref, f32[128,512]{1,0:T(8,128)S(1)} %get-tuple-element.31.conv_ref, bf16[128,512]{1,0:T(8,128)(2,1)S(1)} %bitcast.32, ...), custom_call_target="tpu_custom_call" | custom-call | tf_op jit(solution)/shard_map/branch/pallas_call | solution.py:204
  88.5 3.2 %collective-permute-start.9 = (bf16[128,512]{1,0:T(8,128)(2,1)S(1)}, bf16[128,512]{1,0:T(8,128)(2,1)S(1)}, u32[]{:S(2)}, u32[]{:S(2)}) collective-permute-start(bf16[128,512]{1,0:T(8,128)(2,1)S(1)} %get-tuple-element.34.grad_ref), channel_id=1, source_target_pairs={{8,0},{16,8},{24,16},{32,24},{40,32},{48,40},{56,48},{64,56},{72,6... | collective-permute-start | bytes 393224 | tf_op jit(solution)/shard_map/ppermute | solution.py:35
  91.7 7.6 %all_to_all.20.parts_ref = f32[8,32,128]{2,1,0:T(8,128)S(1)} all-to-all(f32[8,32,128]{2,1,0:T(8,128)S(1)} %get-tuple-element.35), channel_id=1, replica_groups=mesh['zh'=2,'x'=4,'zl'=4,'co'=2,'yq'=4,'yp'=2] {'x','co'}, dimensions={0} | all-to-all | bytes 262144 | tf_op jit(solution)/shard_map/all_to_all | solution.py:237
  100.0 5.7 %all-to-all-start.3 = ((f32[8,32,128]{2,1,0:T(8,128)}), f32[8,32,128]{2,1,0:T(8,128)S(1)}, u32[]{:S(2)}, u32[]{:S(2)}) async-start(f32[8,32,128]{2,1,0:T(8,128)} %sums.1), calls=%async_computation.3 | async-start | bytes 262144 | tf_op jit(solution)/shard_map/all_to_all | solution.py:237
  105.8 2.5 %mixed_grad.1 = (bf16[128,512]{1,0:T(8,128)(2,1)}, bf16[128,512]{1,0:T(8,128)(2,1)}) custom-call(bf16[32,128]{1,0:T(8,128)(2,1)S(1)} %copy-done.8, bf16[128,512]{1,0:T(8,128)(2,1)S(1)} %get-tuple-element.34.grad_ref, bf16[128,512]{1,0:T(8,128)(2,1)S(1)} %collective-permute-done.9.after_ref, bf16[128,512]{1,0:T(8,128)(2,1)S(1)} %bitcast.30, ...), custom_call_target="tpu_custom_call" | custom-call | tf_op jit(solution)/shard_map/mixed_grad/pallas_call | solution.py:190
  108.3 5.3 %all-to-all-done.3 = f32[8,32,128]{2,1,0:T(8,128)S(1)} async-done(((f32[8,32,128]{2,1,0:T(8,128)}), f32[8,32,128]{2,1,0:T(8,128)S(1)}, u32[]{:S(2)}, u32[]{:S(2)}) %all-to-all-start.3) | async-done | bytes 131104 | tf_op jit(solution)/shard_map/all_to_all | solution.py:237
  (37 shorter events, 7.2 us)
Async XLA Ops:
  0.6 1.0 copy-start.2
  3.1 10.4 %copy-start.9 = (bf16[128,512]{1,0:T(8,128)(2,1)S(1)}, bf16[128,512]{1,0:T(8,128)(2,1)}, u32[]{:S(2)}) copy-start(bf16[128,512]{1,0:T(8,128)(2,1)} %param.10) | copy-start | bytes 393220
  3.1 43.7 %all-to-all-start = ((bf16[16,16,2048]{2,1,0:T(8,128)(2,1)}), bf16[16,16,2048]{2,1,0:T(8,128)(2,1)S(1)}, u32[]{:S(2)}, u32[]{:S(2)}) async-start(bf16[16,16,2048]{2,1,0:T(8,128)(2,1)} %bitcast.4), calls=%async_computation | async-start | bytes 2097152 | tf_op jit(solution)/shard_map/all_to_all | solution.py:237
  13.5 3.8 %collective-permute-start = (bf16[128,512]{1,0:T(8,128)(2,1)S(1)}, bf16[128,512]{1,0:T(8,128)(2,1)S(1)}, u32[]{:S(2)}, u32[]{:S(2)}) collective-permute-start(bf16[128,512]{1,0:T(8,128)(2,1)S(1)} %copy-done.9), channel_id=1, source_target_pairs={{0,8},{8,0},{1,9},{9,1},{2,10},{10,2},{3,11},{11,3},{4,12},{12,4},... | collective-permute-start | bytes 393224 | tf_op jit(solution)/shard_map/ppermute | solution.py:24
  17.4 14.0 %collective-permute-start.1 = (bf16[256,512]{1,0:T(8,128)(2,1)S(1)}, bf16[256,512]{1,0:T(8,128)(2,1)S(1)}, u32[]{:S(2)}, u32[]{:S(2)}) collective-permute-start(bf16[256,512]{1,0:T(8,128)(2,1)S(1)} %bitcast.21), channel_id=1, source_target_pairs={{0,16},{16,32},{32,48},{48,256},{256,272},{272,288},{288,304},{304... | collective-permute-start | bytes 786440 | tf_op jit(solution)/shard_map/ppermute | solution.py:249
  28.1 18.7 %collective-permute-start.3 = (bf16[256,512]{1,0:T(8,128)(2,1)S(1)}, bf16[256,512]{1,0:T(8,128)(2,1)S(1)}, u32[]{:S(2)}, u32[]{:S(2)}) collective-permute-start(bf16[256,512]{1,0:T(8,128)(2,1)S(1)} %bitcast.22), channel_id=1, source_target_pairs={{0,256},{16,272},{32,288},{48,304},{256,0},{272,16},{288,32},{304,... | collective-permute-start | bytes 786440 | tf_op jit(solution)/shard_map/ppermute | solution.py:249
  31.4 15.5 %collective-permute-start.2 = (bf16[256,512]{1,0:T(8,128)(2,1)S(1)}, bf16[256,512]{1,0:T(8,128)(2,1)S(1)}, u32[]{:S(2)}, u32[]{:S(2)}) collective-permute-start(bf16[256,512]{1,0:T(8,128)(2,1)S(1)} %collective-permute-done.1.refs_1_), channel_id=1, source_target_pairs={{0,8},{8,0},{1,9},{9,1},{2,10},{10,2},{3,11},{11,3},{4,12},{12,4},... | collective-permute-start | bytes 786440 | tf_op jit(solution)/shard_map/ppermute | solution.py:24
  37.0 20.8 %copy-start = (bf16[1,128,512]{2,1,0:T(8,128)(2,1)S(1)}, bf16[1,128,512]{2,1,0:T(8,128)(2,1)}, u32[]{:S(2)}) copy-start(bf16[1,128,512]{2,1,0:T(8,128)(2,1)} %param.8) | copy-start | bytes 393220
  37.0 20.8 %copy-start.1 = (bf16[1,128,512]{2,1,0:T(8,128)(2,1)S(1)}, bf16[1,128,512]{2,1,0:T(8,128)(2,1)}, u32[]{:S(2)}) copy-start(bf16[1,128,512]{2,1,0:T(8,128)(2,1)} %param.7) | copy-start | bytes 393220
  37.0 18.9 %collective-permute-start.7 = (bf16[512,512]{1,0:T(8,128)(2,1)}, bf16[512,512]{1,0:T(8,128)(2,1)S(1)}, u32[]{:S(2)}, u32[]{:S(2)}) collective-permute-start(bf16[512,512]{1,0:T(8,128)(2,1)} %pad_maximum_fusion), channel_id=1, source_target_pairs={{0,32},{16,48},{32,256},{48,272},{256,288},{272,304},{288,0},{304,... | collective-permute-start | bytes 1572872 | tf_op jit(solution)/shard_map/ppermute | solution.py:249
  46.8 1.1 copy-start.3
  46.8 1.1 copy-start.5
  47.9 19.1 %collective-permute-start.4 = (bf16[8,16,2048]{2,1,0:T(8,128)(2,1)}, bf16[8,16,2048]{2,1,0:T(8,128)(2,1)S(1)}, u32[]{:S(2)}, u32[]{:S(2)}) collective-permute-start(bf16[8,16,2048]{2,1,0:T(8,128)(2,1)} %get-tuple-element.41), channel_id=1, source_target_pairs={{7,0},{0,1},{1,2},{2,3},{3,4},{4,5},{5,6},{6,7},{15,8},{8,9},{9,10... | collective-permute-start | bytes 1572872 | tf_op jit(solution)/shard_map/ppermute | solution.py:242
  50.2 16.8 %collective-permute-start.5 = (bf16[8,16,2048]{2,1,0:T(8,128)(2,1)}, bf16[8,16,2048]{2,1,0:T(8,128)(2,1)S(1)}, u32[]{:S(2)}, u32[]{:S(2)}) collective-permute-start(bf16[8,16,2048]{2,1,0:T(8,128)(2,1)} %get-tuple-element.40), channel_id=1, source_target_pairs={{1,0},{2,1},{3,2},{4,3},{5,4},{6,5},{7,6},{0,7},{9,8},{10,9},{11,1... | collective-permute-start | bytes 1572872 | tf_op jit(solution)/shard_map/ppermute | solution.py:242
  55.9 11.2 %collective-permute-start.8 = (bf16[512,512]{1,0:T(8,128)(2,1)S(1)}, bf16[512,512]{1,0:T(8,128)(2,1)}, u32[]{:S(2)}, u32[]{:S(2)}) collective-permute-start(bf16[512,512]{1,0:T(8,128)(2,1)S(1)} %collective-permute-done.7.refs_4_), channel_id=1, source_target_pairs={{0,8},{8,0},{1,9},{9,1},{2,10},{10,2},{3,11},{11,3},{4,12},{12,4},... | collective-permute-start | bytes 1572872 | tf_op jit(solution)/shard_map/ppermute | solution.py:24
  57.8 9.2 %collective-permute-start.6 = (bf16[128,512]{1,0:T(8,128)(2,1)S(1)}, bf16[128,512]{1,0:T(8,128)(2,1)}, u32[]{:S(2)}, u32[]{:S(2)}) collective-permute-start(bf16[128,512]{1,0:T(8,128)(2,1)S(1)} %multiply_convert_fusion.mixed_ref), channel_id=1, source_target_pairs={{0,8},{8,16},{16,24},{24,32},{32,40},{40,48},{48,56},{56,64},{64,7... | collective-permute-start | bytes 393224 | tf_op jit(solution)/shard_map/ppermute | solution.py:35
  67.0 1.0 copy-start.4
  68.0 0.9 copy-start.6
  72.0 4.4 %copy-start.8 = (bf16[32,128]{1,0:T(8,128)(2,1)S(1)}, bf16[32,128]{1,0:T(8,128)(2,1)}, u32[]{:S(2)}) copy-start(bf16[32,128]{1,0:T(8,128)(2,1)} %filters_ref.3) | copy-start | bytes 24580
  72.0 13.6 %all-to-all-start.1 = ((bf16[4,128,512]{2,1,0:T(8,128)(2,1)}), bf16[4,128,512]{2,1,0:T(8,128)(2,1)S(1)}, u32[]{:S(2)}, u32[]{:S(2)}) async-start(bf16[4,128,512]{2,1,0:T(8,128)(2,1)} %bitcast.13), calls=%async_computation.1 | async-start | bytes 1048576 | tf_op jit(solution)/shard_map/all_to_all | solution.py:237
  76.5 9.1 %copy-start.7 = (bf16[1,128,512]{2,1,0:T(8,128)(2,1)S(1)}, bf16[1,128,512]{2,1,0:T(8,128)(2,1)}, u32[]{:S(2)}) copy-start(bf16[1,128,512]{2,1,0:T(8,128)(2,1)} %param.6) | copy-start | bytes 393220
  88.5 11.5 %collective-permute-start.9 = (bf16[128,512]{1,0:T(8,128)(2,1)S(1)}, bf16[128,512]{1,0:T(8,128)(2,1)S(1)}, u32[]{:S(2)}, u32[]{:S(2)}) collective-permute-start(bf16[128,512]{1,0:T(8,128)(2,1)S(1)} %get-tuple-element.34.grad_ref), channel_id=1, source_target_pairs={{8,0},{16,8},{24,16},{32,24},{40,32},{48,40},{56,48},{64,56},{72,6... | collective-permute-start | bytes 393224 | tf_op jit(solution)/shard_map/ppermute | solution.py:35
  100.0 13.6 %all-to-all-start.3 = ((f32[8,32,128]{2,1,0:T(8,128)}), f32[8,32,128]{2,1,0:T(8,128)S(1)}, u32[]{:S(2)}, u32[]{:S(2)}) async-start(f32[8,32,128]{2,1,0:T(8,128)} %sums.1), calls=%async_computation.3 | async-start | bytes 262144 | tf_op jit(solution)/shard_map/all_to_all | solution.py:237

commit v13 on v12

--- a/solution.py
+++ b/solution.py
@@ -108,12 +108,13 @@
             lag_ref[copy, g : g + 1, :] = sums
 
 
-def product_kernel(place_ref, own_ref, low_ref, high_ref, *refs):
+def product_kernel(place_ref, own_ref, *refs):
     count = (len(refs) - 3) // 2
-    weights_hbm, out_ref, total_ref, weights, sems = refs[:count], refs[count], refs[count + 1], refs[count + 2 : -1], refs[-1]
-    copies = [pltpu.make_async_copy(weights_hbm[i], weights[i], sems.at[i]) for i in range(count)]
+    fetched, out_ref, total_ref, here, sems = refs[:count], refs[count], refs[count + 1], refs[count + 2 : -1], refs[-1]
+    copies = [pltpu.make_async_copy(fetched[i], here[i], sems.at[i]) for i in range(count)]
     for copy in copies:
         copy.start()
+    weights, (low_ref, high_ref) = here[:-2], here[-2:]
     z, core, odd = place_ref[0], place_ref[1], place_ref[2]
     depth = weights[0].shape[0]
     below, above = [lax.rem(z + 8 - i, 8) for i in range(4)], [lax.rem(z + i, 8) for i in range(4)]
@@ -122,13 +123,14 @@
     pieces = [(0, 0, z), (1, 0, mine[1]), (2, 0, theirs[1]), (3, 0, lax.rem(z + 4, 8))]
     pieces += [(4, 0, mine[2]), (4, depth, mine[3]), (5, 0, theirs[2]), (5, depth, theirs[3])]
     half = own_ref.shape[0] // 2
-    parts = ((own_ref, 0), (own_ref, half), (low_ref, 0), (high_ref, 0))
-    for n, (i, offset, place) in enumerate(pieces):
-        if offset == 0:
-            copies[i].wait()
-        weight = weights[i][offset : offset + depth, :]
-        columns = pl.ds(pl.multiple_of(place * depth, LANES), depth)
-        for j, (cot_ref, first) in enumerate(parts):
+    for j, (cot_ref, first) in enumerate(((own_ref, 0), (own_ref, half), (low_ref, 0), (high_ref, 0))):
+        if j >= 2:
+            copies[count - 4 + j].wait()
+        for n, (i, offset, place) in enumerate(pieces):
+            if j == 0 and offset == 0:
+                copies[i].wait()
+            weight = weights[i][offset : offset + depth, :]
+            columns = pl.ds(pl.multiple_of(place * depth, LANES), depth)
             term = jnp.dot(cot_ref[first : first + half, columns], weight, preferred_element_type=F32)
             if n:
                 term = total_ref[j] + term
@@ -220,16 +222,16 @@
     out = pl.pallas_call(
         product_kernel,
         in_specs=[pl.BlockSpec(memory_space=pltpu.SMEM)]
-        + [whole] * 3
-        + [pl.BlockSpec(memory_space=pltpu.HBM)] * len(weights),
+        + [whole]
+        + [pl.BlockSpec(memory_space=pltpu.HBM)] * (len(weights) + 2),
         out_specs=whole,
         out_shape=jax.ShapeDtypeStruct((4, 4, 2, 16, width), BF16),
         scratch_shapes=[pltpu.VMEM((4, TAPS, width), F32)]
-        + [pltpu.VMEM(a.shape, a.dtype) for a in weights]
-        + [pltpu.SemaphoreType.DMA((len(weights),))],
+        + [pltpu.VMEM(a.shape, a.dtype) for a in (*weights, *parts[1:])]
+        + [pltpu.SemaphoreType.DMA((len(weights) + 2,))],
         compiler_params=VMEM,
         name="product",
-    )(place, *parts, *weights)
+    )(place, parts[0], *weights, *parts[1:])
     return out.reshape(4, TAPS, width)
 
 
@@ -249,17 +251,20 @@
     return lax.ppermute(block, Z + ("co",), route)
 
 
-def weight_blocks(chip):
+def weight_blocks(chip, beside):
     one, four = along_z(chip, 1), along_z(chip, 4)
+    one, beside = lax.optimization_barrier((one, beside))
     pair = along_z(jnp.concatenate([chip, one], 0), 2)
-    return [chip, one, swap(one, "co"), four, pair, swap(pair, "co")]
+    return beside, [chip, one, swap(one, "co"), four, pair, swap(pair, "co")]
 
 
 def local(query_branch, key_branch, value_branch, cotangent, out_weight, filters):
     query, keys, values = query_branch[0], key_branch[0], value_branch[0]
     tokens, width = query.shape
     chip = in_order(out_weight, swap(out_weight, "co"), "co").reshape(2 * out_weight.shape[0], width)
-    weights = weight_blocks(chip)
+    keys, values, chip = lax.optimization_barrier((keys, values, chip))
+    mixed = (keys.astype(F32) * values.astype(F32)).astype(BF16)
+    before, weights = weight_blocks(chip, from_behind(mixed, 1))
 
     copies = spread(cotangent[0])
     rows, columns = copies.shape[2:]
@@ -268,9 +273,6 @@
     low, high = ahead(own[:8], Y, -1), ahead(own[8:], Y, 1)
     parts = [part.reshape(-1, columns) for part in (own, low, high)]
 
-    keys, values, own = lax.optimization_barrier((keys, values, own))
-    mixed = (keys.astype(F32) * values.astype(F32)).astype(BF16)
-    parts, before = lax.optimization_barrier((parts, from_behind(mixed, 1)))
     terms = exchange(partial_products(parts, weights), "x")
     conv, turned = convolve(filters, before, mixed)
     query_grad, conv_grad, lags = branch_gradients(terms, conv, query, turned)

time: 116 us -> 135 us (1.16)
  the two profiles are of different devices: /device:TPU:1 before, /device:TPU:24 now
where the time goes in v13:
time: 135 us; the launch traced here: 134 us
  starting transfers between devices  63.9 us (47%)
  waiting for transfers between devices  37.3 us (28%)
  Pallas kernels  13.5 us (10%)
  blocking collectives  13.2 us (10%)
  local copies, waits for them, and re-layouts  4.72 us (3%)
    all_to_all x3, starting transfers between devices, exchange(): return lax.all_to_all(copies, axes, split_axis=0, concat_axis=0)  26.5 us
    ppermute x3, starting transfers between devices, along_z(): return lax.ppermute(block, Z + ('co',), route)  14.7 us
    all_to_all x1, blocking collectives, exchange(): return lax.all_to_all(copies, axes, split_axis=0, concat_axis=0)  13.2 us
    all_to_all x3, waiting for transfers between devices, exchange(): return lax.all_to_all(copies, axes, split_axis=0, concat_axis=0)  12.3 us
    ppermute x2, waiting for transfers between devices, ahead(): lax.ppermute(block, axes, [((i + distance) % n, i) for i in range(n)])  11.9 us
    ppermute x3, waiting for transfers between devices, along_z(): return lax.ppermute(block, Z + ('co',), route)  10.8 us
    ppermute x2, starting transfers between devices, from_behind(): return lax.ppermute(block, CONTEXT, route)  9.73 us
    ppermute x2, starting transfers between devices, ahead(): lax.ppermute(block, axes, [((i + distance) % n, i) for i in range(n)])  7.28 us
  transfers between devices with their start and end apart: 13, of which 9 were waited for; matrix products, arithmetic and copies ran while one was open for 1% of the time, Pallas kernels for 4%

profile of v13, /device:TPU:24, one launch (start us, length us, event | category | flops | bytes accessed | tf_op | source)
XLA Modules:
  0.0 134.3 jit_solution(6046653006038704242)
XLA Ops:
  1.6 1.6 %spread.1 = bf16[4,4,16,2048]{3,2,1,0:T(8,128)(2,1)} custom-call(bf16[16,8192]{1,0:T(8,128)(2,1)S(1)} %bitcast.30), custom_call_target="tpu_custom_call" | custom-call | tf_op jit(solution)/shard_map/spread/pallas_call | solution.py:155
  3.2 9.1 %all-to-all-start = ((bf16[16,16,2048]{2,1,0:T(8,128)(2,1)}), bf16[16,16,2048]{2,1,0:T(8,128)(2,1)S(1)}, u32[]{:S(2)}, u32[]{:S(2)}) async-start(bf16[16,16,2048]{2,1,0:T(8,128)(2,1)} %bitcast.4), calls=%async_computation | async-start | bytes 2097152 | tf_op jit(solution)/shard_map/all_to_all | solution.py:239
  12.3 1.9 %collective-permute-start = (bf16[128,512]{1,0:T(8,128)(2,1)S(1)}, bf16[128,512]{1,0:T(8,128)(2,1)S(1)}, u32[]{:S(2)}, u32[]{:S(2)}) collective-permute-start(bf16[128,512]{1,0:T(8,128)(2,1)S(1)} %copy-done.11), channel_id=1, source_target_pairs={{0,8},{8,0},{1,9},{9,1},{2,10},{10,2},{3,11},{11,3},{4,12},{12,4},... | collective-permute-start | bytes 393224 | tf_op jit(solution)/shard_map/ppermute | solution.py:24
  15.7 4.4 %collective-permute-start.1 = (bf16[256,512]{1,0:T(8,128)(2,1)S(1)}, bf16[256,512]{1,0:T(8,128)(2,1)S(1)}, u32[]{:S(2)}, u32[]{:S(2)}) collective-permute-start(bf16[256,512]{1,0:T(8,128)(2,1)S(1)} %bitcast.21), channel_id=1, source_target_pairs={{0,16},{16,32},{32,48},{48,256},{256,272},{272,288},{288,304},{304... | collective-permute-start | bytes 786440 | tf_op jit(solution)/shard_map/ppermute | solution.py:251
  20.1 8.4 %collective-permute-start.2 = (bf16[128,512]{1,0:T(8,128)(2,1)S(1)}, bf16[128,512]{1,0:T(8,128)(2,1)S(1)}, u32[]{:S(2)}, u32[]{:S(2)}) collective-permute-start(bf16[128,512]{1,0:T(8,128)(2,1)S(1)} %multiply_convert_fusion.mixed_ref), channel_id=1, source_target_pairs={{0,8},{8,16},{16,24},{24,32},{32,40},{40,48},{48,56},{56,64},{64,7... | collective-permute-start | bytes 393224 | tf_op jit(solution)/shard_map/ppermute | solution.py:35
  31.1 2.1 %collective-permute-start.5 = (bf16[512,512]{1,0:T(8,128)(2,1)S(1)}, bf16[512,512]{1,0:T(8,128)(2,1)S(1)}, u32[]{:S(2)}, u32[]{:S(2)}) collective-permute-start(bf16[512,512]{1,0:T(8,128)(2,1)S(1)} %pad_maximum_fusion), channel_id=1, source_target_pairs={{0,32},{16,48},{32,256},{48,272},{256,288},{272,304},{288,0},{304,... | collective-permute-start | bytes 1572872 | tf_op jit(solution)/shard_map/ppermute | solution.py:251
  33.2 8.2 %collective-permute-start.4 = (bf16[256,512]{1,0:T(8,128)(2,1)S(1)}, bf16[256,512]{1,0:T(8,128)(2,1)S(1)}, u32[]{:S(2)}, u32[]{:S(2)}) collective-permute-start(bf16[256,512]{1,0:T(8,128)(2,1)S(1)} %bitcast.23), channel_id=1, source_target_pairs={{0,256},{16,272},{32,288},{48,304},{256,0},{272,16},{288,32},{304,... | collective-permute-start | bytes 786440 | tf_op jit(solution)/shard_map/ppermute | solution.py:251
  41.4 1.9 %collective-permute-start.3 = (bf16[256,512]{1,0:T(8,128)(2,1)S(1)}, bf16[256,512]{1,0:T(8,128)(2,1)S(1)}, u32[]{:S(2)}, u32[]{:S(2)}) collective-permute-start(bf16[256,512]{1,0:T(8,128)(2,1)S(1)} %collective-permute-done.1.refs_1_), channel_id=1, source_target_pairs={{0,8},{8,0},{1,9},{9,1},{2,10},{10,2},{3,11},{11,3},{4,12},{12,4},... | collective-permute-start | bytes 786440 | tf_op jit(solution)/shard_map/ppermute | solution.py:24
  43.4 5.3 %collective-permute-done.5.refs_4_ = bf16[512,512]{1,0:T(8,128)(2,1)S(1)} collective-permute-done((bf16[512,512]{1,0:T(8,128)(2,1)S(1)}, bf16[512,512]{1,0:T(8,128)(2,1)S(1)}, u32[]{:S(2)}, u32[]{:S(2)}) %collective-permute-start.5) | collective-permute-done | bytes 524320 | tf_op jit(solution)/shard_map/ppermute | solution.py:251
  48.7 1.9 %collective-permute-start.6 = (bf16[512,512]{1,0:T(8,128)(2,1)S(1)}, bf16[512,512]{1,0:T(8,128)(2,1)S(1)}, u32[]{:S(2)}, u32[]{:S(2)}) collective-permute-start(bf16[512,512]{1,0:T(8,128)(2,1)S(1)} %collective-permute-done.5.refs_4_), channel_id=1, source_target_pairs={{0,8},{8,0},{1,9},{9,1},{2,10},{10,2},{3,11},{11,3},{4,12},{12,4},... | collective-permute-start | bytes 1572872 | tf_op jit(solution)/shard_map/ppermute | solution.py:24
  50.6 4.6 %collective-permute-done.4.refs_3_ = bf16[256,512]{1,0:T(8,128)(2,1)S(1)} collective-permute-done((bf16[256,512]{1,0:T(8,128)(2,1)S(1)}, bf16[256,512]{1,0:T(8,128)(2,1)S(1)}, u32[]{:S(2)}, u32[]{:S(2)}) %collective-permute-start.4) | collective-permute-done | bytes 262176 | tf_op jit(solution)/shard_map/ppermute | solution.py:251
  56.4 5.4 %collective-permute-start.7 = (bf16[8,16,2048]{2,1,0:T(8,128)(2,1)}, bf16[8,16,2048]{2,1,0:T(8,128)(2,1)S(1)}, u32[]{:S(2)}, u32[]{:S(2)}) collective-permute-start(bf16[8,16,2048]{2,1,0:T(8,128)(2,1)} %get-tuple-element.39), channel_id=1, source_target_pairs={{7,0},{0,1},{1,2},{2,3},{3,4},{4,5},{5,6},{6,7},{15,8},{8,9},{9,10... | collective-permute-start | bytes 1572872 | tf_op jit(solution)/shard_map/ppermute | solution.py:244
  61.8 1.9 %collective-permute-start.8 = (bf16[8,16,2048]{2,1,0:T(8,128)(2,1)}, bf16[8,16,2048]{2,1,0:T(8,128)(2,1)}, u32[]{:S(2)}, u32[]{:S(2)}) collective-permute-start(bf16[8,16,2048]{2,1,0:T(8,128)(2,1)} %get-tuple-element.38), channel_id=1, source_target_pairs={{1,0},{2,1},{3,2},{4,3},{5,4},{6,5},{7,6},{0,7},{9,8},{10,9},{11,1... | collective-permute-start | bytes 1572872 | tf_op jit(solution)/shard_map/ppermute | solution.py:244
  63.8 6.6 %collective-permute-done.7 = bf16[8,16,2048]{2,1,0:T(8,128)(2,1)S(1)} collective-permute-done((bf16[8,16,2048]{2,1,0:T(8,128)(2,1)}, bf16[8,16,2048]{2,1,0:T(8,128)(2,1)S(1)}, u32[]{:S(2)}, u32[]{:S(2)}) %collective-permute-start.7) | collective-permute-done | bytes 524320 | tf_op jit(solution)/shard_map/ppermute | solution.py:244
  70.4 5.3 %collective-permute-done.8 = bf16[8,16,2048]{2,1,0:T(8,128)(2,1)} collective-permute-done((bf16[8,16,2048]{2,1,0:T(8,128)(2,1)}, bf16[8,16,2048]{2,1,0:T(8,128)(2,1)}, u32[]{:S(2)}, u32[]{:S(2)}) %collective-permute-start.8) | collective-permute-done | bytes 524320 | tf_op jit(solution)/shard_map/ppermute | solution.py:244
  77.6 3.5 %product.1 = bf16[4,4,2,16,512]{4,3,2,1,0:T(8,128)(2,1)} custom-call(s32[3]{0:T(128)S(1)} %pad_add_fusion.place_ref, bf16[256,2048]{1,0:T(8,128)(2,1)S(1)} %bitcast.20, bf16[256,512]{1,0:T(8,128)(2,1)S(1)} %bitcast.24, bf16[256,512]{1,0:T(8,128)(2,1)S(1)} %collective-permute-done.1.refs_1_, bf16[256,512]{1,0:T(8,128)(2,1)S(1)} %copy-done.6, ...), custom_call_target="tpu_custom_call" | custom-call | tf_op jit(solution)/shard_map/product/pallas_call | solution.py:222
  81.1 10.2 %all-to-all-start.1 = ((bf16[4,128,512]{2,1,0:T(8,128)(2,1)}), bf16[4,128,512]{2,1,0:T(8,128)(2,1)S(1)}, u32[]{:S(2)}, u32[]{:S(2)}) async-start(bf16[4,128,512]{2,1,0:T(8,128)(2,1)} %bitcast.13), calls=%async_computation.1 | async-start | bytes 1048576 | tf_op jit(solution)/shard_map/all_to_all | solution.py:239
  91.4 2.3 %conv.1 = (f32[128,512]{1,0:T(8,128)S(1)}, bf16[256,512]{1,0:T(8,128)(2,1)S(1)}) custom-call(bf16[32,128]{1,0:T(8,128)(2,1)S(1)} %copy-done.10, bf16[128,512]{1,0:T(8,128)(2,1)S(1)} %copy-done.9, bf16[128,512]{1,0:T(8,128)(2,1)S(1)} %multiply_convert_fusion.mixed_ref), custom_call_target="tpu_custom_call" | custom-call | tf_op jit(solution)/shard_map/conv/pallas_call | solution.py:178
  93.7 5.7 %all-to-all-done.1.terms_ref = bf16[4,128,512]{2,1,0:T(8,128)(2,1)S(1)} async-done(((bf16[4,128,512]{2,1,0:T(8,128)(2,1)}), bf16[4,128,512]{2,1,0:T(8,128)(2,1)S(1)}, u32[]{:S(2)}, u32[]{:S(2)}) %all-to-all-start.1) | async-done | bytes 524320 | tf_op jit(solution)/shard_map/all_to_all | solution.py:239
  99.4 2.9 %branch.1 = (bf16[128,512]{1,0:T(8,128)(2,1)}, bf16[128,512]{1,0:T(8,128)(2,1)S(1)}, f32[8,32,128]{2,1,0:T(8,128)S(1)}) custom-call(bf16[4,128,512]{2,1,0:T(8,128)(2,1)S(1)} %all-to-all-done.1.terms_ref, f32[128,512]{1,0:T(8,128)S(1)} %get-tuple-element.29.conv_ref, bf16[128,512]{1,0:T(8,128)(2,1)S(1)} %bitcast.31, ...), custom_call_target="tpu_custom_call" | custom-call | tf_op jit(solution)/shard_map/branch/pallas_call | solution.py:206
  103.6 13.2 %all_to_all.20.parts_ref = f32[8,32,128]{2,1,0:T(8,128)S(1)} all-to-all(f32[8,32,128]{2,1,0:T(8,128)S(1)} %get-tuple-element.33), channel_id=1, replica_groups=mesh['zh'=2,'x'=4,'zl'=4,'co'=2,'yq'=4,'yp'=2] {'x','co'}, dimensions={0} | all-to-all | bytes 262144 | tf_op jit(solution)/shard_map/all_to_all | solution.py:239
  117.5 7.1 %all-to-all-start.3 = ((f32[8,32,128]{2,1,0:T(8,128)}), f32[8,32,128]{2,1,0:T(8,128)S(1)}, u32[]{:S(2)}, u32[]{:S(2)}) async-start(f32[8,32,128]{2,1,0:T(8,128)} %sums.1), calls=%async_computation.3 | async-start | bytes 262144 | tf_op jit(solution)/shard_map/all_to_all | solution.py:239
  124.6 2.5 %mixed_grad.1 = (bf16[128,512]{1,0:T(8,128)(2,1)}, bf16[128,512]{1,0:T(8,128)(2,1)}) custom-call(bf16[32,128]{1,0:T(8,128)(2,1)S(1)} %copy-done.10, bf16[128,512]{1,0:T(8,128)(2,1)S(1)} %get-tuple-element.32.grad_ref, bf16[128,512]{1,0:T(8,128)(2,1)S(1)} %collective-permute-done.9.after_ref, bf16[128,512]{1,0:T(8,128)(2,1)S(1)} %bitcast.29, ...), custom_call_target="tpu_custom_call" | custom-call | tf_op jit(solution)/shard_map/mixed_grad/pallas_call | solution.py:192
  127.1 6.5 %all-to-all-done.3 = f32[8,32,128]{2,1,0:T(8,128)S(1)} async-done(((f32[8,32,128]{2,1,0:T(8,128)}), f32[8,32,128]{2,1,0:T(8,128)S(1)}, u32[]{:S(2)}, u32[]{:S(2)}) %all-to-all-start.3) | async-done | bytes 131104 | tf_op jit(solution)/shard_map/all_to_all | solution.py:239
  (41 shorter events, 10.6 us)
Async XLA Ops:
  0.6 1.0 copy-start.2
  3.2 9.1 %copy-start.11 = (bf16[128,512]{1,0:T(8,128)(2,1)S(1)}, bf16[128,512]{1,0:T(8,128)(2,1)}, u32[]{:S(2)}) copy-start(bf16[128,512]{1,0:T(8,128)(2,1)} %param.10) | copy-start | bytes 393220
  3.2 52.1 %all-to-all-start = ((bf16[16,16,2048]{2,1,0:T(8,128)(2,1)}), bf16[16,16,2048]{2,1,0:T(8,128)(2,1)S(1)}, u32[]{:S(2)}, u32[]{:S(2)}) async-start(bf16[16,16,2048]{2,1,0:T(8,128)(2,1)} %bitcast.4), calls=%async_computation | async-start | bytes 2097152 | tf_op jit(solution)/shard_map/all_to_all | solution.py:239
  12.3 3.2 %collective-permute-start = (bf16[128,512]{1,0:T(8,128)(2,1)S(1)}, bf16[128,512]{1,0:T(8,128)(2,1)S(1)}, u32[]{:S(2)}, u32[]{:S(2)}) collective-permute-start(bf16[128,512]{1,0:T(8,128)(2,1)S(1)} %copy-done.11), channel_id=1, source_target_pairs={{0,8},{8,0},{1,9},{9,1},{2,10},{10,2},{3,11},{11,3},{4,12},{12,4},... | collective-permute-start | bytes 393224 | tf_op jit(solution)/shard_map/ppermute | solution.py:24
  15.6 4.5 %copy-start = (bf16[1,128,512]{2,1,0:T(8,128)(2,1)S(1)}, bf16[1,128,512]{2,1,0:T(8,128)(2,1)}, u32[]{:S(2)}) copy-start(bf16[1,128,512]{2,1,0:T(8,128)(2,1)} %param.8) | copy-start | bytes 393220
  15.6 4.5 %copy-start.1 = (bf16[1,128,512]{2,1,0:T(8,128)(2,1)S(1)}, bf16[1,128,512]{2,1,0:T(8,128)(2,1)}, u32[]{:S(2)}) copy-start(bf16[1,128,512]{2,1,0:T(8,128)(2,1)} %param.7) | copy-start | bytes 393220
  15.7 15.4 %collective-permute-start.1 = (bf16[256,512]{1,0:T(8,128)(2,1)S(1)}, bf16[256,512]{1,0:T(8,128)(2,1)S(1)}, u32[]{:S(2)}, u32[]{:S(2)}) collective-permute-start(bf16[256,512]{1,0:T(8,128)(2,1)S(1)} %bitcast.21), channel_id=1, source_target_pairs={{0,16},{16,32},{32,48},{48,256},{256,272},{272,288},{288,304},{304... | collective-permute-start | bytes 786440 | tf_op jit(solution)/shard_map/ppermute | solution.py:251
  20.1 9.4 %collective-permute-start.2 = (bf16[128,512]{1,0:T(8,128)(2,1)S(1)}, bf16[128,512]{1,0:T(8,128)(2,1)S(1)}, u32[]{:S(2)}, u32[]{:S(2)}) collective-permute-start(bf16[128,512]{1,0:T(8,128)(2,1)S(1)} %multiply_convert_fusion.mixed_ref), channel_id=1, source_target_pairs={{0,8},{8,16},{16,24},{24,32},{32,40},{40,48},{48,56},{56,64},{64,7... | collective-permute-start | bytes 393224 | tf_op jit(solution)/shard_map/ppermute | solution.py:35
  31.1 17.6 %collective-permute-start.5 = (bf16[512,512]{1,0:T(8,128)(2,1)S(1)}, bf16[512,512]{1,0:T(8,128)(2,1)S(1)}, u32[]{:S(2)}, u32[]{:S(2)}) collective-permute-start(bf16[512,512]{1,0:T(8,128)(2,1)S(1)} %pad_maximum_fusion), channel_id=1, source_target_pairs={{0,32},{16,48},{32,256},{48,272},{256,288},{272,304},{288,0},{304,... | collective-permute-start | bytes 1572872 | tf_op jit(solution)/shard_map/ppermute | solution.py:251
  33.2 22.0 %collective-permute-start.4 = (bf16[256,512]{1,0:T(8,128)(2,1)S(1)}, bf16[256,512]{1,0:T(8,128)(2,1)S(1)}, u32[]{:S(2)}, u32[]{:S(2)}) collective-permute-start(bf16[256,512]{1,0:T(8,128)(2,1)S(1)} %bitcast.23), channel_id=1, source_target_pairs={{0,256},{16,272},{32,288},{48,304},{256,0},{272,16},{288,32},{304,... | collective-permute-start | bytes 786440 | tf_op jit(solution)/shard_map/ppermute | solution.py:251
  41.4 13.8 %collective-permute-start.3 = (bf16[256,512]{1,0:T(8,128)(2,1)S(1)}, bf16[256,512]{1,0:T(8,128)(2,1)S(1)}, u32[]{:S(2)}, u32[]{:S(2)}) collective-permute-start(bf16[256,512]{1,0:T(8,128)(2,1)S(1)} %collective-permute-done.1.refs_1_), channel_id=1, source_target_pairs={{0,8},{8,0},{1,9},{9,1},{2,10},{10,2},{3,11},{11,3},{4,12},{12,4},... | collective-permute-start | bytes 786440 | tf_op jit(solution)/shard_map/ppermute | solution.py:24
  48.7 15.1 %collective-permute-start.6 = (bf16[512,512]{1,0:T(8,128)(2,1)S(1)}, bf16[512,512]{1,0:T(8,128)(2,1)S(1)}, u32[]{:S(2)}, u32[]{:S(2)}) collective-permute-start(bf16[512,512]{1,0:T(8,128)(2,1)S(1)} %collective-permute-done.5.refs_4_), channel_id=1, source_target_pairs={{0,8},{8,0},{1,9},{9,1},{2,10},{10,2},{3,11},{11,3},{4,12},{12,4},... | collective-permute-start | bytes 1572872 | tf_op jit(solution)/shard_map/ppermute | solution.py:24
  55.2 1.2 copy-start.3
  55.2 1.2 copy-start.5
  56.4 14.0 %collective-permute-start.7 = (bf16[8,16,2048]{2,1,0:T(8,128)(2,1)}, bf16[8,16,2048]{2,1,0:T(8,128)(2,1)S(1)}, u32[]{:S(2)}, u32[]{:S(2)}) collective-permute-start(bf16[8,16,2048]{2,1,0:T(8,128)(2,1)} %get-tuple-element.39), channel_id=1, source_target_pairs={{7,0},{0,1},{1,2},{2,3},{3,4},{4,5},{5,6},{6,7},{15,8},{8,9},{9,10... | collective-permute-start | bytes 1572872 | tf_op jit(solution)/shard_map/ppermute | solution.py:244
  61.8 13.9 %collective-permute-start.8 = (bf16[8,16,2048]{2,1,0:T(8,128)(2,1)}, bf16[8,16,2048]{2,1,0:T(8,128)(2,1)}, u32[]{:S(2)}, u32[]{:S(2)}) collective-permute-start(bf16[8,16,2048]{2,1,0:T(8,128)(2,1)} %get-tuple-element.38), channel_id=1, source_target_pairs={{1,0},{2,1},{3,2},{4,3},{5,4},{6,5},{7,6},{0,7},{9,8},{10,9},{11,1... | collective-permute-start | bytes 1572872 | tf_op jit(solution)/shard_map/ppermute | solution.py:244
  75.7 1.0 copy-start.4
  76.7 0.9 copy-start.6
  81.1 10.2 %copy-start.9 = (bf16[128,512]{1,0:T(8,128)(2,1)S(1)}, bf16[128,512]{1,0:T(8,128)(2,1)}, u32[]{:S(2)}) copy-start(bf16[128,512]{1,0:T(8,128)(2,1)} %copy-done.8) | copy-start | bytes 393220
  81.1 10.2 %copy-start.10 = (bf16[32,128]{1,0:T(8,128)(2,1)S(1)}, bf16[32,128]{1,0:T(8,128)(2,1)}, u32[]{:S(2)}) copy-start(bf16[32,128]{1,0:T(8,128)(2,1)} %filters_ref.3) | copy-start | bytes 24580
  81.1 18.3 %all-to-all-start.1 = ((bf16[4,128,512]{2,1,0:T(8,128)(2,1)}), bf16[4,128,512]{2,1,0:T(8,128)(2,1)S(1)}, u32[]{:S(2)}, u32[]{:S(2)}) async-start(bf16[4,128,512]{2,1,0:T(8,128)(2,1)} %bitcast.13), calls=%async_computation.1 | async-start | bytes 1048576 | tf_op jit(solution)/shard_map/all_to_all | solution.py:239
  91.4 8.1 %copy-start.7 = (bf16[1,128,512]{2,1,0:T(8,128)(2,1)S(1)}, bf16[1,128,512]{2,1,0:T(8,128)(2,1)}, u32[]{:S(2)}) copy-start(bf16[1,128,512]{2,1,0:T(8,128)(2,1)} %param.6) | copy-start | bytes 393220
  102.3 15.1 %collective-permute-start.9 = (bf16[128,512]{1,0:T(8,128)(2,1)S(1)}, bf16[128,512]{1,0:T(8,128)(2,1)S(1)}, u32[]{:S(2)}, u32[]{:S(2)}) collective-permute-start(bf16[128,512]{1,0:T(8,128)(2,1)S(1)} %get-tuple-element.32.grad_ref), channel_id=1, source_target_pairs={{8,0},{16,8},{24,16},{32,24},{40,32},{48,40},{56,48},{64,56},{72,6... | collective-permute-start | bytes 393224 | tf_op jit(solution)/shard_map/ppermute | solution.py:35
  117.5 16.2 %all-to-all-start.3 = ((f32[8,32,128]{2,1,0:T(8,128)}), f32[8,32,128]{2,1,0:T(8,128)S(1)}, u32[]{:S(2)}, u32[]{:S(2)}) async-start(f32[8,32,128]{2,1,0:T(8,128)} %sums.1), calls=%async_computation.3 | async-start | bytes 262144 | tf_op jit(solution)/shard_map/all_to_all | solution.py:239
  (1 other events, 0.7 us)

commit v14 on v12

--- a/solution.py
+++ b/solution.py
@@ -268,11 +268,11 @@
     low, high = ahead(own[:8], Y, -1), ahead(own[8:], Y, 1)
     parts = [part.reshape(-1, columns) for part in (own, low, high)]
 
-    keys, values, own = lax.optimization_barrier((keys, values, own))
+    partial = partial_products(parts, weights)
+    terms = exchange(partial, "x")
+    keys, values, partial = lax.optimization_barrier((keys, values, partial))
     mixed = (keys.astype(F32) * values.astype(F32)).astype(BF16)
-    parts, before = lax.optimization_barrier((parts, from_behind(mixed, 1)))
-    terms = exchange(partial_products(parts, weights), "x")
-    conv, turned = convolve(filters, before, mixed)
+    conv, turned = convolve(filters, from_behind(mixed, 1), mixed)
     query_grad, conv_grad, lags = branch_gradients(terms, conv, query, turned)
     lags = summed_copies(exchange(lags, ("x", "co")))
     after = from_behind(conv_grad, -1)

time: 116 us -> 135 us (1.16)
  waiting for transfers between devices: 16.5 us -> 26.4 us
  starting transfers between devices: 69.7 us -> 75.6 us
  blocking collectives: 7.62 us -> 13.5 us
    ppermute x3, starting transfers between devices: 9.52 us -> 24.2 us  [swap(): return lax.ppermute(block, axis, [(0, 1), (1, 0)])]
    ppermute x2, waiting for transfers between devices: 0.01 us -> 13.3 us  [ahead(): lax.ppermute(block, axes, [((i + distance) % n, i) for i in range(n)])]
    all_to_all x3, waiting for transfers between devices: 11.2 us -> 5.34 us  [exchange(): return lax.all_to_all(copies, axes, split_axis=0, concat_axis=0)]
    all_to_all x1, blocking collectives: 7.62 us -> 13.5 us  [exchange(): return lax.all_to_all(copies, axes, split_axis=0, concat_axis=0)]
    ppermute x3, starting transfers between devices: 22.4 us -> 16.7 us  [along_z(): return lax.ppermute(block, Z + ('co',), route)]
    ppermute x2, starting transfers between devices: 10.4 us -> 7.34 us  [from_behind(): return lax.ppermute(block, CONTEXT, route)]
    ppermute x3, waiting for transfers between devices: 2.49 us -> 3.91 us  [along_z(): return lax.ppermute(block, Z + ('co',), route)]
    unnamed x20 -> x16, local copies, waits for them, and re-layouts: 2.87 us -> 1.92 us
  transfers between devices with their start and end apart: 13 -> 13, of which waited for: 6 -> 7; matrix products, arithmetic and copies ran while one was open for 2% -> 1% of each run, Pallas kernels for 6% -> 4%
where the time goes in v14:
time: 135 us; the launch traced here: 134 us
  starting transfers between devices  75.6 us (56%)
  waiting for transfers between devices  26.4 us (20%)
  Pallas kernels  13.7 us (10%)
  blocking collectives  13.5 us (10%)
  local copies, waits for them, and re-layouts  3.02 us (2%)
    ppermute x3, starting transfers between devices, swap(): return lax.ppermute(block, axis, [(0, 1), (1, 0)])  24.2 us
    all_to_all x3, starting transfers between devices, exchange(): return lax.all_to_all(copies, axes, split_axis=0, concat_axis=0)  20.5 us
    ppermute x3, starting transfers between devices, along_z(): return lax.ppermute(block, Z + ('co',), route)  16.7 us
    all_to_all x1, blocking collectives, exchange(): return lax.all_to_all(copies, axes, split_axis=0, concat_axis=0)  13.5 us
    ppermute x2, waiting for transfers between devices, ahead(): lax.ppermute(block, axes, [((i + distance) % n, i) for i in range(n)])  13.3 us
    ppermute x2, starting transfers between devices, from_behind(): return lax.ppermute(block, CONTEXT, route)  7.34 us
    ppermute x2, starting transfers between devices, ahead(): lax.ppermute(block, axes, [((i + distance) % n, i) for i in range(n)])  6.78 us
    all_to_all x3, waiting for transfers between devices, exchange(): return lax.all_to_all(copies, axes, split_axis=0, concat_axis=0)  5.34 us
  transfers between devices with their start and end apart: 13, of which 7 were waited for; matrix products, arithmetic and copies ran while one was open for 1% of the time, Pallas kernels for 4%

profile of v14, /device:TPU:1, one launch (start us, length us, event | category | flops | bytes accessed | tf_op | source)
XLA Modules:
  0.0 133.8 jit_solution(3152943847519269377)
XLA Ops:
  1.6 1.6 %spread.1 = bf16[4,4,16,2048]{3,2,1,0:T(8,128)(2,1)} custom-call(bf16[16,8192]{1,0:T(8,128)(2,1)S(1)} %bitcast.30), custom_call_target="tpu_custom_call" | custom-call | tf_op jit(solution)/shard_map/spread/pallas_call | solution.py:153
  3.2 10.3 %all-to-all-start = ((bf16[16,16,2048]{2,1,0:T(8,128)(2,1)}), bf16[16,16,2048]{2,1,0:T(8,128)(2,1)S(1)}, u32[]{:S(2)}, u32[]{:S(2)}) async-start(bf16[16,16,2048]{2,1,0:T(8,128)(2,1)} %bitcast.4), calls=%async_computation | async-start | bytes 2097152 | tf_op jit(solution)/shard_map/all_to_all | solution.py:237
  13.5 2.9 %collective-permute-start = (bf16[128,512]{1,0:T(8,128)(2,1)S(1)}, bf16[128,512]{1,0:T(8,128)(2,1)S(1)}, u32[]{:S(2)}, u32[]{:S(2)}) collective-permute-start(bf16[128,512]{1,0:T(8,128)(2,1)S(1)} %copy-done.7), channel_id=1, source_target_pairs={{0,8},{8,0},{1,9},{9,1},{2,10},{10,2},{3,11},{11,3},{4,12},{12,4},... | collective-permute-start | bytes 393224 | tf_op jit(solution)/shard_map/ppermute | solution.py:24
  17.4 10.7 %collective-permute-start.1 = (bf16[256,512]{1,0:T(8,128)(2,1)S(1)}, bf16[256,512]{1,0:T(8,128)(2,1)S(1)}, u32[]{:S(2)}, u32[]{:S(2)}) collective-permute-start(bf16[256,512]{1,0:T(8,128)(2,1)S(1)} %bitcast.21), channel_id=1, source_target_pairs={{0,16},{16,32},{32,48},{48,256},{256,272},{272,288},{288,304},{304... | collective-permute-start | bytes 786440 | tf_op jit(solution)/shard_map/ppermute | solution.py:249
  28.1 3.3 %collective-permute-done.1.refs_1_ = bf16[256,512]{1,0:T(8,128)(2,1)S(1)} collective-permute-done((bf16[256,512]{1,0:T(8,128)(2,1)S(1)}, bf16[256,512]{1,0:T(8,128)(2,1)S(1)}, u32[]{:S(2)}, u32[]{:S(2)}) %collective-permute-start.1) | collective-permute-done | bytes 262176 | tf_op jit(solution)/shard_map/ppermute | solution.py:249
  31.4 4.1 %collective-permute-start.6 = (bf16[512,512]{1,0:T(8,128)(2,1)S(1)}, bf16[512,512]{1,0:T(8,128)(2,1)S(1)}, u32[]{:S(2)}, u32[]{:S(2)}) collective-permute-start(bf16[512,512]{1,0:T(8,128)(2,1)S(1)} %pad_maximum_fusion), channel_id=1, source_target_pairs={{0,32},{16,48},{32,256},{48,272},{256,288},{272,304},{288,0},{304,... | collective-permute-start | bytes 1572872 | tf_op jit(solution)/shard_map/ppermute | solution.py:249
  35.5 1.9 %collective-permute-start.3 = (bf16[256,512]{1,0:T(8,128)(2,1)S(1)}, bf16[256,512]{1,0:T(8,128)(2,1)S(1)}, u32[]{:S(2)}, u32[]{:S(2)}) collective-permute-start(bf16[256,512]{1,0:T(8,128)(2,1)S(1)} %bitcast.23), channel_id=1, source_target_pairs={{0,256},{16,272},{32,288},{48,304},{256,0},{272,16},{288,32},{304,... | collective-permute-start | bytes 786440 | tf_op jit(solution)/shard_map/ppermute | solution.py:249
  37.5 5.8 %collective-permute-start.2 = (bf16[256,512]{1,0:T(8,128)(2,1)S(1)}, bf16[256,512]{1,0:T(8,128)(2,1)S(1)}, u32[]{:S(2)}, u32[]{:S(2)}) collective-permute-start(bf16[256,512]{1,0:T(8,128)(2,1)S(1)} %collective-permute-done.1.refs_1_), channel_id=1, source_target_pairs={{0,8},{8,0},{1,9},{9,1},{2,10},{10,2},{3,11},{11,3},{4,12},{12,4},... | collective-permute-start | bytes 786440 | tf_op jit(solution)/shard_map/ppermute | solution.py:24
  43.8 15.6 %collective-permute-start.7 = (bf16[512,512]{1,0:T(8,128)(2,1)S(1)}, bf16[512,512]{1,0:T(8,128)(2,1)S(1)}, u32[]{:S(2)}, u32[]{:S(2)}) collective-permute-start(bf16[512,512]{1,0:T(8,128)(2,1)S(1)} %collective-permute-done.6.refs_4_), channel_id=1, source_target_pairs={{0,8},{8,0},{1,9},{9,1},{2,10},{10,2},{3,11},{11,3},{4,12},{12,4},... | collective-permute-start | bytes 1572872 | tf_op jit(solution)/shard_map/ppermute | solution.py:24
  60.6 4.9 %collective-permute-start.5 = (bf16[8,16,2048]{2,1,0:T(8,128)(2,1)}, bf16[8,16,2048]{2,1,0:T(8,128)(2,1)S(1)}, u32[]{:S(2)}, u32[]{:S(2)}) collective-permute-start(bf16[8,16,2048]{2,1,0:T(8,128)(2,1)} %get-tuple-element.32), channel_id=1, source_target_pairs={{1,0},{2,1},{3,2},{4,3},{5,4},{6,5},{7,6},{0,7},{9,8},{10,9},{11,1... | collective-permute-start | bytes 1572872 | tf_op jit(solution)/shard_map/ppermute | solution.py:242
  65.5 1.9 %collective-permute-start.4 = (bf16[8,16,2048]{2,1,0:T(8,128)(2,1)}, bf16[8,16,2048]{2,1,0:T(8,128)(2,1)}, u32[]{:S(2)}, u32[]{:S(2)}) collective-permute-start(bf16[8,16,2048]{2,1,0:T(8,128)(2,1)} %get-tuple-element.33), channel_id=1, source_target_pairs={{7,0},{0,1},{1,2},{2,3},{3,4},{4,5},{5,6},{6,7},{15,8},{8,9},{9,10... | collective-permute-start | bytes 1572872 | tf_op jit(solution)/shard_map/ppermute | solution.py:242
  67.5 8.2 %collective-permute-done.5 = bf16[8,16,2048]{2,1,0:T(8,128)(2,1)S(1)} collective-permute-done((bf16[8,16,2048]{2,1,0:T(8,128)(2,1)}, bf16[8,16,2048]{2,1,0:T(8,128)(2,1)S(1)}, u32[]{:S(2)}, u32[]{:S(2)}) %collective-permute-start.5) | collective-permute-done | bytes 524320 | tf_op jit(solution)/shard_map/ppermute | solution.py:242
  75.7 5.0 %collective-permute-done.4 = bf16[8,16,2048]{2,1,0:T(8,128)(2,1)} collective-permute-done((bf16[8,16,2048]{2,1,0:T(8,128)(2,1)}, bf16[8,16,2048]{2,1,0:T(8,128)(2,1)}, u32[]{:S(2)}, u32[]{:S(2)}) %collective-permute-start.4) | collective-permute-done | bytes 524320 | tf_op jit(solution)/shard_map/ppermute | solution.py:242
  81.7 3.6 %product.1 = bf16[4,4,2,16,512]{4,3,2,1,0:T(8,128)(2,1)} custom-call(s32[3]{0:T(128)S(1)} %pad_add_fusion.place_ref, bf16[256,2048]{1,0:T(8,128)(2,1)S(1)} %bitcast.20, bf16[128,2048]{1,0:T(8,128)(2,1)} %bitcast.9.low_ref, bf16[128,2048]{1,0:T(8,128)(2,1)S(1)} %bitcast.25, bf16[256,512]{1,0:T(8,128)(2,1)S(1)} %bitcast.24, ...), custom_call_target="tpu_custom_call" | custom-call | tf_op jit(solution)/shard_map/product/pallas_call | solution.py:220
  85.4 4.1 %all-to-all-start.1 = ((bf16[4,128,512]{2,1,0:T(8,128)(2,1)}), bf16[4,128,512]{2,1,0:T(8,128)(2,1)S(1)}, u32[]{:S(2)}, u32[]{:S(2)}) async-start(bf16[4,128,512]{2,1,0:T(8,128)(2,1)} %bitcast.11), calls=%async_computation.1 | async-start | bytes 1048576 | tf_op jit(solution)/shard_map/all_to_all | solution.py:237
  89.6 2.1 %collective-permute-start.8 = (bf16[128,512]{1,0:T(8,128)(2,1)S(1)}, bf16[128,512]{1,0:T(8,128)(2,1)S(1)}, u32[]{:S(2)}, u32[]{:S(2)}) collective-permute-start(bf16[128,512]{1,0:T(8,128)(2,1)S(1)} %multiply_convert_fusion.mixed_ref), channel_id=1, source_target_pairs={{0,8},{8,16},{16,24},{24,32},{32,40},{40,48},{48,56},{56,64},{64,7... | collective-permute-start | bytes 393224 | tf_op jit(solution)/shard_map/ppermute | solution.py:35
  91.6 2.9 %collective-permute-done.8.before_ref = bf16[128,512]{1,0:T(8,128)(2,1)S(1)} collective-permute-done((bf16[128,512]{1,0:T(8,128)(2,1)S(1)}, bf16[128,512]{1,0:T(8,128)(2,1)S(1)}, u32[]{:S(2)}, u32[]{:S(2)}) %collective-permute-start.8) | collective-permute-done | bytes 131104 | tf_op jit(solution)/shard_map/ppermute | solution.py:35
  94.6 2.3 %conv.1 = (f32[128,512]{1,0:T(8,128)S(1)}, bf16[256,512]{1,0:T(8,128)(2,1)S(1)}) custom-call(bf16[32,128]{1,0:T(8,128)(2,1)S(1)} %copy-done.6, bf16[128,512]{1,0:T(8,128)(2,1)S(1)} %collective-permute-done.8.before_ref, bf16[128,512]{1,0:T(8,128)(2,1)S(1)} %multiply_convert_fusion.mixed_ref), custom_call_target="tpu_custom_call" | custom-call | tf_op jit(solution)/shard_map/conv/pallas_call | solution.py:176
  96.9 2.9 %branch.1 = (bf16[128,512]{1,0:T(8,128)(2,1)}, bf16[128,512]{1,0:T(8,128)(2,1)S(1)}, f32[8,32,128]{2,1,0:T(8,128)S(1)}) custom-call(bf16[4,128,512]{2,1,0:T(8,128)(2,1)S(1)} %all-to-all-done.1.terms_ref, f32[128,512]{1,0:T(8,128)S(1)} %get-tuple-element.23.conv_ref, bf16[128,512]{1,0:T(8,128)(2,1)S(1)} %bitcast.31, ...), custom_call_target="tpu_custom_call" | custom-call | tf_op jit(solution)/shard_map/branch/pallas_call | solution.py:204
  99.8 5.3 %collective-permute-start.9 = (bf16[128,512]{1,0:T(8,128)(2,1)S(1)}, bf16[128,512]{1,0:T(8,128)(2,1)S(1)}, u32[]{:S(2)}, u32[]{:S(2)}) collective-permute-start(bf16[128,512]{1,0:T(8,128)(2,1)S(1)} %get-tuple-element.26.grad_ref), channel_id=1, source_target_pairs={{8,0},{16,8},{24,16},{32,24},{40,32},{48,40},{56,48},{64,56},{72,6... | collective-permute-start | bytes 393224 | tf_op jit(solution)/shard_map/ppermute | solution.py:35
  105.1 13.5 %all_to_all.20.parts_ref = f32[8,32,128]{2,1,0:T(8,128)S(1)} all-to-all(f32[8,32,128]{2,1,0:T(8,128)S(1)} %get-tuple-element.27), channel_id=1, replica_groups=mesh['zh'=2,'x'=4,'zl'=4,'co'=2,'yq'=4,'yp'=2] {'x','co'}, dimensions={0} | all-to-all | bytes 262144 | tf_op jit(solution)/shard_map/all_to_all | solution.py:237
  119.2 6.1 %all-to-all-start.3 = ((f32[8,32,128]{2,1,0:T(8,128)}), f32[8,32,128]{2,1,0:T(8,128)S(1)}, u32[]{:S(2)}, u32[]{:S(2)}) async-start(f32[8,32,128]{2,1,0:T(8,128)} %sums.1), calls=%async_computation.3 | async-start | bytes 262144 | tf_op jit(solution)/shard_map/all_to_all | solution.py:237
  125.3 2.5 %mixed_grad.1 = (bf16[128,512]{1,0:T(8,128)(2,1)}, bf16[128,512]{1,0:T(8,128)(2,1)}) custom-call(bf16[32,128]{1,0:T(8,128)(2,1)S(1)} %copy-done.6, bf16[128,512]{1,0:T(8,128)(2,1)S(1)} %get-tuple-element.26.grad_ref, bf16[128,512]{1,0:T(8,128)(2,1)S(1)} %collective-permute-done.9.after_ref, bf16[128,512]{1,0:T(8,128)(2,1)S(1)} %bitcast.29, ...), custom_call_target="tpu_custom_call" | custom-call | tf_op jit(solution)/shard_map/mixed_grad/pallas_call | solution.py:190
  127.9 5.3 %all-to-all-done.3 = f32[8,32,128]{2,1,0:T(8,128)S(1)} async-done(((f32[8,32,128]{2,1,0:T(8,128)}), f32[8,32,128]{2,1,0:T(8,128)S(1)}, u32[]{:S(2)}, u32[]{:S(2)}) %all-to-all-start.3) | async-done | bytes 131104 | tf_op jit(solution)/shard_map/all_to_all | solution.py:237
  (33 shorter events, 6.1 us)
Async XLA Ops:
  0.6 1.0 copy-start.2
  3.2 10.4 %copy-start.7 = (bf16[128,512]{1,0:T(8,128)(2,1)S(1)}, bf16[128,512]{1,0:T(8,128)(2,1)}, u32[]{:S(2)}) copy-start(bf16[128,512]{1,0:T(8,128)(2,1)} %param.10) | copy-start | bytes 393220
  3.2 56.3 %all-to-all-start = ((bf16[16,16,2048]{2,1,0:T(8,128)(2,1)}), bf16[16,16,2048]{2,1,0:T(8,128)(2,1)S(1)}, u32[]{:S(2)}, u32[]{:S(2)}) async-start(bf16[16,16,2048]{2,1,0:T(8,128)(2,1)} %bitcast.4), calls=%async_computation | async-start | bytes 2097152 | tf_op jit(solution)/shard_map/all_to_all | solution.py:237
  13.5 3.8 %collective-permute-start = (bf16[128,512]{1,0:T(8,128)(2,1)S(1)}, bf16[128,512]{1,0:T(8,128)(2,1)S(1)}, u32[]{:S(2)}, u32[]{:S(2)}) collective-permute-start(bf16[128,512]{1,0:T(8,128)(2,1)S(1)} %copy-done.7), channel_id=1, source_target_pairs={{0,8},{8,0},{1,9},{9,1},{2,10},{10,2},{3,11},{11,3},{4,12},{12,4},... | collective-permute-start | bytes 393224 | tf_op jit(solution)/shard_map/ppermute | solution.py:24
  17.4 14.0 %collective-permute-start.1 = (bf16[256,512]{1,0:T(8,128)(2,1)S(1)}, bf16[256,512]{1,0:T(8,128)(2,1)S(1)}, u32[]{:S(2)}, u32[]{:S(2)}) collective-permute-start(bf16[256,512]{1,0:T(8,128)(2,1)S(1)} %bitcast.21), channel_id=1, source_target_pairs={{0,16},{16,32},{32,48},{48,256},{256,272},{272,288},{288,304},{304... | collective-permute-start | bytes 786440 | tf_op jit(solution)/shard_map/ppermute | solution.py:249
  31.4 12.4 %collective-permute-start.6 = (bf16[512,512]{1,0:T(8,128)(2,1)S(1)}, bf16[512,512]{1,0:T(8,128)(2,1)S(1)}, u32[]{:S(2)}, u32[]{:S(2)}) collective-permute-start(bf16[512,512]{1,0:T(8,128)(2,1)S(1)} %pad_maximum_fusion), channel_id=1, source_target_pairs={{0,32},{16,48},{32,256},{48,272},{256,288},{272,304},{288,0},{304,... | collective-permute-start | bytes 1572872 | tf_op jit(solution)/shard_map/ppermute | solution.py:249
  35.5 23.9 %collective-permute-start.3 = (bf16[256,512]{1,0:T(8,128)(2,1)S(1)}, bf16[256,512]{1,0:T(8,128)(2,1)S(1)}, u32[]{:S(2)}, u32[]{:S(2)}) collective-permute-start(bf16[256,512]{1,0:T(8,128)(2,1)S(1)} %bitcast.23), channel_id=1, source_target_pairs={{0,256},{16,272},{32,288},{48,304},{256,0},{272,16},{288,32},{304,... | collective-permute-start | bytes 786440 | tf_op jit(solution)/shard_map/ppermute | solution.py:249
  37.5 22.0 %collective-permute-start.2 = (bf16[256,512]{1,0:T(8,128)(2,1)S(1)}, bf16[256,512]{1,0:T(8,128)(2,1)S(1)}, u32[]{:S(2)}, u32[]{:S(2)}) collective-permute-start(bf16[256,512]{1,0:T(8,128)(2,1)S(1)} %collective-permute-done.1.refs_1_), channel_id=1, source_target_pairs={{0,8},{8,0},{1,9},{9,1},{2,10},{10,2},{3,11},{11,3},{4,12},{12,4},... | collective-permute-start | bytes 786440 | tf_op jit(solution)/shard_map/ppermute | solution.py:24
  43.8 23.6 %collective-permute-start.7 = (bf16[512,512]{1,0:T(8,128)(2,1)S(1)}, bf16[512,512]{1,0:T(8,128)(2,1)S(1)}, u32[]{:S(2)}, u32[]{:S(2)}) collective-permute-start(bf16[512,512]{1,0:T(8,128)(2,1)S(1)} %collective-permute-done.6.refs_4_), channel_id=1, source_target_pairs={{0,8},{8,0},{1,9},{9,1},{2,10},{10,2},{3,11},{11,3},{4,12},{12,4},... | collective-permute-start | bytes 1572872 | tf_op jit(solution)/shard_map/ppermute | solution.py:24
  59.5 1.1 copy-start.3
  60.6 15.1 %collective-permute-start.5 = (bf16[8,16,2048]{2,1,0:T(8,128)(2,1)}, bf16[8,16,2048]{2,1,0:T(8,128)(2,1)S(1)}, u32[]{:S(2)}, u32[]{:S(2)}) collective-permute-start(bf16[8,16,2048]{2,1,0:T(8,128)(2,1)} %get-tuple-element.32), channel_id=1, source_target_pairs={{1,0},{2,1},{3,2},{4,3},{5,4},{6,5},{7,6},{0,7},{9,8},{10,9},{11,1... | collective-permute-start | bytes 1572872 | tf_op jit(solution)/shard_map/ppermute | solution.py:242
  65.5 15.3 %collective-permute-start.4 = (bf16[8,16,2048]{2,1,0:T(8,128)(2,1)}, bf16[8,16,2048]{2,1,0:T(8,128)(2,1)}, u32[]{:S(2)}, u32[]{:S(2)}) collective-permute-start(bf16[8,16,2048]{2,1,0:T(8,128)(2,1)} %get-tuple-element.33), channel_id=1, source_target_pairs={{7,0},{0,1},{1,2},{2,3},{3,4},{4,5},{5,6},{6,7},{15,8},{8,9},{9,10... | collective-permute-start | bytes 1572872 | tf_op jit(solution)/shard_map/ppermute | solution.py:242
  80.8 1.0 copy-start.4
  85.4 4.1 %copy-start = (bf16[1,128,512]{2,1,0:T(8,128)(2,1)S(1)}, bf16[1,128,512]{2,1,0:T(8,128)(2,1)}, u32[]{:S(2)}) copy-start(bf16[1,128,512]{2,1,0:T(8,128)(2,1)} %param.8) | copy-start | bytes 393220
  85.4 4.1 %copy-start.1 = (bf16[1,128,512]{2,1,0:T(8,128)(2,1)S(1)}, bf16[1,128,512]{2,1,0:T(8,128)(2,1)}, u32[]{:S(2)}) copy-start(bf16[1,128,512]{2,1,0:T(8,128)(2,1)} %param.7) | copy-start | bytes 393220
  85.4 11.5 %all-to-all-start.1 = ((bf16[4,128,512]{2,1,0:T(8,128)(2,1)}), bf16[4,128,512]{2,1,0:T(8,128)(2,1)S(1)}, u32[]{:S(2)}, u32[]{:S(2)}) async-start(bf16[4,128,512]{2,1,0:T(8,128)(2,1)} %bitcast.11), calls=%async_computation.1 | async-start | bytes 1048576 | tf_op jit(solution)/shard_map/all_to_all | solution.py:237
  89.5 5.1 %copy-start.6 = (bf16[32,128]{1,0:T(8,128)(2,1)S(1)}, bf16[32,128]{1,0:T(8,128)(2,1)}, u32[]{:S(2)}) copy-start(bf16[32,128]{1,0:T(8,128)(2,1)} %filters_ref.3) | copy-start | bytes 24580
  89.5 7.4 %copy-start.5 = (bf16[1,128,512]{2,1,0:T(8,128)(2,1)S(1)}, bf16[1,128,512]{2,1,0:T(8,128)(2,1)}, u32[]{:S(2)}) copy-start(bf16[1,128,512]{2,1,0:T(8,128)(2,1)} %param.6) | copy-start | bytes 393220
  89.6 5.0 %collective-permute-start.8 = (bf16[128,512]{1,0:T(8,128)(2,1)S(1)}, bf16[128,512]{1,0:T(8,128)(2,1)S(1)}, u32[]{:S(2)}, u32[]{:S(2)}) collective-permute-start(bf16[128,512]{1,0:T(8,128)(2,1)S(1)} %multiply_convert_fusion.mixed_ref), channel_id=1, source_target_pairs={{0,8},{8,16},{16,24},{24,32},{32,40},{40,48},{48,56},{56,64},{64,7... | collective-permute-start | bytes 393224 | tf_op jit(solution)/shard_map/ppermute | solution.py:35
  99.8 19.4 %collective-permute-start.9 = (bf16[128,512]{1,0:T(8,128)(2,1)S(1)}, bf16[128,512]{1,0:T(8,128)(2,1)S(1)}, u32[]{:S(2)}, u32[]{:S(2)}) collective-permute-start(bf16[128,512]{1,0:T(8,128)(2,1)S(1)} %get-tuple-element.26.grad_ref), channel_id=1, source_target_pairs={{8,0},{16,8},{24,16},{32,24},{40,32},{48,40},{56,48},{64,56},{72,6... | collective-permute-start | bytes 393224 | tf_op jit(solution)/shard_map/ppermute | solution.py:35
  119.2 13.9 %all-to-all-start.3 = ((f32[8,32,128]{2,1,0:T(8,128)}), f32[8,32,128]{2,1,0:T(8,128)S(1)}, u32[]{:S(2)}, u32[]{:S(2)}) async-start(f32[8,32,128]{2,1,0:T(8,128)} %sums.1), calls=%async_computation.3 | async-start | bytes 262144 | tf_op jit(solution)/shard_map/all_to_all | solution.py:237

commit v15 on v12

--- a/solution.py
+++ b/solution.py
@@ -249,28 +249,29 @@
     return lax.ppermute(block, Z + ("co",), route)
 
 
-def weight_blocks(chip):
-    one, four = along_z(chip, 1), along_z(chip, 4)
-    pair = along_z(jnp.concatenate([chip, one], 0), 2)
-    return [chip, one, swap(one, "co"), four, pair, swap(pair, "co")]
+def after_these(value, *others):
+    return lax.optimization_barrier((value,) + others)[0]
 
 
 def local(query_branch, key_branch, value_branch, cotangent, out_weight, filters):
     query, keys, values = query_branch[0], key_branch[0], value_branch[0]
     tokens, width = query.shape
     chip = in_order(out_weight, swap(out_weight, "co"), "co").reshape(2 * out_weight.shape[0], width)
-    weights = weight_blocks(chip)
-
     copies = spread(cotangent[0])
     rows, columns = copies.shape[2:]
     own = exchange(copies.reshape(16, rows, columns), ("x", "yq"))
-    own, weights[2], weights[3] = lax.optimization_barrier((own, weights[2], weights[3]))
+
+    one, four = along_z(chip, 1), along_z(chip, 4)
+    keys = after_these(keys, chip)
+    mixed = (keys.astype(F32) * values.astype(F32)).astype(BF16)
+    before = from_behind(mixed, 1)
+    pair = after_these(jnp.concatenate([chip, one], 0), four, before)
+    own = after_these(own, pair)
     low, high = ahead(own[:8], Y, -1), ahead(own[8:], Y, 1)
+    pair = after_these(along_z(pair, 2), own)
+    weights = [chip, one, swap(one, "co"), four, pair, swap(pair, "co")]
     parts = [part.reshape(-1, columns) for part in (own, low, high)]
 
-    keys, values, own = lax.optimization_barrier((keys, values, own))
-    mixed = (keys.astype(F32) * values.astype(F32)).astype(BF16)
-    parts, before = lax.optimization_barrier((parts, from_behind(mixed, 1)))
     terms = exchange(partial_products(parts, weights), "x")
     conv, turned = convolve(filters, before, mixed)
     query_grad, conv_grad, lags = branch_gradients(terms, conv, query, turned)

time: 116 us -> 135 us (1.16)
  the two profiles are of different devices: /device:TPU:1 before, /device:TPU:24 now
where the time goes in v15:
time: 135 us; the launch traced here: 134 us
  starting transfers between devices  59.6 us (44%)
  waiting for transfers between devices  45.3 us (34%)
  Pallas kernels  14.1 us (10%)
  blocking collectives  9.1 us (7%)
  local copies, waits for them, and re-layouts  4.39 us (3%)
    ppermute x3, starting transfers between devices, along_z(): return lax.ppermute(block, Z + ('co',), route)  26.1 us
    all_to_all x3, starting transfers between devices, exchange(): return lax.all_to_all(copies, axes, split_axis=0, concat_axis=0)  17.7 us
    ppermute x3, waiting for transfers between devices, along_z(): return lax.ppermute(block, Z + ('co',), route)  17.3 us
    all_to_all x3, waiting for transfers between devices, exchange(): return lax.all_to_all(copies, axes, split_axis=0, concat_axis=0)  13.2 us
    ppermute x2, waiting for transfers between devices, ahead(): lax.ppermute(block, axes, [((i + distance) % n, i) for i in range(n)])  12 us
    all_to_all x1, blocking collectives, exchange(): return lax.all_to_all(copies, axes, split_axis=0, concat_axis=0)  9.1 us
    ppermute x2, starting transfers between devices, ahead(): lax.ppermute(block, axes, [((i + distance) % n, i) for i in range(n)])  7.29 us
    ppermute x3, starting transfers between devices, swap(): return lax.ppermute(block, axis, [(0, 1), (1, 0)])  5.96 us
  transfers between devices with their start and end apart: 13, of which 10 were waited for; matrix products, arithmetic and copies ran while one was open for 1% of the time, Pallas kernels for 4%

profile of v15, /device:TPU:24, one launch (start us, length us, event | category | flops | bytes accessed | tf_op | source)
XLA Modules:
  0.0 134.2 jit_solution(12235834108611040451)
XLA Ops:
  1.6 1.6 %spread.1 = bf16[4,4,16,2048]{3,2,1,0:T(8,128)(2,1)} custom-call(bf16[16,8192]{1,0:T(8,128)(2,1)S(1)} %bitcast.30), custom_call_target="tpu_custom_call" | custom-call | tf_op jit(solution)/shard_map/spread/pallas_call | solution.py:153
  3.2 9.1 %all-to-all-start = ((bf16[16,16,2048]{2,1,0:T(8,128)(2,1)}), bf16[16,16,2048]{2,1,0:T(8,128)(2,1)S(1)}, u32[]{:S(2)}, u32[]{:S(2)}) async-start(bf16[16,16,2048]{2,1,0:T(8,128)(2,1)} %bitcast.4), calls=%async_computation | async-start | bytes 2097152 | tf_op jit(solution)/shard_map/all_to_all | solution.py:237
  12.3 1.9 %collective-permute-start = (bf16[128,512]{1,0:T(8,128)(2,1)S(1)}, bf16[128,512]{1,0:T(8,128)(2,1)S(1)}, u32[]{:S(2)}, u32[]{:S(2)}) collective-permute-start(bf16[128,512]{1,0:T(8,128)(2,1)S(1)} %copy-done.9), channel_id=1, source_target_pairs={{0,8},{8,0},{1,9},{9,1},{2,10},{10,2},{3,11},{11,3},{4,12},{12,4},... | collective-permute-start | bytes 393224 | tf_op jit(solution)/shard_map/ppermute | solution.py:24
  15.6 4.4 %collective-permute-start.1 = (bf16[256,512]{1,0:T(8,128)(2,1)S(1)}, bf16[256,512]{1,0:T(8,128)(2,1)S(1)}, u32[]{:S(2)}, u32[]{:S(2)}) collective-permute-start(bf16[256,512]{1,0:T(8,128)(2,1)S(1)} %bitcast.22), channel_id=1, source_target_pairs={{0,16},{16,32},{32,48},{48,256},{256,272},{272,288},{288,304},{304... | collective-permute-start | bytes 786440 | tf_op jit(solution)/shard_map/ppermute | solution.py:249
  20.1 10.0 %collective-permute-start.2 = (bf16[256,512]{1,0:T(8,128)(2,1)S(1)}, bf16[256,512]{1,0:T(8,128)(2,1)S(1)}, u32[]{:S(2)}, u32[]{:S(2)}) collective-permute-start(bf16[256,512]{1,0:T(8,128)(2,1)S(1)} %bitcast.23), channel_id=1, source_target_pairs={{0,256},{16,272},{32,288},{48,304},{256,0},{272,16},{288,32},{304,... | collective-permute-start | bytes 786440 | tf_op jit(solution)/shard_map/ppermute | solution.py:249
  33.1 4.6 %collective-permute-done.2.refs_3_ = bf16[256,512]{1,0:T(8,128)(2,1)S(1)} collective-permute-done((bf16[256,512]{1,0:T(8,128)(2,1)S(1)}, bf16[256,512]{1,0:T(8,128)(2,1)S(1)}, u32[]{:S(2)}, u32[]{:S(2)}) %collective-permute-start.2) | collective-permute-done | bytes 262176 | tf_op jit(solution)/shard_map/ppermute | solution.py:249
  38.4 11.7 %collective-permute-start.7 = (bf16[512,512]{1,0:T(8,128)(2,1)S(1)}, bf16[512,512]{1,0:T(8,128)(2,1)S(1)}, u32[]{:S(2)}, u32[]{:S(2)}) collective-permute-start(bf16[512,512]{1,0:T(8,128)(2,1)S(1)} %pad_maximum_fusion), channel_id=1, source_target_pairs={{0,32},{16,48},{32,256},{48,272},{256,288},{272,304},{288,0},{304,... | collective-permute-start | bytes 1572872 | tf_op jit(solution)/shard_map/ppermute | solution.py:249
  51.2 11.9 %collective-permute-done.7.refs_4_ = bf16[512,512]{1,0:T(8,128)(2,1)S(1)} collective-permute-done((bf16[512,512]{1,0:T(8,128)(2,1)S(1)}, bf16[512,512]{1,0:T(8,128)(2,1)S(1)}, u32[]{:S(2)}, u32[]{:S(2)}) %collective-permute-start.7) | collective-permute-done | bytes 524320 | tf_op jit(solution)/shard_map/ppermute | solution.py:249
  63.1 1.9 %collective-permute-start.8 = (bf16[512,512]{1,0:T(8,128)(2,1)S(1)}, bf16[512,512]{1,0:T(8,128)(2,1)S(1)}, u32[]{:S(2)}, u32[]{:S(2)}) collective-permute-start(bf16[512,512]{1,0:T(8,128)(2,1)S(1)} %collective-permute-done.7.refs_4_), channel_id=1, source_target_pairs={{0,8},{8,0},{1,9},{9,1},{2,10},{10,2},{3,11},{11,3},{4,12},{12,4},... | collective-permute-start | bytes 1572872 | tf_op jit(solution)/shard_map/ppermute | solution.py:24
  65.0 5.4 %collective-permute-start.4 = (bf16[8,16,2048]{2,1,0:T(8,128)(2,1)}, bf16[8,16,2048]{2,1,0:T(8,128)(2,1)S(1)}, u32[]{:S(2)}, u32[]{:S(2)}) collective-permute-start(bf16[8,16,2048]{2,1,0:T(8,128)(2,1)} %get-tuple-element.31), channel_id=1, source_target_pairs={{7,0},{0,1},{1,2},{2,3},{3,4},{4,5},{5,6},{6,7},{15,8},{8,9},{9,10... | collective-permute-start | bytes 1572872 | tf_op jit(solution)/shard_map/ppermute | solution.py:242
  70.4 1.9 %collective-permute-start.5 = (bf16[8,16,2048]{2,1,0:T(8,128)(2,1)}, bf16[8,16,2048]{2,1,0:T(8,128)(2,1)}, u32[]{:S(2)}, u32[]{:S(2)}) collective-permute-start(bf16[8,16,2048]{2,1,0:T(8,128)(2,1)} %get-tuple-element.30), channel_id=1, source_target_pairs={{1,0},{2,1},{3,2},{4,3},{5,4},{6,5},{7,6},{0,7},{9,8},{10,9},{11,1... | collective-permute-start | bytes 1572872 | tf_op jit(solution)/shard_map/ppermute | solution.py:242
  72.3 2.1 %collective-permute-start.6 = (bf16[256,512]{1,0:T(8,128)(2,1)S(1)}, bf16[256,512]{1,0:T(8,128)(2,1)}, u32[]{:S(2)}, u32[]{:S(2)}) collective-permute-start(bf16[256,512]{1,0:T(8,128)(2,1)S(1)} %collective-permute-done.1.refs_1_), channel_id=1, source_target_pairs={{0,8},{8,0},{1,9},{9,1},{2,10},{10,2},{3,11},{11,3},{4,12},{12,4},... | collective-permute-start | bytes 786440 | tf_op jit(solution)/shard_map/ppermute | solution.py:24
  74.5 1.3 %collective-permute-done.6.refs_2_ = bf16[256,512]{1,0:T(8,128)(2,1)} collective-permute-done((bf16[256,512]{1,0:T(8,128)(2,1)S(1)}, bf16[256,512]{1,0:T(8,128)(2,1)}, u32[]{:S(2)}, u32[]{:S(2)}) %collective-permute-start.6) | collective-permute-done | bytes 262176 | tf_op jit(solution)/shard_map/ppermute | solution.py:24
  75.9 6.6 %collective-permute-done.4 = bf16[8,16,2048]{2,1,0:T(8,128)(2,1)S(1)} collective-permute-done((bf16[8,16,2048]{2,1,0:T(8,128)(2,1)}, bf16[8,16,2048]{2,1,0:T(8,128)(2,1)S(1)}, u32[]{:S(2)}, u32[]{:S(2)}) %collective-permute-start.4) | collective-permute-done | bytes 524320 | tf_op jit(solution)/shard_map/ppermute | solution.py:242
  82.5 5.3 %collective-permute-done.5 = bf16[8,16,2048]{2,1,0:T(8,128)(2,1)} collective-permute-done((bf16[8,16,2048]{2,1,0:T(8,128)(2,1)}, bf16[8,16,2048]{2,1,0:T(8,128)(2,1)}, u32[]{:S(2)}, u32[]{:S(2)}) %collective-permute-start.5) | collective-permute-done | bytes 524320 | tf_op jit(solution)/shard_map/ppermute | solution.py:242
  88.8 4.1 %product.1 = bf16[4,4,2,16,512]{4,3,2,1,0:T(8,128)(2,1)} custom-call(s32[3]{0:T(128)S(1)} %pad_add_fusion.place_ref, bf16[256,2048]{1,0:T(8,128)(2,1)S(1)} %bitcast.21, bf16[128,2048]{1,0:T(8,128)(2,1)S(1)} %bitcast.26, bf16[128,2048]{1,0:T(8,128)(2,1)} %bitcast.12.high_ref, bf16[256,512]{1,0:T(8,128)(2,1)S(1)} %bitcast.25, ...), custom_call_target="tpu_custom_call" | custom-call | tf_op jit(solution)/shard_map/product/pallas_call | solution.py:220
  92.9 4.7 %all-to-all-start.1 = ((bf16[4,128,512]{2,1,0:T(8,128)(2,1)}), bf16[4,128,512]{2,1,0:T(8,128)(2,1)S(1)}, u32[]{:S(2)}, u32[]{:S(2)}) async-start(bf16[4,128,512]{2,1,0:T(8,128)(2,1)} %bitcast.13), calls=%async_computation.1 | async-start | bytes 1048576 | tf_op jit(solution)/shard_map/all_to_all | solution.py:237
  97.6 2.3 %conv.1 = (f32[128,512]{1,0:T(8,128)S(1)}, bf16[256,512]{1,0:T(8,128)(2,1)S(1)}) custom-call(bf16[32,128]{1,0:T(8,128)(2,1)S(1)} %copy-done.8, bf16[128,512]{1,0:T(8,128)(2,1)S(1)} %copy-done.7, bf16[128,512]{1,0:T(8,128)(2,1)S(1)} %multiply_convert_fusion.mixed_ref), custom_call_target="tpu_custom_call" | custom-call | tf_op jit(solution)/shard_map/conv/pallas_call | solution.py:176
  100.0 6.7 %all-to-all-done.1.terms_ref = bf16[4,128,512]{2,1,0:T(8,128)(2,1)S(1)} async-done(((bf16[4,128,512]{2,1,0:T(8,128)(2,1)}), bf16[4,128,512]{2,1,0:T(8,128)(2,1)S(1)}, u32[]{:S(2)}, u32[]{:S(2)}) %all-to-all-start.1) | async-done | bytes 524320 | tf_op jit(solution)/shard_map/all_to_all | solution.py:237
  106.7 2.9 %branch.1 = (bf16[128,512]{1,0:T(8,128)(2,1)}, bf16[128,512]{1,0:T(8,128)(2,1)S(1)}, f32[8,32,128]{2,1,0:T(8,128)S(1)}) custom-call(bf16[4,128,512]{2,1,0:T(8,128)(2,1)S(1)} %all-to-all-done.1.terms_ref, f32[128,512]{1,0:T(8,128)S(1)} %get-tuple-element.21.conv_ref, bf16[128,512]{1,0:T(8,128)(2,1)S(1)} %bitcast.31, ...), custom_call_target="tpu_custom_call" | custom-call | tf_op jit(solution)/shard_map/branch/pallas_call | solution.py:204
  110.9 9.1 %all_to_all.20.parts_ref = f32[8,32,128]{2,1,0:T(8,128)S(1)} all-to-all(f32[8,32,128]{2,1,0:T(8,128)S(1)} %get-tuple-element.25), channel_id=1, replica_groups=mesh['zh'=2,'x'=4,'zl'=4,'co'=2,'yq'=4,'yp'=2] {'x','co'}, dimensions={0} | all-to-all | bytes 262144 | tf_op jit(solution)/shard_map/all_to_all | solution.py:237
  120.7 3.8 %all-to-all-start.3 = ((f32[8,32,128]{2,1,0:T(8,128)}), f32[8,32,128]{2,1,0:T(8,128)S(1)}, u32[]{:S(2)}, u32[]{:S(2)}) async-start(f32[8,32,128]{2,1,0:T(8,128)} %sums.1), calls=%async_computation.3 | async-start | bytes 262144 | tf_op jit(solution)/shard_map/all_to_all | solution.py:237
  124.5 2.5 %mixed_grad.1 = (bf16[128,512]{1,0:T(8,128)(2,1)}, bf16[128,512]{1,0:T(8,128)(2,1)}) custom-call(bf16[32,128]{1,0:T(8,128)(2,1)S(1)} %copy-done.8, bf16[128,512]{1,0:T(8,128)(2,1)S(1)} %get-tuple-element.24.grad_ref, bf16[128,512]{1,0:T(8,128)(2,1)S(1)} %collective-permute-done.9.after_ref, bf16[128,512]{1,0:T(8,128)(2,1)S(1)} %bitcast.28, ...), custom_call_target="tpu_custom_call" | custom-call | tf_op jit(solution)/shard_map/mixed_grad/pallas_call | solution.py:190
  127.0 6.5 %all-to-all-done.3 = f32[8,32,128]{2,1,0:T(8,128)S(1)} async-done(((f32[8,32,128]{2,1,0:T(8,128)}), f32[8,32,128]{2,1,0:T(8,128)S(1)}, u32[]{:S(2)}, u32[]{:S(2)}) %all-to-all-start.3) | async-done | bytes 131104 | tf_op jit(solution)/shard_map/all_to_all | solution.py:237
  (37 shorter events, 10.7 us)
Async XLA Ops:
  0.6 1.0 copy-start.2
  3.2 9.1 %copy-start.9 = (bf16[128,512]{1,0:T(8,128)(2,1)S(1)}, bf16[128,512]{1,0:T(8,128)(2,1)}, u32[]{:S(2)}) copy-start(bf16[128,512]{1,0:T(8,128)(2,1)} %param.10) | copy-start | bytes 393220
  3.2 47.0 %all-to-all-start = ((bf16[16,16,2048]{2,1,0:T(8,128)(2,1)}), bf16[16,16,2048]{2,1,0:T(8,128)(2,1)S(1)}, u32[]{:S(2)}, u32[]{:S(2)}) async-start(bf16[16,16,2048]{2,1,0:T(8,128)(2,1)} %bitcast.4), calls=%async_computation | async-start | bytes 2097152 | tf_op jit(solution)/shard_map/all_to_all | solution.py:237
  12.3 3.2 %collective-permute-start = (bf16[128,512]{1,0:T(8,128)(2,1)S(1)}, bf16[128,512]{1,0:T(8,128)(2,1)S(1)}, u32[]{:S(2)}, u32[]{:S(2)}) collective-permute-start(bf16[128,512]{1,0:T(8,128)(2,1)S(1)} %copy-done.9), channel_id=1, source_target_pairs={{0,8},{8,0},{1,9},{9,1},{2,10},{10,2},{3,11},{11,3},{4,12},{12,4},... | collective-permute-start | bytes 393224 | tf_op jit(solution)/shard_map/ppermute | solution.py:24
  15.6 14.5 %copy-start = (bf16[1,128,512]{2,1,0:T(8,128)(2,1)S(1)}, bf16[1,128,512]{2,1,0:T(8,128)(2,1)}, u32[]{:S(2)}) copy-start(bf16[1,128,512]{2,1,0:T(8,128)(2,1)} %param.7) | copy-start | bytes 393220
  15.6 14.5 %copy-start.1 = (bf16[1,128,512]{2,1,0:T(8,128)(2,1)S(1)}, bf16[1,128,512]{2,1,0:T(8,128)(2,1)}, u32[]{:S(2)}) copy-start(bf16[1,128,512]{2,1,0:T(8,128)(2,1)} %param.8) | copy-start | bytes 393220
  15.6 16.6 %collective-permute-start.1 = (bf16[256,512]{1,0:T(8,128)(2,1)S(1)}, bf16[256,512]{1,0:T(8,128)(2,1)S(1)}, u32[]{:S(2)}, u32[]{:S(2)}) collective-permute-start(bf16[256,512]{1,0:T(8,128)(2,1)S(1)} %bitcast.22), channel_id=1, source_target_pairs={{0,16},{16,32},{32,48},{48,256},{256,272},{272,288},{288,304},{304... | collective-permute-start | bytes 786440 | tf_op jit(solution)/shard_map/ppermute | solution.py:249
  20.1 17.6 %collective-permute-start.2 = (bf16[256,512]{1,0:T(8,128)(2,1)S(1)}, bf16[256,512]{1,0:T(8,128)(2,1)S(1)}, u32[]{:S(2)}, u32[]{:S(2)}) collective-permute-start(bf16[256,512]{1,0:T(8,128)(2,1)S(1)} %bitcast.23), channel_id=1, source_target_pairs={{0,256},{16,272},{32,288},{48,304},{256,0},{272,16},{288,32},{304,... | collective-permute-start | bytes 786440 | tf_op jit(solution)/shard_map/ppermute | solution.py:249
  30.1 2.3 %collective-permute-start.3 = (bf16[128,512]{1,0:T(8,128)(2,1)S(1)}, bf16[128,512]{1,0:T(8,128)(2,1)S(1)}, u32[]{:S(2)}, u32[]{:S(2)}) collective-permute-start(bf16[128,512]{1,0:T(8,128)(2,1)S(1)} %multiply_convert_fusion.mixed_ref), channel_id=1, source_target_pairs={{0,8},{8,16},{16,24},{24,32},{32,40},{40,48},{48,56},{56,64},{64,7... | collective-permute-start | bytes 393224 | tf_op jit(solution)/shard_map/ppermute | solution.py:35
  32.4 0.7 copy-start.6
  37.7 0.7 copy-start.3
  38.4 24.7 %collective-permute-start.7 = (bf16[512,512]{1,0:T(8,128)(2,1)S(1)}, bf16[512,512]{1,0:T(8,128)(2,1)S(1)}, u32[]{:S(2)}, u32[]{:S(2)}) collective-permute-start(bf16[512,512]{1,0:T(8,128)(2,1)S(1)} %pad_maximum_fusion), channel_id=1, source_target_pairs={{0,32},{16,48},{32,256},{48,272},{256,288},{272,304},{288,0},{304,... | collective-permute-start | bytes 1572872 | tf_op jit(solution)/shard_map/ppermute | solution.py:249
  63.1 12.8 %collective-permute-start.8 = (bf16[512,512]{1,0:T(8,128)(2,1)S(1)}, bf16[512,512]{1,0:T(8,128)(2,1)S(1)}, u32[]{:S(2)}, u32[]{:S(2)}) collective-permute-start(bf16[512,512]{1,0:T(8,128)(2,1)S(1)} %collective-permute-done.7.refs_4_), channel_id=1, source_target_pairs={{0,8},{8,0},{1,9},{9,1},{2,10},{10,2},{3,11},{11,3},{4,12},{12,4},... | collective-permute-start | bytes 1572872 | tf_op jit(solution)/shard_map/ppermute | solution.py:24
  65.0 17.5 %collective-permute-start.4 = (bf16[8,16,2048]{2,1,0:T(8,128)(2,1)}, bf16[8,16,2048]{2,1,0:T(8,128)(2,1)S(1)}, u32[]{:S(2)}, u32[]{:S(2)}) collective-permute-start(bf16[8,16,2048]{2,1,0:T(8,128)(2,1)} %get-tuple-element.31), channel_id=1, source_target_pairs={{7,0},{0,1},{1,2},{2,3},{3,4},{4,5},{5,6},{6,7},{15,8},{8,9},{9,10... | collective-permute-start | bytes 1572872 | tf_op jit(solution)/shard_map/ppermute | solution.py:242
  70.4 17.5 %collective-permute-start.5 = (bf16[8,16,2048]{2,1,0:T(8,128)(2,1)}, bf16[8,16,2048]{2,1,0:T(8,128)(2,1)}, u32[]{:S(2)}, u32[]{:S(2)}) collective-permute-start(bf16[8,16,2048]{2,1,0:T(8,128)(2,1)} %get-tuple-element.30), channel_id=1, source_target_pairs={{1,0},{2,1},{3,2},{4,3},{5,4},{6,5},{7,6},{0,7},{9,8},{10,9},{11,1... | collective-permute-start | bytes 1572872 | tf_op jit(solution)/shard_map/ppermute | solution.py:242
  72.3 3.6 %collective-permute-start.6 = (bf16[256,512]{1,0:T(8,128)(2,1)S(1)}, bf16[256,512]{1,0:T(8,128)(2,1)}, u32[]{:S(2)}, u32[]{:S(2)}) collective-permute-start(bf16[256,512]{1,0:T(8,128)(2,1)S(1)} %collective-permute-done.1.refs_1_), channel_id=1, source_target_pairs={{0,8},{8,0},{1,9},{9,1},{2,10},{10,2},{3,11},{11,3},{4,12},{12,4},... | collective-permute-start | bytes 786440 | tf_op jit(solution)/shard_map/ppermute | solution.py:24
  87.9 1.0 copy-start.4
  92.9 4.7 %copy-start.7 = (bf16[128,512]{1,0:T(8,128)(2,1)S(1)}, bf16[128,512]{1,0:T(8,128)(2,1)}, u32[]{:S(2)}) copy-start(bf16[128,512]{1,0:T(8,128)(2,1)} %copy-done.6) | copy-start | bytes 393220
  92.9 4.7 %copy-start.8 = (bf16[32,128]{1,0:T(8,128)(2,1)S(1)}, bf16[32,128]{1,0:T(8,128)(2,1)}, u32[]{:S(2)}) copy-start(bf16[32,128]{1,0:T(8,128)(2,1)} %filters_ref.3) | copy-start | bytes 24580
  92.9 13.8 %all-to-all-start.1 = ((bf16[4,128,512]{2,1,0:T(8,128)(2,1)}), bf16[4,128,512]{2,1,0:T(8,128)(2,1)S(1)}, u32[]{:S(2)}, u32[]{:S(2)}) async-start(bf16[4,128,512]{2,1,0:T(8,128)(2,1)} %bitcast.13), calls=%async_computation.1 | async-start | bytes 1048576 | tf_op jit(solution)/shard_map/all_to_all | solution.py:237
  97.6 9.0 %copy-start.5 = (bf16[1,128,512]{2,1,0:T(8,128)(2,1)S(1)}, bf16[1,128,512]{2,1,0:T(8,128)(2,1)}, u32[]{:S(2)}) copy-start(bf16[1,128,512]{2,1,0:T(8,128)(2,1)} %param.6) | copy-start | bytes 393220
  109.6 11.1 %collective-permute-start.9 = (bf16[128,512]{1,0:T(8,128)(2,1)S(1)}, bf16[128,512]{1,0:T(8,128)(2,1)S(1)}, u32[]{:S(2)}, u32[]{:S(2)}) collective-permute-start(bf16[128,512]{1,0:T(8,128)(2,1)S(1)} %get-tuple-element.24.grad_ref), channel_id=1, source_target_pairs={{8,0},{16,8},{24,16},{32,24},{40,32},{48,40},{56,48},{64,56},{72,6... | collective-permute-start | bytes 393224 | tf_op jit(solution)/shard_map/ppermute | solution.py:35
  120.7 12.9 %all-to-all-start.3 = ((f32[8,32,128]{2,1,0:T(8,128)}), f32[8,32,128]{2,1,0:T(8,128)S(1)}, u32[]{:S(2)}, u32[]{:S(2)}) async-start(f32[8,32,128]{2,1,0:T(8,128)} %sums.1), calls=%async_computation.3 | async-start | bytes 262144 | tf_op jit(solution)/shard_map/all_to_all | solution.py:237

commit v16 on v14

--- a/solution.py
+++ b/solution.py
@@ -108,37 +108,32 @@
             lag_ref[copy, g : g + 1, :] = sums
 
 
-def product_kernel(place_ref, own_ref, low_ref, high_ref, *refs):
+def product_kernel(place_ref, cot_ref, *refs):
     count = (len(refs) - 3) // 2
     weights_hbm, out_ref, total_ref, weights, sems = refs[:count], refs[count], refs[count + 1], refs[count + 2 : -1], refs[-1]
     copies = [pltpu.make_async_copy(weights_hbm[i], weights[i], sems.at[i]) for i in range(count)]
     for copy in copies:
         copy.start()
-    z, core, odd = place_ref[0], place_ref[1], place_ref[2]
+    z, core = place_ref[0], place_ref[1]
     depth = weights[0].shape[0]
     below, above = [lax.rem(z + 8 - i, 8) for i in range(4)], [lax.rem(z + i, 8) for i in range(4)]
     mine = [jnp.where(core == 0, b, a) for b, a in zip(below, above)]
     theirs = [jnp.where(core == 0, a, b) for b, a in zip(below, above)]
     pieces = [(0, 0, z), (1, 0, mine[1]), (2, 0, theirs[1]), (3, 0, lax.rem(z + 4, 8))]
     pieces += [(4, 0, mine[2]), (4, depth, mine[3]), (5, 0, theirs[2]), (5, depth, theirs[3])]
-    half = own_ref.shape[0] // 2
-    parts = ((own_ref, 0), (own_ref, half), (low_ref, 0), (high_ref, 0))
     for n, (i, offset, place) in enumerate(pieces):
         if offset == 0:
             copies[i].wait()
         weight = weights[i][offset : offset + depth, :]
         columns = pl.ds(pl.multiple_of(place * depth, LANES), depth)
-        for j, (cot_ref, first) in enumerate(parts):
-            term = jnp.dot(cot_ref[first : first + half, columns], weight, preferred_element_type=F32)
+        for x in range(4):
+            term = jnp.dot(cot_ref[x * TAPS : (x + 1) * TAPS, columns], weight, preferred_element_type=F32)
             if n:
-                term = total_ref[j] + term
+                term = total_ref[x] + term
             if n < len(pieces) - 1:
-                total_ref[j] = term
-                continue
-            term = term.astype(BF16).reshape(2, 4, 16, term.shape[1])
-            for x in range(2):
-                for pair in range(4):
-                    out_ref[2 * (j % 2) + x, pair, odd if j < 2 else 1 - odd] = term[x, pair]
+                total_ref[x] = term
+            else:
+                out_ref[x] = term.astype(BF16)
 
 
 def lane_blocks(*lead):
@@ -152,10 +147,10 @@
     rows, width = cotangent.shape
     return pl.pallas_call(
         spread_kernel,
-        grid=(4,),
+        grid=(8,),
         in_specs=[pl.BlockSpec((rows, width), lambda i: (0, 0))],
         out_specs=pl.BlockSpec((4, 1, rows, width // 4), lambda i: (0, i, 0, 0)),
-        out_shape=jax.ShapeDtypeStruct((4, 4, rows, width // 4), cotangent.dtype),
+        out_shape=jax.ShapeDtypeStruct((4, 8, rows, width // 4), cotangent.dtype),
         compiler_params=VMEM,
         name="spread",
     )(cotangent)
@@ -213,33 +208,30 @@
     )(terms, conv, query, turned)
 
 
-def partial_products(parts, weights):
+def partial_products(cotangent, weights):
     width = weights[0].shape[1]
-    place = jnp.stack([lax.axis_index(Z), lax.axis_index("co"), lax.axis_index("yp")]).astype(jnp.int32)
+    place = jnp.stack([lax.axis_index(Z), lax.axis_index("co")]).astype(jnp.int32)
     whole = pl.BlockSpec(memory_space=pltpu.VMEM)
-    out = pl.pallas_call(
+    return pl.pallas_call(
         product_kernel,
-        in_specs=[pl.BlockSpec(memory_space=pltpu.SMEM)]
-        + [whole] * 3
+        in_specs=[pl.BlockSpec(memory_space=pltpu.SMEM), whole]
         + [pl.BlockSpec(memory_space=pltpu.HBM)] * len(weights),
         out_specs=whole,
-        out_shape=jax.ShapeDtypeStruct((4, 4, 2, 16, width), BF16),
+        out_shape=jax.ShapeDtypeStruct((4, TAPS, width), BF16),
         scratch_shapes=[pltpu.VMEM((4, TAPS, width), F32)]
         + [pltpu.VMEM(a.shape, a.dtype) for a in weights]
         + [pltpu.SemaphoreType.DMA((len(weights),))],
         compiler_params=VMEM,
         name="product",
-    )(place, *parts, *weights)
-    return out.reshape(4, TAPS, width)
+    )(place, cotangent, *weights)
 
 
 def exchange(copies, axes):
     return lax.all_to_all(copies, axes, split_axis=0, concat_axis=0)
 
 
-def ahead(block, axes, distance):
-    n = lax.axis_size(axes)
-    return lax.ppermute(block, axes, [((i + distance) % n, i) for i in range(n)])
+def after_these(value, *others):
+    return lax.optimization_barrier((value,) + others)[0]
 
 
 def along_z(block, steps):
@@ -259,20 +251,15 @@
     query, keys, values = query_branch[0], key_branch[0], value_branch[0]
     tokens, width = query.shape
     chip = in_order(out_weight, swap(out_weight, "co"), "co").reshape(2 * out_weight.shape[0], width)
-    weights = weight_blocks(chip)
-
     copies = spread(cotangent[0])
-    rows, columns = copies.shape[2:]
-    own = exchange(copies.reshape(16, rows, columns), ("x", "yq"))
-    own, weights[2], weights[3] = lax.optimization_barrier((own, weights[2], weights[3]))
-    low, high = ahead(own[:8], Y, -1), ahead(own[8:], Y, 1)
-    parts = [part.reshape(-1, columns) for part in (own, low, high)]
-
-    partial = partial_products(parts, weights)
-    terms = exchange(partial, "x")
-    keys, values, partial = lax.optimization_barrier((keys, values, partial))
+    gathered = exchange(copies.reshape((32,) + copies.shape[2:]), ("x",) + Y).reshape(4 * TAPS, -1)
+
+    keys = after_these(keys, chip)
     mixed = (keys.astype(F32) * values.astype(F32)).astype(BF16)
     conv, turned = convolve(filters, from_behind(mixed, 1), mixed)
+    weights = weight_blocks(chip)
+    gathered = after_these(gathered, conv, *weights)
+    terms = exchange(partial_products(gathered, weights), "x")
     query_grad, conv_grad, lags = branch_gradients(terms, conv, query, turned)
     lags = summed_copies(exchange(lags, ("x", "co")))
     after = from_behind(conv_grad, -1)

time: 135 us -> 121 us (0.90)
  starting transfers between devices: 75.6 us -> 55.9 us
  blocking collectives: 13.5 us -> 19.6 us
    ppermute x2 -> x0, waiting for transfers between devices: 13.3 us -> none  [ahead(): lax.ppermute(block, axes, [((i + distance) % n, i) for i in range(n)])]
    ppermute x3, starting transfers between devices: 24.2 us -> 15.2 us  [swap(): return lax.ppermute(block, axis, [(0, 1), (1, 0)])]
    ppermute x3, waiting for transfers between devices: 3.91 us -> 11.6 us  [along_z(): return lax.ppermute(block, Z + ('co',), route)]
    ppermute x2 -> x0, starting transfers between devices: 6.78 us -> none  [ahead(): lax.ppermute(block, axes, [((i + distance) % n, i) for i in range(n)])]
    all_to_all x1 -> x2, blocking collectives: 13.5 us -> 19.6 us  [exchange(): return lax.all_to_all(copies, axes, split_axis=0, concat_axis=0)]
    ppermute x2, waiting for transfers between devices: 2.94 us -> 8.55 us  [from_behind(): return lax.ppermute(block, CONTEXT, route)]
    all_to_all x3 -> x2, starting transfers between devices: 20.5 us -> 15.7 us  [exchange(): return lax.all_to_all(copies, axes, split_axis=0, concat_axis=0)]
    ppermute x3, starting transfers between devices: 16.7 us -> 18.7 us  [along_z(): return lax.ppermute(block, Z + ('co',), route)]
  transfers between devices with their start and end apart: 13 -> 10, of which waited for: 7 -> 5; matrix products, arithmetic and copies ran while one was open for 1% -> 0% of each run, Pallas kernels for 4% -> 5%
where the time goes in v16:
time: 121 us; the launch traced here: 120 us
  starting transfers between devices  55.9 us (46%)
  waiting for transfers between devices  26.4 us (22%)
  blocking collectives  19.6 us (16%)
  Pallas kernels  12.4 us (10%)
  local copies, waits for them, and re-layouts  3.7 us (3%)
    all_to_all x2, blocking collectives, exchange(): return lax.all_to_all(copies, axes, split_axis=0, concat_axis=0)  19.6 us
    ppermute x3, starting transfers between devices, along_z(): return lax.ppermute(block, Z + ('co',), route)  18.7 us
    all_to_all x2, starting transfers between devices, exchange(): return lax.all_to_all(copies, axes, split_axis=0, concat_axis=0)  15.7 us
    ppermute x3, starting transfers between devices, swap(): return lax.ppermute(block, axis, [(0, 1), (1, 0)])  15.2 us
    ppermute x3, waiting for transfers between devices, along_z(): return lax.ppermute(block, Z + ('co',), route)  11.6 us
    ppermute x2, waiting for transfers between devices, from_behind(): return lax.ppermute(block, CONTEXT, route)  8.55 us
    ppermute x2, starting transfers between devices, from_behind(): return lax.ppermute(block, CONTEXT, route)  6.36 us
    all_to_all x2, waiting for transfers between devices, exchange(): return lax.all_to_all(copies, axes, split_axis=0, concat_axis=0)  5.33 us
  transfers between devices with their start and end apart: 10, of which 5 were waited for; matrix products, arithmetic and copies ran while one was open for 0% of the time, Pallas kernels for 5%

profile of v16, /device:TPU:1, one launch (start us, length us, event | category | flops | bytes accessed | tf_op | source)
XLA Modules:
  0.0 119.7 jit_solution(5614648151668261230)
XLA Ops:
  0.6 0.9 copy-done.3
  2.0 1.3 %copy-done = bf16[4,8,16,2048]{3,2,1,0:T(8,128)(2,1)} copy-done((bf16[4,8,16,2048]{3,2,1,0:T(8,128)(2,1)}, bf16[4,8,16,2048]{3,2,1,0:T(8,128)(2,1)S(1)}, u32[]{:S(2)}) %copy-start) | copy-done | bytes 2097176
  3.3 10.6 %all-to-all-start = ((bf16[32,16,2048]{2,1,0:T(8,128)(2,1)}), bf16[32,16,2048]{2,1,0:T(8,128)(2,1)S(1)}, u32[]{:S(2)}, u32[]{:S(2)}) async-start(bf16[32,16,2048]{2,1,0:T(8,128)(2,1)} %bitcast.18), calls=%async_computation | async-start | bytes 4194304 | tf_op jit(solution)/shard_map/all_to_all | solution.py:230
  14.0 3.0 %collective-permute-start = (bf16[128,512]{1,0:T(8,128)(2,1)S(1)}, bf16[128,512]{1,0:T(8,128)(2,1)S(1)}, u32[]{:S(2)}, u32[]{:S(2)}) collective-permute-start(bf16[128,512]{1,0:T(8,128)(2,1)S(1)} %copy-done.10), channel_id=1, source_target_pairs={{0,8},{8,0},{1,9},{9,1},{2,10},{10,2},{3,11},{11,3},{4,12},{12,4},... | collective-permute-start | bytes 393224 | tf_op jit(solution)/shard_map/ppermute | solution.py:24
  17.0 1.0 collective-permute-done
  18.0 10.7 %collective-permute-start.2 = (bf16[256,512]{1,0:T(8,128)(2,1)S(1)}, bf16[256,512]{1,0:T(8,128)(2,1)S(1)}, u32[]{:S(2)}, u32[]{:S(2)}) collective-permute-start(bf16[256,512]{1,0:T(8,128)(2,1)S(1)} %bitcast.19), channel_id=1, source_target_pairs={{0,16},{16,32},{32,48},{48,256},{256,272},{272,288},{288,304},{304... | collective-permute-start | bytes 786440 | tf_op jit(solution)/shard_map/ppermute | solution.py:241
  28.7 3.3 %collective-permute-done.2.refs_1_ = bf16[256,512]{1,0:T(8,128)(2,1)S(1)} collective-permute-done((bf16[256,512]{1,0:T(8,128)(2,1)S(1)}, bf16[256,512]{1,0:T(8,128)(2,1)S(1)}, u32[]{:S(2)}, u32[]{:S(2)}) %collective-permute-start.2) | collective-permute-done | bytes 262176 | tf_op jit(solution)/shard_map/ppermute | solution.py:241
  32.0 4.1 %collective-permute-start.5 = (bf16[512,512]{1,0:T(8,128)(2,1)S(1)}, bf16[512,512]{1,0:T(8,128)(2,1)S(1)}, u32[]{:S(2)}, u32[]{:S(2)}) collective-permute-start(bf16[512,512]{1,0:T(8,128)(2,1)S(1)} %pad_maximum_fusion), channel_id=1, source_target_pairs={{0,32},{16,48},{32,256},{48,272},{256,288},{272,304},{288,0},{304,... | collective-permute-start | bytes 1572872 | tf_op jit(solution)/shard_map/ppermute | solution.py:241
  36.1 8.3 %collective-permute-done.5.refs_4_ = bf16[512,512]{1,0:T(8,128)(2,1)S(1)} collective-permute-done((bf16[512,512]{1,0:T(8,128)(2,1)S(1)}, bf16[512,512]{1,0:T(8,128)(2,1)S(1)}, u32[]{:S(2)}, u32[]{:S(2)}) %collective-permute-start.5) | collective-permute-done | bytes 524320 | tf_op jit(solution)/shard_map/ppermute | solution.py:241
  44.4 10.0 %collective-permute-start.6 = (bf16[512,512]{1,0:T(8,128)(2,1)S(1)}, bf16[512,512]{1,0:T(8,128)(2,1)}, u32[]{:S(2)}, u32[]{:S(2)}) collective-permute-start(bf16[512,512]{1,0:T(8,128)(2,1)S(1)} %collective-permute-done.5.refs_4_), channel_id=1, source_target_pairs={{0,8},{8,0},{1,9},{9,1},{2,10},{10,2},{3,11},{11,3},{4,12},{12,4},... | collective-permute-start | bytes 1572872 | tf_op jit(solution)/shard_map/ppermute | solution.py:24
  54.4 3.9 %collective-permute-start.4 = (bf16[256,512]{1,0:T(8,128)(2,1)S(1)}, bf16[256,512]{1,0:T(8,128)(2,1)}, u32[]{:S(2)}, u32[]{:S(2)}) collective-permute-start(bf16[256,512]{1,0:T(8,128)(2,1)S(1)} %bitcast.21), channel_id=1, source_target_pairs={{0,256},{16,272},{32,288},{48,304},{256,0},{272,16},{288,32},{304,... | collective-permute-start | bytes 786440 | tf_op jit(solution)/shard_map/ppermute | solution.py:241
  58.3 2.2 %collective-permute-start.3 = (bf16[256,512]{1,0:T(8,128)(2,1)S(1)}, bf16[256,512]{1,0:T(8,128)(2,1)}, u32[]{:S(2)}, u32[]{:S(2)}) collective-permute-start(bf16[256,512]{1,0:T(8,128)(2,1)S(1)} %collective-permute-done.2.refs_1_), channel_id=1, source_target_pairs={{0,8},{8,0},{1,9},{9,1},{2,10},{10,2},{3,11},{11,3},{4,12},{12,4},... | collective-permute-start | bytes 786440 | tf_op jit(solution)/shard_map/ppermute | solution.py:24
  60.6 1.9 %collective-permute-start.1 = (bf16[128,512]{1,0:T(8,128)(2,1)S(1)}, bf16[128,512]{1,0:T(8,128)(2,1)}, u32[]{:S(2)}, u32[]{:S(2)}) collective-permute-start(bf16[128,512]{1,0:T(8,128)(2,1)S(1)} %multiply_convert_fusion.mixed_ref), channel_id=1, source_target_pairs={{0,8},{8,16},{16,24},{24,32},{32,40},{40,48},{48,56},{56,64},{64,7... | collective-permute-start | bytes 393224 | tf_op jit(solution)/shard_map/ppermute | solution.py:35
  62.6 8.5 %collective-permute-done.1.before_ref = bf16[128,512]{1,0:T(8,128)(2,1)} collective-permute-done((bf16[128,512]{1,0:T(8,128)(2,1)S(1)}, bf16[128,512]{1,0:T(8,128)(2,1)}, u32[]{:S(2)}, u32[]{:S(2)}) %collective-permute-start.1) | collective-permute-done | bytes 131104 | tf_op jit(solution)/shard_map/ppermute | solution.py:35
  71.2 3.2 %conv.1 = (f32[128,512]{1,0:T(8,128)S(1)}, bf16[256,512]{1,0:T(8,128)(2,1)S(1)}) custom-call(bf16[32,128]{1,0:T(8,128)(2,1)S(1)} %copy-done.9, bf16[128,512]{1,0:T(8,128)(2,1)} %collective-permute-done.1.before_ref, bf16[128,512]{1,0:T(8,128)(2,1)S(1)} %multiply_convert_fusion.mixed_ref), custom_call_target="tpu_custom_call" | custom-call | tf_op jit(solution)/shard_map/conv/pallas_call | solution.py:171
  74.4 0.7 copy-done.4
  75.8 2.7 %product.1 = bf16[4,128,512]{2,1,0:T(8,128)(2,1)S(1)} custom-call(s32[2]{0:T(128)S(1)} %pad_add_fusion.place_ref, bf16[512,2048]{1,0:T(8,128)(2,1)S(1)} %bitcast.17, bf16[256,512]{1,0:T(8,128)(2,1)S(1)} %bitcast.22, bf16[256,512]{1,0:T(8,128)(2,1)S(1)} %collective-permute-done.2.refs_1_, bf16[256,512]{1,0:T(8,128)(2,1)} %collective-permute-done.3.refs_2_, ...), custom_call_target="tpu_custom_call" | custom-call | tf_op jit(solution)/shard_map/product/pallas_call | solution.py:215
  78.6 12.0 %all_to_all.20.terms_ref = bf16[4,128,512]{2,1,0:T(8,128)(2,1)S(1)} all-to-all(bf16[4,128,512]{2,1,0:T(8,128)(2,1)S(1)} %product.1), channel_id=1, replica_groups=mesh['zh'=2,'x'=4,'zl'=4,'co'=2,'yq'=4,'yp'=2] {'x'}, dimensions={0} | all-to-all | bytes 1048576 | tf_op jit(solution)/shard_map/all_to_all | solution.py:230
  90.6 2.9 %branch.1 = (bf16[128,512]{1,0:T(8,128)(2,1)}, bf16[128,512]{1,0:T(8,128)(2,1)S(1)}, f32[8,32,128]{2,1,0:T(8,128)S(1)}) custom-call(bf16[4,128,512]{2,1,0:T(8,128)(2,1)S(1)} %all_to_all.20.terms_ref, f32[128,512]{1,0:T(8,128)S(1)} %copy-done.5, bf16[128,512]{1,0:T(8,128)(2,1)S(1)} %bitcast.27, bf16[256,512]{1,0:T(8,128)(2,1)S(1)} %copy-done.7), custom_call_target="tpu_custom_call" | custom-call | tf_op jit(solution)/shard_map/branch/pallas_call | solution.py:199
  93.5 4.4 %collective-permute-start.7 = (bf16[128,512]{1,0:T(8,128)(2,1)S(1)}, bf16[128,512]{1,0:T(8,128)(2,1)S(1)}, u32[]{:S(2)}, u32[]{:S(2)}) collective-permute-start(bf16[128,512]{1,0:T(8,128)(2,1)S(1)} %get-tuple-element.20.grad_ref), channel_id=1, source_target_pairs={{8,0},{16,8},{24,16},{32,24},{40,32},{48,40},{56,48},{64,56},{72,6... | collective-permute-start | bytes 393224 | tf_op jit(solution)/shard_map/ppermute | solution.py:35
  98.0 7.6 %all_to_all.21.parts_ref = f32[8,32,128]{2,1,0:T(8,128)S(1)} all-to-all(f32[8,32,128]{2,1,0:T(8,128)S(1)} %get-tuple-element.21), channel_id=1, replica_groups=mesh['zh'=2,'x'=4,'zl'=4,'co'=2,'yq'=4,'yp'=2] {'x','co'}, dimensions={0} | all-to-all | bytes 262144 | tf_op jit(solution)/shard_map/all_to_all | solution.py:230
  106.2 5.0 %all-to-all-start.3 = ((f32[8,32,128]{2,1,0:T(8,128)}), f32[8,32,128]{2,1,0:T(8,128)S(1)}, u32[]{:S(2)}, u32[]{:S(2)}) async-start(f32[8,32,128]{2,1,0:T(8,128)} %sums.1), calls=%async_computation.3 | async-start | bytes 262144 | tf_op jit(solution)/shard_map/all_to_all | solution.py:230
  111.3 2.5 %mixed_grad.1 = (bf16[128,512]{1,0:T(8,128)(2,1)}, bf16[128,512]{1,0:T(8,128)(2,1)}) custom-call(bf16[32,128]{1,0:T(8,128)(2,1)S(1)} %copy-done.9, bf16[128,512]{1,0:T(8,128)(2,1)S(1)} %get-tuple-element.20.grad_ref, bf16[128,512]{1,0:T(8,128)(2,1)S(1)} %collective-permute-done.7.after_ref, bf16[128,512]{1,0:T(8,128)(2,1)S(1)} %bitcast.24, ...), custom_call_target="tpu_custom_call" | custom-call | tf_op jit(solution)/shard_map/mixed_grad/pallas_call | solution.py:185
  113.8 5.3 %all-to-all-done.3 = f32[8,32,128]{2,1,0:T(8,128)S(1)} async-done(((f32[8,32,128]{2,1,0:T(8,128)}), f32[8,32,128]{2,1,0:T(8,128)S(1)}, u32[]{:S(2)}, u32[]{:S(2)}) %all-to-all-start.3) | async-done | bytes 131104 | tf_op jit(solution)/shard_map/all_to_all | solution.py:230
  (33 shorter events, 2.6 us)
Async XLA Ops:
  0.6 1.0 copy-start.3
  1.9 1.3 %copy-start = (bf16[4,8,16,2048]{3,2,1,0:T(8,128)(2,1)}, bf16[4,8,16,2048]{3,2,1,0:T(8,128)(2,1)S(1)}, u32[]{:S(2)}) copy-start(bf16[4,8,16,2048]{3,2,1,0:T(8,128)(2,1)S(1)} %spread.1) | copy-start | bytes 6291460
  3.3 10.6 %copy-start.10 = (bf16[128,512]{1,0:T(8,128)(2,1)S(1)}, bf16[128,512]{1,0:T(8,128)(2,1)}, u32[]{:S(2)}) copy-start(bf16[128,512]{1,0:T(8,128)(2,1)} %param.10) | copy-start | bytes 393220
  3.3 72.5 %all-to-all-start = ((bf16[32,16,2048]{2,1,0:T(8,128)(2,1)}), bf16[32,16,2048]{2,1,0:T(8,128)(2,1)S(1)}, u32[]{:S(2)}, u32[]{:S(2)}) async-start(bf16[32,16,2048]{2,1,0:T(8,128)(2,1)} %bitcast.18), calls=%async_computation | async-start | bytes 4194304 | tf_op jit(solution)/shard_map/all_to_all | solution.py:230
  13.9 46.6 %copy-start.1 = (bf16[1,128,512]{2,1,0:T(8,128)(2,1)S(1)}, bf16[1,128,512]{2,1,0:T(8,128)(2,1)}, u32[]{:S(2)}) copy-start(bf16[1,128,512]{2,1,0:T(8,128)(2,1)} %param.7) | copy-start | bytes 393220
  14.0 46.6 %copy-start.2 = (bf16[1,128,512]{2,1,0:T(8,128)(2,1)S(1)}, bf16[1,128,512]{2,1,0:T(8,128)(2,1)}, u32[]{:S(2)}) copy-start(bf16[1,128,512]{2,1,0:T(8,128)(2,1)} %param.8) | copy-start | bytes 393220
  14.0 57.2 %copy-start.9 = (bf16[32,128]{1,0:T(8,128)(2,1)S(1)}, bf16[32,128]{1,0:T(8,128)(2,1)}, u32[]{:S(2)}) copy-start(bf16[32,128]{1,0:T(8,128)(2,1)} %filters_ref.3) | copy-start | bytes 24580
  14.0 4.0 %collective-permute-start = (bf16[128,512]{1,0:T(8,128)(2,1)S(1)}, bf16[128,512]{1,0:T(8,128)(2,1)S(1)}, u32[]{:S(2)}, u32[]{:S(2)}) collective-permute-start(bf16[128,512]{1,0:T(8,128)(2,1)S(1)} %copy-done.10), channel_id=1, source_target_pairs={{0,8},{8,0},{1,9},{9,1},{2,10},{10,2},{3,11},{11,3},{4,12},{12,4},... | collective-permute-start | bytes 393224 | tf_op jit(solution)/shard_map/ppermute | solution.py:24
  18.0 14.0 %collective-permute-start.2 = (bf16[256,512]{1,0:T(8,128)(2,1)S(1)}, bf16[256,512]{1,0:T(8,128)(2,1)S(1)}, u32[]{:S(2)}, u32[]{:S(2)}) collective-permute-start(bf16[256,512]{1,0:T(8,128)(2,1)S(1)} %bitcast.19), channel_id=1, source_target_pairs={{0,16},{16,32},{32,48},{48,256},{256,272},{272,288},{288,304},{304... | collective-permute-start | bytes 786440 | tf_op jit(solution)/shard_map/ppermute | solution.py:241
  32.0 12.4 %collective-permute-start.5 = (bf16[512,512]{1,0:T(8,128)(2,1)S(1)}, bf16[512,512]{1,0:T(8,128)(2,1)S(1)}, u32[]{:S(2)}, u32[]{:S(2)}) collective-permute-start(bf16[512,512]{1,0:T(8,128)(2,1)S(1)} %pad_maximum_fusion), channel_id=1, source_target_pairs={{0,32},{16,48},{32,256},{48,272},{256,288},{272,304},{288,0},{304,... | collective-permute-start | bytes 1572872 | tf_op jit(solution)/shard_map/ppermute | solution.py:241
  44.4 31.4 %collective-permute-start.6 = (bf16[512,512]{1,0:T(8,128)(2,1)S(1)}, bf16[512,512]{1,0:T(8,128)(2,1)}, u32[]{:S(2)}, u32[]{:S(2)}) collective-permute-start(bf16[512,512]{1,0:T(8,128)(2,1)S(1)} %collective-permute-done.5.refs_4_), channel_id=1, source_target_pairs={{0,8},{8,0},{1,9},{9,1},{2,10},{10,2},{3,11},{11,3},{4,12},{12,4},... | collective-permute-start | bytes 1572872 | tf_op jit(solution)/shard_map/ppermute | solution.py:24
  54.4 21.4 %collective-permute-start.4 = (bf16[256,512]{1,0:T(8,128)(2,1)S(1)}, bf16[256,512]{1,0:T(8,128)(2,1)}, u32[]{:S(2)}, u32[]{:S(2)}) collective-permute-start(bf16[256,512]{1,0:T(8,128)(2,1)S(1)} %bitcast.21), channel_id=1, source_target_pairs={{0,256},{16,272},{32,288},{48,304},{256,0},{272,16},{288,32},{304,... | collective-permute-start | bytes 786440 | tf_op jit(solution)/shard_map/ppermute | solution.py:241
  58.3 17.5 %collective-permute-start.3 = (bf16[256,512]{1,0:T(8,128)(2,1)S(1)}, bf16[256,512]{1,0:T(8,128)(2,1)}, u32[]{:S(2)}, u32[]{:S(2)}) collective-permute-start(bf16[256,512]{1,0:T(8,128)(2,1)S(1)} %collective-permute-done.2.refs_1_), channel_id=1, source_target_pairs={{0,8},{8,0},{1,9},{9,1},{2,10},{10,2},{3,11},{11,3},{4,12},{12,4},... | collective-permute-start | bytes 786440 | tf_op jit(solution)/shard_map/ppermute | solution.py:24
  60.6 10.6 %collective-permute-start.1 = (bf16[128,512]{1,0:T(8,128)(2,1)S(1)}, bf16[128,512]{1,0:T(8,128)(2,1)}, u32[]{:S(2)}, u32[]{:S(2)}) collective-permute-start(bf16[128,512]{1,0:T(8,128)(2,1)S(1)} %multiply_convert_fusion.mixed_ref), channel_id=1, source_target_pairs={{0,8},{8,16},{16,24},{24,32},{32,40},{40,48},{48,56},{56,64},{64,7... | collective-permute-start | bytes 393224 | tf_op jit(solution)/shard_map/ppermute | solution.py:35
  74.4 0.7 copy-start.4
  75.1 0.7 copy-start.6
  75.8 14.8 %copy-start.5 = (f32[128,512]{1,0:T(8,128)S(1)}, f32[128,512]{1,0:T(8,128)}, u32[]{:S(2)}) copy-start(f32[128,512]{1,0:T(8,128)} %copy-done.4) | copy-start | bytes 786436
  75.8 14.8 %copy-start.7 = (bf16[256,512]{1,0:T(8,128)(2,1)S(1)}, bf16[256,512]{1,0:T(8,128)(2,1)}, u32[]{:S(2)}) copy-start(bf16[256,512]{1,0:T(8,128)(2,1)} %copy-done.6) | copy-start | bytes 786436
  75.8 14.7 %copy-start.8 = (bf16[1,128,512]{2,1,0:T(8,128)(2,1)S(1)}, bf16[1,128,512]{2,1,0:T(8,128)(2,1)}, u32[]{:S(2)}) copy-start(bf16[1,128,512]{2,1,0:T(8,128)(2,1)} %param.6) | copy-start | bytes 393220
  93.5 12.7 %collective-permute-start.7 = (bf16[128,512]{1,0:T(8,128)(2,1)S(1)}, bf16[128,512]{1,0:T(8,128)(2,1)S(1)}, u32[]{:S(2)}, u32[]{:S(2)}) collective-permute-start(bf16[128,512]{1,0:T(8,128)(2,1)S(1)} %get-tuple-element.20.grad_ref), channel_id=1, source_target_pairs={{8,0},{16,8},{24,16},{32,24},{40,32},{48,40},{56,48},{64,56},{72,6... | collective-permute-start | bytes 393224 | tf_op jit(solution)/shard_map/ppermute | solution.py:35
  106.2 12.9 %all-to-all-start.3 = ((f32[8,32,128]{2,1,0:T(8,128)}), f32[8,32,128]{2,1,0:T(8,128)S(1)}, u32[]{:S(2)}, u32[]{:S(2)}) async-start(f32[8,32,128]{2,1,0:T(8,128)} %sums.1), calls=%async_computation.3 | async-start | bytes 262144 | tf_op jit(solution)/shard_map/all_to_all | solution.py:230

commit v17 on v16

--- a/solution.py
+++ b/solution.py
@@ -241,10 +241,12 @@
     return lax.ppermute(block, Z + ("co",), route)
 
 
-def weight_blocks(chip):
+def weight_blocks(chip, beside):
     one, four = along_z(chip, 1), along_z(chip, 4)
     pair = along_z(jnp.concatenate([chip, one], 0), 2)
-    return [chip, one, swap(one, "co"), four, pair, swap(pair, "co")]
+    other = swap(one, "co")
+    pair = after_these(pair, four, other, beside)
+    return [chip, one, other, four, pair, swap(pair, "co")]
 
 
 def local(query_branch, key_branch, value_branch, cotangent, out_weight, filters):
@@ -257,7 +259,7 @@
     keys = after_these(keys, chip)
     mixed = (keys.astype(F32) * values.astype(F32)).astype(BF16)
     conv, turned = convolve(filters, from_behind(mixed, 1), mixed)
-    weights = weight_blocks(chip)
+    weights = weight_blocks(chip, conv)
     gathered = after_these(gathered, conv, *weights)
     terms = exchange(partial_products(gathered, weights), "x")
     query_grad, conv_grad, lags = branch_gradients(terms, conv, query, turned)

time: 121 us -> 117 us (0.967)
  the two profiles are of different devices: /device:TPU:1 before, /device:TPU:8 now
where the time goes in v17:
time: 117 us
  starting transfers between devices  38.7 us (33%)
  waiting for transfers between devices  33.4 us (29%)
  blocking collectives  24.6 us (21%)
  Pallas kernels  11.1 us (9%)
  local copies, waits for them, and re-layouts  7.08 us (6%)
    all_to_all x2, blocking collectives, exchange(): return lax.all_to_all(copies, axes, split_axis=0, concat_axis=0)  24.6 us
    ppermute x3, waiting for transfers between devices, along_z(): return lax.ppermute(block, Z + ('co',), route)  22.6 us
    all_to_all x2, starting transfers between devices, exchange(): return lax.all_to_all(copies, axes, split_axis=0, concat_axis=0)  16.7 us
    ppermute x3, starting transfers between devices, along_z(): return lax.ppermute(block, Z + ('co',), route)  12.5 us
    unnamed x30, local copies, waits for them, and re-layouts  7.08 us
    all_to_all x2, waiting for transfers between devices, exchange(): return lax.all_to_all(copies, axes, split_axis=0, concat_axis=0)  6.56 us
    ppermute x3, starting transfers between devices, swap(): return lax.ppermute(block, axis, [(0, 1), (1, 0)])  5.88 us
    ppermute x2, starting transfers between devices, from_behind(): return lax.ppermute(block, CONTEXT, route)  3.69 us
  transfers between devices with their start and end apart: 10, of which 6 were waited for; matrix products, arithmetic and copies ran while one was open for 0% of the time, Pallas kernels for 5%

profile of v17, /device:TPU:8, one launch (start us, length us, event | category | flops | bytes accessed | tf_op | source)
XLA Modules:
  0.0 116.5 jit_solution(3309923347727024587)
XLA Ops:
  2.0 1.3 %copy-done = bf16[4,8,16,2048]{3,2,1,0:T(8,128)(2,1)} copy-done((bf16[4,8,16,2048]{3,2,1,0:T(8,128)(2,1)}, bf16[4,8,16,2048]{3,2,1,0:T(8,128)(2,1)S(1)}, u32[]{:S(2)}) %copy-start) | copy-done | bytes 2097176
  3.3 10.3 %all-to-all-start = ((bf16[32,16,2048]{2,1,0:T(8,128)(2,1)}), bf16[32,16,2048]{2,1,0:T(8,128)(2,1)S(1)}, u32[]{:S(2)}, u32[]{:S(2)}) async-start(bf16[32,16,2048]{2,1,0:T(8,128)(2,1)} %bitcast.18), calls=%async_computation | async-start | bytes 4194304 | tf_op jit(solution)/shard_map/all_to_all | solution.py:230
  13.6 2.1 %collective-permute-start = (bf16[128,512]{1,0:T(8,128)(2,1)S(1)}, bf16[128,512]{1,0:T(8,128)(2,1)S(1)}, u32[]{:S(2)}, u32[]{:S(2)}) collective-permute-start(bf16[128,512]{1,0:T(8,128)(2,1)S(1)} %copy-done.14), channel_id=1, source_target_pairs={{0,8},{8,0},{1,9},{9,1},{2,10},{10,2},{3,11},{11,3},{4,12},{12,4},... | collective-permute-start | bytes 393224 | tf_op jit(solution)/shard_map/ppermute | solution.py:24
  15.7 1.3 %collective-permute-done = bf16[128,512]{1,0:T(8,128)(2,1)S(1)} collective-permute-done((bf16[128,512]{1,0:T(8,128)(2,1)S(1)}, bf16[128,512]{1,0:T(8,128)(2,1)S(1)}, u32[]{:S(2)}, u32[]{:S(2)}) %collective-permute-start) | collective-permute-done | bytes 131104 | tf_op jit(solution)/shard_map/ppermute | solution.py:24
  17.1 4.3 %collective-permute-start.2 = (bf16[256,512]{1,0:T(8,128)(2,1)S(1)}, bf16[256,512]{1,0:T(8,128)(2,1)S(1)}, u32[]{:S(2)}, u32[]{:S(2)}) collective-permute-start(bf16[256,512]{1,0:T(8,128)(2,1)S(1)} %bitcast.19), channel_id=1, source_target_pairs={{0,16},{16,32},{32,48},{48,256},{256,272},{272,288},{288,304},{304... | collective-permute-start | bytes 786440 | tf_op jit(solution)/shard_map/ppermute | solution.py:241
  21.4 11.0 %collective-permute-done.2.refs_1_ = bf16[256,512]{1,0:T(8,128)(2,1)S(1)} collective-permute-done((bf16[256,512]{1,0:T(8,128)(2,1)S(1)}, bf16[256,512]{1,0:T(8,128)(2,1)S(1)}, u32[]{:S(2)}, u32[]{:S(2)}) %collective-permute-start.2) | collective-permute-done | bytes 262176 | tf_op jit(solution)/shard_map/ppermute | solution.py:241
  32.4 1.9 %collective-permute-start.5 = (bf16[512,512]{1,0:T(8,128)(2,1)S(1)}, bf16[512,512]{1,0:T(8,128)(2,1)S(1)}, u32[]{:S(2)}, u32[]{:S(2)}) collective-permute-start(bf16[512,512]{1,0:T(8,128)(2,1)S(1)} %pad_maximum_fusion), channel_id=1, source_target_pairs={{0,32},{16,48},{32,256},{48,272},{256,288},{272,304},{288,0},{304,... | collective-permute-start | bytes 1572872 | tf_op jit(solution)/shard_map/ppermute | solution.py:241
  34.3 6.3 %collective-permute-start.4 = (bf16[256,512]{1,0:T(8,128)(2,1)S(1)}, bf16[256,512]{1,0:T(8,128)(2,1)S(1)}, u32[]{:S(2)}, u32[]{:S(2)}) collective-permute-start(bf16[256,512]{1,0:T(8,128)(2,1)S(1)} %bitcast.21), channel_id=1, source_target_pairs={{0,256},{16,272},{32,288},{48,304},{256,0},{272,16},{288,32},{304,... | collective-permute-start | bytes 786440 | tf_op jit(solution)/shard_map/ppermute | solution.py:241
  40.6 1.9 %collective-permute-start.3 = (bf16[256,512]{1,0:T(8,128)(2,1)S(1)}, bf16[256,512]{1,0:T(8,128)(2,1)S(1)}, u32[]{:S(2)}, u32[]{:S(2)}) collective-permute-start(bf16[256,512]{1,0:T(8,128)(2,1)S(1)} %collective-permute-done.2.refs_1_), channel_id=1, source_target_pairs={{0,8},{8,0},{1,9},{9,1},{2,10},{10,2},{3,11},{11,3},{4,12},{12,4},... | collective-permute-start | bytes 786440 | tf_op jit(solution)/shard_map/ppermute | solution.py:24
  42.6 2.4 %collective-permute-start.1 = (bf16[128,512]{1,0:T(8,128)(2,1)S(1)}, bf16[128,512]{1,0:T(8,128)(2,1)S(1)}, u32[]{:S(2)}, u32[]{:S(2)}) collective-permute-start(bf16[128,512]{1,0:T(8,128)(2,1)S(1)} %multiply_convert_fusion.mixed_ref), channel_id=1, source_target_pairs={{0,8},{8,16},{16,24},{24,32},{32,40},{40,48},{48,56},{56,64},{64,7... | collective-permute-start | bytes 393224 | tf_op jit(solution)/shard_map/ppermute | solution.py:35
  45.0 1.0 collective-permute-done.1.before_ref
  46.0 2.3 %conv.1 = (f32[128,512]{1,0:T(8,128)S(1)}, bf16[256,512]{1,0:T(8,128)(2,1)S(1)}) custom-call(bf16[32,128]{1,0:T(8,128)(2,1)S(1)} %copy-done.13, bf16[128,512]{1,0:T(8,128)(2,1)S(1)} %collective-permute-done.1.before_ref, bf16[128,512]{1,0:T(8,128)(2,1)S(1)} %multiply_convert_fusion.mixed_ref), custom_call_target="tpu_custom_call" | custom-call | tf_op jit(solution)/shard_map/conv/pallas_call | solution.py:171
  49.8 11.6 %collective-permute-done.4.refs_3_ = bf16[256,512]{1,0:T(8,128)(2,1)S(1)} collective-permute-done((bf16[256,512]{1,0:T(8,128)(2,1)S(1)}, bf16[256,512]{1,0:T(8,128)(2,1)S(1)}, u32[]{:S(2)}, u32[]{:S(2)}) %collective-permute-start.4) | collective-permute-done | bytes 262176 | tf_op jit(solution)/shard_map/ppermute | solution.py:241
  62.8 1.9 %collective-permute-start.6 = (bf16[512,512]{1,0:T(8,128)(2,1)S(1)}, bf16[512,512]{1,0:T(8,128)(2,1)}, u32[]{:S(2)}, u32[]{:S(2)}) collective-permute-start(bf16[512,512]{1,0:T(8,128)(2,1)S(1)} %collective-permute-done.5.refs_4_), channel_id=1, source_target_pairs={{0,8},{8,0},{1,9},{9,1},{2,10},{10,2},{3,11},{11,3},{4,12},{12,4},... | collective-permute-start | bytes 1572872 | tf_op jit(solution)/shard_map/ppermute | solution.py:24
  64.8 1.9 %collective-permute-done.6.refs_5_ = bf16[512,512]{1,0:T(8,128)(2,1)} collective-permute-done((bf16[512,512]{1,0:T(8,128)(2,1)S(1)}, bf16[512,512]{1,0:T(8,128)(2,1)}, u32[]{:S(2)}, u32[]{:S(2)}) %collective-permute-start.6) | collective-permute-done | bytes 524320 | tf_op jit(solution)/shard_map/ppermute | solution.py:24
  66.7 0.9 copy-done.5
  68.7 2.3 %product.1 = bf16[4,128,512]{2,1,0:T(8,128)(2,1)S(1)} custom-call(s32[2]{0:T(128)S(1)} %pad_add_fusion.place_ref, bf16[512,2048]{1,0:T(8,128)(2,1)S(1)} %bitcast.17, bf16[256,512]{1,0:T(8,128)(2,1)S(1)} %bitcast.22, bf16[256,512]{1,0:T(8,128)(2,1)S(1)} %collective-permute-done.2.refs_1_, bf16[256,512]{1,0:T(8,128)(2,1)S(1)} %copy-done.7, ...), custom_call_target="tpu_custom_call" | custom-call | tf_op jit(solution)/shard_map/product/pallas_call | solution.py:215
  70.9 15.5 %all_to_all.20.terms_ref = bf16[4,128,512]{2,1,0:T(8,128)(2,1)S(1)} all-to-all(bf16[4,128,512]{2,1,0:T(8,128)(2,1)S(1)} %product.1), channel_id=1, replica_groups=mesh['zh'=2,'x'=4,'zl'=4,'co'=2,'yq'=4,'yp'=2] {'x'}, dimensions={0} | all-to-all | bytes 1048576 | tf_op jit(solution)/shard_map/all_to_all | solution.py:230
  86.4 2.9 %branch.1 = (bf16[128,512]{1,0:T(8,128)(2,1)}, bf16[128,512]{1,0:T(8,128)(2,1)S(1)}, f32[8,32,128]{2,1,0:T(8,128)S(1)}) custom-call(bf16[4,128,512]{2,1,0:T(8,128)(2,1)S(1)} %all_to_all.20.terms_ref, f32[128,512]{1,0:T(8,128)S(1)} %copy-done.9, bf16[128,512]{1,0:T(8,128)(2,1)S(1)} %bitcast.27, bf16[256,512]{1,0:T(8,128)(2,1)S(1)} %copy-done.11), custom_call_target="tpu_custom_call" | custom-call | tf_op jit(solution)/shard_map/branch/pallas_call | solution.py:199
  89.3 1.3 %collective-permute-start.7 = (bf16[128,512]{1,0:T(8,128)(2,1)S(1)}, bf16[128,512]{1,0:T(8,128)(2,1)S(1)}, u32[]{:S(2)}, u32[]{:S(2)}) collective-permute-start(bf16[128,512]{1,0:T(8,128)(2,1)S(1)} %get-tuple-element.22.grad_ref), channel_id=1, source_target_pairs={{8,0},{16,8},{24,16},{32,24},{40,32},{48,40},{56,48},{64,56},{72,6... | collective-permute-start | bytes 393224 | tf_op jit(solution)/shard_map/ppermute | solution.py:35
  90.6 9.1 %all_to_all.21.parts_ref = f32[8,32,128]{2,1,0:T(8,128)S(1)} all-to-all(f32[8,32,128]{2,1,0:T(8,128)S(1)} %get-tuple-element.23), channel_id=1, replica_groups=mesh['zh'=2,'x'=4,'zl'=4,'co'=2,'yq'=4,'yp'=2] {'x','co'}, dimensions={0} | all-to-all | bytes 262144 | tf_op jit(solution)/shard_map/all_to_all | solution.py:230
  100.4 6.4 %all-to-all-start.3 = ((f32[8,32,128]{2,1,0:T(8,128)}), f32[8,32,128]{2,1,0:T(8,128)S(1)}, u32[]{:S(2)}, u32[]{:S(2)}) async-start(f32[8,32,128]{2,1,0:T(8,128)} %sums.1), calls=%async_computation.3 | async-start | bytes 262144 | tf_op jit(solution)/shard_map/all_to_all | solution.py:230
  106.8 2.5 %mixed_grad.1 = (bf16[128,512]{1,0:T(8,128)(2,1)}, bf16[128,512]{1,0:T(8,128)(2,1)}) custom-call(bf16[32,128]{1,0:T(8,128)(2,1)S(1)} %copy-done.13, bf16[128,512]{1,0:T(8,128)(2,1)S(1)} %get-tuple-element.22.grad_ref, bf16[128,512]{1,0:T(8,128)(2,1)S(1)} %collective-permute-done.7.after_ref, bf16[128,512]{1,0:T(8,128)(2,1)S(1)} %bitcast.24, ...), custom_call_target="tpu_custom_call" | custom-call | tf_op jit(solution)/shard_map/mixed_grad/pallas_call | solution.py:185
  109.4 6.6 %all-to-all-done.3 = f32[8,32,128]{2,1,0:T(8,128)S(1)} async-done(((f32[8,32,128]{2,1,0:T(8,128)}), f32[8,32,128]{2,1,0:T(8,128)S(1)}, u32[]{:S(2)}, u32[]{:S(2)}) %all-to-all-start.3) | async-done | bytes 131104 | tf_op jit(solution)/shard_map/all_to_all | solution.py:230
  (41 shorter events, 6.7 us)
Async XLA Ops:
  0.6 1.0 copy-start.3
  1.9 1.3 %copy-start = (bf16[4,8,16,2048]{3,2,1,0:T(8,128)(2,1)}, bf16[4,8,16,2048]{3,2,1,0:T(8,128)(2,1)S(1)}, u32[]{:S(2)}) copy-start(bf16[4,8,16,2048]{3,2,1,0:T(8,128)(2,1)S(1)} %spread.1) | copy-start | bytes 6291460
  3.3 10.3 %copy-start.14 = (bf16[128,512]{1,0:T(8,128)(2,1)S(1)}, bf16[128,512]{1,0:T(8,128)(2,1)}, u32[]{:S(2)}) copy-start(bf16[128,512]{1,0:T(8,128)(2,1)} %param.10) | copy-start | bytes 393220
  3.3 63.4 %all-to-all-start = ((bf16[32,16,2048]{2,1,0:T(8,128)(2,1)}), bf16[32,16,2048]{2,1,0:T(8,128)(2,1)S(1)}, u32[]{:S(2)}, u32[]{:S(2)}) async-start(bf16[32,16,2048]{2,1,0:T(8,128)(2,1)} %bitcast.18), calls=%async_computation | async-start | bytes 4194304 | tf_op jit(solution)/shard_map/all_to_all | solution.py:230
  13.6 28.9 %copy-start.1 = (bf16[1,128,512]{2,1,0:T(8,128)(2,1)S(1)}, bf16[1,128,512]{2,1,0:T(8,128)(2,1)}, u32[]{:S(2)}) copy-start(bf16[1,128,512]{2,1,0:T(8,128)(2,1)} %param.7) | copy-start | bytes 393220
  13.6 28.9 %copy-start.2 = (bf16[1,128,512]{2,1,0:T(8,128)(2,1)S(1)}, bf16[1,128,512]{2,1,0:T(8,128)(2,1)}, u32[]{:S(2)}) copy-start(bf16[1,128,512]{2,1,0:T(8,128)(2,1)} %param.8) | copy-start | bytes 393220
  13.6 32.3 %copy-start.13 = (bf16[32,128]{1,0:T(8,128)(2,1)S(1)}, bf16[32,128]{1,0:T(8,128)(2,1)}, u32[]{:S(2)}) copy-start(bf16[32,128]{1,0:T(8,128)(2,1)} %filters_ref.3) | copy-start | bytes 24580
  13.6 3.4 %collective-permute-start = (bf16[128,512]{1,0:T(8,128)(2,1)S(1)}, bf16[128,512]{1,0:T(8,128)(2,1)S(1)}, u32[]{:S(2)}, u32[]{:S(2)}) collective-permute-start(bf16[128,512]{1,0:T(8,128)(2,1)S(1)} %copy-done.14), channel_id=1, source_target_pairs={{0,8},{8,0},{1,9},{9,1},{2,10},{10,2},{3,11},{11,3},{4,12},{12,4},... | collective-permute-start | bytes 393224 | tf_op jit(solution)/shard_map/ppermute | solution.py:24
  17.1 15.3 %collective-permute-start.2 = (bf16[256,512]{1,0:T(8,128)(2,1)S(1)}, bf16[256,512]{1,0:T(8,128)(2,1)S(1)}, u32[]{:S(2)}, u32[]{:S(2)}) collective-permute-start(bf16[256,512]{1,0:T(8,128)(2,1)S(1)} %bitcast.19), channel_id=1, source_target_pairs={{0,16},{16,32},{32,48},{48,256},{256,272},{272,288},{288,304},{304... | collective-permute-start | bytes 786440 | tf_op jit(solution)/shard_map/ppermute | solution.py:241
  32.4 30.4 %collective-permute-start.5 = (bf16[512,512]{1,0:T(8,128)(2,1)S(1)}, bf16[512,512]{1,0:T(8,128)(2,1)S(1)}, u32[]{:S(2)}, u32[]{:S(2)}) collective-permute-start(bf16[512,512]{1,0:T(8,128)(2,1)S(1)} %pad_maximum_fusion), channel_id=1, source_target_pairs={{0,32},{16,48},{32,256},{48,272},{256,288},{272,304},{288,0},{304,... | collective-permute-start | bytes 1572872 | tf_op jit(solution)/shard_map/ppermute | solution.py:241
  34.3 27.0 %collective-permute-start.4 = (bf16[256,512]{1,0:T(8,128)(2,1)S(1)}, bf16[256,512]{1,0:T(8,128)(2,1)S(1)}, u32[]{:S(2)}, u32[]{:S(2)}) collective-permute-start(bf16[256,512]{1,0:T(8,128)(2,1)S(1)} %bitcast.21), channel_id=1, source_target_pairs={{0,256},{16,272},{32,288},{48,304},{256,0},{272,16},{288,32},{304,... | collective-permute-start | bytes 786440 | tf_op jit(solution)/shard_map/ppermute | solution.py:241
  40.6 21.5 %collective-permute-start.3 = (bf16[256,512]{1,0:T(8,128)(2,1)S(1)}, bf16[256,512]{1,0:T(8,128)(2,1)S(1)}, u32[]{:S(2)}, u32[]{:S(2)}) collective-permute-start(bf16[256,512]{1,0:T(8,128)(2,1)S(1)} %collective-permute-done.2.refs_1_), channel_id=1, source_target_pairs={{0,8},{8,0},{1,9},{9,1},{2,10},{10,2},{3,11},{11,3},{4,12},{12,4},... | collective-permute-start | bytes 786440 | tf_op jit(solution)/shard_map/ppermute | solution.py:24
  42.6 3.4 %collective-permute-start.1 = (bf16[128,512]{1,0:T(8,128)(2,1)S(1)}, bf16[128,512]{1,0:T(8,128)(2,1)S(1)}, u32[]{:S(2)}, u32[]{:S(2)}) collective-permute-start(bf16[128,512]{1,0:T(8,128)(2,1)S(1)} %multiply_convert_fusion.mixed_ref), channel_id=1, source_target_pairs={{0,8},{8,16},{16,24},{24,32},{32,40},{40,48},{48,56},{56,64},{64,7... | collective-permute-start | bytes 393224 | tf_op jit(solution)/shard_map/ppermute | solution.py:35
  48.3 0.7 copy-start.8
  49.0 0.7 copy-start.10
  61.4 0.7 copy-start.4
  62.8 3.9 %collective-permute-start.6 = (bf16[512,512]{1,0:T(8,128)(2,1)S(1)}, bf16[512,512]{1,0:T(8,128)(2,1)}, u32[]{:S(2)}, u32[]{:S(2)}) collective-permute-start(bf16[512,512]{1,0:T(8,128)(2,1)S(1)} %collective-permute-done.5.refs_4_), channel_id=1, source_target_pairs={{0,8},{8,0},{1,9},{9,1},{2,10},{10,2},{3,11},{11,3},{4,12},{12,4},... | collective-permute-start | bytes 1572872 | tf_op jit(solution)/shard_map/ppermute | solution.py:24
  66.7 1.0 copy-start.5
  67.7 0.9 copy-start.7
  68.6 17.8 %copy-start.9 = (f32[128,512]{1,0:T(8,128)S(1)}, f32[128,512]{1,0:T(8,128)}, u32[]{:S(2)}) copy-start(f32[128,512]{1,0:T(8,128)} %copy-done.8) | copy-start | bytes 786436
  68.6 17.8 %copy-start.11 = (bf16[256,512]{1,0:T(8,128)(2,1)S(1)}, bf16[256,512]{1,0:T(8,128)(2,1)}, u32[]{:S(2)}) copy-start(bf16[256,512]{1,0:T(8,128)(2,1)} %copy-done.10) | copy-start | bytes 786436
  68.6 17.8 %copy-start.12 = (bf16[1,128,512]{2,1,0:T(8,128)(2,1)S(1)}, bf16[1,128,512]{2,1,0:T(8,128)(2,1)}, u32[]{:S(2)}) copy-start(bf16[1,128,512]{2,1,0:T(8,128)(2,1)} %param.6) | copy-start | bytes 393220
  89.3 11.1 %collective-permute-start.7 = (bf16[128,512]{1,0:T(8,128)(2,1)S(1)}, bf16[128,512]{1,0:T(8,128)(2,1)S(1)}, u32[]{:S(2)}, u32[]{:S(2)}) collective-permute-start(bf16[128,512]{1,0:T(8,128)(2,1)S(1)} %get-tuple-element.22.grad_ref), channel_id=1, source_target_pairs={{8,0},{16,8},{24,16},{32,24},{40,32},{48,40},{56,48},{64,56},{72,6... | collective-permute-start | bytes 393224 | tf_op jit(solution)/shard_map/ppermute | solution.py:35
  100.4 15.5 %all-to-all-start.3 = ((f32[8,32,128]{2,1,0:T(8,128)}), f32[8,32,128]{2,1,0:T(8,128)S(1)}, u32[]{:S(2)}, u32[]{:S(2)}) async-start(f32[8,32,128]{2,1,0:T(8,128)} %sums.1), calls=%async_computation.3 | async-start | bytes 262144 | tf_op jit(solution)/shard_map/all_to_all | solution.py:230
  (1 other events, 0.7 us)

commit v18 on v16

--- a/solution.py
+++ b/solution.py
@@ -17,7 +17,8 @@
 Z = ("zh", "zl")
 CONTEXT = ("x", "zl", "co")
 Y = ("yq", "yp")
-VMEM = pltpu.CompilerParams(vmem_limit_bytes=8 * 1024 * 1024)
+VMEM = pltpu.CompilerParams(vmem_limit_bytes=3 * 1024 * 1024)
+PRODUCT_VMEM = pltpu.CompilerParams(vmem_limit_bytes=8 * 1024 * 1024)
 
 
 def swap(block, axis):
@@ -221,7 +222,7 @@
         scratch_shapes=[pltpu.VMEM((4, TAPS, width), F32)]
         + [pltpu.VMEM(a.shape, a.dtype) for a in weights]
         + [pltpu.SemaphoreType.DMA((len(weights),))],
-        compiler_params=VMEM,
+        compiler_params=PRODUCT_VMEM,
         name="product",
     )(place, cotangent, *weights)
 
@@ -239,12 +240,6 @@
     route = [(2 * i, 2 * ((i + steps) % n)) for i in range(n)]
     route += [(2 * i + 1, 2 * ((i - steps) % n) + 1) for i in range(n)]
     return lax.ppermute(block, Z + ("co",), route)
-
-
-def weight_blocks(chip):
-    one, four = along_z(chip, 1), along_z(chip, 4)
-    pair = along_z(jnp.concatenate([chip, one], 0), 2)
-    return [chip, one, swap(one, "co"), four, pair, swap(pair, "co")]
 
 
 def local(query_branch, key_branch, value_branch, cotangent, out_weight, filters):
@@ -254,10 +249,14 @@
     copies = spread(cotangent[0])
     gathered = exchange(copies.reshape((32,) + copies.shape[2:]), ("x",) + Y).reshape(4 * TAPS, -1)
 
-    keys = after_these(keys, chip)
+    one, four = along_z(chip, 1), along_z(chip, 4)
+    keys = after_these(keys, four)
     mixed = (keys.astype(F32) * values.astype(F32)).astype(BF16)
     conv, turned = convolve(filters, from_behind(mixed, 1), mixed)
-    weights = weight_blocks(chip)
+    pair = along_z(jnp.concatenate([chip, one], 0), 2)
+    other = swap(one, "co")
+    pair = after_these(pair, other, conv)
+    weights = [chip, one, other, four, pair, swap(pair, "co")]
     gathered = after_these(gathered, conv, *weights)
     terms = exchange(partial_products(gathered, weights), "x")
     query_grad, conv_grad, lags = branch_gradients(terms, conv, query, turned)

time: 121 us -> 117 us (0.967)
  the two profiles are of different devices: /device:TPU:1 before, /device:TPU:8 now
where the time goes in v18:
time: 117 us
  starting transfers between devices  56.5 us (48%)
  blocking collectives  25.7 us (22%)
  waiting for transfers between devices  15.3 us (13%)
  Pallas kernels  11.1 us (9%)
  local copies, waits for them, and re-layouts  6.38 us (5%)
    all_to_all x2, blocking collectives, exchange(): return lax.all_to_all(copies, axes, split_axis=0, concat_axis=0)  25.7 us
    ppermute x3, starting transfers between devices, swap(): return lax.ppermute(block, axis, [(0, 1), (1, 0)])  19 us
    all_to_all x2, starting transfers between devices, exchange(): return lax.all_to_all(copies, axes, split_axis=0, concat_axis=0)  17.9 us
    ppermute x3, starting transfers between devices, along_z(): return lax.ppermute(block, Z + ('co',), route)  16.5 us
    all_to_all x2, waiting for transfers between devices, exchange(): return lax.all_to_all(copies, axes, split_axis=0, concat_axis=0)  6.56 us
    unnamed x30, local copies, waits for them, and re-layouts  6.38 us
    ppermute x3, waiting for transfers between devices, along_z(): return lax.ppermute(block, Z + ('co',), route)  4.86 us
    ppermute x2, starting transfers between devices, from_behind(): return lax.ppermute(block, CONTEXT, route)  3.2 us
  transfers between devices with their start and end apart: 10, of which 7 were waited for; matrix products, arithmetic and copies ran while one was open for 0% of the time, Pallas kernels for 5%

profile of v18, /device:TPU:8, one launch (start us, length us, event | category | flops | bytes accessed | tf_op | source)
XLA Modules:
  0.0 116.5 jit_solution(7304472245507304502)
XLA Ops:
  2.0 1.3 %copy-done = bf16[4,8,16,2048]{3,2,1,0:T(8,128)(2,1)} copy-done((bf16[4,8,16,2048]{3,2,1,0:T(8,128)(2,1)}, bf16[4,8,16,2048]{3,2,1,0:T(8,128)(2,1)S(1)}, u32[]{:S(2)}) %copy-start) | copy-done | bytes 2097176
  3.3 10.3 %all-to-all-start = ((bf16[32,16,2048]{2,1,0:T(8,128)(2,1)}), bf16[32,16,2048]{2,1,0:T(8,128)(2,1)S(1)}, u32[]{:S(2)}, u32[]{:S(2)}) async-start(bf16[32,16,2048]{2,1,0:T(8,128)(2,1)} %bitcast.18), calls=%async_computation | async-start | bytes 4194304 | tf_op jit(solution)/shard_map/all_to_all | solution.py:231
  13.6 2.1 %collective-permute-start = (bf16[128,512]{1,0:T(8,128)(2,1)S(1)}, bf16[128,512]{1,0:T(8,128)(2,1)S(1)}, u32[]{:S(2)}, u32[]{:S(2)}) collective-permute-start(bf16[128,512]{1,0:T(8,128)(2,1)S(1)} %copy-done.14), channel_id=1, source_target_pairs={{0,8},{8,0},{1,9},{9,1},{2,10},{10,2},{3,11},{11,3},{4,12},{12,4},... | collective-permute-start | bytes 393224 | tf_op jit(solution)/shard_map/ppermute | solution.py:25
  15.7 1.3 %collective-permute-done = bf16[128,512]{1,0:T(8,128)(2,1)S(1)} collective-permute-done((bf16[128,512]{1,0:T(8,128)(2,1)S(1)}, bf16[128,512]{1,0:T(8,128)(2,1)S(1)}, u32[]{:S(2)}, u32[]{:S(2)}) %collective-permute-start) | collective-permute-done | bytes 131104 | tf_op jit(solution)/shard_map/ppermute | solution.py:25
  17.1 4.3 %collective-permute-start.3 = (bf16[256,512]{1,0:T(8,128)(2,1)S(1)}, bf16[256,512]{1,0:T(8,128)(2,1)S(1)}, u32[]{:S(2)}, u32[]{:S(2)}) collective-permute-start(bf16[256,512]{1,0:T(8,128)(2,1)S(1)} %bitcast.19), channel_id=1, source_target_pairs={{0,16},{16,32},{32,48},{48,256},{256,272},{272,288},{288,304},{304... | collective-permute-start | bytes 786440 | tf_op jit(solution)/shard_map/ppermute | solution.py:242
  21.4 10.0 %collective-permute-start.1 = (bf16[256,512]{1,0:T(8,128)(2,1)S(1)}, bf16[256,512]{1,0:T(8,128)(2,1)S(1)}, u32[]{:S(2)}, u32[]{:S(2)}) collective-permute-start(bf16[256,512]{1,0:T(8,128)(2,1)S(1)} %bitcast.20), channel_id=1, source_target_pairs={{0,256},{16,272},{32,288},{48,304},{256,0},{272,16},{288,32},{304,... | collective-permute-start | bytes 786440 | tf_op jit(solution)/shard_map/ppermute | solution.py:242
  31.4 2.1 %collective-permute-done.3.refs_1_ = bf16[256,512]{1,0:T(8,128)(2,1)S(1)} collective-permute-done((bf16[256,512]{1,0:T(8,128)(2,1)S(1)}, bf16[256,512]{1,0:T(8,128)(2,1)S(1)}, u32[]{:S(2)}, u32[]{:S(2)}) %collective-permute-start.3) | collective-permute-done | bytes 262176 | tf_op jit(solution)/shard_map/ppermute | solution.py:242
  33.6 2.2 %collective-permute-start.5 = (bf16[512,512]{1,0:T(8,128)(2,1)S(1)}, bf16[512,512]{1,0:T(8,128)(2,1)S(1)}, u32[]{:S(2)}, u32[]{:S(2)}) collective-permute-start(bf16[512,512]{1,0:T(8,128)(2,1)S(1)} %pad_maximum_fusion), channel_id=1, source_target_pairs={{0,32},{16,48},{32,256},{48,272},{256,288},{272,304},{288,0},{304,... | collective-permute-start | bytes 1572872 | tf_op jit(solution)/shard_map/ppermute | solution.py:242
  35.7 2.0 %collective-permute-done.1.refs_3_ = bf16[256,512]{1,0:T(8,128)(2,1)S(1)} collective-permute-done((bf16[256,512]{1,0:T(8,128)(2,1)S(1)}, bf16[256,512]{1,0:T(8,128)(2,1)S(1)}, u32[]{:S(2)}, u32[]{:S(2)}) %collective-permute-start.1) | collective-permute-done | bytes 262176 | tf_op jit(solution)/shard_map/ppermute | solution.py:242
  37.8 4.9 %collective-permute-start.4 = (bf16[256,512]{1,0:T(8,128)(2,1)S(1)}, bf16[256,512]{1,0:T(8,128)(2,1)S(1)}, u32[]{:S(2)}, u32[]{:S(2)}) collective-permute-start(bf16[256,512]{1,0:T(8,128)(2,1)S(1)} %collective-permute-done.3.refs_1_), channel_id=1, source_target_pairs={{0,8},{8,0},{1,9},{9,1},{2,10},{10,2},{3,11},{11,3},{4,12},{12,4},... | collective-permute-start | bytes 786440 | tf_op jit(solution)/shard_map/ppermute | solution.py:25
  42.8 1.9 %collective-permute-start.2 = (bf16[128,512]{1,0:T(8,128)(2,1)S(1)}, bf16[128,512]{1,0:T(8,128)(2,1)S(1)}, u32[]{:S(2)}, u32[]{:S(2)}) collective-permute-start(bf16[128,512]{1,0:T(8,128)(2,1)S(1)} %multiply_convert_fusion.mixed_ref), channel_id=1, source_target_pairs={{0,8},{8,16},{16,24},{24,32},{32,40},{40,48},{48,56},{56,64},{64,7... | collective-permute-start | bytes 393224 | tf_op jit(solution)/shard_map/ppermute | solution.py:36
  44.7 1.0 collective-permute-done.2.before_ref
  45.7 2.3 %conv.1 = (f32[128,512]{1,0:T(8,128)S(1)}, bf16[256,512]{1,0:T(8,128)(2,1)S(1)}) custom-call(bf16[32,128]{1,0:T(8,128)(2,1)S(1)} %copy-done.13, bf16[128,512]{1,0:T(8,128)(2,1)S(1)} %collective-permute-done.2.before_ref, bf16[128,512]{1,0:T(8,128)(2,1)S(1)} %multiply_convert_fusion.mixed_ref), custom_call_target="tpu_custom_call" | custom-call | tf_op jit(solution)/shard_map/conv/pallas_call | solution.py:172
  50.9 12.0 %collective-permute-start.6 = (bf16[512,512]{1,0:T(8,128)(2,1)S(1)}, bf16[512,512]{1,0:T(8,128)(2,1)}, u32[]{:S(2)}, u32[]{:S(2)}) collective-permute-start(bf16[512,512]{1,0:T(8,128)(2,1)S(1)} %collective-permute-done.5.refs_4_), channel_id=1, source_target_pairs={{0,8},{8,0},{1,9},{9,1},{2,10},{10,2},{3,11},{11,3},{4,12},{12,4},... | collective-permute-start | bytes 1572872 | tf_op jit(solution)/shard_map/ppermute | solution.py:25
  62.9 1.6 %collective-permute-done.6.refs_5_ = bf16[512,512]{1,0:T(8,128)(2,1)} collective-permute-done((bf16[512,512]{1,0:T(8,128)(2,1)S(1)}, bf16[512,512]{1,0:T(8,128)(2,1)}, u32[]{:S(2)}, u32[]{:S(2)}) %collective-permute-start.6) | collective-permute-done | bytes 524320 | tf_op jit(solution)/shard_map/ppermute | solution.py:25
  64.5 0.9 copy-done.5
  66.4 2.3 %product.1 = bf16[4,128,512]{2,1,0:T(8,128)(2,1)S(1)} custom-call(s32[2]{0:T(128)S(1)} %pad_add_fusion.place_ref, bf16[512,2048]{1,0:T(8,128)(2,1)S(1)} %bitcast.17, bf16[256,512]{1,0:T(8,128)(2,1)S(1)} %bitcast.22, bf16[256,512]{1,0:T(8,128)(2,1)S(1)} %collective-permute-done.3.refs_1_, bf16[256,512]{1,0:T(8,128)(2,1)S(1)} %copy-done.7, ...), custom_call_target="tpu_custom_call" | custom-call | tf_op jit(solution)/shard_map/product/pallas_call | solution.py:216
  68.7 15.0 %all_to_all.20.terms_ref = bf16[4,128,512]{2,1,0:T(8,128)(2,1)S(1)} all-to-all(bf16[4,128,512]{2,1,0:T(8,128)(2,1)S(1)} %product.1), channel_id=1, replica_groups=mesh['zh'=2,'x'=4,'zl'=4,'co'=2,'yq'=4,'yp'=2] {'x'}, dimensions={0} | all-to-all | bytes 1048576 | tf_op jit(solution)/shard_map/all_to_all | solution.py:231
  83.7 2.9 %branch.1 = (bf16[128,512]{1,0:T(8,128)(2,1)}, bf16[128,512]{1,0:T(8,128)(2,1)S(1)}, f32[8,32,128]{2,1,0:T(8,128)S(1)}) custom-call(bf16[4,128,512]{2,1,0:T(8,128)(2,1)S(1)} %all_to_all.20.terms_ref, f32[128,512]{1,0:T(8,128)S(1)} %copy-done.9, bf16[128,512]{1,0:T(8,128)(2,1)S(1)} %bitcast.27, bf16[256,512]{1,0:T(8,128)(2,1)S(1)} %copy-done.11), custom_call_target="tpu_custom_call" | custom-call | tf_op jit(solution)/shard_map/branch/pallas_call | solution.py:200
  86.6 1.3 %collective-permute-start.7 = (bf16[128,512]{1,0:T(8,128)(2,1)S(1)}, bf16[128,512]{1,0:T(8,128)(2,1)S(1)}, u32[]{:S(2)}, u32[]{:S(2)}) collective-permute-start(bf16[128,512]{1,0:T(8,128)(2,1)S(1)} %get-tuple-element.22.grad_ref), channel_id=1, source_target_pairs={{8,0},{16,8},{24,16},{32,24},{40,32},{48,40},{56,48},{64,56},{72,6... | collective-permute-start | bytes 393224 | tf_op jit(solution)/shard_map/ppermute | solution.py:36
  87.9 10.7 %all_to_all.21.parts_ref = f32[8,32,128]{2,1,0:T(8,128)S(1)} all-to-all(f32[8,32,128]{2,1,0:T(8,128)S(1)} %get-tuple-element.23), channel_id=1, replica_groups=mesh['zh'=2,'x'=4,'zl'=4,'co'=2,'yq'=4,'yp'=2] {'x','co'}, dimensions={0} | all-to-all | bytes 262144 | tf_op jit(solution)/shard_map/all_to_all | solution.py:231
  99.3 7.6 %all-to-all-start.3 = ((f32[8,32,128]{2,1,0:T(8,128)}), f32[8,32,128]{2,1,0:T(8,128)S(1)}, u32[]{:S(2)}, u32[]{:S(2)}) async-start(f32[8,32,128]{2,1,0:T(8,128)} %sums.1), calls=%async_computation.3 | async-start | bytes 262144 | tf_op jit(solution)/shard_map/all_to_all | solution.py:231
  106.8 2.5 %mixed_grad.1 = (bf16[128,512]{1,0:T(8,128)(2,1)}, bf16[128,512]{1,0:T(8,128)(2,1)}) custom-call(bf16[32,128]{1,0:T(8,128)(2,1)S(1)} %copy-done.13, bf16[128,512]{1,0:T(8,128)(2,1)S(1)} %get-tuple-element.22.grad_ref, bf16[128,512]{1,0:T(8,128)(2,1)S(1)} %collective-permute-done.7.after_ref, bf16[128,512]{1,0:T(8,128)(2,1)S(1)} %bitcast.24, ...), custom_call_target="tpu_custom_call" | custom-call | tf_op jit(solution)/shard_map/mixed_grad/pallas_call | solution.py:186
  109.4 6.6 %all-to-all-done.3 = f32[8,32,128]{2,1,0:T(8,128)S(1)} async-done(((f32[8,32,128]{2,1,0:T(8,128)}), f32[8,32,128]{2,1,0:T(8,128)S(1)}, u32[]{:S(2)}, u32[]{:S(2)}) %all-to-all-start.3) | async-done | bytes 131104 | tf_op jit(solution)/shard_map/all_to_all | solution.py:231
  (41 shorter events, 6.6 us)
Async XLA Ops:
  0.6 1.0 copy-start.3
  1.9 1.3 %copy-start = (bf16[4,8,16,2048]{3,2,1,0:T(8,128)(2,1)}, bf16[4,8,16,2048]{3,2,1,0:T(8,128)(2,1)S(1)}, u32[]{:S(2)}) copy-start(bf16[4,8,16,2048]{3,2,1,0:T(8,128)(2,1)S(1)} %spread.1) | copy-start | bytes 6291460
  3.3 10.3 %copy-start.14 = (bf16[128,512]{1,0:T(8,128)(2,1)S(1)}, bf16[128,512]{1,0:T(8,128)(2,1)}, u32[]{:S(2)}) copy-start(bf16[128,512]{1,0:T(8,128)(2,1)} %param.10) | copy-start | bytes 393220
  3.3 61.2 %all-to-all-start = ((bf16[32,16,2048]{2,1,0:T(8,128)(2,1)}), bf16[32,16,2048]{2,1,0:T(8,128)(2,1)S(1)}, u32[]{:S(2)}, u32[]{:S(2)}) async-start(bf16[32,16,2048]{2,1,0:T(8,128)(2,1)} %bitcast.18), calls=%async_computation | async-start | bytes 4194304 | tf_op jit(solution)/shard_map/all_to_all | solution.py:231
  13.6 29.1 %copy-start.1 = (bf16[1,128,512]{2,1,0:T(8,128)(2,1)S(1)}, bf16[1,128,512]{2,1,0:T(8,128)(2,1)}, u32[]{:S(2)}) copy-start(bf16[1,128,512]{2,1,0:T(8,128)(2,1)} %param.7) | copy-start | bytes 393220
  13.6 29.1 %copy-start.2 = (bf16[1,128,512]{2,1,0:T(8,128)(2,1)S(1)}, bf16[1,128,512]{2,1,0:T(8,128)(2,1)}, u32[]{:S(2)}) copy-start(bf16[1,128,512]{2,1,0:T(8,128)(2,1)} %param.8) | copy-start | bytes 393220
  13.6 32.0 %copy-start.13 = (bf16[32,128]{1,0:T(8,128)(2,1)S(1)}, bf16[32,128]{1,0:T(8,128)(2,1)}, u32[]{:S(2)}) copy-start(bf16[32,128]{1,0:T(8,128)(2,1)} %filters_ref.3) | copy-start | bytes 24580
  13.6 3.4 %collective-permute-start = (bf16[128,512]{1,0:T(8,128)(2,1)S(1)}, bf16[128,512]{1,0:T(8,128)(2,1)S(1)}, u32[]{:S(2)}, u32[]{:S(2)}) collective-permute-start(bf16[128,512]{1,0:T(8,128)(2,1)S(1)} %copy-done.14), channel_id=1, source_target_pairs={{0,8},{8,0},{1,9},{9,1},{2,10},{10,2},{3,11},{11,3},{4,12},{12,4},... | collective-permute-start | bytes 393224 | tf_op jit(solution)/shard_map/ppermute | solution.py:25
  17.1 16.5 %collective-permute-start.3 = (bf16[256,512]{1,0:T(8,128)(2,1)S(1)}, bf16[256,512]{1,0:T(8,128)(2,1)S(1)}, u32[]{:S(2)}, u32[]{:S(2)}) collective-permute-start(bf16[256,512]{1,0:T(8,128)(2,1)S(1)} %bitcast.19), channel_id=1, source_target_pairs={{0,16},{16,32},{32,48},{48,256},{256,272},{272,288},{288,304},{304... | collective-permute-start | bytes 786440 | tf_op jit(solution)/shard_map/ppermute | solution.py:242
  21.4 16.4 %collective-permute-start.1 = (bf16[256,512]{1,0:T(8,128)(2,1)S(1)}, bf16[256,512]{1,0:T(8,128)(2,1)S(1)}, u32[]{:S(2)}, u32[]{:S(2)}) collective-permute-start(bf16[256,512]{1,0:T(8,128)(2,1)S(1)} %bitcast.20), channel_id=1, source_target_pairs={{0,256},{16,272},{32,288},{48,304},{256,0},{272,16},{288,32},{304,... | collective-permute-start | bytes 786440 | tf_op jit(solution)/shard_map/ppermute | solution.py:242
  33.6 17.3 %collective-permute-start.5 = (bf16[512,512]{1,0:T(8,128)(2,1)S(1)}, bf16[512,512]{1,0:T(8,128)(2,1)S(1)}, u32[]{:S(2)}, u32[]{:S(2)}) collective-permute-start(bf16[512,512]{1,0:T(8,128)(2,1)S(1)} %pad_maximum_fusion), channel_id=1, source_target_pairs={{0,32},{16,48},{32,256},{48,272},{256,288},{272,304},{288,0},{304,... | collective-permute-start | bytes 1572872 | tf_op jit(solution)/shard_map/ppermute | solution.py:242
  37.8 13.1 %copy-start.4 = (bf16[256,512]{1,0:T(8,128)(2,1)}, bf16[256,512]{1,0:T(8,128)(2,1)S(1)}, u32[]{:S(2)}) copy-start(bf16[256,512]{1,0:T(8,128)(2,1)S(1)} %collective-permute-done.1.refs_3_) | copy-start | bytes 786436
  37.8 11.7 %collective-permute-start.4 = (bf16[256,512]{1,0:T(8,128)(2,1)S(1)}, bf16[256,512]{1,0:T(8,128)(2,1)S(1)}, u32[]{:S(2)}, u32[]{:S(2)}) collective-permute-start(bf16[256,512]{1,0:T(8,128)(2,1)S(1)} %collective-permute-done.3.refs_1_), channel_id=1, source_target_pairs={{0,8},{8,0},{1,9},{9,1},{2,10},{10,2},{3,11},{11,3},{4,12},{12,4},... | collective-permute-start | bytes 786440 | tf_op jit(solution)/shard_map/ppermute | solution.py:25
  42.8 2.9 %collective-permute-start.2 = (bf16[128,512]{1,0:T(8,128)(2,1)S(1)}, bf16[128,512]{1,0:T(8,128)(2,1)S(1)}, u32[]{:S(2)}, u32[]{:S(2)}) collective-permute-start(bf16[128,512]{1,0:T(8,128)(2,1)S(1)} %multiply_convert_fusion.mixed_ref), channel_id=1, source_target_pairs={{0,8},{8,16},{16,24},{24,32},{32,40},{40,48},{48,56},{56,64},{64,7... | collective-permute-start | bytes 393224 | tf_op jit(solution)/shard_map/ppermute | solution.py:36
  48.0 0.7 copy-start.8
  49.5 0.7 copy-start.6
  50.9 13.6 %collective-permute-start.6 = (bf16[512,512]{1,0:T(8,128)(2,1)S(1)}, bf16[512,512]{1,0:T(8,128)(2,1)}, u32[]{:S(2)}, u32[]{:S(2)}) collective-permute-start(bf16[512,512]{1,0:T(8,128)(2,1)S(1)} %collective-permute-done.5.refs_4_), channel_id=1, source_target_pairs={{0,8},{8,0},{1,9},{9,1},{2,10},{10,2},{3,11},{11,3},{4,12},{12,4},... | collective-permute-start | bytes 1572872 | tf_op jit(solution)/shard_map/ppermute | solution.py:25
  64.5 1.0 copy-start.5
  65.5 0.9 copy-start.7
  66.4 17.3 %copy-start.9 = (f32[128,512]{1,0:T(8,128)S(1)}, f32[128,512]{1,0:T(8,128)}, u32[]{:S(2)}) copy-start(f32[128,512]{1,0:T(8,128)} %copy-done.8) | copy-start | bytes 786436
  66.4 17.3 %copy-start.11 = (bf16[256,512]{1,0:T(8,128)(2,1)S(1)}, bf16[256,512]{1,0:T(8,128)(2,1)}, u32[]{:S(2)}) copy-start(bf16[256,512]{1,0:T(8,128)(2,1)} %copy-done.10) | copy-start | bytes 786436
  66.4 17.3 %copy-start.12 = (bf16[1,128,512]{2,1,0:T(8,128)(2,1)S(1)}, bf16[1,128,512]{2,1,0:T(8,128)(2,1)}, u32[]{:S(2)}) copy-start(bf16[1,128,512]{2,1,0:T(8,128)(2,1)} %param.6) | copy-start | bytes 393220
  86.6 12.7 %collective-permute-start.7 = (bf16[128,512]{1,0:T(8,128)(2,1)S(1)}, bf16[128,512]{1,0:T(8,128)(2,1)S(1)}, u32[]{:S(2)}, u32[]{:S(2)}) collective-permute-start(bf16[128,512]{1,0:T(8,128)(2,1)S(1)} %get-tuple-element.22.grad_ref), channel_id=1, source_target_pairs={{8,0},{16,8},{24,16},{32,24},{40,32},{48,40},{56,48},{64,56},{72,6... | collective-permute-start | bytes 393224 | tf_op jit(solution)/shard_map/ppermute | solution.py:36
  99.3 16.7 %all-to-all-start.3 = ((f32[8,32,128]{2,1,0:T(8,128)}), f32[8,32,128]{2,1,0:T(8,128)S(1)}, u32[]{:S(2)}, u32[]{:S(2)}) async-start(f32[8,32,128]{2,1,0:T(8,128)} %sums.1), calls=%async_computation.3 | async-start | bytes 262144 | tf_op jit(solution)/shard_map/all_to_all | solution.py:231
  (1 other events, 0.7 us)

commit v19 on v18

--- a/solution.py
+++ b/solution.py
@@ -252,13 +252,14 @@
     one, four = along_z(chip, 1), along_z(chip, 4)
     keys = after_these(keys, four)
     mixed = (keys.astype(F32) * values.astype(F32)).astype(BF16)
-    conv, turned = convolve(filters, from_behind(mixed, 1), mixed)
+    before = from_behind(mixed, 1)
     pair = along_z(jnp.concatenate([chip, one], 0), 2)
     other = swap(one, "co")
-    pair = after_these(pair, other, conv)
+    pair = after_these(pair, other)
     weights = [chip, one, other, four, pair, swap(pair, "co")]
-    gathered = after_these(gathered, conv, *weights)
+    gathered = after_these(gathered, before, *weights)
     terms = exchange(partial_products(gathered, weights), "x")
+    conv, turned = convolve(filters, before, mixed)
     query_grad, conv_grad, lags = branch_gradients(terms, conv, query, turned)
     lags = summed_copies(exchange(lags, ("x", "co")))
     after = from_behind(conv_grad, -1)

time: 117 us -> 119 us (1.017)
  waiting for transfers between devices: 15.3 us -> 40.2 us
  blocking collectives: 25.7 us -> 9.36 us
  starting transfers between devices: 56.5 us -> 48.1 us
  Pallas kernels: 11.1 us -> 12.7 us
    ppermute x3, waiting for transfers between devices: 4.86 us -> 27.1 us  [along_z(): return lax.ppermute(block, Z + ('co',), route)]
    all_to_all x2 -> x1, blocking collectives: 25.7 us -> 9.36 us  [exchange(): return lax.all_to_all(copies, axes, split_axis=0, concat_axis=0)]
    ppermute x3, starting transfers between devices: 19 us -> 6.87 us  [swap(): return lax.ppermute(block, axis, [(0, 1), (1, 0)])]
    all_to_all x2 -> x3, starting transfers between devices: 17.9 us -> 25.4 us  [exchange(): return lax.all_to_all(copies, axes, split_axis=0, concat_axis=0)]
    ppermute x3, starting transfers between devices: 16.5 us -> 11.5 us  [along_z(): return lax.ppermute(block, Z + ('co',), route)]
    all_to_all x2 -> x3, waiting for transfers between devices: 6.56 us -> 11.4 us  [exchange(): return lax.all_to_all(copies, axes, split_axis=0, concat_axis=0)]
    ppermute x3, waiting for transfers between devices: 2.87 us -> 1.31 us  [swap(): return lax.ppermute(block, axis, [(0, 1), (1, 0)])]
    unnamed x30 -> x22, local copies, waits for them, and re-layouts: 6.38 us -> 6.48 us
  transfers between devices with their start and end apart: 10 -> 11, of which waited for: 7 -> 6; matrix products, arithmetic and copies ran while one was open for 0% -> 0% of each run, Pallas kernels for 5% -> 5%
where the time goes in v19:
time: 119 us
  starting transfers between devices  48.1 us (40%)
  waiting for transfers between devices  40.2 us (34%)
  Pallas kernels  12.7 us (11%)
  blocking collectives  9.36 us (8%)
  local copies, waits for them, and re-layouts  6.48 us (5%)
    ppermute x3, waiting for transfers between devices, along_z(): return lax.ppermute(block, Z + ('co',), route)  27.1 us
    all_to_all x3, starting transfers between devices, exchange(): return lax.all_to_all(copies, axes, split_axis=0, concat_axis=0)  25.4 us
    ppermute x3, starting transfers between devices, along_z(): return lax.ppermute(block, Z + ('co',), route)  11.5 us
    all_to_all x3, waiting for transfers between devices, exchange(): return lax.all_to_all(copies, axes, split_axis=0, concat_axis=0)  11.4 us
    all_to_all x1, blocking collectives, exchange(): return lax.all_to_all(copies, axes, split_axis=0, concat_axis=0)  9.36 us
    ppermute x3, starting transfers between devices, swap(): return lax.ppermute(block, axis, [(0, 1), (1, 0)])  6.87 us
    unnamed x22, local copies, waits for them, and re-layouts  6.48 us
    ppermute x2, starting transfers between devices, from_behind(): return lax.ppermute(block, CONTEXT, route)  4.34 us
  transfers between devices with their start and end apart: 11, of which 6 were waited for; matrix products, arithmetic and copies ran while one was open for 0% of the time, Pallas kernels for 5%

profile of v19, /device:TPU:8, one launch (start us, length us, event | category | flops | bytes accessed | tf_op | source)
XLA Modules:
  0.0 118.6 jit_solution(13246710279252713066)
XLA Ops:
  2.0 1.3 %copy-done = bf16[4,8,16,2048]{3,2,1,0:T(8,128)(2,1)} copy-done((bf16[4,8,16,2048]{3,2,1,0:T(8,128)(2,1)}, bf16[4,8,16,2048]{3,2,1,0:T(8,128)(2,1)S(1)}, u32[]{:S(2)}) %copy-start) | copy-done | bytes 2097176
  3.3 10.3 %all-to-all-start = ((bf16[32,16,2048]{2,1,0:T(8,128)(2,1)}), bf16[32,16,2048]{2,1,0:T(8,128)(2,1)S(1)}, u32[]{:S(2)}, u32[]{:S(2)}) async-start(bf16[32,16,2048]{2,1,0:T(8,128)(2,1)} %bitcast.18), calls=%async_computation | async-start | bytes 4194304 | tf_op jit(solution)/shard_map/all_to_all | solution.py:231
  13.6 2.1 %collective-permute-start = (bf16[128,512]{1,0:T(8,128)(2,1)S(1)}, bf16[128,512]{1,0:T(8,128)(2,1)S(1)}, u32[]{:S(2)}, u32[]{:S(2)}) collective-permute-start(bf16[128,512]{1,0:T(8,128)(2,1)S(1)} %copy-done.10), channel_id=1, source_target_pairs={{0,8},{8,0},{1,9},{9,1},{2,10},{10,2},{3,11},{11,3},{4,12},{12,4},... | collective-permute-start | bytes 393224 | tf_op jit(solution)/shard_map/ppermute | solution.py:25
  15.7 1.3 %collective-permute-done = bf16[128,512]{1,0:T(8,128)(2,1)S(1)} collective-permute-done((bf16[128,512]{1,0:T(8,128)(2,1)S(1)}, bf16[128,512]{1,0:T(8,128)(2,1)S(1)}, u32[]{:S(2)}, u32[]{:S(2)}) %collective-permute-start) | collective-permute-done | bytes 131104 | tf_op jit(solution)/shard_map/ppermute | solution.py:25
  17.1 4.3 %collective-permute-start.3 = (bf16[256,512]{1,0:T(8,128)(2,1)S(1)}, bf16[256,512]{1,0:T(8,128)(2,1)S(1)}, u32[]{:S(2)}, u32[]{:S(2)}) collective-permute-start(bf16[256,512]{1,0:T(8,128)(2,1)S(1)} %bitcast.19), channel_id=1, source_target_pairs={{0,16},{16,32},{32,48},{48,256},{256,272},{272,288},{288,304},{304... | collective-permute-start | bytes 786440 | tf_op jit(solution)/shard_map/ppermute | solution.py:242
  21.3 11.0 %collective-permute-done.3.refs_1_ = bf16[256,512]{1,0:T(8,128)(2,1)S(1)} collective-permute-done((bf16[256,512]{1,0:T(8,128)(2,1)S(1)}, bf16[256,512]{1,0:T(8,128)(2,1)S(1)}, u32[]{:S(2)}, u32[]{:S(2)}) %collective-permute-start.3) | collective-permute-done | bytes 262176 | tf_op jit(solution)/shard_map/ppermute | solution.py:242
  32.4 1.9 %collective-permute-start.5 = (bf16[512,512]{1,0:T(8,128)(2,1)S(1)}, bf16[512,512]{1,0:T(8,128)(2,1)S(1)}, u32[]{:S(2)}, u32[]{:S(2)}) collective-permute-start(bf16[512,512]{1,0:T(8,128)(2,1)S(1)} %pad_maximum_fusion), channel_id=1, source_target_pairs={{0,32},{16,48},{32,256},{48,272},{256,288},{272,304},{288,0},{304,... | collective-permute-start | bytes 1572872 | tf_op jit(solution)/shard_map/ppermute | solution.py:242
  34.3 2.9 %collective-permute-start.4 = (bf16[256,512]{1,0:T(8,128)(2,1)S(1)}, bf16[256,512]{1,0:T(8,128)(2,1)S(1)}, u32[]{:S(2)}, u32[]{:S(2)}) collective-permute-start(bf16[256,512]{1,0:T(8,128)(2,1)S(1)} %collective-permute-done.3.refs_1_), channel_id=1, source_target_pairs={{0,8},{8,0},{1,9},{9,1},{2,10},{10,2},{3,11},{11,3},{4,12},{12,4},... | collective-permute-start | bytes 786440 | tf_op jit(solution)/shard_map/ppermute | solution.py:25
  37.2 5.3 %collective-permute-start.1 = (bf16[256,512]{1,0:T(8,128)(2,1)S(1)}, bf16[256,512]{1,0:T(8,128)(2,1)S(1)}, u32[]{:S(2)}, u32[]{:S(2)}) collective-permute-start(bf16[256,512]{1,0:T(8,128)(2,1)S(1)} %bitcast.21), channel_id=1, source_target_pairs={{0,256},{16,272},{32,288},{48,304},{256,0},{272,16},{288,32},{304,... | collective-permute-start | bytes 786440 | tf_op jit(solution)/shard_map/ppermute | solution.py:242
  43.2 16.1 %collective-permute-done.5.refs_4_ = bf16[512,512]{1,0:T(8,128)(2,1)S(1)} collective-permute-done((bf16[512,512]{1,0:T(8,128)(2,1)S(1)}, bf16[512,512]{1,0:T(8,128)(2,1)S(1)}, u32[]{:S(2)}, u32[]{:S(2)}) %collective-permute-start.5) | collective-permute-done | bytes 524320 | tf_op jit(solution)/shard_map/ppermute | solution.py:242
  59.4 1.9 %collective-permute-start.6 = (bf16[512,512]{1,0:T(8,128)(2,1)S(1)}, bf16[512,512]{1,0:T(8,128)(2,1)}, u32[]{:S(2)}, u32[]{:S(2)}) collective-permute-start(bf16[512,512]{1,0:T(8,128)(2,1)S(1)} %collective-permute-done.5.refs_4_), channel_id=1, source_target_pairs={{0,8},{8,0},{1,9},{9,1},{2,10},{10,2},{3,11},{11,3},{4,12},{12,4},... | collective-permute-start | bytes 1572872 | tf_op jit(solution)/shard_map/ppermute | solution.py:25
  62.0 3.1 %collective-permute-start.2 = (bf16[128,512]{1,0:T(8,128)(2,1)S(1)}, bf16[128,512]{1,0:T(8,128)(2,1)}, u32[]{:S(2)}, u32[]{:S(2)}) collective-permute-start(bf16[128,512]{1,0:T(8,128)(2,1)S(1)} %multiply_convert_fusion.mixed_ref), channel_id=1, source_target_pairs={{0,8},{8,16},{16,24},{24,32},{32,40},{40,48},{48,56},{56,64},{64,7... | collective-permute-start | bytes 393224 | tf_op jit(solution)/shard_map/ppermute | solution.py:36
  65.6 0.9 copy-done.5
  66.5 0.9 copy-done.7
  67.5 3.1 %product.1 = bf16[4,128,512]{2,1,0:T(8,128)(2,1)} custom-call(s32[2]{0:T(128)S(1)} %pad_add_fusion.place_ref, bf16[512,2048]{1,0:T(8,128)(2,1)S(1)} %bitcast.17, bf16[256,512]{1,0:T(8,128)(2,1)S(1)} %bitcast.22, bf16[256,512]{1,0:T(8,128)(2,1)S(1)} %collective-permute-done.3.refs_1_, bf16[256,512]{1,0:T(8,128)(2,1)S(1)} %copy-done.5, ...), custom_call_target="tpu_custom_call" | custom-call | tf_op jit(solution)/shard_map/product/pallas_call | solution.py:216
  70.5 9.8 %all-to-all-start.1 = ((bf16[4,128,512]{2,1,0:T(8,128)(2,1)}), bf16[4,128,512]{2,1,0:T(8,128)(2,1)S(1)}, u32[]{:S(2)}, u32[]{:S(2)}) async-start(bf16[4,128,512]{2,1,0:T(8,128)(2,1)} %product.1), calls=%async_computation.1 | async-start | bytes 1048576 | tf_op jit(solution)/shard_map/all_to_all | solution.py:231
  80.4 3.2 %conv.1 = (f32[128,512]{1,0:T(8,128)S(1)}, bf16[256,512]{1,0:T(8,128)(2,1)S(1)}) custom-call(bf16[32,128]{1,0:T(8,128)(2,1)S(1)} %copy-done.9, bf16[128,512]{1,0:T(8,128)(2,1)} %collective-permute-done.2.before_ref, bf16[128,512]{1,0:T(8,128)(2,1)S(1)} %multiply_convert_fusion.mixed_ref), custom_call_target="tpu_custom_call" | custom-call | tf_op jit(solution)/shard_map/conv/pallas_call | solution.py:172
  83.6 4.9 %all-to-all-done.1.terms_ref = bf16[4,128,512]{2,1,0:T(8,128)(2,1)S(1)} async-done(((bf16[4,128,512]{2,1,0:T(8,128)(2,1)}), bf16[4,128,512]{2,1,0:T(8,128)(2,1)S(1)}, u32[]{:S(2)}, u32[]{:S(2)}) %all-to-all-start.1) | async-done | bytes 524320 | tf_op jit(solution)/shard_map/all_to_all | solution.py:231
  89.4 2.9 %branch.1 = (bf16[128,512]{1,0:T(8,128)(2,1)}, bf16[128,512]{1,0:T(8,128)(2,1)S(1)}, f32[8,32,128]{2,1,0:T(8,128)S(1)}) custom-call(bf16[4,128,512]{2,1,0:T(8,128)(2,1)S(1)} %all-to-all-done.1.terms_ref, f32[128,512]{1,0:T(8,128)S(1)} %get-tuple-element.19.conv_ref, bf16[128,512]{1,0:T(8,128)(2,1)S(1)} %bitcast.27, ...), custom_call_target="tpu_custom_call" | custom-call | tf_op jit(solution)/shard_map/branch/pallas_call | solution.py:200
  92.3 1.3 %collective-permute-start.7 = (bf16[128,512]{1,0:T(8,128)(2,1)S(1)}, bf16[128,512]{1,0:T(8,128)(2,1)S(1)}, u32[]{:S(2)}, u32[]{:S(2)}) collective-permute-start(bf16[128,512]{1,0:T(8,128)(2,1)S(1)} %get-tuple-element.22.grad_ref), channel_id=1, source_target_pairs={{8,0},{16,8},{24,16},{32,24},{40,32},{48,40},{56,48},{64,56},{72,6... | collective-permute-start | bytes 393224 | tf_op jit(solution)/shard_map/ppermute | solution.py:36
  93.5 9.4 %all_to_all.20.parts_ref = f32[8,32,128]{2,1,0:T(8,128)S(1)} all-to-all(f32[8,32,128]{2,1,0:T(8,128)S(1)} %get-tuple-element.23), channel_id=1, replica_groups=mesh['zh'=2,'x'=4,'zl'=4,'co'=2,'yq'=4,'yp'=2] {'x','co'}, dimensions={0} | all-to-all | bytes 262144 | tf_op jit(solution)/shard_map/all_to_all | solution.py:231
  103.6 5.3 %all-to-all-start.3 = ((f32[8,32,128]{2,1,0:T(8,128)}), f32[8,32,128]{2,1,0:T(8,128)S(1)}, u32[]{:S(2)}, u32[]{:S(2)}) async-start(f32[8,32,128]{2,1,0:T(8,128)} %sums.1), calls=%async_computation.3 | async-start | bytes 262144 | tf_op jit(solution)/shard_map/all_to_all | solution.py:231
  108.9 2.5 %mixed_grad.1 = (bf16[128,512]{1,0:T(8,128)(2,1)}, bf16[128,512]{1,0:T(8,128)(2,1)}) custom-call(bf16[32,128]{1,0:T(8,128)(2,1)S(1)} %copy-done.9, bf16[128,512]{1,0:T(8,128)(2,1)S(1)} %get-tuple-element.22.grad_ref, bf16[128,512]{1,0:T(8,128)(2,1)S(1)} %collective-permute-done.7.after_ref, bf16[128,512]{1,0:T(8,128)(2,1)S(1)} %bitcast.24, ...), custom_call_target="tpu_custom_call" | custom-call | tf_op jit(solution)/shard_map/mixed_grad/pallas_call | solution.py:186
  111.4 6.6 %all-to-all-done.3 = f32[8,32,128]{2,1,0:T(8,128)S(1)} async-done(((f32[8,32,128]{2,1,0:T(8,128)}), f32[8,32,128]{2,1,0:T(8,128)S(1)}, u32[]{:S(2)}, u32[]{:S(2)}) %all-to-all-start.3) | async-done | bytes 131104 | tf_op jit(solution)/shard_map/all_to_all | solution.py:231
  (34 shorter events, 5.5 us)
Async XLA Ops:
  0.6 1.0 copy-start.3
  1.9 1.3 %copy-start = (bf16[4,8,16,2048]{3,2,1,0:T(8,128)(2,1)}, bf16[4,8,16,2048]{3,2,1,0:T(8,128)(2,1)S(1)}, u32[]{:S(2)}) copy-start(bf16[4,8,16,2048]{3,2,1,0:T(8,128)(2,1)S(1)} %spread.1) | copy-start | bytes 6291460
  3.3 10.3 %copy-start.10 = (bf16[128,512]{1,0:T(8,128)(2,1)S(1)}, bf16[128,512]{1,0:T(8,128)(2,1)}, u32[]{:S(2)}) copy-start(bf16[128,512]{1,0:T(8,128)(2,1)} %param.10) | copy-start | bytes 393220
  3.3 62.3 %all-to-all-start = ((bf16[32,16,2048]{2,1,0:T(8,128)(2,1)}), bf16[32,16,2048]{2,1,0:T(8,128)(2,1)S(1)}, u32[]{:S(2)}, u32[]{:S(2)}) async-start(bf16[32,16,2048]{2,1,0:T(8,128)(2,1)} %bitcast.18), calls=%async_computation | async-start | bytes 4194304 | tf_op jit(solution)/shard_map/all_to_all | solution.py:231
  13.6 48.4 %copy-start.1 = (bf16[1,128,512]{2,1,0:T(8,128)(2,1)S(1)}, bf16[1,128,512]{2,1,0:T(8,128)(2,1)}, u32[]{:S(2)}) copy-start(bf16[1,128,512]{2,1,0:T(8,128)(2,1)} %param.7) | copy-start | bytes 393220
  13.6 48.4 %copy-start.2 = (bf16[1,128,512]{2,1,0:T(8,128)(2,1)S(1)}, bf16[1,128,512]{2,1,0:T(8,128)(2,1)}, u32[]{:S(2)}) copy-start(bf16[1,128,512]{2,1,0:T(8,128)(2,1)} %param.8) | copy-start | bytes 393220
  13.6 3.4 %collective-permute-start = (bf16[128,512]{1,0:T(8,128)(2,1)S(1)}, bf16[128,512]{1,0:T(8,128)(2,1)S(1)}, u32[]{:S(2)}, u32[]{:S(2)}) collective-permute-start(bf16[128,512]{1,0:T(8,128)(2,1)S(1)} %copy-done.10), channel_id=1, source_target_pairs={{0,8},{8,0},{1,9},{9,1},{2,10},{10,2},{3,11},{11,3},{4,12},{12,4},... | collective-permute-start | bytes 393224 | tf_op jit(solution)/shard_map/ppermute | solution.py:25
  17.1 15.3 %collective-permute-start.3 = (bf16[256,512]{1,0:T(8,128)(2,1)S(1)}, bf16[256,512]{1,0:T(8,128)(2,1)S(1)}, u32[]{:S(2)}, u32[]{:S(2)}) collective-permute-start(bf16[256,512]{1,0:T(8,128)(2,1)S(1)} %bitcast.19), channel_id=1, source_target_pairs={{0,16},{16,32},{32,48},{48,256},{256,272},{272,288},{288,304},{304... | collective-permute-start | bytes 786440 | tf_op jit(solution)/shard_map/ppermute | solution.py:242
  32.4 27.0 %collective-permute-start.5 = (bf16[512,512]{1,0:T(8,128)(2,1)S(1)}, bf16[512,512]{1,0:T(8,128)(2,1)S(1)}, u32[]{:S(2)}, u32[]{:S(2)}) collective-permute-start(bf16[512,512]{1,0:T(8,128)(2,1)S(1)} %pad_maximum_fusion), channel_id=1, source_target_pairs={{0,32},{16,48},{32,256},{48,272},{256,288},{272,304},{288,0},{304,... | collective-permute-start | bytes 1572872 | tf_op jit(solution)/shard_map/ppermute | solution.py:242
  34.3 8.2 %collective-permute-start.4 = (bf16[256,512]{1,0:T(8,128)(2,1)S(1)}, bf16[256,512]{1,0:T(8,128)(2,1)S(1)}, u32[]{:S(2)}, u32[]{:S(2)}) collective-permute-start(bf16[256,512]{1,0:T(8,128)(2,1)S(1)} %collective-permute-done.3.refs_1_), channel_id=1, source_target_pairs={{0,8},{8,0},{1,9},{9,1},{2,10},{10,2},{3,11},{11,3},{4,12},{12,4},... | collective-permute-start | bytes 786440 | tf_op jit(solution)/shard_map/ppermute | solution.py:25
  37.2 24.0 %collective-permute-start.1 = (bf16[256,512]{1,0:T(8,128)(2,1)S(1)}, bf16[256,512]{1,0:T(8,128)(2,1)S(1)}, u32[]{:S(2)}, u32[]{:S(2)}) collective-permute-start(bf16[256,512]{1,0:T(8,128)(2,1)S(1)} %bitcast.21), channel_id=1, source_target_pairs={{0,256},{16,272},{32,288},{48,304},{256,0},{272,16},{288,32},{304,... | collective-permute-start | bytes 786440 | tf_op jit(solution)/shard_map/ppermute | solution.py:242
  42.5 0.7 copy-start.4
  59.4 6.2 %collective-permute-start.6 = (bf16[512,512]{1,0:T(8,128)(2,1)S(1)}, bf16[512,512]{1,0:T(8,128)(2,1)}, u32[]{:S(2)}, u32[]{:S(2)}) collective-permute-start(bf16[512,512]{1,0:T(8,128)(2,1)S(1)} %collective-permute-done.5.refs_4_), channel_id=1, source_target_pairs={{0,8},{8,0},{1,9},{9,1},{2,10},{10,2},{3,11},{11,3},{4,12},{12,4},... | collective-permute-start | bytes 1572872 | tf_op jit(solution)/shard_map/ppermute | solution.py:25
  61.3 0.7 copy-start.6
  62.0 3.5 %collective-permute-start.2 = (bf16[128,512]{1,0:T(8,128)(2,1)S(1)}, bf16[128,512]{1,0:T(8,128)(2,1)}, u32[]{:S(2)}, u32[]{:S(2)}) collective-permute-start(bf16[128,512]{1,0:T(8,128)(2,1)S(1)} %multiply_convert_fusion.mixed_ref), channel_id=1, source_target_pairs={{0,8},{8,16},{16,24},{24,32},{32,40},{40,48},{48,56},{56,64},{64,7... | collective-permute-start | bytes 393224 | tf_op jit(solution)/shard_map/ppermute | solution.py:36
  65.5 1.0 copy-start.5
  66.5 0.9 copy-start.7
  67.5 12.9 %copy-start.9 = (bf16[32,128]{1,0:T(8,128)(2,1)S(1)}, bf16[32,128]{1,0:T(8,128)(2,1)}, u32[]{:S(2)}) copy-start(bf16[32,128]{1,0:T(8,128)(2,1)} %filters_ref.3) | copy-start | bytes 24580
  70.5 17.9 %all-to-all-start.1 = ((bf16[4,128,512]{2,1,0:T(8,128)(2,1)}), bf16[4,128,512]{2,1,0:T(8,128)(2,1)S(1)}, u32[]{:S(2)}, u32[]{:S(2)}) async-start(bf16[4,128,512]{2,1,0:T(8,128)(2,1)} %product.1), calls=%async_computation.1 | async-start | bytes 1048576 | tf_op jit(solution)/shard_map/all_to_all | solution.py:231
  88.5 0.9 copy-start.8
  92.3 11.3 %collective-permute-start.7 = (bf16[128,512]{1,0:T(8,128)(2,1)S(1)}, bf16[128,512]{1,0:T(8,128)(2,1)S(1)}, u32[]{:S(2)}, u32[]{:S(2)}) collective-permute-start(bf16[128,512]{1,0:T(8,128)(2,1)S(1)} %get-tuple-element.22.grad_ref), channel_id=1, source_target_pairs={{8,0},{16,8},{24,16},{32,24},{40,32},{48,40},{56,48},{64,56},{72,6... | collective-permute-start | bytes 393224 | tf_op jit(solution)/shard_map/ppermute | solution.py:36
  103.6 14.4 %all-to-all-start.3 = ((f32[8,32,128]{2,1,0:T(8,128)}), f32[8,32,128]{2,1,0:T(8,128)S(1)}, u32[]{:S(2)}, u32[]{:S(2)}) async-start(f32[8,32,128]{2,1,0:T(8,128)} %sums.1), calls=%async_computation.3 | async-start | bytes 262144 | tf_op jit(solution)/shard_map/all_to_all | solution.py:231

commit v20 on v19

--- a/solution.py
+++ b/solution.py
@@ -255,11 +255,12 @@
     before = from_behind(mixed, 1)
     pair = along_z(jnp.concatenate([chip, one], 0), 2)
     other = swap(one, "co")
-    pair = after_these(pair, other)
+    pair = after_these(pair, other, before)
     weights = [chip, one, other, four, pair, swap(pair, "co")]
-    gathered = after_these(gathered, before, *weights)
-    terms = exchange(partial_products(gathered, weights), "x")
-    conv, turned = convolve(filters, before, mixed)
+    gathered = after_these(gathered, *weights)
+    partial = partial_products(gathered, weights)
+    terms = exchange(partial, "x")
+    conv, turned = convolve(filters, after_these(before, partial), mixed)
     query_grad, conv_grad, lags = branch_gradients(terms, conv, query, turned)
     lags = summed_copies(exchange(lags, ("x", "co")))
     after = from_behind(conv_grad, -1)

time: 119 us -> 119 us (level)
  waiting for transfers between devices: 40.2 us -> 26.2 us
  starting transfers between devices: 48.1 us -> 57.6 us
  blocking collectives: 9.36 us -> 13.9 us
    ppermute x3, waiting for transfers between devices: 27.1 us -> 7.97 us  [along_z(): return lax.ppermute(block, Z + ('co',), route)]
    ppermute x3, starting transfers between devices: 6.87 us -> 15.9 us  [swap(): return lax.ppermute(block, axis, [(0, 1), (1, 0)])]
    ppermute x3, starting transfers between devices: 11.5 us -> 16.5 us  [along_z(): return lax.ppermute(block, Z + ('co',), route)]
    all_to_all x1, blocking collectives: 9.36 us -> 13.9 us  [exchange(): return lax.all_to_all(copies, axes, split_axis=0, concat_axis=0)]
    all_to_all x3, starting transfers between devices: 25.4 us -> 22.1 us  [exchange(): return lax.all_to_all(copies, axes, split_axis=0, concat_axis=0)]
    all_to_all x3, waiting for transfers between devices: 11.4 us -> 14.4 us  [exchange(): return lax.all_to_all(copies, axes, split_axis=0, concat_axis=0)]
    ppermute x3, waiting for transfers between devices: 1.31 us -> 2.87 us  [swap(): return lax.ppermute(block, axis, [(0, 1), (1, 0)])]
    unnamed x22 -> x26, local copies, waits for them, and re-layouts: 6.48 us -> 7.4 us
  transfers between devices with their start and end apart: 11 -> 11, of which waited for: 6 -> 9; matrix products, arithmetic and copies ran while one was open for 0% -> 0% of each run, Pallas kernels for 5% -> 5%
where the time goes in v20:
time: 119 us
  starting transfers between devices  57.6 us (48%)
  waiting for transfers between devices  26.2 us (22%)
  blocking collectives  13.9 us (12%)
  Pallas kernels  11.9 us (10%)
  local copies, waits for them, and re-layouts  7.4 us (6%)
    all_to_all x3, starting transfers between devices, exchange(): return lax.all_to_all(copies, axes, split_axis=0, concat_axis=0)  22.1 us
    ppermute x3, starting transfers between devices, along_z(): return lax.ppermute(block, Z + ('co',), route)  16.5 us
    ppermute x3, starting transfers between devices, swap(): return lax.ppermute(block, axis, [(0, 1), (1, 0)])  15.9 us
    all_to_all x3, waiting for transfers between devices, exchange(): return lax.all_to_all(copies, axes, split_axis=0, concat_axis=0)  14.4 us
    all_to_all x1, blocking collectives, exchange(): return lax.all_to_all(copies, axes, split_axis=0, concat_axis=0)  13.9 us
    ppermute x3, waiting for transfers between devices, along_z(): return lax.ppermute(block, Z + ('co',), route)  7.97 us
    unnamed x26, local copies, waits for them, and re-layouts  7.4 us
    ppermute x2, starting transfers between devices, from_behind(): return lax.ppermute(block, CONTEXT, route)  3.2 us
  transfers between devices with their start and end apart: 11, of which 9 were waited for; matrix products, arithmetic and copies ran while one was open for 0% of the time, Pallas kernels for 5%

profile of v20, /device:TPU:8, one launch (start us, length us, event | category | flops | bytes accessed | tf_op | source)
XLA Modules:
  0.0 118.6 jit_solution(2327812170690189856)
XLA Ops:
  2.0 1.3 %copy-done = bf16[4,8,16,2048]{3,2,1,0:T(8,128)(2,1)} copy-done((bf16[4,8,16,2048]{3,2,1,0:T(8,128)(2,1)}, bf16[4,8,16,2048]{3,2,1,0:T(8,128)(2,1)S(1)}, u32[]{:S(2)}) %copy-start) | copy-done | bytes 2097176
  3.3 10.3 %all-to-all-start = ((bf16[32,16,2048]{2,1,0:T(8,128)(2,1)}), bf16[32,16,2048]{2,1,0:T(8,128)(2,1)S(1)}, u32[]{:S(2)}, u32[]{:S(2)}) async-start(bf16[32,16,2048]{2,1,0:T(8,128)(2,1)} %bitcast.18), calls=%async_computation | async-start | bytes 4194304 | tf_op jit(solution)/shard_map/all_to_all | solution.py:231
  13.6 2.1 %collective-permute-start = (bf16[128,512]{1,0:T(8,128)(2,1)S(1)}, bf16[128,512]{1,0:T(8,128)(2,1)S(1)}, u32[]{:S(2)}, u32[]{:S(2)}) collective-permute-start(bf16[128,512]{1,0:T(8,128)(2,1)S(1)} %copy-done.12), channel_id=1, source_target_pairs={{0,8},{8,0},{1,9},{9,1},{2,10},{10,2},{3,11},{11,3},{4,12},{12,4},... | collective-permute-start | bytes 393224 | tf_op jit(solution)/shard_map/ppermute | solution.py:25
  15.7 1.3 %collective-permute-done = bf16[128,512]{1,0:T(8,128)(2,1)S(1)} collective-permute-done((bf16[128,512]{1,0:T(8,128)(2,1)S(1)}, bf16[128,512]{1,0:T(8,128)(2,1)S(1)}, u32[]{:S(2)}, u32[]{:S(2)}) %collective-permute-start) | collective-permute-done | bytes 131104 | tf_op jit(solution)/shard_map/ppermute | solution.py:25
  17.1 4.3 %collective-permute-start.1 = (bf16[256,512]{1,0:T(8,128)(2,1)S(1)}, bf16[256,512]{1,0:T(8,128)(2,1)S(1)}, u32[]{:S(2)}, u32[]{:S(2)}) collective-permute-start(bf16[256,512]{1,0:T(8,128)(2,1)S(1)} %bitcast.19), channel_id=1, source_target_pairs={{0,16},{16,32},{32,48},{48,256},{256,272},{272,288},{288,304},{304... | collective-permute-start | bytes 786440 | tf_op jit(solution)/shard_map/ppermute | solution.py:242
  21.4 10.0 %collective-permute-start.3 = (bf16[256,512]{1,0:T(8,128)(2,1)S(1)}, bf16[256,512]{1,0:T(8,128)(2,1)S(1)}, u32[]{:S(2)}, u32[]{:S(2)}) collective-permute-start(bf16[256,512]{1,0:T(8,128)(2,1)S(1)} %bitcast.20), channel_id=1, source_target_pairs={{0,256},{16,272},{32,288},{48,304},{256,0},{272,16},{288,32},{304,... | collective-permute-start | bytes 786440 | tf_op jit(solution)/shard_map/ppermute | solution.py:242
  31.4 2.1 %collective-permute-done.1.refs_1_ = bf16[256,512]{1,0:T(8,128)(2,1)S(1)} collective-permute-done((bf16[256,512]{1,0:T(8,128)(2,1)S(1)}, bf16[256,512]{1,0:T(8,128)(2,1)S(1)}, u32[]{:S(2)}, u32[]{:S(2)}) %collective-permute-start.1) | collective-permute-done | bytes 262176 | tf_op jit(solution)/shard_map/ppermute | solution.py:242
  33.6 2.2 %collective-permute-start.4 = (bf16[512,512]{1,0:T(8,128)(2,1)S(1)}, bf16[512,512]{1,0:T(8,128)(2,1)S(1)}, u32[]{:S(2)}, u32[]{:S(2)}) collective-permute-start(bf16[512,512]{1,0:T(8,128)(2,1)S(1)} %pad_maximum_fusion), channel_id=1, source_target_pairs={{0,32},{16,48},{32,256},{48,272},{256,288},{272,304},{288,0},{304,... | collective-permute-start | bytes 1572872 | tf_op jit(solution)/shard_map/ppermute | solution.py:242
  35.7 2.0 %collective-permute-done.3.refs_3_ = bf16[256,512]{1,0:T(8,128)(2,1)S(1)} collective-permute-done((bf16[256,512]{1,0:T(8,128)(2,1)S(1)}, bf16[256,512]{1,0:T(8,128)(2,1)S(1)}, u32[]{:S(2)}, u32[]{:S(2)}) %collective-permute-start.3) | collective-permute-done | bytes 262176 | tf_op jit(solution)/shard_map/ppermute | solution.py:242
  37.8 4.9 %collective-permute-start.2 = (bf16[256,512]{1,0:T(8,128)(2,1)S(1)}, bf16[256,512]{1,0:T(8,128)(2,1)S(1)}, u32[]{:S(2)}, u32[]{:S(2)}) collective-permute-start(bf16[256,512]{1,0:T(8,128)(2,1)S(1)} %collective-permute-done.1.refs_1_), channel_id=1, source_target_pairs={{0,8},{8,0},{1,9},{9,1},{2,10},{10,2},{3,11},{11,3},{4,12},{12,4},... | collective-permute-start | bytes 786440 | tf_op jit(solution)/shard_map/ppermute | solution.py:25
  42.8 1.9 %collective-permute-start.5 = (bf16[128,512]{1,0:T(8,128)(2,1)S(1)}, bf16[128,512]{1,0:T(8,128)(2,1)S(1)}, u32[]{:S(2)}, u32[]{:S(2)}) collective-permute-start(bf16[128,512]{1,0:T(8,128)(2,1)S(1)} %multiply_convert_fusion.mixed_ref), channel_id=1, source_target_pairs={{0,8},{8,16},{16,24},{24,32},{32,40},{40,48},{48,56},{56,64},{64,7... | collective-permute-start | bytes 393224 | tf_op jit(solution)/shard_map/ppermute | solution.py:36
  47.1 3.8 %collective-permute-done.4.refs_4_ = bf16[512,512]{1,0:T(8,128)(2,1)S(1)} collective-permute-done((bf16[512,512]{1,0:T(8,128)(2,1)S(1)}, bf16[512,512]{1,0:T(8,128)(2,1)S(1)}, u32[]{:S(2)}, u32[]{:S(2)}) %collective-permute-start.4) | collective-permute-done | bytes 524320 | tf_op jit(solution)/shard_map/ppermute | solution.py:242
  50.9 8.9 %collective-permute-start.6 = (bf16[512,512]{1,0:T(8,128)(2,1)S(1)}, bf16[512,512]{1,0:T(8,128)(2,1)}, u32[]{:S(2)}, u32[]{:S(2)}) collective-permute-start(bf16[512,512]{1,0:T(8,128)(2,1)S(1)} %collective-permute-done.4.refs_4_), channel_id=1, source_target_pairs={{0,8},{8,0},{1,9},{9,1},{2,10},{10,2},{3,11},{11,3},{4,12},{12,4},... | collective-permute-start | bytes 1572872 | tf_op jit(solution)/shard_map/ppermute | solution.py:25
  59.8 1.6 %collective-permute-done.6.refs_5_ = bf16[512,512]{1,0:T(8,128)(2,1)} collective-permute-done((bf16[512,512]{1,0:T(8,128)(2,1)S(1)}, bf16[512,512]{1,0:T(8,128)(2,1)}, u32[]{:S(2)}, u32[]{:S(2)}) %collective-permute-start.6) | collective-permute-done | bytes 524320 | tf_op jit(solution)/shard_map/ppermute | solution.py:25
  64.6 3.1 %product.1 = bf16[4,128,512]{2,1,0:T(8,128)(2,1)} custom-call(s32[2]{0:T(128)S(1)} %pad_add_fusion.place_ref, bf16[512,2048]{1,0:T(8,128)(2,1)S(1)} %bitcast.17, bf16[256,512]{1,0:T(8,128)(2,1)S(1)} %bitcast.22, bf16[256,512]{1,0:T(8,128)(2,1)S(1)} %collective-permute-done.1.refs_1_, bf16[256,512]{1,0:T(8,128)(2,1)S(1)} %copy-done.7, ...), custom_call_target="tpu_custom_call" | custom-call | tf_op jit(solution)/shard_map/product/pallas_call | solution.py:216
  67.6 4.2 %all-to-all-start.1 = ((bf16[4,128,512]{2,1,0:T(8,128)(2,1)}), bf16[4,128,512]{2,1,0:T(8,128)(2,1)S(1)}, u32[]{:S(2)}, u32[]{:S(2)}) async-start(bf16[4,128,512]{2,1,0:T(8,128)(2,1)} %product.1), calls=%async_computation.1 | async-start | bytes 1048576 | tf_op jit(solution)/shard_map/all_to_all | solution.py:231
  72.7 2.3 %conv.1 = (f32[128,512]{1,0:T(8,128)S(1)}, bf16[256,512]{1,0:T(8,128)(2,1)S(1)}) custom-call(bf16[32,128]{1,0:T(8,128)(2,1)S(1)} %copy-done.11, bf16[128,512]{1,0:T(8,128)(2,1)S(1)} %copy-done.10, bf16[128,512]{1,0:T(8,128)(2,1)S(1)} %multiply_convert_fusion.mixed_ref), custom_call_target="tpu_custom_call" | custom-call | tf_op jit(solution)/shard_map/conv/pallas_call | solution.py:172
  75.1 6.5 %all-to-all-done.1.terms_ref = bf16[4,128,512]{2,1,0:T(8,128)(2,1)S(1)} async-done(((bf16[4,128,512]{2,1,0:T(8,128)(2,1)}), bf16[4,128,512]{2,1,0:T(8,128)(2,1)S(1)}, u32[]{:S(2)}, u32[]{:S(2)}) %all-to-all-start.1) | async-done | bytes 524320 | tf_op jit(solution)/shard_map/all_to_all | solution.py:231
  82.5 2.9 %branch.1 = (bf16[128,512]{1,0:T(8,128)(2,1)}, bf16[128,512]{1,0:T(8,128)(2,1)S(1)}, f32[8,32,128]{2,1,0:T(8,128)S(1)}) custom-call(bf16[4,128,512]{2,1,0:T(8,128)(2,1)S(1)} %all-to-all-done.1.terms_ref, f32[128,512]{1,0:T(8,128)S(1)} %get-tuple-element.21.conv_ref, bf16[128,512]{1,0:T(8,128)(2,1)S(1)} %bitcast.27, ...), custom_call_target="tpu_custom_call" | custom-call | tf_op jit(solution)/shard_map/branch/pallas_call | solution.py:200
  85.4 1.3 %collective-permute-start.7 = (bf16[128,512]{1,0:T(8,128)(2,1)S(1)}, bf16[128,512]{1,0:T(8,128)(2,1)S(1)}, u32[]{:S(2)}, u32[]{:S(2)}) collective-permute-start(bf16[128,512]{1,0:T(8,128)(2,1)S(1)} %get-tuple-element.24.grad_ref), channel_id=1, source_target_pairs={{8,0},{16,8},{24,16},{32,24},{40,32},{48,40},{56,48},{64,56},{72,6... | collective-permute-start | bytes 393224 | tf_op jit(solution)/shard_map/ppermute | solution.py:36
  86.7 13.9 %all_to_all.20.parts_ref = f32[8,32,128]{2,1,0:T(8,128)S(1)} all-to-all(f32[8,32,128]{2,1,0:T(8,128)S(1)} %get-tuple-element.25), channel_id=1, replica_groups=mesh['zh'=2,'x'=4,'zl'=4,'co'=2,'yq'=4,'yp'=2] {'x','co'}, dimensions={0} | all-to-all | bytes 262144 | tf_op jit(solution)/shard_map/all_to_all | solution.py:231
  101.3 7.6 %all-to-all-start.3 = ((f32[8,32,128]{2,1,0:T(8,128)}), f32[8,32,128]{2,1,0:T(8,128)S(1)}, u32[]{:S(2)}, u32[]{:S(2)}) async-start(f32[8,32,128]{2,1,0:T(8,128)} %sums.1), calls=%async_computation.3 | async-start | bytes 262144 | tf_op jit(solution)/shard_map/all_to_all | solution.py:231
  108.9 2.5 %mixed_grad.1 = (bf16[128,512]{1,0:T(8,128)(2,1)}, bf16[128,512]{1,0:T(8,128)(2,1)}) custom-call(bf16[32,128]{1,0:T(8,128)(2,1)S(1)} %copy-done.11, bf16[128,512]{1,0:T(8,128)(2,1)S(1)} %get-tuple-element.24.grad_ref, bf16[128,512]{1,0:T(8,128)(2,1)S(1)} %collective-permute-done.7.after_ref, bf16[128,512]{1,0:T(8,128)(2,1)S(1)} %bitcast.24, ...), custom_call_target="tpu_custom_call" | custom-call | tf_op jit(solution)/shard_map/mixed_grad/pallas_call | solution.py:186
  111.4 6.6 %all-to-all-done.3 = f32[8,32,128]{2,1,0:T(8,128)S(1)} async-done(((f32[8,32,128]{2,1,0:T(8,128)}), f32[8,32,128]{2,1,0:T(8,128)S(1)}, u32[]{:S(2)}, u32[]{:S(2)}) %all-to-all-start.3) | async-done | bytes 131104 | tf_op jit(solution)/shard_map/all_to_all | solution.py:231
  (38 shorter events, 10.2 us)
Async XLA Ops:
  0.6 1.0 copy-start.3
  1.9 1.3 %copy-start = (bf16[4,8,16,2048]{3,2,1,0:T(8,128)(2,1)}, bf16[4,8,16,2048]{3,2,1,0:T(8,128)(2,1)S(1)}, u32[]{:S(2)}) copy-start(bf16[4,8,16,2048]{3,2,1,0:T(8,128)(2,1)S(1)} %spread.1) | copy-start | bytes 6291460
  3.3 10.3 %copy-start.12 = (bf16[128,512]{1,0:T(8,128)(2,1)S(1)}, bf16[128,512]{1,0:T(8,128)(2,1)}, u32[]{:S(2)}) copy-start(bf16[128,512]{1,0:T(8,128)(2,1)} %param.10) | copy-start | bytes 393220
  3.3 59.4 %all-to-all-start = ((bf16[32,16,2048]{2,1,0:T(8,128)(2,1)}), bf16[32,16,2048]{2,1,0:T(8,128)(2,1)S(1)}, u32[]{:S(2)}, u32[]{:S(2)}) async-start(bf16[32,16,2048]{2,1,0:T(8,128)(2,1)} %bitcast.18), calls=%async_computation | async-start | bytes 4194304 | tf_op jit(solution)/shard_map/all_to_all | solution.py:231
  13.6 29.1 %copy-start.1 = (bf16[1,128,512]{2,1,0:T(8,128)(2,1)S(1)}, bf16[1,128,512]{2,1,0:T(8,128)(2,1)}, u32[]{:S(2)}) copy-start(bf16[1,128,512]{2,1,0:T(8,128)(2,1)} %param.7) | copy-start | bytes 393220
  13.6 29.1 %copy-start.2 = (bf16[1,128,512]{2,1,0:T(8,128)(2,1)S(1)}, bf16[1,128,512]{2,1,0:T(8,128)(2,1)}, u32[]{:S(2)}) copy-start(bf16[1,128,512]{2,1,0:T(8,128)(2,1)} %param.8) | copy-start | bytes 393220
  13.6 3.4 %collective-permute-start = (bf16[128,512]{1,0:T(8,128)(2,1)S(1)}, bf16[128,512]{1,0:T(8,128)(2,1)S(1)}, u32[]{:S(2)}, u32[]{:S(2)}) collective-permute-start(bf16[128,512]{1,0:T(8,128)(2,1)S(1)} %copy-done.12), channel_id=1, source_target_pairs={{0,8},{8,0},{1,9},{9,1},{2,10},{10,2},{3,11},{11,3},{4,12},{12,4},... | collective-permute-start | bytes 393224 | tf_op jit(solution)/shard_map/ppermute | solution.py:25
  17.1 16.5 %collective-permute-start.1 = (bf16[256,512]{1,0:T(8,128)(2,1)S(1)}, bf16[256,512]{1,0:T(8,128)(2,1)S(1)}, u32[]{:S(2)}, u32[]{:S(2)}) collective-permute-start(bf16[256,512]{1,0:T(8,128)(2,1)S(1)} %bitcast.19), channel_id=1, source_target_pairs={{0,16},{16,32},{32,48},{48,256},{256,272},{272,288},{288,304},{304... | collective-permute-start | bytes 786440 | tf_op jit(solution)/shard_map/ppermute | solution.py:242
  21.4 16.4 %collective-permute-start.3 = (bf16[256,512]{1,0:T(8,128)(2,1)S(1)}, bf16[256,512]{1,0:T(8,128)(2,1)S(1)}, u32[]{:S(2)}, u32[]{:S(2)}) collective-permute-start(bf16[256,512]{1,0:T(8,128)(2,1)S(1)} %bitcast.20), channel_id=1, source_target_pairs={{0,256},{16,272},{32,288},{48,304},{256,0},{272,16},{288,32},{304,... | collective-permute-start | bytes 786440 | tf_op jit(solution)/shard_map/ppermute | solution.py:242
  33.6 17.3 %collective-permute-start.4 = (bf16[512,512]{1,0:T(8,128)(2,1)S(1)}, bf16[512,512]{1,0:T(8,128)(2,1)S(1)}, u32[]{:S(2)}, u32[]{:S(2)}) collective-permute-start(bf16[512,512]{1,0:T(8,128)(2,1)S(1)} %pad_maximum_fusion), channel_id=1, source_target_pairs={{0,32},{16,48},{32,256},{48,272},{256,288},{272,304},{288,0},{304,... | collective-permute-start | bytes 1572872 | tf_op jit(solution)/shard_map/ppermute | solution.py:242
  37.8 13.1 %copy-start.4 = (bf16[256,512]{1,0:T(8,128)(2,1)}, bf16[256,512]{1,0:T(8,128)(2,1)S(1)}, u32[]{:S(2)}) copy-start(bf16[256,512]{1,0:T(8,128)(2,1)S(1)} %collective-permute-done.3.refs_3_) | copy-start | bytes 786436
  37.8 8.5 %collective-permute-start.2 = (bf16[256,512]{1,0:T(8,128)(2,1)S(1)}, bf16[256,512]{1,0:T(8,128)(2,1)S(1)}, u32[]{:S(2)}, u32[]{:S(2)}) collective-permute-start(bf16[256,512]{1,0:T(8,128)(2,1)S(1)} %collective-permute-done.1.refs_1_), channel_id=1, source_target_pairs={{0,8},{8,0},{1,9},{9,1},{2,10},{10,2},{3,11},{11,3},{4,12},{12,4},... | collective-permute-start | bytes 786440 | tf_op jit(solution)/shard_map/ppermute | solution.py:25
  42.8 2.9 %collective-permute-start.5 = (bf16[128,512]{1,0:T(8,128)(2,1)S(1)}, bf16[128,512]{1,0:T(8,128)(2,1)S(1)}, u32[]{:S(2)}, u32[]{:S(2)}) collective-permute-start(bf16[128,512]{1,0:T(8,128)(2,1)S(1)} %multiply_convert_fusion.mixed_ref), channel_id=1, source_target_pairs={{0,8},{8,16},{16,24},{24,32},{32,40},{40,48},{48,56},{56,64},{64,7... | collective-permute-start | bytes 393224 | tf_op jit(solution)/shard_map/ppermute | solution.py:36
  45.7 0.7 copy-start.9
  46.3 0.7 copy-start.6
  50.9 10.5 %collective-permute-start.6 = (bf16[512,512]{1,0:T(8,128)(2,1)S(1)}, bf16[512,512]{1,0:T(8,128)(2,1)}, u32[]{:S(2)}, u32[]{:S(2)}) collective-permute-start(bf16[512,512]{1,0:T(8,128)(2,1)S(1)} %collective-permute-done.4.refs_4_), channel_id=1, source_target_pairs={{0,8},{8,0},{1,9},{9,1},{2,10},{10,2},{3,11},{11,3},{4,12},{12,4},... | collective-permute-start | bytes 1572872 | tf_op jit(solution)/shard_map/ppermute | solution.py:25
  62.6 1.0 copy-start.5
  63.6 0.9 copy-start.7
  64.5 7.3 %copy-start.11 = (bf16[32,128]{1,0:T(8,128)(2,1)S(1)}, bf16[32,128]{1,0:T(8,128)(2,1)}, u32[]{:S(2)}) copy-start(bf16[32,128]{1,0:T(8,128)(2,1)} %filters_ref.3) | copy-start | bytes 24580
  67.6 13.9 %all-to-all-start.1 = ((bf16[4,128,512]{2,1,0:T(8,128)(2,1)}), bf16[4,128,512]{2,1,0:T(8,128)(2,1)S(1)}, u32[]{:S(2)}, u32[]{:S(2)}) async-start(bf16[4,128,512]{2,1,0:T(8,128)(2,1)} %product.1), calls=%async_computation.1 | async-start | bytes 1048576 | tf_op jit(solution)/shard_map/all_to_all | solution.py:231
  71.8 0.9 copy-start.10
  81.6 0.9 copy-start.8
  85.4 15.9 %collective-permute-start.7 = (bf16[128,512]{1,0:T(8,128)(2,1)S(1)}, bf16[128,512]{1,0:T(8,128)(2,1)S(1)}, u32[]{:S(2)}, u32[]{:S(2)}) collective-permute-start(bf16[128,512]{1,0:T(8,128)(2,1)S(1)} %get-tuple-element.24.grad_ref), channel_id=1, source_target_pairs={{8,0},{16,8},{24,16},{32,24},{40,32},{48,40},{56,48},{64,56},{72,6... | collective-permute-start | bytes 393224 | tf_op jit(solution)/shard_map/ppermute | solution.py:36
  101.3 16.7 %all-to-all-start.3 = ((f32[8,32,128]{2,1,0:T(8,128)}), f32[8,32,128]{2,1,0:T(8,128)S(1)}, u32[]{:S(2)}, u32[]{:S(2)}) async-start(f32[8,32,128]{2,1,0:T(8,128)} %sums.1), calls=%async_computation.3 | async-start | bytes 262144 | tf_op jit(solution)/shard_map/all_to_all | solution.py:231

commit v21 on v20

--- a/solution.py
+++ b/solution.py
@@ -263,8 +263,7 @@
     conv, turned = convolve(filters, after_these(before, partial), mixed)
     query_grad, conv_grad, lags = branch_gradients(terms, conv, query, turned)
     lags = summed_copies(exchange(lags, ("x", "co")))
-    after = from_behind(conv_grad, -1)
-    lags, after = lax.optimization_barrier((lags, after))
+    after = from_behind(after_these(conv_grad, lags), -1)
     scale = 1.0 / math.sqrt(2 * lax.axis_size(CONTEXT) * tokens * GROUP)
     filter_grad = jnp.sum(exchange(lags, Z), axis=0) * scale
     key_grad, value_grad = mixed_gradient(filters, conv_grad, after, keys, values)

time: 119 us -> 116 us (0.975)
  the two profiles are of different devices: /device:TPU:8 before, /device:TPU:1 now
where the time goes in v21:
time: 116 us; the launch traced here: 115 us
  starting transfers between devices  57.2 us (49%)
  waiting for transfers between devices  27.7 us (24%)
  Pallas kernels  11.9 us (10%)
  blocking collectives  9.15 us (8%)
  local copies, waits for them, and re-layouts  7.4 us (6%)
    all_to_all x3, starting transfers between devices, exchange(): return lax.all_to_all(copies, axes, split_axis=0, concat_axis=0)  24.1 us
    ppermute x3, starting transfers between devices, along_z(): return lax.ppermute(block, Z + ('co',), route)  16.7 us
    ppermute x2, waiting for transfers between devices, from_behind(): return lax.ppermute(block, CONTEXT, route)  12.3 us
    ppermute x2, starting transfers between devices, from_behind(): return lax.ppermute(block, CONTEXT, route)  9.56 us
    all_to_all x1, blocking collectives, exchange(): return lax.all_to_all(copies, axes, split_axis=0, concat_axis=0)  9.15 us
    unnamed x26, local copies, waits for them, and re-layouts  7.4 us
    ppermute x3, starting transfers between devices, swap(): return lax.ppermute(block, axis, [(0, 1), (1, 0)])  6.82 us
    ppermute x3, waiting for transfers between devices, along_z(): return lax.ppermute(block, Z + ('co',), route)  6.59 us
  transfers between devices with their start and end apart: 11, of which 8 were waited for; matrix products, arithmetic and copies ran while one was open for 0% of the time, Pallas kernels for 4%

profile of v21, /device:TPU:1, one launch (start us, length us, event | category | flops | bytes accessed | tf_op | source)
XLA Modules:
  0.0 115.0 jit_solution(1639690486127967480)
XLA Ops:
  2.0 1.3 %copy-done = bf16[4,8,16,2048]{3,2,1,0:T(8,128)(2,1)} copy-done((bf16[4,8,16,2048]{3,2,1,0:T(8,128)(2,1)}, bf16[4,8,16,2048]{3,2,1,0:T(8,128)(2,1)S(1)}, u32[]{:S(2)}) %copy-start) | copy-done | bytes 2097176
  3.3 10.6 %all-to-all-start = ((bf16[32,16,2048]{2,1,0:T(8,128)(2,1)}), bf16[32,16,2048]{2,1,0:T(8,128)(2,1)S(1)}, u32[]{:S(2)}, u32[]{:S(2)}) async-start(bf16[32,16,2048]{2,1,0:T(8,128)(2,1)} %bitcast.18), calls=%async_computation | async-start | bytes 4194304 | tf_op jit(solution)/shard_map/all_to_all | solution.py:231
  14.0 3.0 %collective-permute-start = (bf16[128,512]{1,0:T(8,128)(2,1)S(1)}, bf16[128,512]{1,0:T(8,128)(2,1)S(1)}, u32[]{:S(2)}, u32[]{:S(2)}) collective-permute-start(bf16[128,512]{1,0:T(8,128)(2,1)S(1)} %copy-done.12), channel_id=1, source_target_pairs={{0,8},{8,0},{1,9},{9,1},{2,10},{10,2},{3,11},{11,3},{4,12},{12,4},... | collective-permute-start | bytes 393224 | tf_op jit(solution)/shard_map/ppermute | solution.py:25
  17.0 1.0 collective-permute-done
  18.0 10.7 %collective-permute-start.1 = (bf16[256,512]{1,0:T(8,128)(2,1)S(1)}, bf16[256,512]{1,0:T(8,128)(2,1)S(1)}, u32[]{:S(2)}, u32[]{:S(2)}) collective-permute-start(bf16[256,512]{1,0:T(8,128)(2,1)S(1)} %bitcast.19), channel_id=1, source_target_pairs={{0,16},{16,32},{32,48},{48,256},{256,272},{272,288},{288,304},{304... | collective-permute-start | bytes 786440 | tf_op jit(solution)/shard_map/ppermute | solution.py:242
  28.7 1.9 %collective-permute-start.3 = (bf16[256,512]{1,0:T(8,128)(2,1)S(1)}, bf16[256,512]{1,0:T(8,128)(2,1)S(1)}, u32[]{:S(2)}, u32[]{:S(2)}) collective-permute-start(bf16[256,512]{1,0:T(8,128)(2,1)S(1)} %bitcast.20), channel_id=1, source_target_pairs={{0,256},{16,272},{32,288},{48,304},{256,0},{272,16},{288,32},{304,... | collective-permute-start | bytes 786440 | tf_op jit(solution)/shard_map/ppermute | solution.py:242
  30.6 1.4 %collective-permute-done.1.refs_1_ = bf16[256,512]{1,0:T(8,128)(2,1)S(1)} collective-permute-done((bf16[256,512]{1,0:T(8,128)(2,1)S(1)}, bf16[256,512]{1,0:T(8,128)(2,1)S(1)}, u32[]{:S(2)}, u32[]{:S(2)}) %collective-permute-start.1) | collective-permute-done | bytes 262176 | tf_op jit(solution)/shard_map/ppermute | solution.py:242
  32.0 4.1 %collective-permute-start.4 = (bf16[512,512]{1,0:T(8,128)(2,1)S(1)}, bf16[512,512]{1,0:T(8,128)(2,1)S(1)}, u32[]{:S(2)}, u32[]{:S(2)}) collective-permute-start(bf16[512,512]{1,0:T(8,128)(2,1)S(1)} %pad_maximum_fusion), channel_id=1, source_target_pairs={{0,32},{16,48},{32,256},{48,272},{256,288},{272,304},{288,0},{304,... | collective-permute-start | bytes 1572872 | tf_op jit(solution)/shard_map/ppermute | solution.py:242
  36.1 5.2 %collective-permute-done.3.refs_3_ = bf16[256,512]{1,0:T(8,128)(2,1)S(1)} collective-permute-done((bf16[256,512]{1,0:T(8,128)(2,1)S(1)}, bf16[256,512]{1,0:T(8,128)(2,1)S(1)}, u32[]{:S(2)}, u32[]{:S(2)}) %collective-permute-start.3) | collective-permute-done | bytes 262176 | tf_op jit(solution)/shard_map/ppermute | solution.py:242
  41.3 1.9 %collective-permute-start.2 = (bf16[256,512]{1,0:T(8,128)(2,1)S(1)}, bf16[256,512]{1,0:T(8,128)(2,1)S(1)}, u32[]{:S(2)}, u32[]{:S(2)}) collective-permute-start(bf16[256,512]{1,0:T(8,128)(2,1)S(1)} %collective-permute-done.1.refs_1_), channel_id=1, source_target_pairs={{0,8},{8,0},{1,9},{9,1},{2,10},{10,2},{3,11},{11,3},{4,12},{12,4},... | collective-permute-start | bytes 786440 | tf_op jit(solution)/shard_map/ppermute | solution.py:25
  43.3 6.5 %collective-permute-start.5 = (bf16[128,512]{1,0:T(8,128)(2,1)S(1)}, bf16[128,512]{1,0:T(8,128)(2,1)S(1)}, u32[]{:S(2)}, u32[]{:S(2)}) collective-permute-start(bf16[128,512]{1,0:T(8,128)(2,1)S(1)} %multiply_convert_fusion.mixed_ref), channel_id=1, source_target_pairs={{0,8},{8,16},{16,24},{24,32},{32,40},{40,48},{48,56},{56,64},{64,7... | collective-permute-start | bytes 393224 | tf_op jit(solution)/shard_map/ppermute | solution.py:36
  49.8 7.4 %collective-permute-done.5.before_ref = bf16[128,512]{1,0:T(8,128)(2,1)S(1)} collective-permute-done((bf16[128,512]{1,0:T(8,128)(2,1)S(1)}, bf16[128,512]{1,0:T(8,128)(2,1)S(1)}, u32[]{:S(2)}, u32[]{:S(2)}) %collective-permute-start.5) | collective-permute-done | bytes 131104 | tf_op jit(solution)/shard_map/ppermute | solution.py:36
  58.6 1.9 %collective-permute-start.6 = (bf16[512,512]{1,0:T(8,128)(2,1)S(1)}, bf16[512,512]{1,0:T(8,128)(2,1)}, u32[]{:S(2)}, u32[]{:S(2)}) collective-permute-start(bf16[512,512]{1,0:T(8,128)(2,1)S(1)} %collective-permute-done.4.refs_4_), channel_id=1, source_target_pairs={{0,8},{8,0},{1,9},{9,1},{2,10},{10,2},{3,11},{11,3},{4,12},{12,4},... | collective-permute-start | bytes 1572872 | tf_op jit(solution)/shard_map/ppermute | solution.py:25
  60.6 1.9 %collective-permute-done.6.refs_5_ = bf16[512,512]{1,0:T(8,128)(2,1)} collective-permute-done((bf16[512,512]{1,0:T(8,128)(2,1)S(1)}, bf16[512,512]{1,0:T(8,128)(2,1)}, u32[]{:S(2)}, u32[]{:S(2)}) %collective-permute-start.6) | collective-permute-done | bytes 524320 | tf_op jit(solution)/shard_map/ppermute | solution.py:25
  64.7 3.1 %product.1 = bf16[4,128,512]{2,1,0:T(8,128)(2,1)} custom-call(s32[2]{0:T(128)S(1)} %pad_add_fusion.place_ref, bf16[512,2048]{1,0:T(8,128)(2,1)S(1)} %bitcast.17, bf16[256,512]{1,0:T(8,128)(2,1)S(1)} %bitcast.22, bf16[256,512]{1,0:T(8,128)(2,1)S(1)} %collective-permute-done.1.refs_1_, bf16[256,512]{1,0:T(8,128)(2,1)S(1)} %copy-done.7, ...), custom_call_target="tpu_custom_call" | custom-call | tf_op jit(solution)/shard_map/product/pallas_call | solution.py:216
  67.8 5.7 %all-to-all-start.1 = ((bf16[4,128,512]{2,1,0:T(8,128)(2,1)}), bf16[4,128,512]{2,1,0:T(8,128)(2,1)S(1)}, u32[]{:S(2)}, u32[]{:S(2)}) async-start(bf16[4,128,512]{2,1,0:T(8,128)(2,1)} %product.1), calls=%async_computation.1 | async-start | bytes 1048576 | tf_op jit(solution)/shard_map/all_to_all | solution.py:231
  74.4 2.3 %conv.1 = (f32[128,512]{1,0:T(8,128)S(1)}, bf16[256,512]{1,0:T(8,128)(2,1)S(1)}) custom-call(bf16[32,128]{1,0:T(8,128)(2,1)S(1)} %copy-done.11, bf16[128,512]{1,0:T(8,128)(2,1)S(1)} %copy-done.10, bf16[128,512]{1,0:T(8,128)(2,1)S(1)} %multiply_convert_fusion.mixed_ref), custom_call_target="tpu_custom_call" | custom-call | tf_op jit(solution)/shard_map/conv/pallas_call | solution.py:172
  76.7 5.7 %all-to-all-done.1.terms_ref = bf16[4,128,512]{2,1,0:T(8,128)(2,1)S(1)} async-done(((bf16[4,128,512]{2,1,0:T(8,128)(2,1)}), bf16[4,128,512]{2,1,0:T(8,128)(2,1)S(1)}, u32[]{:S(2)}, u32[]{:S(2)}) %all-to-all-start.1) | async-done | bytes 524320 | tf_op jit(solution)/shard_map/all_to_all | solution.py:231
  83.3 2.9 %branch.1 = (bf16[128,512]{1,0:T(8,128)(2,1)}, bf16[128,512]{1,0:T(8,128)(2,1)S(1)}, f32[8,32,128]{2,1,0:T(8,128)S(1)}) custom-call(bf16[4,128,512]{2,1,0:T(8,128)(2,1)S(1)} %all-to-all-done.1.terms_ref, f32[128,512]{1,0:T(8,128)S(1)} %get-tuple-element.20.conv_ref, bf16[128,512]{1,0:T(8,128)(2,1)S(1)} %bitcast.27, ...), custom_call_target="tpu_custom_call" | custom-call | tf_op jit(solution)/shard_map/branch/pallas_call | solution.py:200
  86.2 9.2 %all_to_all.20.parts_ref = f32[8,32,128]{2,1,0:T(8,128)S(1)} all-to-all(f32[8,32,128]{2,1,0:T(8,128)S(1)} %get-tuple-element.24), channel_id=1, replica_groups=mesh['zh'=2,'x'=4,'zl'=4,'co'=2,'yq'=4,'yp'=2] {'x','co'}, dimensions={0} | all-to-all | bytes 262144 | tf_op jit(solution)/shard_map/all_to_all | solution.py:231
  96.1 7.8 %all-to-all-start.3 = ((f32[8,32,128]{2,1,0:T(8,128)}), f32[8,32,128]{2,1,0:T(8,128)S(1)}, u32[]{:S(2)}, u32[]{:S(2)}) async-start(f32[8,32,128]{2,1,0:T(8,128)} %sums.1), calls=%async_computation.3 | async-start | bytes 262144 | tf_op jit(solution)/shard_map/all_to_all | solution.py:231
  103.9 3.0 %collective-permute-start.7 = (bf16[128,512]{1,0:T(8,128)(2,1)S(1)}, bf16[128,512]{1,0:T(8,128)(2,1)S(1)}, u32[]{:S(2)}, u32[]{:S(2)}) collective-permute-start(bf16[128,512]{1,0:T(8,128)(2,1)S(1)} %get-tuple-element.25.grad_ref), channel_id=1, source_target_pairs={{8,0},{16,8},{24,16},{32,24},{40,32},{48,40},{56,48},{64,56},{72,6... | collective-permute-start | bytes 393224 | tf_op jit(solution)/shard_map/ppermute | solution.py:36
  106.9 4.9 %collective-permute-done.7.after_ref = bf16[128,512]{1,0:T(8,128)(2,1)S(1)} collective-permute-done((bf16[128,512]{1,0:T(8,128)(2,1)S(1)}, bf16[128,512]{1,0:T(8,128)(2,1)S(1)}, u32[]{:S(2)}, u32[]{:S(2)}) %collective-permute-start.7) | collective-permute-done | bytes 131104 | tf_op jit(solution)/shard_map/ppermute | solution.py:36
  111.8 2.5 %mixed_grad.1 = (bf16[128,512]{1,0:T(8,128)(2,1)}, bf16[128,512]{1,0:T(8,128)(2,1)}) custom-call(bf16[32,128]{1,0:T(8,128)(2,1)S(1)} %copy-done.11, bf16[128,512]{1,0:T(8,128)(2,1)S(1)} %get-tuple-element.25.grad_ref, bf16[128,512]{1,0:T(8,128)(2,1)S(1)} %collective-permute-done.7.after_ref, bf16[128,512]{1,0:T(8,128)(2,1)S(1)} %bitcast.24, ...), custom_call_target="tpu_custom_call" | custom-call | tf_op jit(solution)/shard_map/mixed_grad/pallas_call | solution.py:186
  (38 shorter events, 8.2 us)
Async XLA Ops:
  0.6 1.0 copy-start.3
  1.9 1.3 %copy-start = (bf16[4,8,16,2048]{3,2,1,0:T(8,128)(2,1)}, bf16[4,8,16,2048]{3,2,1,0:T(8,128)(2,1)S(1)}, u32[]{:S(2)}) copy-start(bf16[4,8,16,2048]{3,2,1,0:T(8,128)(2,1)S(1)} %spread.1) | copy-start | bytes 6291460
  3.3 10.6 %copy-start.12 = (bf16[128,512]{1,0:T(8,128)(2,1)S(1)}, bf16[128,512]{1,0:T(8,128)(2,1)}, u32[]{:S(2)}) copy-start(bf16[128,512]{1,0:T(8,128)(2,1)} %param.10) | copy-start | bytes 393220
  3.3 59.5 %all-to-all-start = ((bf16[32,16,2048]{2,1,0:T(8,128)(2,1)}), bf16[32,16,2048]{2,1,0:T(8,128)(2,1)S(1)}, u32[]{:S(2)}, u32[]{:S(2)}) async-start(bf16[32,16,2048]{2,1,0:T(8,128)(2,1)} %bitcast.18), calls=%async_computation | async-start | bytes 4194304 | tf_op jit(solution)/shard_map/all_to_all | solution.py:231
  13.9 29.3 %copy-start.1 = (bf16[1,128,512]{2,1,0:T(8,128)(2,1)S(1)}, bf16[1,128,512]{2,1,0:T(8,128)(2,1)}, u32[]{:S(2)}) copy-start(bf16[1,128,512]{2,1,0:T(8,128)(2,1)} %param.7) | copy-start | bytes 393220
  14.0 29.3 %copy-start.2 = (bf16[1,128,512]{2,1,0:T(8,128)(2,1)S(1)}, bf16[1,128,512]{2,1,0:T(8,128)(2,1)}, u32[]{:S(2)}) copy-start(bf16[1,128,512]{2,1,0:T(8,128)(2,1)} %param.8) | copy-start | bytes 393220
  14.0 4.0 %collective-permute-start = (bf16[128,512]{1,0:T(8,128)(2,1)S(1)}, bf16[128,512]{1,0:T(8,128)(2,1)S(1)}, u32[]{:S(2)}, u32[]{:S(2)}) collective-permute-start(bf16[128,512]{1,0:T(8,128)(2,1)S(1)} %copy-done.12), channel_id=1, source_target_pairs={{0,8},{8,0},{1,9},{9,1},{2,10},{10,2},{3,11},{11,3},{4,12},{12,4},... | collective-permute-start | bytes 393224 | tf_op jit(solution)/shard_map/ppermute | solution.py:25
  18.0 14.0 %collective-permute-start.1 = (bf16[256,512]{1,0:T(8,128)(2,1)S(1)}, bf16[256,512]{1,0:T(8,128)(2,1)S(1)}, u32[]{:S(2)}, u32[]{:S(2)}) collective-permute-start(bf16[256,512]{1,0:T(8,128)(2,1)S(1)} %bitcast.19), channel_id=1, source_target_pairs={{0,16},{16,32},{32,48},{48,256},{256,272},{272,288},{288,304},{304... | collective-permute-start | bytes 786440 | tf_op jit(solution)/shard_map/ppermute | solution.py:242
  28.7 12.7 %collective-permute-start.3 = (bf16[256,512]{1,0:T(8,128)(2,1)S(1)}, bf16[256,512]{1,0:T(8,128)(2,1)S(1)}, u32[]{:S(2)}, u32[]{:S(2)}) collective-permute-start(bf16[256,512]{1,0:T(8,128)(2,1)S(1)} %bitcast.20), channel_id=1, source_target_pairs={{0,256},{16,272},{32,288},{48,304},{256,0},{272,16},{288,32},{304,... | collective-permute-start | bytes 786440 | tf_op jit(solution)/shard_map/ppermute | solution.py:242
  32.0 26.6 %collective-permute-start.4 = (bf16[512,512]{1,0:T(8,128)(2,1)S(1)}, bf16[512,512]{1,0:T(8,128)(2,1)S(1)}, u32[]{:S(2)}, u32[]{:S(2)}) collective-permute-start(bf16[512,512]{1,0:T(8,128)(2,1)S(1)} %pad_maximum_fusion), channel_id=1, source_target_pairs={{0,32},{16,48},{32,256},{48,272},{256,288},{272,304},{288,0},{304,... | collective-permute-start | bytes 1572872 | tf_op jit(solution)/shard_map/ppermute | solution.py:242
  41.3 17.3 %copy-start.4 = (bf16[256,512]{1,0:T(8,128)(2,1)}, bf16[256,512]{1,0:T(8,128)(2,1)S(1)}, u32[]{:S(2)}) copy-start(bf16[256,512]{1,0:T(8,128)(2,1)S(1)} %collective-permute-done.3.refs_3_) | copy-start | bytes 786436
  41.3 16.5 %collective-permute-start.2 = (bf16[256,512]{1,0:T(8,128)(2,1)S(1)}, bf16[256,512]{1,0:T(8,128)(2,1)S(1)}, u32[]{:S(2)}, u32[]{:S(2)}) collective-permute-start(bf16[256,512]{1,0:T(8,128)(2,1)S(1)} %collective-permute-done.1.refs_1_), channel_id=1, source_target_pairs={{0,8},{8,0},{1,9},{9,1},{2,10},{10,2},{3,11},{11,3},{4,12},{12,4},... | collective-permute-start | bytes 786440 | tf_op jit(solution)/shard_map/ppermute | solution.py:25
  43.3 13.9 %collective-permute-start.5 = (bf16[128,512]{1,0:T(8,128)(2,1)S(1)}, bf16[128,512]{1,0:T(8,128)(2,1)S(1)}, u32[]{:S(2)}, u32[]{:S(2)}) collective-permute-start(bf16[128,512]{1,0:T(8,128)(2,1)S(1)} %multiply_convert_fusion.mixed_ref), channel_id=1, source_target_pairs={{0,8},{8,16},{16,24},{24,32},{32,40},{40,48},{48,56},{56,64},{64,7... | collective-permute-start | bytes 393224 | tf_op jit(solution)/shard_map/ppermute | solution.py:36
  57.2 0.7 copy-start.9
  57.9 0.7 copy-start.6
  58.6 3.9 %collective-permute-start.6 = (bf16[512,512]{1,0:T(8,128)(2,1)S(1)}, bf16[512,512]{1,0:T(8,128)(2,1)}, u32[]{:S(2)}, u32[]{:S(2)}) collective-permute-start(bf16[512,512]{1,0:T(8,128)(2,1)S(1)} %collective-permute-done.4.refs_4_), channel_id=1, source_target_pairs={{0,8},{8,0},{1,9},{9,1},{2,10},{10,2},{3,11},{11,3},{4,12},{12,4},... | collective-permute-start | bytes 1572872 | tf_op jit(solution)/shard_map/ppermute | solution.py:25
  62.8 1.0 copy-start.5
  63.8 0.9 copy-start.7
  64.7 8.8 %copy-start.11 = (bf16[32,128]{1,0:T(8,128)(2,1)S(1)}, bf16[32,128]{1,0:T(8,128)(2,1)}, u32[]{:S(2)}) copy-start(bf16[32,128]{1,0:T(8,128)(2,1)} %filters_ref.3) | copy-start | bytes 24580
  67.8 14.6 %all-to-all-start.1 = ((bf16[4,128,512]{2,1,0:T(8,128)(2,1)}), bf16[4,128,512]{2,1,0:T(8,128)(2,1)S(1)}, u32[]{:S(2)}, u32[]{:S(2)}) async-start(bf16[4,128,512]{2,1,0:T(8,128)(2,1)} %product.1), calls=%async_computation.1 | async-start | bytes 1048576 | tf_op jit(solution)/shard_map/all_to_all | solution.py:231
  73.5 0.9 copy-start.10
  82.4 0.9 copy-start.8
  96.1 18.3 %all-to-all-start.3 = ((f32[8,32,128]{2,1,0:T(8,128)}), f32[8,32,128]{2,1,0:T(8,128)S(1)}, u32[]{:S(2)}, u32[]{:S(2)}) async-start(f32[8,32,128]{2,1,0:T(8,128)} %sums.1), calls=%async_computation.3 | async-start | bytes 262144 | tf_op jit(solution)/shard_map/all_to_all | solution.py:231
  103.9 8.0 %collective-permute-start.7 = (bf16[128,512]{1,0:T(8,128)(2,1)S(1)}, bf16[128,512]{1,0:T(8,128)(2,1)S(1)}, u32[]{:S(2)}, u32[]{:S(2)}) collective-permute-start(bf16[128,512]{1,0:T(8,128)(2,1)S(1)} %get-tuple-element.25.grad_ref), channel_id=1, source_target_pairs={{8,0},{16,8},{24,16},{32,24},{40,32},{48,40},{56,48},{64,56},{72,6... | collective-permute-start | bytes 393224 | tf_op jit(solution)/shard_map/ppermute | solution.py:36

commit v22 on v12

--- a/solution.py
+++ b/solution.py
@@ -275,8 +275,8 @@
     conv, turned = convolve(filters, before, mixed)
     query_grad, conv_grad, lags = branch_gradients(terms, conv, query, turned)
     lags = summed_copies(exchange(lags, ("x", "co")))
-    after = from_behind(conv_grad, -1)
-    lags, after = lax.optimization_barrier((lags, after))
+    tied_grad, _ = lax.optimization_barrier((conv_grad, lags))
+    after = from_behind(tied_grad, -1)
     scale = 1.0 / math.sqrt(2 * lax.axis_size(CONTEXT) * tokens * GROUP)
     filter_grad = jnp.sum(exchange(lags, Z), axis=0) * scale
     key_grad, value_grad = mixed_gradient(filters, conv_grad, after, keys, values)

time: 116 us -> 116 us (level)
  blocking collectives: 7.62 us -> 8.94 us
    all_to_all x3, waiting for transfers between devices: 11.2 us -> 5.87 us  [exchange(): return lax.all_to_all(copies, axes, split_axis=0, concat_axis=0)]
    ppermute x2, waiting for transfers between devices: 1.84 us -> 6.75 us  [from_behind(): return lax.ppermute(block, CONTEXT, route)]
    all_to_all x1, blocking collectives: 7.62 us -> 8.94 us  [exchange(): return lax.all_to_all(copies, axes, split_axis=0, concat_axis=0)]
  transfers between devices with their start and end apart: 13 -> 13, of which waited for: 6 -> 6; matrix products, arithmetic and copies ran while one was open for 2% -> 2% of each run, Pallas kernels for 6% -> 5%
where the time goes in v22:
time: 116 us; the launch traced here: 115 us
  starting transfers between devices  69.5 us (60%)
  waiting for transfers between devices  16.1 us (14%)
  Pallas kernels  14 us (12%)
  blocking collectives  8.94 us (8%)
  local copies, waits for them, and re-layouts  3.94 us (3%)
  other arithmetic  1.63 us (1%)
    ppermute x3, starting transfers between devices, along_z(): return lax.ppermute(block, Z + ('co',), route)  22.4 us
    all_to_all x3, starting transfers between devices, exchange(): return lax.all_to_all(copies, axes, split_axis=0, concat_axis=0)  20.5 us
    ppermute x2, starting transfers between devices, from_behind(): return lax.ppermute(block, CONTEXT, route)  10.3 us
    ppermute x3, starting transfers between devices, swap(): return lax.ppermute(block, axis, [(0, 1), (1, 0)])  9.52 us
    all_to_all x1, blocking collectives, exchange(): return lax.all_to_all(copies, axes, split_axis=0, concat_axis=0)  8.94 us
    ppermute x2, starting transfers between devices, ahead(): lax.ppermute(block, axes, [((i + distance) % n, i) for i in range(n)])  6.78 us
    ppermute x2, waiting for transfers between devices, from_behind(): return lax.ppermute(block, CONTEXT, route)  6.75 us
    all_to_all x3, waiting for transfers between devices, exchange(): return lax.all_to_all(copies, axes, split_axis=0, concat_axis=0)  5.87 us
  transfers between devices with their start and end apart: 13, of which 6 were waited for; matrix products, arithmetic and copies ran while one was open for 2% of the time, Pallas kernels for 5%

profile of v22, /device:TPU:1, one launch (start us, length us, event | category | flops | bytes accessed | tf_op | source)
XLA Modules:
  0.0 115.0 jit_solution(751371442773569406)
XLA Ops:
  1.6 1.6 %spread.1 = bf16[4,4,16,2048]{3,2,1,0:T(8,128)(2,1)} custom-call(bf16[16,8192]{1,0:T(8,128)(2,1)S(1)} %bitcast.31), custom_call_target="tpu_custom_call" | custom-call | tf_op jit(solution)/shard_map/spread/pallas_call | solution.py:153
  3.1 10.3 %all-to-all-start = ((bf16[16,16,2048]{2,1,0:T(8,128)(2,1)}), bf16[16,16,2048]{2,1,0:T(8,128)(2,1)S(1)}, u32[]{:S(2)}, u32[]{:S(2)}) async-start(bf16[16,16,2048]{2,1,0:T(8,128)(2,1)} %bitcast.4), calls=%async_computation | async-start | bytes 2097152 | tf_op jit(solution)/shard_map/all_to_all | solution.py:237
  13.5 2.9 %collective-permute-start = (bf16[128,512]{1,0:T(8,128)(2,1)S(1)}, bf16[128,512]{1,0:T(8,128)(2,1)S(1)}, u32[]{:S(2)}, u32[]{:S(2)}) collective-permute-start(bf16[128,512]{1,0:T(8,128)(2,1)S(1)} %copy-done.9), channel_id=1, source_target_pairs={{0,8},{8,0},{1,9},{9,1},{2,10},{10,2},{3,11},{11,3},{4,12},{12,4},... | collective-permute-start | bytes 393224 | tf_op jit(solution)/shard_map/ppermute | solution.py:24
  17.4 10.7 %collective-permute-start.1 = (bf16[256,512]{1,0:T(8,128)(2,1)S(1)}, bf16[256,512]{1,0:T(8,128)(2,1)S(1)}, u32[]{:S(2)}, u32[]{:S(2)}) collective-permute-start(bf16[256,512]{1,0:T(8,128)(2,1)S(1)} %bitcast.21), channel_id=1, source_target_pairs={{0,16},{16,32},{32,48},{48,256},{256,272},{272,288},{288,304},{304... | collective-permute-start | bytes 786440 | tf_op jit(solution)/shard_map/ppermute | solution.py:249
  28.1 1.9 %collective-permute-start.3 = (bf16[256,512]{1,0:T(8,128)(2,1)S(1)}, bf16[256,512]{1,0:T(8,128)(2,1)S(1)}, u32[]{:S(2)}, u32[]{:S(2)}) collective-permute-start(bf16[256,512]{1,0:T(8,128)(2,1)S(1)} %bitcast.22), channel_id=1, source_target_pairs={{0,256},{16,272},{32,288},{48,304},{256,0},{272,16},{288,32},{304,... | collective-permute-start | bytes 786440 | tf_op jit(solution)/shard_map/ppermute | solution.py:249
  30.0 1.4 %collective-permute-done.1.refs_1_ = bf16[256,512]{1,0:T(8,128)(2,1)S(1)} collective-permute-done((bf16[256,512]{1,0:T(8,128)(2,1)S(1)}, bf16[256,512]{1,0:T(8,128)(2,1)S(1)}, u32[]{:S(2)}, u32[]{:S(2)}) %collective-permute-start.1) | collective-permute-done | bytes 262176 | tf_op jit(solution)/shard_map/ppermute | solution.py:249
  31.4 4.7 %collective-permute-start.2 = (bf16[256,512]{1,0:T(8,128)(2,1)S(1)}, bf16[256,512]{1,0:T(8,128)(2,1)S(1)}, u32[]{:S(2)}, u32[]{:S(2)}) collective-permute-start(bf16[256,512]{1,0:T(8,128)(2,1)S(1)} %collective-permute-done.1.refs_1_), channel_id=1, source_target_pairs={{0,8},{8,0},{1,9},{9,1},{2,10},{10,2},{3,11},{11,3},{4,12},{12,4},... | collective-permute-start | bytes 786440 | tf_op jit(solution)/shard_map/ppermute | solution.py:24
  37.0 9.8 %collective-permute-start.7 = (bf16[512,512]{1,0:T(8,128)(2,1)}, bf16[512,512]{1,0:T(8,128)(2,1)S(1)}, u32[]{:S(2)}, u32[]{:S(2)}) collective-permute-start(bf16[512,512]{1,0:T(8,128)(2,1)} %pad_maximum_fusion), channel_id=1, source_target_pairs={{0,32},{16,48},{32,256},{48,272},{256,288},{272,304},{288,0},{304,... | collective-permute-start | bytes 1572872 | tf_op jit(solution)/shard_map/ppermute | solution.py:249
  47.9 2.3 %collective-permute-start.4 = (bf16[8,16,2048]{2,1,0:T(8,128)(2,1)}, bf16[8,16,2048]{2,1,0:T(8,128)(2,1)S(1)}, u32[]{:S(2)}, u32[]{:S(2)}) collective-permute-start(bf16[8,16,2048]{2,1,0:T(8,128)(2,1)} %get-tuple-element.39), channel_id=1, source_target_pairs={{7,0},{0,1},{1,2},{2,3},{3,4},{4,5},{5,6},{6,7},{15,8},{8,9},{9,10... | collective-permute-start | bytes 1572872 | tf_op jit(solution)/shard_map/ppermute | solution.py:242
  50.2 4.5 %collective-permute-start.5 = (bf16[8,16,2048]{2,1,0:T(8,128)(2,1)}, bf16[8,16,2048]{2,1,0:T(8,128)(2,1)S(1)}, u32[]{:S(2)}, u32[]{:S(2)}) collective-permute-start(bf16[8,16,2048]{2,1,0:T(8,128)(2,1)} %get-tuple-element.38), channel_id=1, source_target_pairs={{1,0},{2,1},{3,2},{4,3},{5,4},{6,5},{7,6},{0,7},{9,8},{10,9},{11,1... | collective-permute-start | bytes 1572872 | tf_op jit(solution)/shard_map/ppermute | solution.py:242
  54.7 1.1 collective-permute-done.7.refs_4_
  55.9 1.9 %collective-permute-start.8 = (bf16[512,512]{1,0:T(8,128)(2,1)S(1)}, bf16[512,512]{1,0:T(8,128)(2,1)}, u32[]{:S(2)}, u32[]{:S(2)}) collective-permute-start(bf16[512,512]{1,0:T(8,128)(2,1)S(1)} %collective-permute-done.7.refs_4_), channel_id=1, source_target_pairs={{0,8},{8,0},{1,9},{9,1},{2,10},{10,2},{3,11},{11,3},{4,12},{12,4},... | collective-permute-start | bytes 1572872 | tf_op jit(solution)/shard_map/ppermute | solution.py:24
  57.8 7.2 %collective-permute-start.6 = (bf16[128,512]{1,0:T(8,128)(2,1)S(1)}, bf16[128,512]{1,0:T(8,128)(2,1)}, u32[]{:S(2)}, u32[]{:S(2)}) collective-permute-start(bf16[128,512]{1,0:T(8,128)(2,1)S(1)} %multiply_convert_fusion.mixed_ref), channel_id=1, source_target_pairs={{0,8},{8,16},{16,24},{24,32},{32,40},{40,48},{48,56},{56,64},{64,7... | collective-permute-start | bytes 393224 | tf_op jit(solution)/shard_map/ppermute | solution.py:35
  65.2 1.8 %collective-permute-done.6.before_ref = bf16[128,512]{1,0:T(8,128)(2,1)} collective-permute-done((bf16[128,512]{1,0:T(8,128)(2,1)S(1)}, bf16[128,512]{1,0:T(8,128)(2,1)}, u32[]{:S(2)}, u32[]{:S(2)}) %collective-permute-start.6) | collective-permute-done | bytes 131104 | tf_op jit(solution)/shard_map/ppermute | solution.py:35
  68.9 3.1 %product.1 = bf16[4,4,2,16,512]{4,3,2,1,0:T(8,128)(2,1)} custom-call(s32[3]{0:T(128)S(1)} %pad_add_fusion.place_ref, bf16[256,2048]{1,0:T(8,128)(2,1)S(1)} %bitcast.20, bf16[128,2048]{1,0:T(8,128)(2,1)S(1)} %bitcast.25, bf16[128,2048]{1,0:T(8,128)(2,1)S(1)} %bitcast.26, bf16[256,512]{1,0:T(8,128)(2,1)S(1)} %bitcast.24, ...), custom_call_target="tpu_custom_call" | custom-call | tf_op jit(solution)/shard_map/product/pallas_call | solution.py:220
  72.0 4.4 %all-to-all-start.1 = ((bf16[4,128,512]{2,1,0:T(8,128)(2,1)}), bf16[4,128,512]{2,1,0:T(8,128)(2,1)S(1)}, u32[]{:S(2)}, u32[]{:S(2)}) async-start(bf16[4,128,512]{2,1,0:T(8,128)(2,1)} %bitcast.13), calls=%async_computation.1 | async-start | bytes 1048576 | tf_op jit(solution)/shard_map/all_to_all | solution.py:237
  76.5 3.3 %conv.1 = (f32[128,512]{1,0:T(8,128)S(1)}, bf16[256,512]{1,0:T(8,128)(2,1)S(1)}) custom-call(bf16[32,128]{1,0:T(8,128)(2,1)S(1)} %copy-done.8, bf16[128,512]{1,0:T(8,128)(2,1)} %collective-permute-done.6.before_ref, bf16[128,512]{1,0:T(8,128)(2,1)S(1)} %multiply_convert_fusion.mixed_ref), custom_call_target="tpu_custom_call" | custom-call | tf_op jit(solution)/shard_map/conv/pallas_call | solution.py:176
  79.7 5.9 %all-to-all-done.1.terms_ref = bf16[4,128,512]{2,1,0:T(8,128)(2,1)S(1)} async-done(((bf16[4,128,512]{2,1,0:T(8,128)(2,1)}), bf16[4,128,512]{2,1,0:T(8,128)(2,1)S(1)}, u32[]{:S(2)}, u32[]{:S(2)}) %all-to-all-start.1) | async-done | bytes 524320 | tf_op jit(solution)/shard_map/all_to_all | solution.py:237
  85.6 2.9 %branch.1 = (bf16[128,512]{1,0:T(8,128)(2,1)}, bf16[128,512]{1,0:T(8,128)(2,1)S(1)}, f32[8,32,128]{2,1,0:T(8,128)S(1)}) custom-call(bf16[4,128,512]{2,1,0:T(8,128)(2,1)S(1)} %all-to-all-done.1.terms_ref, f32[128,512]{1,0:T(8,128)S(1)} %get-tuple-element.30.conv_ref, bf16[128,512]{1,0:T(8,128)(2,1)S(1)} %bitcast.32, ...), custom_call_target="tpu_custom_call" | custom-call | tf_op jit(solution)/shard_map/branch/pallas_call | solution.py:204
  88.5 8.9 %all_to_all.20.parts_ref = f32[8,32,128]{2,1,0:T(8,128)S(1)} all-to-all(f32[8,32,128]{2,1,0:T(8,128)S(1)} %get-tuple-element.34), channel_id=1, replica_groups=mesh['zh'=2,'x'=4,'zl'=4,'co'=2,'yq'=4,'yp'=2] {'x','co'}, dimensions={0} | all-to-all | bytes 262144 | tf_op jit(solution)/shard_map/all_to_all | solution.py:237
  98.1 5.7 %all-to-all-start.3 = ((f32[8,32,128]{2,1,0:T(8,128)}), f32[8,32,128]{2,1,0:T(8,128)S(1)}, u32[]{:S(2)}, u32[]{:S(2)}) async-start(f32[8,32,128]{2,1,0:T(8,128)} %sums.1), calls=%async_computation.3 | async-start | bytes 262144 | tf_op jit(solution)/shard_map/all_to_all | solution.py:237
  103.9 3.0 %collective-permute-start.9 = (bf16[128,512]{1,0:T(8,128)(2,1)S(1)}, bf16[128,512]{1,0:T(8,128)(2,1)S(1)}, u32[]{:S(2)}, u32[]{:S(2)}) collective-permute-start(bf16[128,512]{1,0:T(8,128)(2,1)S(1)} %get-tuple-element.35.grad_ref), channel_id=1, source_target_pairs={{8,0},{16,8},{24,16},{32,24},{40,32},{48,40},{56,48},{64,56},{72,6... | collective-permute-start | bytes 393224 | tf_op jit(solution)/shard_map/ppermute | solution.py:35
  106.9 4.9 %collective-permute-done.9.after_ref = bf16[128,512]{1,0:T(8,128)(2,1)S(1)} collective-permute-done((bf16[128,512]{1,0:T(8,128)(2,1)S(1)}, bf16[128,512]{1,0:T(8,128)(2,1)S(1)}, u32[]{:S(2)}, u32[]{:S(2)}) %collective-permute-start.9) | collective-permute-done | bytes 131104 | tf_op jit(solution)/shard_map/ppermute | solution.py:35
  111.8 2.5 %mixed_grad.1 = (bf16[128,512]{1,0:T(8,128)(2,1)}, bf16[128,512]{1,0:T(8,128)(2,1)}) custom-call(bf16[32,128]{1,0:T(8,128)(2,1)S(1)} %copy-done.8, bf16[128,512]{1,0:T(8,128)(2,1)S(1)} %get-tuple-element.35.grad_ref, bf16[128,512]{1,0:T(8,128)(2,1)S(1)} %collective-permute-done.9.after_ref, bf16[128,512]{1,0:T(8,128)(2,1)S(1)} %bitcast.30, ...), custom_call_target="tpu_custom_call" | custom-call | tf_op jit(solution)/shard_map/mixed_grad/pallas_call | solution.py:190
  (37 shorter events, 7.2 us)
Async XLA Ops:
  0.6 1.0 copy-start.2
  3.1 10.4 %copy-start.9 = (bf16[128,512]{1,0:T(8,128)(2,1)S(1)}, bf16[128,512]{1,0:T(8,128)(2,1)}, u32[]{:S(2)}) copy-start(bf16[128,512]{1,0:T(8,128)(2,1)} %param.10) | copy-start | bytes 393220
  3.1 43.7 %all-to-all-start = ((bf16[16,16,2048]{2,1,0:T(8,128)(2,1)}), bf16[16,16,2048]{2,1,0:T(8,128)(2,1)S(1)}, u32[]{:S(2)}, u32[]{:S(2)}) async-start(bf16[16,16,2048]{2,1,0:T(8,128)(2,1)} %bitcast.4), calls=%async_computation | async-start | bytes 2097152 | tf_op jit(solution)/shard_map/all_to_all | solution.py:237
  13.5 3.8 %collective-permute-start = (bf16[128,512]{1,0:T(8,128)(2,1)S(1)}, bf16[128,512]{1,0:T(8,128)(2,1)S(1)}, u32[]{:S(2)}, u32[]{:S(2)}) collective-permute-start(bf16[128,512]{1,0:T(8,128)(2,1)S(1)} %copy-done.9), channel_id=1, source_target_pairs={{0,8},{8,0},{1,9},{9,1},{2,10},{10,2},{3,11},{11,3},{4,12},{12,4},... | collective-permute-start | bytes 393224 | tf_op jit(solution)/shard_map/ppermute | solution.py:24
  17.4 14.0 %collective-permute-start.1 = (bf16[256,512]{1,0:T(8,128)(2,1)S(1)}, bf16[256,512]{1,0:T(8,128)(2,1)S(1)}, u32[]{:S(2)}, u32[]{:S(2)}) collective-permute-start(bf16[256,512]{1,0:T(8,128)(2,1)S(1)} %bitcast.21), channel_id=1, source_target_pairs={{0,16},{16,32},{32,48},{48,256},{256,272},{272,288},{288,304},{304... | collective-permute-start | bytes 786440 | tf_op jit(solution)/shard_map/ppermute | solution.py:249
  28.1 18.7 %collective-permute-start.3 = (bf16[256,512]{1,0:T(8,128)(2,1)S(1)}, bf16[256,512]{1,0:T(8,128)(2,1)S(1)}, u32[]{:S(2)}, u32[]{:S(2)}) collective-permute-start(bf16[256,512]{1,0:T(8,128)(2,1)S(1)} %bitcast.22), channel_id=1, source_target_pairs={{0,256},{16,272},{32,288},{48,304},{256,0},{272,16},{288,32},{304,... | collective-permute-start | bytes 786440 | tf_op jit(solution)/shard_map/ppermute | solution.py:249
  31.4 15.5 %collective-permute-start.2 = (bf16[256,512]{1,0:T(8,128)(2,1)S(1)}, bf16[256,512]{1,0:T(8,128)(2,1)S(1)}, u32[]{:S(2)}, u32[]{:S(2)}) collective-permute-start(bf16[256,512]{1,0:T(8,128)(2,1)S(1)} %collective-permute-done.1.refs_1_), channel_id=1, source_target_pairs={{0,8},{8,0},{1,9},{9,1},{2,10},{10,2},{3,11},{11,3},{4,12},{12,4},... | collective-permute-start | bytes 786440 | tf_op jit(solution)/shard_map/ppermute | solution.py:24
  37.0 20.8 %copy-start = (bf16[1,128,512]{2,1,0:T(8,128)(2,1)S(1)}, bf16[1,128,512]{2,1,0:T(8,128)(2,1)}, u32[]{:S(2)}) copy-start(bf16[1,128,512]{2,1,0:T(8,128)(2,1)} %param.8) | copy-start | bytes 393220
  37.0 20.8 %copy-start.1 = (bf16[1,128,512]{2,1,0:T(8,128)(2,1)S(1)}, bf16[1,128,512]{2,1,0:T(8,128)(2,1)}, u32[]{:S(2)}) copy-start(bf16[1,128,512]{2,1,0:T(8,128)(2,1)} %param.7) | copy-start | bytes 393220
  37.0 18.9 %collective-permute-start.7 = (bf16[512,512]{1,0:T(8,128)(2,1)}, bf16[512,512]{1,0:T(8,128)(2,1)S(1)}, u32[]{:S(2)}, u32[]{:S(2)}) collective-permute-start(bf16[512,512]{1,0:T(8,128)(2,1)} %pad_maximum_fusion), channel_id=1, source_target_pairs={{0,32},{16,48},{32,256},{48,272},{256,288},{272,304},{288,0},{304,... | collective-permute-start | bytes 1572872 | tf_op jit(solution)/shard_map/ppermute | solution.py:249
  46.8 1.1 copy-start.3
  46.8 1.1 copy-start.5
  47.9 19.1 %collective-permute-start.4 = (bf16[8,16,2048]{2,1,0:T(8,128)(2,1)}, bf16[8,16,2048]{2,1,0:T(8,128)(2,1)S(1)}, u32[]{:S(2)}, u32[]{:S(2)}) collective-permute-start(bf16[8,16,2048]{2,1,0:T(8,128)(2,1)} %get-tuple-element.39), channel_id=1, source_target_pairs={{7,0},{0,1},{1,2},{2,3},{3,4},{4,5},{5,6},{6,7},{15,8},{8,9},{9,10... | collective-permute-start | bytes 1572872 | tf_op jit(solution)/shard_map/ppermute | solution.py:242
  50.2 16.8 %collective-permute-start.5 = (bf16[8,16,2048]{2,1,0:T(8,128)(2,1)}, bf16[8,16,2048]{2,1,0:T(8,128)(2,1)S(1)}, u32[]{:S(2)}, u32[]{:S(2)}) collective-permute-start(bf16[8,16,2048]{2,1,0:T(8,128)(2,1)} %get-tuple-element.38), channel_id=1, source_target_pairs={{1,0},{2,1},{3,2},{4,3},{5,4},{6,5},{7,6},{0,7},{9,8},{10,9},{11,1... | collective-permute-start | bytes 1572872 | tf_op jit(solution)/shard_map/ppermute | solution.py:242
  55.9 11.2 %collective-permute-start.8 = (bf16[512,512]{1,0:T(8,128)(2,1)S(1)}, bf16[512,512]{1,0:T(8,128)(2,1)}, u32[]{:S(2)}, u32[]{:S(2)}) collective-permute-start(bf16[512,512]{1,0:T(8,128)(2,1)S(1)} %collective-permute-done.7.refs_4_), channel_id=1, source_target_pairs={{0,8},{8,0},{1,9},{9,1},{2,10},{10,2},{3,11},{11,3},{4,12},{12,4},... | collective-permute-start | bytes 1572872 | tf_op jit(solution)/shard_map/ppermute | solution.py:24
  57.8 9.2 %collective-permute-start.6 = (bf16[128,512]{1,0:T(8,128)(2,1)S(1)}, bf16[128,512]{1,0:T(8,128)(2,1)}, u32[]{:S(2)}, u32[]{:S(2)}) collective-permute-start(bf16[128,512]{1,0:T(8,128)(2,1)S(1)} %multiply_convert_fusion.mixed_ref), channel_id=1, source_target_pairs={{0,8},{8,16},{16,24},{24,32},{32,40},{40,48},{48,56},{56,64},{64,7... | collective-permute-start | bytes 393224 | tf_op jit(solution)/shard_map/ppermute | solution.py:35
  67.0 1.0 copy-start.4
  68.0 0.9 copy-start.6
  72.0 4.4 %copy-start.8 = (bf16[32,128]{1,0:T(8,128)(2,1)S(1)}, bf16[32,128]{1,0:T(8,128)(2,1)}, u32[]{:S(2)}) copy-start(bf16[32,128]{1,0:T(8,128)(2,1)} %filters_ref.3) | copy-start | bytes 24580
  72.0 13.6 %all-to-all-start.1 = ((bf16[4,128,512]{2,1,0:T(8,128)(2,1)}), bf16[4,128,512]{2,1,0:T(8,128)(2,1)S(1)}, u32[]{:S(2)}, u32[]{:S(2)}) async-start(bf16[4,128,512]{2,1,0:T(8,128)(2,1)} %bitcast.13), calls=%async_computation.1 | async-start | bytes 1048576 | tf_op jit(solution)/shard_map/all_to_all | solution.py:237
  76.5 9.1 %copy-start.7 = (bf16[1,128,512]{2,1,0:T(8,128)(2,1)S(1)}, bf16[1,128,512]{2,1,0:T(8,128)(2,1)}, u32[]{:S(2)}) copy-start(bf16[1,128,512]{2,1,0:T(8,128)(2,1)} %param.6) | copy-start | bytes 393220
  98.1 16.2 %all-to-all-start.3 = ((f32[8,32,128]{2,1,0:T(8,128)}), f32[8,32,128]{2,1,0:T(8,128)S(1)}, u32[]{:S(2)}, u32[]{:S(2)}) async-start(f32[8,32,128]{2,1,0:T(8,128)} %sums.1), calls=%async_computation.3 | async-start | bytes 262144 | tf_op jit(solution)/shard_map/all_to_all | solution.py:237
  103.9 8.0 %collective-permute-start.9 = (bf16[128,512]{1,0:T(8,128)(2,1)S(1)}, bf16[128,512]{1,0:T(8,128)(2,1)S(1)}, u32[]{:S(2)}, u32[]{:S(2)}) collective-permute-start(bf16[128,512]{1,0:T(8,128)(2,1)S(1)} %get-tuple-element.35.grad_ref), channel_id=1, source_target_pairs={{8,0},{16,8},{24,16},{32,24},{40,32},{48,40},{56,48},{64,56},{72,6... | collective-permute-start | bytes 393224 | tf_op jit(solution)/shard_map/ppermute | solution.py:35
